TPU v7x, 32 devices: a whole 2x2x4 slice. The times are simulated.
32 devices in a mesh: ctx: 8 (over y, x, core), tp: 4 (over z).
Axes of the slice: x: 2, y: 2, z: 4, core: 2. Of those that a mesh axis runs over, the one named last changes fastest.
Arguments:
- upstream: bfloat16 [2048, 5120], P('ctx', 'tp'), may hold values from -6 to 6
- advantage: float32 [2048], P('ctx'), may hold values from -4 to 4
- out_weight: bfloat16 [8192, 5120], P('tp'), may hold values from -0.078125 to 0.078125
- query_heads: bfloat16 [2048, 8192], P('ctx', 'tp'), may hold values from -4 to 4
- key_heads: bfloat16 [2048, 1024], P('ctx', 'tp'), may hold values from -4 to 4
- value_heads: bfloat16 [2048, 1024], P('ctx', 'tp'), may hold values from -4 to 4
- segment_ids: int32 [2048], replicated, may hold values from 0 to 8, as said below
- tile_mask: int32 [16, 16], P('ctx'), may hold values from 0 to 1, as said below
Outputs:
- grad_queries: bfloat16 [2048, 8192], P('ctx', 'tp')
- grad_keys: bfloat16 [2048, 1024], P('ctx', 'tp')
- grad_values: bfloat16 [2048, 1024], P('ctx', 'tp')
Inputs may be any that keep to these rules, and one draw needn't show every extreme that they name: `segment_ids`: the first 1024 tokens carry 0; after them come 8 runs carrying the numbers 1 to 8 in some order; run k (counted from 0) begins within 64 tokens of 1024 + k * 128, the first exactly at 1024. `tile_mask`: ones only where the key tile is not after the query tile; every tile lying wholly within the first 1024 tokens is marked for all query tiles at or after it; a marked key tile after the prompt begins no more than 384 tokens before the first token of the run that holds the query tile's first token.
All inputs are finite; a program needn't handle non-finite values.
Results may differ from a plain program's by a relative error of at most 0.0076.
Values may be sent and summed in bfloat16 or wider, within the bound.
No kernel may reach another device: no remote copies, remote signals or barrier semaphores. Data moves between devices by JAX's collectives and lax.ppermute only.
A program may use at most 128 MiB of HBM per device.

v0:
```python
import math

import jax
import jax.numpy as jnp
from jax import lax
from jax.sharding import PartitionSpec as P

HEADS = 64
KV_HEADS = 8
HD = 128
TILE = 128


HIGHEST = lax.Precision.HIGHEST


def visible_block(seg_rows, seg_all, tile_rows, row_start, col_start, span):
    row_count = seg_rows.shape[0]
    query_pos = row_start + jnp.arange(row_count, dtype=jnp.int32)
    key_pos = col_start + jnp.arange(span, dtype=jnp.int32)
    seg_cols = lax.dynamic_slice_in_dim(seg_all, col_start, span, 0)
    tile_cols = lax.dynamic_slice_in_dim(tile_rows, col_start // TILE, span // TILE, 1)
    tile_full = jnp.repeat(jnp.repeat(tile_cols, TILE, axis=0), TILE, axis=1)
    return (key_pos[None, :] <= query_pos[:, None]) & (
        (seg_rows[:, None] == seg_cols[None, :]) | (tile_full == 1)
    )


def head_scores(query_rows, key_block, tiled_mask, scale):
    product = (
        lax.dot_general(
            query_rows, key_block, (((1,), (1,)), ((), ())), preferred_element_type=jnp.float32
        )
        * scale
    )
    return jnp.where(tiled_mask, product, -1e30)


def backward_terms(group_data, col_start, span, visible, share, scale):
    query_rows, grad_rows, key_group, value_group, log_total, delta = group_data
    key_block = lax.dynamic_slice_in_dim(key_group, col_start, span, 0)
    value_block = lax.dynamic_slice_in_dim(value_group, col_start, span, 0)
    tiled_mask = jnp.tile(visible, (share, 1))
    scores = head_scores(query_rows, key_block, tiled_mask, scale)
    probs = jnp.where(tiled_mask, jnp.exp(scores - log_total[:, None]), 0.0)
    dprobs = lax.dot_general(
        grad_rows, value_block, (((1,), (1,)), ((), ())), preferred_element_type=jnp.float32
    )
    dscores = (probs * (dprobs - delta[:, None])).astype(jnp.bfloat16)
    return (key_block, probs.astype(jnp.bfloat16), dscores)


def key_terms(group_data, probs_low, dscores):
    query_rows, grad_rows = (group_data[0], group_data[1])
    key_part = lax.dot_general(
        dscores, query_rows, (((0,), (0,)), ((), ())), preferred_element_type=jnp.float32
    )
    value_part = lax.dot_general(
        probs_low, grad_rows, (((0,), (0,)), ((), ())), preferred_element_type=jnp.float32
    )
    return jnp.stack([key_part, value_part], axis=1)


def shards(
    upstream, advantage, out_weight, query_heads, key_heads, value_heads, segment_ids, tile_mask
):
    tok_rows = query_heads.shape[0]
    total_rows = tok_rows * lax.axis_size("ctx")
    row_start = lax.axis_index("ctx") * tok_rows
    share = HEADS // KV_HEADS
    groups = key_heads.shape[1] // HD
    scale = 1.0 / math.sqrt(HD)
    width = 4 * TILE
    block_count = total_rows // width
    projected = lax.dot_general(
        lax.all_gather(upstream, "tp", axis=1, tiled=True),
        out_weight,
        (((1,), (1,)), ((), ())),
        preferred_element_type=jnp.float32,
    )
    grad_heads = (projected * advantage[:, None]).astype(jnp.bfloat16)
    key_all, value_all = (
        lax.all_gather(key_heads, "ctx", axis=0, tiled=True),
        lax.all_gather(value_heads, "ctx", axis=0, tiled=True),
    )
    seg_rows = lax.dynamic_slice_in_dim(segment_ids, row_start, tok_rows, 0)

    def mask_for(col_start, span):
        return visible_block(seg_rows, segment_ids, tile_mask, row_start, col_start, span)

    query_four = query_heads.reshape(tok_rows, groups, share, HD)
    grad_four = grad_heads.reshape(tok_rows, groups, share, HD)
    saved = []
    query_out = []
    partial_groups = []
    stacked_rows = share * tok_rows
    for group_index in range(groups):
        query_rows = query_four[:, group_index].transpose(1, 0, 2).reshape(stacked_rows, HD)
        grad_rows = grad_four[:, group_index].transpose(1, 0, 2).reshape(stacked_rows, HD)
        key_group = key_all[:, group_index * HD : (group_index + 1) * HD]
        value_group = value_all[:, group_index * HD : (group_index + 1) * HD]

        def forward_step(block_index, state_now):
            col_start = block_index * width
            visible = mask_for(col_start, width)

            def forward_compute(unused):
                running_max, running_sum, accumulate = state_now
                key_block = lax.dynamic_slice_in_dim(key_group, col_start, width, 0)
                value_block = lax.dynamic_slice_in_dim(value_group, col_start, width, 0).astype(
                    jnp.float32
                )
                tiled_mask = jnp.tile(visible, (share, 1))
                scores = head_scores(query_rows, key_block, tiled_mask, scale)
                new_max = jnp.maximum(running_max, jnp.max(scores, axis=1))
                probs = jnp.where(tiled_mask, jnp.exp(scores - new_max[:, None]), 0.0)
                decay = jnp.exp(running_max - new_max)
                return (
                    new_max,
                    running_sum * decay + jnp.sum(probs, axis=1),
                    accumulate * decay[:, None] + jnp.dot(probs, value_block, precision=HIGHEST),
                )

            return lax.cond(jnp.any(visible), forward_compute, lambda unused: state_now, 0)

        start_state = (
            jnp.full((stacked_rows,), -1e30, jnp.float32),
            jnp.zeros((stacked_rows,), jnp.float32),
            jnp.zeros((stacked_rows, HD), jnp.float32),
        )
        running_max, running_sum, accumulate = lax.fori_loop(
            0, block_count, forward_step, start_state
        )
        log_total = running_max + jnp.log(running_sum)
        attn_out = accumulate / running_sum[:, None]
        delta = jnp.sum(grad_rows.astype(jnp.float32) * attn_out, axis=1)
        group_data = (query_rows, grad_rows, key_group, value_group, log_total, delta)
        saved.append(group_data)

        def joint_step(block_index, state_now):
            col_start = block_index * width
            visible = mask_for(col_start, width)

            def joint_compute(unused):
                query_acc, partial_value = state_now
                key_block, probs_low, dscores = backward_terms(
                    group_data, col_start, width, visible, share, scale
                )
                query_acc = query_acc + jnp.dot(
                    dscores, key_block, preferred_element_type=jnp.float32
                )
                partial_value = lax.dynamic_update_slice_in_dim(
                    partial_value, key_terms(group_data, probs_low, dscores), col_start, 0
                )
                return (query_acc, partial_value)

            return lax.cond(jnp.any(visible), joint_compute, lambda unused: state_now, 0)

        query_acc, partial_value = lax.fori_loop(
            0,
            block_count,
            joint_step,
            (
                jnp.zeros((stacked_rows, HD), jnp.float32),
                jnp.zeros((total_rows, 2, HD), jnp.float32),
            ),
        )
        partial_groups.append(partial_value)
        query_out.append(
            (query_acc * scale)
            .reshape(share, tok_rows, HD)
            .transpose(1, 0, 2)
            .reshape(tok_rows, share * HD)
        )
    partial_all = jnp.concatenate(partial_groups, axis=2)
    key_grads = lax.psum_scatter(partial_all, "ctx", scatter_dimension=0, tiled=True)
    grad_queries = jnp.concatenate(query_out, axis=1).astype(jnp.bfloat16)
    grad_keys = (key_grads[:, 0] * scale).astype(jnp.bfloat16)
    grad_values = key_grads[:, 1].astype(jnp.bfloat16)
    return (grad_queries, grad_keys, grad_values)


def solution(mesh):
    placed = (
        P("ctx", "tp"),
        P("ctx"),
        P("tp", None),
        P("ctx", "tp"),
        P("ctx", "tp"),
        P("ctx", "tp"),
        P(),
        P("ctx", None),
    )
    return jax.shard_map(
        shards,
        mesh=mesh,
        in_specs=placed,
        out_specs=(P("ctx", "tp"), P("ctx", "tp"), P("ctx", "tp")),
        check_vma=False,
    )
```

profile of v0, /device:TPU:10, one launch (start us, length us, event | category | flops | bytes accessed | tf_op | source)
XLA Modules:
  0.0 326.7 jit_solution(12908882461013047073)
XLA Ops:
  10.2 1.4 copy.45
  12.8 21.8 %all-gather.4.cloned.1.call-done = bf16[2048,256]{1,0:T(8,128)(2,1)} async-done(((bf16[256,256]{1,0:T(8,128)(2,1)}), bf16[2048,256]{1,0:T(8,128)(2,1)}) %all-gather.4.cloned.1.call-update) | async-done | bytes 1048592 | tf_op jit(solution)/shard_map/all_gather | solution.py:83
  34.6 1.3 fusion.69
  35.8 24.1 %all-gather.6.cloned.1.call-done = bf16[2048,256]{1,0:T(8,128)(2,1)} async-done(((bf16[256,256]{1,0:T(8,128)(2,1)}), bf16[2048,256]{1,0:T(8,128)(2,1)}) %all-gather.6.cloned.1.call-update) | async-done | bytes 1048592 | tf_op jit(solution)/shard_map/all_gather | solution.py:84
  60.0 2.1 fusion.67
  62.1 26.5 %while.74 = (s32[]{:T(128)}, f32[2048]{0:T(1024)S(1)}, f32[2048]{0:T(1024)S(1)}, f32[2048,128]{1,0:T(8,128)S(1)}, s32[]{:T(128)}, /*index=5*/s32[256]{0:T(256)S(...) while((s32[]{:T(128)}, f32[2048]{0:T(1024)S(1)}, ...), condition=%wide.region_19.20_spmd, body=%wide.region_13.19_spmd.sunk | while | flops 1893343488 | bytes 22206152 | solution.py:131
  64.1 9.3 %conditional.10 = ((f32[2048]{0:T(1024)S(1)}, f32[2048]{0:T(1024)S(1)}, f32[2048,128]{1,0:T(8,128)S(1)})) conditional(s32[]{:T(128)} %convert_element_type.104, (f32[2048]{0:T(1024)S(1)}, f32[2048]{0:T(1024)S(1)}, f32[2048,128]{1,0:T(8,128)S(1)}) %tuple.189, (s32[]{:T(128)}, s32[1,512]{1,0:T(1,128)S(1)}, s32[256]{0:T(256)S(1)}, s32[256]{0:T(256)S(1)}, ...), branch_computations={%region_15.15_spmd, %region_16.18_spmd} | conditional | flops 1892685312 | bytes 22167630 | solution.py:124
  65.5 1.9 fusion.31
  67.4 1.2 fusion.32
  68.7 4.6 %convolution_add_fusion.2 = f32[2048,128]{1,0:T(8,128)S(1)} fusion(pred[2048,512]{0,1:T(8,128)(4,1)S(1)} %bitcast.223, f32[512,2048]{1,0:T(8,128)S(1)} %get-tuple-element.1670, f32[2048]{0:T(1024)S(1)} %max.5, f32[2048,128]{1,0:T(8,128)S(1)} %get-tuple-element.1401, f32[2048]{0:T(1024)S(1)} %get-tuple-element.1666, ...), kind=kOutput, calls=%fused_computation.62 | convolution fusion | flops 1615331328 | bytes 7487492 | tf_op jit(solution)/shard_map/while/body/eval_jaxpr/cond/branch_1_fun/dot_general | solution.py:121
  75.3 9.3 %conditional.10 = ((f32[2048]{0:T(1024)S(1)}, f32[2048]{0:T(1024)S(1)}, f32[2048,128]{1,0:T(8,128)S(1)})) conditional(s32[]{:T(128)} %convert_element_type.104, (f32[2048]{0:T(1024)S(1)}, f32[2048]{0:T(1024)S(1)}, f32[2048,128]{1,0:T(8,128)S(1)}) %tuple.189, (s32[]{:T(128)}, s32[1,512]{1,0:T(1,128)S(1)}, s32[256]{0:T(256)S(1)}, s32[256]{0:T(256)S(1)}, ...), branch_computations={%region_15.15_spmd, %region_16.18_spmd} | conditional | flops 1892685312 | bytes 22167630 | solution.py:124
  76.7 1.9 fusion.31
  78.7 1.2 fusion.32
  79.9 4.6 %convolution_add_fusion.2 = f32[2048,128]{1,0:T(8,128)S(1)} fusion(pred[2048,512]{0,1:T(8,128)(4,1)S(1)} %bitcast.223, f32[512,2048]{1,0:T(8,128)S(1)} %get-tuple-element.1670, f32[2048]{0:T(1024)S(1)} %max.5, f32[2048,128]{1,0:T(8,128)S(1)} %get-tuple-element.1401, f32[2048]{0:T(1024)S(1)} %get-tuple-element.1666, ...), kind=kOutput, calls=%fused_computation.62 | convolution fusion | flops 1615331328 | bytes 7487492 | tf_op jit(solution)/shard_map/while/body/eval_jaxpr/cond/branch_1_fun/dot_general | solution.py:121
  89.7 25.5 %while.72 = (s32[]{:T(128)}, f32[2048]{0:T(1024)S(1)}, f32[2048]{0:T(1024)S(1)}, f32[2048,128]{1,0:T(8,128)S(1)}, s32[]{:T(128)}, /*index=5*/s32[256]{0:T(256)S(...) while((s32[]{:T(128)}, f32[2048]{0:T(1024)S(1)}, ...), condition=%wide.region_6.7_spmd, body=%wide.region_0.6_spmd.sunk | while | flops 1893343488 | bytes 22206152 | solution.py:131
  91.6 9.1 %conditional.8 = ((f32[2048]{0:T(1024)S(1)}, f32[2048]{0:T(1024)S(1)}, f32[2048,128]{1,0:T(8,128)S(1)})) conditional(s32[]{:T(128)} %convert_element_type.102, (f32[2048]{0:T(1024)S(1)}, f32[2048]{0:T(1024)S(1)}, f32[2048,128]{1,0:T(8,128)S(1)}) %tuple.183, (s32[]{:T(128)}, s32[1,512]{1,0:T(1,128)S(1)}, s32[256]{0:T(256)S(1)}, s32[256]{0:T(256)S(1)}, ...), branch_computations={%region_2.2_spmd, %region_3.5_spmd} | conditional | flops 1892685312 | bytes 22167630 | solution.py:124
  93.9 1.2 fusion.1
  95.2 5.6 %convolution_add_fusion = f32[2048,128]{1,0:T(8,128)S(1)} fusion(pred[2048,512]{0,1:T(8,128)(4,1)S(1)} %bitcast.226, f32[512,2048]{1,0:T(8,128)S(1)} %get-tuple-element.1668, f32[2048]{0:T(1024)S(1)} %max.4, f32[2048,128]{1,0:T(8,128)S(1)} %get-tuple-element.1344, f32[2048]{0:T(1024)S(1)} %get-tuple-element.1664, bf16[2048,128]{1,0:T(8,128)(2,1)} %get-tuple-element.1345, ...), kind=kOutput, calls=%fused_computation.3 | convolution fusion | flops 1615331328 | bytes 7487492 | tf_op jit(solution)/shard_map/while/body/eval_jaxpr/cond/branch_1_fun/dot_general | solution.py:121
  102.5 9.1 %conditional.8 = ((f32[2048]{0:T(1024)S(1)}, f32[2048]{0:T(1024)S(1)}, f32[2048,128]{1,0:T(8,128)S(1)})) conditional(s32[]{:T(128)} %convert_element_type.102, (f32[2048]{0:T(1024)S(1)}, f32[2048]{0:T(1024)S(1)}, f32[2048,128]{1,0:T(8,128)S(1)}) %tuple.183, (s32[]{:T(128)}, s32[1,512]{1,0:T(1,128)S(1)}, s32[256]{0:T(256)S(1)}, s32[256]{0:T(256)S(1)}, ...), branch_computations={%region_2.2_spmd, %region_3.5_spmd} | conditional | flops 1892685312 | bytes 22167630 | solution.py:124
  104.8 1.2 fusion.1
  106.1 5.6 %convolution_add_fusion = f32[2048,128]{1,0:T(8,128)S(1)} fusion(pred[2048,512]{0,1:T(8,128)(4,1)S(1)} %bitcast.226, f32[512,2048]{1,0:T(8,128)S(1)} %get-tuple-element.1668, f32[2048]{0:T(1024)S(1)} %max.4, f32[2048,128]{1,0:T(8,128)S(1)} %get-tuple-element.1344, f32[2048]{0:T(1024)S(1)} %get-tuple-element.1664, bf16[2048,128]{1,0:T(8,128)(2,1)} %get-tuple-element.1345, ...), kind=kOutput, calls=%fused_computation.3 | convolution fusion | flops 1615331328 | bytes 7487492 | tf_op jit(solution)/shard_map/while/body/eval_jaxpr/cond/branch_1_fun/dot_general | solution.py:121
  115.3 11.4 %fusion.63 = bf16[32,8,16,128]{3,1,2,0:T(8,128)(2,1)S(1)} fusion(bf16[256,5120]{1,0:T(8,128)(2,1)} %all-gather.8.cloned.1.call-done, bf16[2048,5120]{1,0:T(8,128)(2,1)} %param.26, f32[256]{0:T(256)S(1)} %copy-done.6), kind=kOutput, calls=%fused_computation.121 | convolution fusion | flops 5369757696 | bytes 24642560 | tf_op jit(solution)/shard_map/dot_general | solution.py:75
  127.9 1.5 broadcast.411.clone
  129.4 27.2 %while.75 = (s32[]{:T(128)}, f32[2048,128]{1,0:T(8,128)S(1)}, f32[2048,2,128]{2,0,1:T(8,128)}, s32[]{:T(128)}, s32[256]{0:T(256)S(1)}, /*index=5*/s32[2048]{0:T(...) while((s32[]{:T(128)}, f32[2048,128]{1,0:T(8,128)S(1)}, ...), condition=%wide.region_25.26_spmd, body=%wide.region_21.25_spmd.sunk | while | flops 1352143104 | bytes 29562592 | solution.py:159
  131.3 9.7 %conditional.11 = ((f32[2048,128]{1,0:T(8,128)S(1)}, f32[2048,2,128]{2,0,1:T(8,128)})) conditional(s32[]{:T(128)} %convert_element_type.105, (f32[2048,128]{1,0:T(8,128)S(1)}, f32[2048,2,128]{2,0,1:T(8,128)}) %tuple.192, (s32[]{:T(128)}, s32[1,512]{1,0:T(1,128)S(1)}, s32[256]{0:T(256)S(1)}, s32[256]{0:T(256)S(1)}, s32[512]{0:T(512)S(1)}, ...), branch_computations={%region_23.23_spmd, %region_24.24_spmd} | conditional | flops 1351484928 | bytes 29524046 | solution.py:157
  132.7 2.4 fusion.49
  135.8 1.6 fusion.46
  137.5 1.8 convolution_bitcast_fusion.1
  142.9 9.7 %conditional.11 = ((f32[2048,128]{1,0:T(8,128)S(1)}, f32[2048,2,128]{2,0,1:T(8,128)})) conditional(s32[]{:T(128)} %convert_element_type.105, (f32[2048,128]{1,0:T(8,128)S(1)}, f32[2048,2,128]{2,0,1:T(8,128)}) %tuple.192, (s32[]{:T(128)}, s32[1,512]{1,0:T(1,128)S(1)}, s32[256]{0:T(256)S(1)}, s32[256]{0:T(256)S(1)}, s32[512]{0:T(512)S(1)}, ...), branch_computations={%region_23.23_spmd, %region_24.24_spmd} | conditional | flops 1351484928 | bytes 29524046 | solution.py:157
  144.3 2.4 fusion.49
  147.5 1.6 fusion.46
  149.1 1.8 convolution_bitcast_fusion.1
  156.6 1.9 multiply_reduce_fusion.1
  158.5 1.5 broadcast.411.clone.1
  160.0 26.2 %while.73 = (s32[]{:T(128)}, f32[2048,128]{1,0:T(8,128)S(1)}, f32[2048,2,128]{2,0,1:T(8,128)}, s32[]{:T(128)}, s32[256]{0:T(256)S(1)}, /*index=5*/s32[2048]{0:T(...) while((s32[]{:T(128)}, f32[2048,128]{1,0:T(8,128)S(1)}, ...), condition=%wide.region_12.13_spmd, body=%wide.region_8.12_spmd.sunk | while | flops 1352143104 | bytes 29562592 | solution.py:159
  161.8 9.4 %conditional.9 = ((f32[2048,128]{1,0:T(8,128)S(1)}, f32[2048,2,128]{2,0,1:T(8,128)})) conditional(s32[]{:T(128)} %convert_element_type.103, (f32[2048,128]{1,0:T(8,128)S(1)}, f32[2048,2,128]{2,0,1:T(8,128)}) %tuple.186, (s32[]{:T(128)}, s32[1,512]{1,0:T(1,128)S(1)}, s32[256]{0:T(256)S(1)}, s32[256]{0:T(256)S(1)}, s32[512]{0:T(512)S(1)}, ...), branch_computations={%region_10.10_spmd, %region_11.11_spmd} | conditional | flops 1351484928 | bytes 29524046 | solution.py:157
  163.2 2.3 fusion.18
  166.2 1.6 fusion.15
  168.6 1.8 convolution_add_fusion.1
  173.1 9.4 %conditional.9 = ((f32[2048,128]{1,0:T(8,128)S(1)}, f32[2048,2,128]{2,0,1:T(8,128)})) conditional(s32[]{:T(128)} %convert_element_type.103, (f32[2048,128]{1,0:T(8,128)S(1)}, f32[2048,2,128]{2,0,1:T(8,128)}) %tuple.186, (s32[]{:T(128)}, s32[1,512]{1,0:T(1,128)S(1)}, s32[256]{0:T(256)S(1)}, s32[256]{0:T(256)S(1)}, s32[512]{0:T(512)S(1)}, ...), branch_computations={%region_10.10_spmd, %region_11.11_spmd} | conditional | flops 1351484928 | bytes 29524046 | solution.py:157
  174.4 2.3 fusion.18
  177.4 1.6 fusion.15
  179.8 1.8 convolution_add_fusion.1
  186.2 4.5 %pad_maximum_fusion = f32[2048,2,256]{2,0,1:T(8,128)} fusion(f32[2048,2,128]{2,0,1:T(8,128)} %get-tuple-element.1470, f32[2048,2,128]{2,0,1:T(8,128)} %get-tuple-element.1469), kind=kLoop, calls=%fused_computation.118 | loop fusion | flops 1048576 | bytes 8388608 | tf_op jit(solution)/shard_map/concatenate | solution.py:175
  191.8 1.1 pad_maximum_fusion.1
  192.8 124.0 %reduce-scatter.2.cloned.1.call-done = f32[256,2,256]{2,0,1:T(8,128)} async-done(((f32[2048,2,256]{2,0,1:T(8,128)}), f32[256,2,256]{2,0,1:T(8,128)}) %reduce-scatter.2.cloned.1.call-update) | async-done | bytes 524304 | tf_op jit(solution)/shard_map/reduce_scatter | solution.py:176
  316.9 1.6 fusion.66
  318.5 1.6 fusion.65
  (282 shorter events, 48.5 us)
Async XLA Ops:
  7.2 5.5 %copy-start.5 = (s32[2048]{0:T(1024)S(1)}, s32[2048]{0:T(1024)}, u32[]{:S(2)}) copy-start(s32[2048]{0:T(1024)} %param.30) | copy-start | bytes 24580
  7.2 27.4 %all-gather.4.cloned.1.call-start = ((), (), s32[]{:S(2)}) async-start(), calls=%async_computation.1 | async-start | bytes 1179648 | tf_op jit(solution)/shard_map/all_gather | solution.py:83
  7.9 52.1 %all-gather.6.cloned.1.call-start = ((), (), s32[]{:S(2)}) async-start(), calls=%async_computation.2 | async-start | bytes 1179648 | tf_op jit(solution)/shard_map/all_gather | solution.py:84
  8.7 106.6 %all-gather.8.cloned.1.call-start = ((), (), s32[]{:S(2)}) async-start(), calls=%async_computation.3 | async-start | bytes 3276800 | tf_op jit(solution)/shard_map/all_gather | solution.py:76
  9.4 307.5 %reduce-scatter.2.cloned.1.call-start = ((), (), s32[]{:S(2)}) async-start(), calls=%async_computation.4 | async-start | bytes 4718592 | tf_op jit(solution)/shard_map/reduce_scatter | solution.py:176
  88.6 0.8 copy-start.2
  88.6 1.0 copy-start.4
  89.7 25.6 %copy-start.6 = (f32[256]{0:T(256)S(1)}, f32[256]{0:T(256)}, u32[]{:S(2)}) copy-start(f32[256]{0:T(256)} %param.25) | copy-start | bytes 3076
  115.2 11.4 %copy-start = (f32[2048,128]{1,0:T(8,128)}, f32[2048,128]{1,0:T(8,128)S(1)}, u32[]{:S(2)}) copy-start(f32[2048,128]{1,0:T(8,128)S(1)} %get-tuple-element.1463) | copy-start | bytes 3145732
  115.2 11.4 %copy-start.1 = (bf16[2048,128]{1,0:T(8,128)(2,1)}, bf16[2048,128]{1,0:T(8,128)(2,1)S(1)}, u32[]{:S(2)}) copy-start(bf16[2048,128]{1,0:T(8,128)(2,1)S(1)} %get-tuple-element.2270) | copy-start | bytes 1572868
  126.9 2.4 copy-start.3
Sparse Core Ops, SparseCore 0:
  9.9 24.6 all-gather.3
  36.4 23.4 all-gather.5
  61.5 52.9 all-gather.7
  190.8 126.0 reduce-scatter.1
where the time goes:
time: 330 us; the launch traced here: 327 us
  waiting for transfers between devices  172 us (52%)
  matrix products  66.6 us (20%)
  other arithmetic  35.1 us (11%)
  local copies, waits for them, and re-layouts  26.4 us (8%)
  between operations  14.1 us (4%)
  loops' own time  12.3 us (4%)
    reduce_scatter x1, waiting for transfers between devices, shards(): lax.psum_scatter(partial_all, 'ctx', scatter_dimension=0, tiled=True)  124 us
    all_gather x1, waiting for transfers between devices, shards(): lax.all_gather(value_heads, 'ctx', axis=0, tiled=True)  24.1 us
    all_gather x1, waiting for transfers between devices, shards(): lax.all_gather(key_heads, 'ctx', axis=0, tiled=True)  21.8 us
    dot_general x4, matrix products, forward_compute(): jnp.dot(probs, value_block, precision=HIGHEST)  20.4 us
    dot_general x8, matrix products, head_scores(): lax.dot_general(query_rows, key_block, (((1,), (1,)), ((), ())), preferre...  15 us
    dot_general x1, matrix products, shards(): lax.dot_general(lax.all_gather(upstream, 'tp', axis=1, tiled=True), out_w...  11.4 us
    reduce_or x8, other arithmetic, joint_step(): jnp.any(visible)  7.52 us
    reduce_or x8, other arithmetic, forward_step(): jnp.any(visible)  7.39 us
  transfers between devices with their start and end apart: 4, of which 3 were waited for; matrix products, arithmetic and copies ran while one was open for 17% of the time, Pallas kernels for 0%

commit v1 on v0

v1 whole, which is shorter than its diff:
```python
import functools
import math

import jax
import jax.numpy as jnp
from jax import lax
from jax.experimental import pallas as pl
from jax.experimental.pallas import tpu as pltpu
from jax.sharding import PartitionSpec as P

HEADS = 64
KV_HEADS = 8
SHARE = HEADS // KV_HEADS
HD = 128
TILE = 128
ROLLOUTS = 8
JITTER = 64
KB = 256
SCALE = 1.0 / math.sqrt(HD)
LOG2E = 1.4426950408889634
F32 = jnp.float32
BF16 = jnp.bfloat16
NT = (((1,), (1,)), ((), ()))


def dot(a, b):
    return jnp.dot(a, b, preferred_element_type=F32)


def dot_nt(a, b):
    return lax.dot_general(a, b, NT, preferred_element_type=F32)


def probs_kernel(n_kb, slot_ref, q_ref, k_ref, v_ref, bias_ref, p_ref, o_ref, s_ref):
    q = q_ref[...]
    top = None
    for kb in range(n_kb):
        s = dot_nt(k_ref[slot_ref[kb]], q) * (SCALE * LOG2E) + bias_ref[kb]
        s_ref[kb] = s
        m = jnp.max(s, axis=0, keepdims=True)
        top = m if top is None else jnp.maximum(top, m)
    total = jnp.zeros_like(top)
    for kb in range(n_kb):
        e = jnp.exp2(s_ref[kb] - top)
        s_ref[kb] = e
        total += jnp.sum(e, axis=0, keepdims=True)
    inv = 1.0 / total
    low = jnp.zeros_like(top)
    acc = jnp.zeros((HD, q.shape[0]), F32)
    for kb in range(n_kb):
        p = (s_ref[kb] * inv).astype(BF16)
        p_ref[0, kb] = p
        low += jnp.sum(p.astype(F32), axis=0, keepdims=True)
        acc += dot(v_ref[slot_ref[kb]].T, p)
    o_ref[...] = (acc * (1.0 / low)).T


def probs_call(slots, q, kv, bias, groups, n_kb):
    rows = q.shape[0]
    rb = rows // KB
    n_slot = kv.shape[0]
    return pl.pallas_call(
        functools.partial(probs_kernel, n_kb),
        grid_spec=pltpu.PrefetchScalarGridSpec(
            num_scalar_prefetch=1,
            grid=(groups, SHARE, rb),
            in_specs=[
                pl.BlockSpec((KB, HD), lambda g, h, r, s: (r, g * SHARE + h)),
                pl.BlockSpec((n_slot, KB, HD), lambda g, h, r, s: (0, 0, g)),
                pl.BlockSpec((n_slot, KB, HD), lambda g, h, r, s: (0, 0, groups + g)),
                pl.BlockSpec((n_kb, KB, KB), lambda g, h, r, s: (0, 0, r)),
            ],
            out_specs=[
                pl.BlockSpec((1, n_kb, KB, KB), lambda g, h, r, s: (g, 0, 0, h * rb + r)),
                pl.BlockSpec((KB, HD), lambda g, h, r, s: (r, g * SHARE + h)),
            ],
            scratch_shapes=[pltpu.VMEM((n_kb, KB, KB), F32)],
        ),
        out_shape=[
            jax.ShapeDtypeStruct((groups, n_kb, KB, SHARE * rows), BF16),
            jax.ShapeDtypeStruct((rows, groups * SHARE * HD), F32),
        ],
        compiler_params=pltpu.CompilerParams(vmem_limit_bytes=48 << 20),
        cost_estimate=pl.CostEstimate(
            flops=4 * groups * SHARE * rows * n_kb * KB * HD,
            bytes_accessed=groups * SHARE * rows * n_kb * KB * 2,
            transcendentals=groups * SHARE * rows * n_kb * KB,
        ),
    )(slots, q, kv, kv, bias)


def back_kernel(
    n_kb, slot_ref, live_ref, proj_ref, adv_ref, o_ref, q_ref, k_ref, v_ref, p_ref,
    dq_ref, dkv_ref, dox_ref, qs_ref, ds_ref, dqt_ref,
):
    kb = pl.program_id(1)
    rows = proj_ref.shape[0]

    @pl.when(kb == 0)
    def _():
        dqt_ref[...] = jnp.zeros_like(dqt_ref)
        lane = lax.broadcasted_iota(jnp.int32, (rows, HD), 1)
        for h in range(SHARE):
            cols = pl.ds(h * HD, HD)
            here = pl.ds(h * rows, rows)
            grad = (proj_ref[:, cols] * adv_ref[...]).astype(BF16)
            delta = jnp.sum(grad.astype(F32) * o_ref[:, cols], axis=1, keepdims=True)
            one = delta.astype(BF16).astype(F32)
            two = (delta - one).astype(BF16).astype(F32)
            three = delta - one - two
            ext = jnp.where(
                lane == 0, one, jnp.where(lane == 1, two, jnp.where(lane == 2, three, 0.0))
            )
            dox_ref[here, :HD] = grad
            dox_ref[here, HD:] = ext.astype(BF16)
            qs_ref[here, :] = q_ref[:, cols]

    @pl.when(live_ref[kb] != 0)
    def _():
        lane = lax.broadcasted_iota(jnp.int32, (KB, HD), 1)
        ext = jnp.where(lane < 3, -1.0, 0.0).astype(BF16)
        vx = jnp.concatenate([v_ref[0], ext], axis=1)
        kt = k_ref[0].T
        for h in range(SHARE * rows // KB):
            here = pl.ds(h * KB, KB)
            dp = dot_nt(vx, dox_ref[here, :])
            ds_ref[:, here] = (p_ref[0, 0, :, here].astype(F32) * dp).astype(BF16)
        dkv_ref[0, 0] = dot(ds_ref[...], qs_ref[...]).astype(dkv_ref.dtype)
        dkv_ref[0, 1] = dot(p_ref[0, 0], dox_ref[:, :HD]).astype(dkv_ref.dtype)
        dqt_ref[...] += dot(kt, ds_ref[...])

    @pl.when(live_ref[kb] == 0)
    def _():
        dkv_ref[...] = jnp.zeros_like(dkv_ref)

    @pl.when(kb == n_kb - 1)
    def _():
        for h in range(SHARE):
            dq_ref[:, h * HD : (h + 1) * HD] = (
                (dqt_ref[:, h * rows : (h + 1) * rows] * SCALE).T.astype(BF16)
            )


def back_call(slots, live, proj, adv, o, q, kv, p, groups, n_kb, part_dtype):
    rows = q.shape[0]
    wide = SHARE * HD
    return pl.pallas_call(
        functools.partial(back_kernel, n_kb),
        grid_spec=pltpu.PrefetchScalarGridSpec(
            num_scalar_prefetch=2,
            grid=(groups, n_kb),
            in_specs=[
                pl.BlockSpec((rows, wide), lambda g, b, s, e: (0, g)),
                pl.BlockSpec((rows, 1), lambda g, b, s, e: (0, 0)),
                pl.BlockSpec((rows, wide), lambda g, b, s, e: (0, g)),
                pl.BlockSpec((rows, wide), lambda g, b, s, e: (0, g)),
                pl.BlockSpec((1, KB, HD), lambda g, b, s, e: (s[b], 0, g)),
                pl.BlockSpec((1, KB, HD), lambda g, b, s, e: (s[b], 0, groups + g)),
                pl.BlockSpec((1, 1, KB, SHARE * rows), lambda g, b, s, e: (g, b, 0, 0)),
            ],
            out_specs=[
                pl.BlockSpec((rows, wide), lambda g, b, s, e: (0, g)),
                pl.BlockSpec((1, 2, KB, HD), lambda g, b, s, e: (b, 0, 0, g)),
            ],
            scratch_shapes=[
                pltpu.VMEM((SHARE * rows, 2 * HD), BF16),
                pltpu.VMEM((SHARE * rows, HD), BF16),
                pltpu.VMEM((KB, SHARE * rows), BF16),
                pltpu.VMEM((HD, SHARE * rows), F32),
            ],
        ),
        out_shape=[
            jax.ShapeDtypeStruct((rows, groups * wide), BF16),
            jax.ShapeDtypeStruct((n_kb, 2, KB, groups * HD), part_dtype),
        ],
        compiler_params=pltpu.CompilerParams(vmem_limit_bytes=48 << 20),
        cost_estimate=pl.CostEstimate(
            flops=10 * groups * SHARE * rows * n_kb * KB * HD,
            bytes_accessed=groups * SHARE * rows * n_kb * KB * 2,
            transcendentals=0,
        ),
    )(slots, live, proj, adv, o, q, kv, kv, p)


def project_kernel(count, shard_ref, *refs):
    xs, ws, out_ref = refs[:count], refs[count : 2 * count], refs[-1]
    acc = dot_nt(xs[0][...], ws[0][...])
    for x, w in zip(xs[1:], ws[1:]):
        acc += dot_nt(x[...], w[...])
    out_ref[...] = acc


def project_last_kernel(shard_ref, acc_ref, c_ref, d_ref, w_ref, out_ref):
    out_ref[...] = acc_ref[...] + dot_nt(c_ref[...] + d_ref[...], w_ref[...])


def project_call(shards_of, xs, weight):
    rows, depth = xs[0].shape
    wide = weight.shape[0]
    block = 512
    count = len(xs)
    return pl.pallas_call(
        functools.partial(project_kernel, count),
        grid_spec=pltpu.PrefetchScalarGridSpec(
            num_scalar_prefetch=1,
            grid=(wide // block,),
            in_specs=[pl.BlockSpec((rows, depth), lambda n, s: (0, 0))] * count
            + [pl.BlockSpec((block, depth), lambda n, s, i=i: (n, s[i])) for i in range(count)],
            out_specs=pl.BlockSpec((rows, block), lambda n, s: (0, n)),
        ),
        out_shape=jax.ShapeDtypeStruct((rows, wide), F32),
        compiler_params=pltpu.CompilerParams(vmem_limit_bytes=48 << 20),
        cost_estimate=pl.CostEstimate(
            flops=2 * rows * wide * depth * count,
            bytes_accessed=2 * wide * depth * count,
            transcendentals=0,
        ),
    )(shards_of, *xs, *([weight] * count))


def project_last_call(shards_of, acc, c, d, weight):
    rows, depth = c.shape
    wide = weight.shape[0]
    block = 512
    return pl.pallas_call(
        project_last_kernel,
        grid_spec=pltpu.PrefetchScalarGridSpec(
            num_scalar_prefetch=1,
            grid=(wide // block,),
            in_specs=[
                pl.BlockSpec((rows, block), lambda n, s: (0, n)),
                pl.BlockSpec((rows, depth), lambda n, s: (0, 0)),
                pl.BlockSpec((rows, depth), lambda n, s: (0, 0)),
                pl.BlockSpec((block, depth), lambda n, s: (n, s[0])),
            ],
            out_specs=pl.BlockSpec((rows, block), lambda n, s: (0, n)),
        ),
        out_shape=jax.ShapeDtypeStruct((rows, wide), F32),
        compiler_params=pltpu.CompilerParams(vmem_limit_bytes=48 << 20),
        cost_estimate=pl.CostEstimate(
            flops=2 * rows * wide * depth, bytes_accessed=2 * wide * depth, transcendentals=0
        ),
    )(shards_of, acc, c, d, weight)


def key_window(tok_rows, total):
    span = (total - total // 2) // ROLLOUTS
    reach = 3 * span + TILE + JITTER
    reach = reach // TILE * TILE
    return -(-reach // tok_rows)


def shards(
    upstream, advantage, out_weight, query_heads, key_heads, value_heads, segment_ids, tile_mask
):
    rows = query_heads.shape[0]
    n_ctx = lax.axis_size("ctx")
    n_tp = lax.axis_size("tp")
    total = rows * n_ctx
    prompt = total // 2
    groups = key_heads.shape[1] // HD
    me = lax.axis_index("ctx")
    z = lax.axis_index("tp")
    per = rows // KB
    back = key_window(rows, total)
    prompt_kb = prompt // KB
    n_kb = prompt_kb + (back + 1) * per
    fast = n_ctx == 8 and n_tp == 4 and per == 1 and back == 2
    part_dtype = BF16

    own = jnp.concatenate([key_heads, value_heads], axis=1)

    def hop(value, pairs):
        return lax.ppermute(value, "tp", pairs)

    def flip(value, bit, pairs=None):
        return lax.ppermute(value, "ctx", pairs or [(i, i ^ bit) for i in range(n_ctx)])

    if fast:
        near = jnp.stack([own] + [flip(own, d) for d in (2, 4, 6)])
        far = flip(near, 1)
        kv = jnp.stack([near, far], axis=1).reshape(n_ctx, rows, 2 * groups * HD)
        up_b = hop(upstream, [(0, 2), (2, 0), (1, 3), (3, 1)])
        up_a = hop(upstream, [(0, 1), (1, 0), (2, 3), (3, 2)])
        up_c = hop(upstream, [(1, 2), (2, 1)])
        up_d = hop(up_b, [(1, 0), (2, 3)])
    else:
        kv = lax.all_gather(own, "ctx", axis=0)

    row_start = me * rows
    behind = me - back
    roll = row_start >= prompt
    win_start = jnp.maximum(behind * rows, 0)
    win = (back + 1) * rows
    pos = jnp.concatenate(
        [jnp.arange(prompt, dtype=jnp.int32), win_start + jnp.arange(win, dtype=jnp.int32)]
    )
    seg_k = jnp.concatenate(
        [segment_ids[:prompt], lax.dynamic_slice_in_dim(segment_ids, win_start, win, 0)]
    )
    seg_q = lax.dynamic_slice_in_dim(segment_ids, row_start, rows, 0)
    marks = jnp.concatenate(
        [
            tile_mask[:, : prompt // TILE],
            lax.dynamic_slice_in_dim(tile_mask, win_start // TILE, win // TILE, 1),
        ],
        axis=1,
    )
    marks = jnp.repeat(jnp.repeat(marks.T, TILE, axis=0), TILE, axis=1) == 1
    query_pos = row_start + jnp.arange(rows, dtype=jnp.int32)
    counted = (jnp.arange(prompt + win) < prompt) | (roll & (pos >= prompt))
    visible = (
        (pos[:, None] <= query_pos[None, :])
        & ((seg_k[:, None] == seg_q[None, :]) | marks)
        & counted[:, None]
    )
    bias = jnp.where(visible, 0.0, -1e30).astype(F32).reshape(n_kb, KB, rows)
    live = jnp.any(visible.reshape(n_kb, KB * rows), axis=1).astype(jnp.int32)
    block = jnp.arange(n_kb, dtype=jnp.int32)
    holder = jnp.where(
        block < prompt_kb,
        block // per,
        jnp.where(roll, behind + (block - prompt_kb) // per, me),
    )
    slot = (holder ^ me) if fast else holder
    slots = (slot * per + block % per).astype(jnp.int32)
    kv = kv.reshape(n_ctx * per, KB, 2 * groups * HD)

    probs, attn = probs_call(slots, query_heads, kv, bias, groups, n_kb)

    if fast:
        three = jnp.stack([z, z ^ 1, z ^ 2]).astype(jnp.int32)
        acc = project_call(three, [upstream, up_a, up_b], out_weight)
        last = (z ^ 3).astype(jnp.int32)[None]
        proj = project_last_call(last, acc, up_c, up_d, out_weight)
    else:
        proj = lax.dot_general(
            lax.all_gather(upstream, "tp", axis=1, tiled=True), out_weight, NT,
            preferred_element_type=F32,
        )

    grad_queries, part = back_call(
        slots, live, proj, advantage[:, None], attn, query_heads, kv, probs, groups, n_kb,
        part_dtype,
    )

    if fast:
        core = me & 1
        side = (me >> 1) & 1
        pick = lambda i: lax.dynamic_index_in_dim(part, i, 0, keepdims=False)
        sent = jnp.stack([pick(1 - core), pick(3 - core), part[prompt_kb + 1]])
        got = flip(sent, 1).astype(F32)
        sums = jnp.stack([pick(core), pick(core + 2)]).astype(F32) + got[:2]
        here = lax.dynamic_index_in_dim(sums, side, 0, keepdims=False)
        there = lax.dynamic_index_in_dim(sums, 1 - side, 0, keepdims=False)
        older = part[prompt_kb].astype(F32) + jnp.where(core == 1, got[2], 0.0)
        mine = part[prompt_kb + 2].astype(F32) + jnp.where(core == 0, got[2], 0.0)
        low = there.astype(BF16)
        by_y = flip(here.astype(BF16), 4, [(4, 0), (5, 1), (6, 2), (7, 3)])
        by_d = flip(low, 6, [(4, 2), (5, 3), (6, 0), (7, 1)])
        by_x = flip(
            jnp.where(roll, older.astype(BF16), low), 2,
            [(0, 2), (2, 0), (1, 3), (3, 1), (6, 4), (7, 5)],
        )
        grads = (
            jnp.where(roll, mine, here)
            + by_x.astype(F32) + by_y.astype(F32) + by_d.astype(F32)
        )
        grad_keys, grad_values = grads[0], grads[1]
    else:
        width = groups * HD
        front = part[:prompt_kb].astype(F32).transpose(0, 2, 1, 3).reshape(prompt, 2, width)
        rear = part[prompt_kb:].astype(F32).transpose(0, 2, 1, 3).reshape(win, 2, width)
        whole = jnp.zeros((total, 2, width), F32).at[:prompt].set(front)
        old = lax.dynamic_slice_in_dim(whole, win_start, win, 0)
        whole = lax.dynamic_update_slice_in_dim(whole, old + rear, win_start, 0)
        reduced = lax.psum_scatter(whole, "ctx", scatter_dimension=0, tiled=True)
        grad_keys, grad_values = reduced[:, 0], reduced[:, 1]
    return (grad_queries, (grad_keys * SCALE).astype(BF16), grad_values.astype(BF16))


def solution(mesh):
    placed = (
        P("ctx", "tp"),
        P("ctx"),
        P("tp", None),
        P("ctx", "tp"),
        P("ctx", "tp"),
        P("ctx", "tp"),
        P(),
        P("ctx", None),
    )
    return jax.shard_map(
        shards,
        mesh=mesh,
        in_specs=placed,
        out_specs=(P("ctx", "tp"), P("ctx", "tp"), P("ctx", "tp")),
        check_vma=False,
    )
```

time: 330 us -> 130 us (0.39)
  the two profiles are of different devices: /device:TPU:10 before, /device:TPU:0 now
where the time goes in v1:
time: 130 us; the launch traced here: 129 us
  Pallas kernels  54.2 us (42%)
  waiting for transfers between devices  27.4 us (21%)
  starting transfers between devices  19.5 us (15%)
  local copies, waits for them, and re-layouts  14 us (11%)
  other arithmetic  12.8 us (10%)
    pallas_call x1, Pallas kernels, probs_call(): pl.pallas_call(functools.partial(probs_kernel, n_kb), grid_spec=pltpu.Pre...  23.7 us
    ppermute x8, waiting for transfers between devices, flip(): lax.ppermute(value, 'ctx', pairs or [(i, i ^ bit) for i in range(n_ctx)])  21.3 us
    pallas_call x1, Pallas kernels, back_call(): pl.pallas_call(functools.partial(back_kernel, n_kb), grid_spec=pltpu.Pref...  17.1 us
    ppermute x8, starting transfers between devices, flip(): lax.ppermute(value, 'ctx', pairs or [(i, i ^ bit) for i in range(n_ctx)])  11.9 us
    pallas_call x1, Pallas kernels, project_call(): pl.pallas_call(functools.partial(project_kernel, count), grid_spec=pltpu....  8.78 us
    ppermute x4, starting transfers between devices, hop(): return lax.ppermute(value, 'tp', pairs)  7.65 us
    ppermute x4, waiting for transfers between devices, hop(): return lax.ppermute(value, 'tp', pairs)  6.06 us
    pallas_call x1, Pallas kernels, project_last_call(): pl.pallas_call(project_last_kernel, grid_spec=pltpu.PrefetchScalarGridSpe...  4.61 us
  transfers between devices with their start and end apart: 12, of which 7 were waited for; matrix products, arithmetic and copies ran while one was open for 14% of the time, Pallas kernels for 25%

profile of v1, /device:TPU:0, one launch (start us, length us, event | category | flops | bytes accessed | tf_op | source)
XLA Modules:
  0.0 128.9 jit_solution(15765530799809238292)
XLA Ops:
  0.6 3.1 %collective-permute-start = (bf16[256,1280]{1,0:T(8,128)(2,1)}, bf16[256,1280]{1,0:T(8,128)(2,1)S(1)}, u32[]{:S(2)}, u32[]{:S(2)}) collective-permute-start(bf16[256,1280]{1,0:T(8,128)(2,1)} %refs_0_.1), channel_id=1, source_target_pairs={{0,1},{1,0},{2,3},{3,2},{4,5},{5,4},{6,7},{7,6},{8,9},{9,8},{10,11... | collective-permute-start | bytes 1966088 | tf_op jit(solution)/shard_map/ppermute | solution.py:274
  3.7 2.6 %collective-permute-start.1 = (bf16[256,1280]{1,0:T(8,128)(2,1)}, bf16[256,1280]{1,0:T(8,128)(2,1)S(1)}, u32[]{:S(2)}, u32[]{:S(2)}) collective-permute-start(bf16[256,1280]{1,0:T(8,128)(2,1)} %refs_0_.1), channel_id=1, source_target_pairs={{0,2},{2,0},{1,3},{3,1},{4,6},{6,4},{5,7},{7,5},{8,10},{10,8},{9,1... | collective-permute-start | bytes 1966088 | tf_op jit(solution)/shard_map/ppermute | solution.py:274
  6.3 0.9 constant_dynamic-update-slice_fusion.1
  7.2 0.9 constant_dynamic-update-slice_fusion
  8.2 2.5 %collective-permute-start.6 = (bf16[256,512]{1,0:T(8,128)(2,1)S(1)}, bf16[256,512]{1,0:T(8,128)(2,1)S(1)}, u32[]{:S(2)}, u32[]{:S(2)}) collective-permute-start(bf16[256,512]{1,0:T(8,128)(2,1)S(1)} %constant_dynamic-update-slice_fusion), channel_id=1, source_target_pairs={{0,24},{4,28},{8,16},{12,20},{16,8},{20,12},{24,0},{28,4},{1,25},{... | collective-permute-start | bytes 786440 | tf_op jit(solution)/shard_map/ppermute | solution.py:277
  10.7 0.5 collective-permute-start.5
  11.2 0.5 collective-permute-start.4
  11.7 0.8 dynamic_slice.29
  12.5 0.7 slice.29
  13.2 0.8 dynamic-slice_bitcast_fusion
  14.0 0.8 constant_dynamic-slice_fusion.4
  14.8 0.8 compare_bitcast_fusion
  15.7 0.7 and_reduce_fusion
  16.4 2.0 %collective-permute-done.6 = bf16[256,512]{1,0:T(8,128)(2,1)S(1)} collective-permute-done((bf16[256,512]{1,0:T(8,128)(2,1)S(1)}, bf16[256,512]{1,0:T(8,128)(2,1)S(1)}, u32[]{:S(2)}, u32[]{:S(2)}) %collective-permute-start.6) | collective-permute-done | bytes 262176 | tf_op jit(solution)/shard_map/ppermute | solution.py:277
  18.4 0.7 collective-permute-start.2
  19.1 3.1 %collective-permute-done.5 = bf16[256,512]{1,0:T(8,128)(2,1)S(1)} collective-permute-done((bf16[256,512]{1,0:T(8,128)(2,1)S(1)}, bf16[256,512]{1,0:T(8,128)(2,1)S(1)}, u32[]{:S(2)}, u32[]{:S(2)}) %collective-permute-start.5) | collective-permute-done | bytes 262176 | tf_op jit(solution)/shard_map/ppermute | solution.py:277
  22.3 1.5 %fusion.11 = (bf16[4,1,256,512]{3,2,0,1:T(8,128)(2,1)}, bf16[4,256,512]{2,1,0:T(8,128)(2,1)}) fusion(bf16[1,256,512]{2,1,0:T(8,128)(2,1)S(1)} %bitcast.51, bf16[1,256,512]{2,1,0:T(8,128)(2,1)S(1)} %bitcast.52, bf16[1,256,512]{2,1,0:T(8,128)(2,1)S(1)} %bitcast.53, bf16[1,256,512]{2,1,0:T(8,128)(2,1)S(1)} %bitcast.50), kind=kLoop, calls=%fused_computation.44 | loop fusion | flops 1572864 | bytes 3145728 | tf_op jit(solution)/shard_map/stack | solution.py:282
  23.9 0.8 dynamic_slice.30
  24.7 0.1 reduce_or.18
  24.8 0.1 copy.18.adv_ref
  25.0 0.1 broadcast_in_dim.36
  25.1 1.1 eq.72
  26.2 1.7 %copy.17 = pred[7,256,256]{2,1,0:T(8,128)(4,1)} copy(pred[7,256,256]{1,0,2:T(8,128)(4,1)S(1)} %eq.72) | data formatting | bytes 917504 | tf_op jit(solution)/shard_map/eq | solution.py:309
  27.9 2.6 %and_select_fusion.bias_ref = f32[7,256,256]{2,1,0:T(8,128)S(1)} fusion(pred[7,256,256]{2,1,0:T(8,128)(4,1)} %copy.17, s32[256]{0:T(256)S(1)} %dynamic_slice.30, s32[7,256]{1,0:T(8,128)S(1)} %eq.68, s32[256]{0:T(256)S(1)} %iota_add_fusion.2, s32[7,256]{1,0:T(8,128)S(1)} %le.28, pred[7,256]{1,0:T(8,128)(4,1)S(1)} %fusion.9), kind=kLoop, calls=%fused_computation.1 | loop fusion | flops 2752512 | bytes 2311936 | tf_op jit(solution)/shard_map/jit(_where)/select_n | solution.py:317
  30.5 6.0 %collective-permute-done.1.refs_2_ = bf16[256,1280]{1,0:T(8,128)(2,1)S(1)} collective-permute-done((bf16[256,1280]{1,0:T(8,128)(2,1)}, bf16[256,1280]{1,0:T(8,128)(2,1)S(1)}, u32[]{:S(2)}, u32[]{:S(2)}) %collective-permute-start.1) | collective-permute-done | bytes 655392 | tf_op jit(solution)/shard_map/ppermute | solution.py:274
  36.5 1.3 collective-permute-start.3
  37.8 8.8 %shard_map.103.acc_ref = f32[256,2048]{1,0:T(8,128)S(1)} custom-call(s32[3]{0:T(128)S(1)} %pad_add_fusion.2.shard_ref, bf16[256,1280]{1,0:T(8,128)(2,1)S(1)} %copy-done, bf16[256,1280]{1,0:T(8,128)(2,1)S(1)} %collective-permute-done.refs_1_, bf16[256,1280]{1,0:T(8,128)(2,1)S(1)} %collective-permute-done.1.refs_2_, bf16[2048,5120]{1,0:T(8,128)(2,1)} %w_ref.1, ...), custom_call_target="tpu_custom_call" | custom-call | flops 4026531840 | bytes 15728640 | tf_op jit(solution)/shard_map/pallas_call | solution.py:202
  46.6 1.4 %pad_maximum_fusion = bf16[4,2,256,512]{3,2,0,1:T(8,128)(2,1)S(1)} fusion(bf16[4,1,256,512]{3,2,0,1:T(8,128)(2,1)} %bitcast.12, bf16[4,1,256,512]{3,2,0,1:T(8,128)(2,1)S(1)} %copy-done.3), kind=kLoop, calls=%fused_computation | loop fusion | flops 1048576 | bytes 4194304 | tf_op jit(solution)/shard_map/stack | solution.py:282
  48.1 1.4 %copy.16 = bf16[4,2,256,512]{3,2,1,0:T(8,128)(2,1)} copy(bf16[4,2,256,512]{3,2,0,1:T(8,128)(2,1)S(1)} %pad_maximum_fusion) | data formatting | bytes 4194304 | tf_op jit(solution)/shard_map/stack | solution.py:282
  49.5 0.2 copy-done.1
  49.7 23.7 %shard_map.105 = (bf16[2,7,256,2048]{3,2,1,0:T(8,128)(2,1)}, f32[256,2048]{1,0:T(8,128)S(1)}) custom-call(s32[7]{0:T(128)S(1)} %fusion.10.slot_ref, bf16[256,2048]{1,0:T(8,128)(2,1)S(1)} %copy-done.1, bf16[8,256,512]{2,1,0:T(8,128)(2,1)} %bitcast.46, bf16[8,256,512]{2,1,0:T(8,128)(2,1)} %bitcast.47, f32[7,256,256]{2,1,0:T(8,128)S(1)} %and_select_fusion.bias_ref), custom_call_target="tpu_custom_call" | custom-call | flops 3758096384 | bytes 14680064 | tf_op jit(solution)/shard_map/pallas_call | solution.py:62
  73.4 1.3 %copy-done.2 = f32[256,2048]{1,0:T(8,128)} copy-done((f32[256,2048]{1,0:T(8,128)}, f32[256,2048]{1,0:T(8,128)S(1)}, u32[]{:S(2)}) %copy-start.2) | copy-done | bytes 2097176
  74.7 4.6 %shard_map.104.proj_ref = f32[256,2048]{1,0:T(8,128)S(1)} custom-call(s32[1]{0:T(128)} %bitcast.2.shard_ref, f32[256,2048]{1,0:T(8,128)S(1)} %shard_map.103.acc_ref, bf16[256,1280]{1,0:T(8,128)(2,1)S(1)} %collective-permute-done.2.c_ref, bf16[256,1280]{1,0:T(8,128)(2,1)S(1)} %collective-permute-done.3.d_ref, bf16[2048,5120]{1,0:T(8,128)(2,1)} %w_ref.1), custom_call_target="tpu_custom_call" | custom-call | flops 1342177280 | bytes 5242880 | tf_op jit(solution)/shard_map/pallas_call | solution.py:225
  79.4 17.1 %shard_map.106 = (bf16[256,2048]{1,0:T(8,128)(2,1)}, bf16[7,2,256,256]{3,2,1,0:T(8,128)(2,1)S(1)}) custom-call(s32[7]{0:T(128)S(1)} %fusion.10.slot_ref, s32[7]{0:T(128)S(1)} %convert_element_type.54.live_ref, f32[256,2048]{1,0:T(8,128)S(1)} %shard_map.104.proj_ref, f32[256,1]{1,0:T(8,128)S(1)} %copy.18.adv_ref, f32[256,2048]{1,0:T(8,128)} %copy-done.2, ...), custom_call_target="tpu_custom_call" | custom-call | flops 9395240960 | bytes 14680064 | tf_op jit(solution)/shard_map/pallas_call | solution.py:147
  96.5 0.9 constant_dynamic-slice_fusion.1
  97.6 2.4 %collective-permute-done.8 = bf16[3,2,256,256]{3,2,1,0:T(8,128)(2,1)} collective-permute-done((bf16[3,2,256,256]{3,2,1,0:T(8,128)(2,1)S(1)}, bf16[3,2,256,256]{3,2,1,0:T(8,128)(2,1)}, u32[]{:S(2)}, u32[]{:S(2)}) %collective-permute-start.8) | collective-permute-done | bytes 786464 | tf_op jit(solution)/shard_map/ppermute | solution.py:277
  100.0 1.3 convert_element_type.56
  101.2 1.1 slice_add_fusion
  102.4 1.0 fusion.4
  103.4 1.3 collective-permute-start.11
  104.7 0.7 fusion.2
  105.4 1.3 collective-permute-start.10
  106.7 5.7 %collective-permute-start.9 = (bf16[2,256,256]{2,1,0:T(8,128)(2,1)}, bf16[2,256,256]{2,1,0:T(8,128)(2,1)}, u32[]{:S(2)}, u32[]{:S(2)}) collective-permute-start(bf16[2,256,256]{2,1,0:T(8,128)(2,1)} %get-tuple-element.11), channel_id=1, source_target_pairs={{0,8},{8,0},{4,12},{12,4},{24,16},{28,20},{1,9},{9,1},{5,13},{13,5... | collective-permute-start | bytes 786440 | tf_op jit(solution)/shard_map/ppermute | solution.py:277
  112.4 8.8 %collective-permute-done.11 = bf16[2,256,256]{2,1,0:T(8,128)(2,1)} collective-permute-done((bf16[2,256,256]{2,1,0:T(8,128)(2,1)}, bf16[2,256,256]{2,1,0:T(8,128)(2,1)}, u32[]{:S(2)}, u32[]{:S(2)}) %collective-permute-start.11) | collective-permute-done | bytes 262176 | tf_op jit(solution)/shard_map/ppermute | solution.py:277
  121.2 4.9 %collective-permute-done.10 = bf16[2,256,256]{2,1,0:T(8,128)(2,1)} collective-permute-done((bf16[2,256,256]{2,1,0:T(8,128)(2,1)}, bf16[2,256,256]{2,1,0:T(8,128)(2,1)}, u32[]{:S(2)}, u32[]{:S(2)}) %collective-permute-start.10) | collective-permute-done | bytes 262176 | tf_op jit(solution)/shard_map/ppermute | solution.py:277
  126.1 1.5 %fusion.1 = f32[2,256,256]{2,1,0:T(8,128)S(1)} fusion(bf16[2,256,256]{2,1,0:T(8,128)(2,1)} %collective-permute-done.11, bf16[2,256,256]{2,1,0:T(8,128)(2,1)} %collective-permute-done.10, bf16[2,256,256]{2,1,0:T(8,128)(2,1)} %collective-permute-done.9, f32[3,2,256,256]{3,2,1,0:T(8,128)S(1)} %convert_element_type.56, f32[2,2,256,256]{3,2,1,0:T(8,128)} %copy-done.4, ...), kind=kLoop, calls=%fused_computation.8 | loop fusion | flops 1310720 | bytes 2621446 | tf_op jit(solution)/shard_map/add | solution.py:366
  127.5 0.7 fusion.7
  128.2 0.7 fusion.8
  (40 shorter events, 0.6 us)
Async XLA Ops:
  0.6 37.2 %collective-permute-start = (bf16[256,1280]{1,0:T(8,128)(2,1)}, bf16[256,1280]{1,0:T(8,128)(2,1)S(1)}, u32[]{:S(2)}, u32[]{:S(2)}) collective-permute-start(bf16[256,1280]{1,0:T(8,128)(2,1)} %refs_0_.1), channel_id=1, source_target_pairs={{0,1},{1,0},{2,3},{3,2},{4,5},{5,4},{6,7},{7,6},{8,9},{9,8},{10,11... | collective-permute-start | bytes 1966088 | tf_op jit(solution)/shard_map/ppermute | solution.py:274
  3.7 32.8 %collective-permute-start.1 = (bf16[256,1280]{1,0:T(8,128)(2,1)}, bf16[256,1280]{1,0:T(8,128)(2,1)S(1)}, u32[]{:S(2)}, u32[]{:S(2)}) collective-permute-start(bf16[256,1280]{1,0:T(8,128)(2,1)} %refs_0_.1), channel_id=1, source_target_pairs={{0,2},{2,0},{1,3},{3,1},{4,6},{6,4},{5,7},{7,5},{8,10},{10,8},{9,1... | collective-permute-start | bytes 1966088 | tf_op jit(solution)/shard_map/ppermute | solution.py:274
  7.2 17.6 %copy-start.5 = (f32[256]{0:T(256)S(1)}, f32[256]{0:T(256)}, u32[]{:S(2)}) copy-start(f32[256]{0:T(256)} %param.9) | copy-start | bytes 3076
  8.2 10.3 %collective-permute-start.6 = (bf16[256,512]{1,0:T(8,128)(2,1)S(1)}, bf16[256,512]{1,0:T(8,128)(2,1)S(1)}, u32[]{:S(2)}, u32[]{:S(2)}) collective-permute-start(bf16[256,512]{1,0:T(8,128)(2,1)S(1)} %constant_dynamic-update-slice_fusion), channel_id=1, source_target_pairs={{0,24},{4,28},{8,16},{12,20},{16,8},{20,12},{24,0},{28,4},{1,25},{... | collective-permute-start | bytes 786440 | tf_op jit(solution)/shard_map/ppermute | solution.py:277
  10.7 11.6 %collective-permute-start.5 = (bf16[256,512]{1,0:T(8,128)(2,1)S(1)}, bf16[256,512]{1,0:T(8,128)(2,1)S(1)}, u32[]{:S(2)}, u32[]{:S(2)}) collective-permute-start(bf16[256,512]{1,0:T(8,128)(2,1)S(1)} %constant_dynamic-update-slice_fusion), channel_id=1, source_target_pairs={{0,16},{4,20},{8,24},{12,28},{16,0},{20,4},{24,8},{28,12},{1,17},{... | collective-permute-start | bytes 786440 | tf_op jit(solution)/shard_map/ppermute | solution.py:277
  11.2 11.1 %collective-permute-start.4 = (bf16[256,512]{1,0:T(8,128)(2,1)S(1)}, bf16[256,512]{1,0:T(8,128)(2,1)S(1)}, u32[]{:S(2)}, u32[]{:S(2)}) collective-permute-start(bf16[256,512]{1,0:T(8,128)(2,1)S(1)} %constant_dynamic-update-slice_fusion), channel_id=1, source_target_pairs={{0,8},{4,12},{8,0},{12,4},{16,24},{20,28},{24,16},{28,20},{1,9},{5... | collective-permute-start | bytes 786440 | tf_op jit(solution)/shard_map/ppermute | solution.py:277
  18.4 56.3 %collective-permute-start.2 = (bf16[256,1280]{1,0:T(8,128)(2,1)}, bf16[256,1280]{1,0:T(8,128)(2,1)S(1)}, u32[]{:S(2)}, u32[]{:S(2)}) collective-permute-start(bf16[256,1280]{1,0:T(8,128)(2,1)} %refs_0_.1), channel_id=1, source_target_pairs={{1,2},{2,1},{5,6},{6,5},{9,10},{10,9},{13,14},{14,13},{17,18},{18,... | collective-permute-start | bytes 1966088 | tf_op jit(solution)/shard_map/ppermute | solution.py:274
  23.8 22.8 %collective-permute-start.7 = (bf16[4,256,512]{2,1,0:T(8,128)(2,1)}, bf16[4,256,512]{2,1,0:T(8,128)(2,1)}, u32[]{:S(2)}, u32[]{:S(2)}) collective-permute-start(bf16[4,256,512]{2,1,0:T(8,128)(2,1)} %get-tuple-element.19), channel_id=1, source_target_pairs={{0,4},{4,0},{8,12},{12,8},{16,20},{20,16},{24,28},{28,24},{1,5},{5... | collective-permute-start | bytes 3145736 | tf_op jit(solution)/shard_map/ppermute | solution.py:277
  26.2 11.7 %copy-start = (bf16[256,1280]{1,0:T(8,128)(2,1)S(1)}, bf16[256,1280]{1,0:T(8,128)(2,1)}, u32[]{:S(2)}) copy-start(bf16[256,1280]{1,0:T(8,128)(2,1)} %refs_0_.1) | copy-start | bytes 1966084
  30.5 16.2 %copy-start.3 = (bf16[4,1,256,512]{3,2,0,1:T(8,128)(2,1)S(1)}, bf16[4,1,256,512]{3,2,0,1:T(8,128)(2,1)}, u32[]{:S(2)}) copy-start(bf16[4,1,256,512]{3,2,0,1:T(8,128)(2,1)} %get-tuple-element.18) | copy-start | bytes 3145732
  36.5 38.2 %collective-permute-start.3 = (bf16[256,1280]{1,0:T(8,128)(2,1)S(1)}, bf16[256,1280]{1,0:T(8,128)(2,1)S(1)}, u32[]{:S(2)}, u32[]{:S(2)}) collective-permute-start(bf16[256,1280]{1,0:T(8,128)(2,1)S(1)} %collective-permute-done.1.refs_2_), channel_id=1, source_target_pairs={{1,0},{2,3},{5,4},{6,7},{9,8},{10,11},{13,12},{14,15},{17,16},{18,... | collective-permute-start | bytes 1966088 | tf_op jit(solution)/shard_map/ppermute | solution.py:274
  48.1 1.6 %copy-start.1 = (bf16[256,2048]{1,0:T(8,128)(2,1)S(1)}, bf16[256,2048]{1,0:T(8,128)(2,1)}, u32[]{:S(2)}) copy-start(bf16[256,2048]{1,0:T(8,128)(2,1)} %q_ref.3) | copy-start | bytes 3145732
  73.4 1.3 %copy-start.2 = (f32[256,2048]{1,0:T(8,128)}, f32[256,2048]{1,0:T(8,128)S(1)}, u32[]{:S(2)}) copy-start(f32[256,2048]{1,0:T(8,128)S(1)} %get-tuple-element.7.o_ref) | copy-start | bytes 6291460
  97.5 2.5 %collective-permute-start.8 = (bf16[3,2,256,256]{3,2,1,0:T(8,128)(2,1)S(1)}, bf16[3,2,256,256]{3,2,1,0:T(8,128)(2,1)}, u32[]{:S(2)}, u32[]{:S(2)}) collective-permute-start(bf16[3,2,256,256]{3,2,1,0:T(8,128)(2,1)S(1)} %pad_maximum_fusion.2), channel_id=1, source_target_pairs={{0,4},{4,0},{8,12},{12,8},{16,20},{20,16},{24,28},{28,24},{1,5},{5... | collective-permute-start | bytes 2359304 | tf_op jit(solution)/shard_map/ppermute | solution.py:277
  102.4 2.3 %copy-start.4 = (f32[2,2,256,256]{3,2,1,0:T(8,128)}, f32[2,2,256,256]{3,2,1,0:T(8,128)S(1)}, u32[]{:S(2)}) copy-start(f32[2,2,256,256]{3,2,1,0:T(8,128)S(1)} %slice_add_fusion) | copy-start | bytes 3145732
  103.4 17.8 %collective-permute-start.11 = (bf16[2,256,256]{2,1,0:T(8,128)(2,1)}, bf16[2,256,256]{2,1,0:T(8,128)(2,1)}, u32[]{:S(2)}, u32[]{:S(2)}) collective-permute-start(bf16[2,256,256]{2,1,0:T(8,128)(2,1)} %get-tuple-element.12), channel_id=1, source_target_pairs={{16,8},{20,12},{24,0},{28,4},{17,9},{21,13},{25,1},{29,5},{18,10},... | collective-permute-start | bytes 786440 | tf_op jit(solution)/shard_map/ppermute | solution.py:277
  105.4 20.7 %collective-permute-start.10 = (bf16[2,256,256]{2,1,0:T(8,128)(2,1)}, bf16[2,256,256]{2,1,0:T(8,128)(2,1)}, u32[]{:S(2)}, u32[]{:S(2)}) collective-permute-start(bf16[2,256,256]{2,1,0:T(8,128)(2,1)} %fusion.2), channel_id=1, source_target_pairs={{16,0},{20,4},{24,8},{28,12},{17,1},{21,5},{25,9},{29,13},{18,2},{... | collective-permute-start | bytes 786440 | tf_op jit(solution)/shard_map/ppermute | solution.py:277
  106.7 19.4 %collective-permute-start.9 = (bf16[2,256,256]{2,1,0:T(8,128)(2,1)}, bf16[2,256,256]{2,1,0:T(8,128)(2,1)}, u32[]{:S(2)}, u32[]{:S(2)}) collective-permute-start(bf16[2,256,256]{2,1,0:T(8,128)(2,1)} %get-tuple-element.11), channel_id=1, source_target_pairs={{0,8},{8,0},{4,12},{12,4},{24,16},{28,20},{1,9},{9,1},{5,13},{13,5... | collective-permute-start | bytes 786440 | tf_op jit(solution)/shard_map/ppermute | solution.py:277

commit v2 on v0

v2 whole, which is shorter than its diff:
```python
import functools
import math

import jax
import jax.numpy as jnp
from jax import lax
from jax.experimental import pallas as pl
from jax.experimental.pallas import tpu as pltpu
from jax.sharding import PartitionSpec as P

HEADS = 64
KV_HEADS = 8
SHARE = HEADS // KV_HEADS
HD = 128
TILE = 128
ROLLOUTS = 8
JITTER = 64
KB = 256
VMEM_LIMIT = 24 << 20
SCALE = 1.0 / math.sqrt(HD)
LOG2E = 1.4426950408889634
F32 = jnp.float32
BF16 = jnp.bfloat16
NT = (((1,), (1,)), ((), ()))


def dot(a, b):
    return jnp.dot(a, b, preferred_element_type=F32)


def dot_nt(a, b):
    return lax.dot_general(a, b, NT, preferred_element_type=F32)


SMEM = pl.BlockSpec(memory_space=pltpu.SMEM)
VMEM = pl.BlockSpec(memory_space=pltpu.VMEM)


def at(start, size):
    return pl.ds(pl.multiple_of(start, size), size)


def call(kernel, ins, in_specs, outs, scratch=(), out_specs=None, flops=0, size=0, exps=0):
    return pl.pallas_call(
        kernel,
        in_specs=in_specs,
        out_specs=out_specs or [VMEM] * len(outs),
        out_shape=[jax.ShapeDtypeStruct(shape, dtype) for shape, dtype in outs],
        scratch_shapes=list(scratch),
        compiler_params=pltpu.CompilerParams(vmem_limit_bytes=VMEM_LIMIT),
        cost_estimate=pl.CostEstimate(flops=flops, bytes_accessed=size, transcendentals=exps),
    )(*ins)


def mask_kernel(n_kb, prompt, back, total, me_ref, seg_ref, tile_ref, bias_ref, live_ref):
    rows = bias_ref.shape[2]
    per = rows // KB
    me = me_ref[0]
    row_start = me * rows
    win_kb = jnp.maximum(me - back, 0) * per
    key_at = lax.broadcasted_iota(jnp.int32, (KB, KB), 0)
    query_at = lax.broadcasted_iota(jnp.int32, (KB, KB), 1)
    for kb in range(n_kb):
        window = kb >= prompt // KB
        block = win_kb + (kb - prompt // KB) if window else kb
        key_pos = block * KB + key_at
        seg_k = jnp.broadcast_to(seg_ref[block], (KB, KB)).T
        some = jnp.int32(0)
        for r in range(per):
            same = seg_k == jnp.broadcast_to(seg_ref[me * per + r], (KB, KB))
            for a in range(KB // TILE):
                for b in range(KB // TILE):
                    mark = tile_ref[r * (KB // TILE) + b, block * (KB // TILE) + a]
                    inside = (key_at // TILE == a) & (query_at // TILE == b)
                    same = same | (inside & (jnp.full((KB, KB), mark) == 1))
            seen = same & (key_pos <= row_start + r * KB + query_at)
            if window:
                seen = seen & (key_pos >= prompt) & (jnp.full((KB, KB), me) >= prompt // rows)
            bias_ref[kb, :, r * KB : (r + 1) * KB] = jnp.where(seen, 0.0, -1e30)
            some = jnp.maximum(some, jnp.max(seen.astype(jnp.int32)))
        live_ref[kb] = some


def mask_call(me, segment_ids, tile_mask, rows, n_kb, prompt, back):
    total = segment_ids.shape[0]
    return call(
        functools.partial(mask_kernel, n_kb, prompt, back, total),
        (me[None], segment_ids.reshape(total // KB, 1, KB), tile_mask),
        [SMEM, VMEM, SMEM],
        [((n_kb, KB, rows), F32), ((n_kb,), jnp.int32)],
        out_specs=[VMEM, SMEM],
        size=n_kb * KB * rows * 4,
    )


def probs_kernel(
    n_kb, groups, slot_ref, q_ref, near_ref, far_ref, bias_ref,
    p_ref, o_ref, inv_ref, k_ref, v_ref, kx_ref, vt_ref, s_ref,
):
    rows = q_ref.shape[0]
    per = rows // KB
    n_near = near_ref.shape[0]
    lane = lax.broadcasted_iota(jnp.int32, (KB, HD), 1)
    inv_ref[...] = jnp.zeros_like(inv_ref)
    vt_ref[:, HD:, :] = jnp.ones((groups, 16, n_kb * KB), BF16)
    for kb in range(n_kb):
        slot = slot_ref[kb]
        keys = pl.ds(kb * KB, KB)

        def place(source, index):
            for g in range(groups):
                k_ref[g, keys, :] = source[index, :, g * HD : (g + 1) * HD]
                v_ref[g, keys, :] = source[index, :, (groups + g) * HD : (groups + g + 1) * HD]

        @pl.when(slot < n_near)
        def _():
            place(near_ref, slot)

        @pl.when(slot >= n_near)
        def _():
            place(far_ref, slot - n_near)

    for g in range(groups):
        for kb in range(n_kb):
            keys = pl.ds(kb * KB, KB)
            k = k_ref[g, keys, :]
            kx_ref[g, keys, :HD] = k
            kx_ref[g, keys, HD:] = k
            vt_ref[g, :HD, keys] = v_ref[g, keys, :].T

    def step(i, carry):
        head, r = i // per, i % per
        g, h = head // SHARE, head % SHARE
        cols = at((h * per + r) * KB, KB)
        here = at(r * KB, KB)
        q = q_ref[here, at(head * HD, HD)].astype(F32) * (SCALE * LOG2E)
        q_hi = q.astype(BF16)
        q_lo = (q - q_hi.astype(F32)).astype(BF16)
        qx = jnp.concatenate([q_hi, q_lo], axis=1)
        s_ref[...] = dot_nt(kx_ref[g], qx) + bias_ref[:, :, here].reshape(n_kb * KB, KB)
        top = jnp.max(s_ref[...], axis=0, keepdims=True)
        p_ref[g, :, cols] = jnp.exp2(s_ref[...] - top).astype(BF16)
        acc = dot(vt_ref[g], p_ref[g, :, cols])
        inv = 1.0 / acc[HD : HD + 1, :]
        o_ref[here, at(head * HD, HD)] = (acc[:HD] * inv).T
        inv_ref[here, :] += jnp.where(lane == head, jnp.broadcast_to(inv, (HD, KB)).T, 0.0)
        return carry

    lax.fori_loop(0, groups * SHARE * per, step, 0, unroll=UNROLL)


UNROLL = 2


def probs_call(slots, q, near, far, bias, groups, n_kb):
    rows = q.shape[0]
    keys = n_kb * KB
    return call(
        functools.partial(probs_kernel, n_kb, groups),
        (slots, q, near, far, bias),
        [SMEM, VMEM, VMEM, VMEM, VMEM],
        [
            ((groups, keys, SHARE * rows), BF16),
            ((rows, groups * SHARE * HD), F32),
            ((rows, HD), F32),
            ((groups, keys, HD), BF16),
            ((groups, keys, HD), BF16),
        ],
        scratch=[
            pltpu.VMEM((groups, keys, 2 * HD), BF16),
            pltpu.VMEM((groups, HD + 16, keys), BF16),
            pltpu.VMEM((keys, KB), F32),
        ],
        flops=6 * groups * SHARE * rows * keys * HD,
        size=groups * SHARE * rows * keys * 2,
        exps=groups * SHARE * rows * keys,
    )


def back_kernel(
    n_kb, n_send, first, live_ref, pos_ref, proj_ref, x1_ref, x2_ref, w_ref, adv_ref, o_ref,
    inv_ref, q_ref, k_ref, v_ref, p_ref,
    dq_ref, send_ref, keep_ref, dox_ref, qs_ref, ds_ref, dqt_ref,
):
    rows = proj_ref.shape[0]
    group = first // SHARE
    lane = lax.broadcasted_iota(jnp.int32, (rows, HD), 1)
    minus = jnp.where(lax.broadcasted_iota(jnp.int32, (KB, HD), 1) < 3, -1.0, 0.0).astype(BF16)
    x = x1_ref[...] + x2_ref[...]
    dqt_ref[...] = jnp.zeros_like(dqt_ref)
    for h in range(SHARE):
        head = first + h
        cols = pl.ds(head * HD, HD)
        here = pl.ds(h * rows, rows)
        inv = inv_ref[:, head : head + 1]
        proj = proj_ref[:, cols] + dot_nt(x, w_ref[cols, :])
        grad = (proj * (adv_ref[...] * inv)).astype(BF16)
        delta = jnp.sum(grad.astype(F32) * o_ref[:, cols], axis=1, keepdims=True)
        one = delta.astype(BF16).astype(F32)
        two = (delta - one).astype(BF16).astype(F32)
        three = delta - one - two
        ext = jnp.where(
            lane == 0, one, jnp.where(lane == 1, two, jnp.where(lane == 2, three, 0.0))
        )
        dox_ref[here, :HD] = grad
        dox_ref[here, HD:] = ext.astype(BF16)
        qs_ref[here, :] = q_ref[:, cols]

    def step(kb, carry):
        pos = pos_ref[kb]

        def put(value):
            @pl.when(pos < n_send)
            def _():
                send_ref[pos] = value

            @pl.when(pos >= n_send)
            def _():
                keep_ref[pos - n_send] = value

        @pl.when(live_ref[kb] != 0)
        def _():
            keys = at(kb * KB, KB)
            vx = jnp.concatenate([v_ref[group, keys, :], minus], axis=1)
            kt = k_ref[group, keys, :].T
            dv = dot(p_ref[group, keys, :], dox_ref[:, :HD])
            for h in range(SHARE * rows // KB):
                here = pl.ds(h * KB, KB)
                dp = dot_nt(vx, dox_ref[here, :])
                ds_ref[:, here] = (p_ref[group, keys, here].astype(F32) * dp).astype(BF16)
            dqt_ref[...] += dot(kt, ds_ref[...])
            dk = dot(ds_ref[...], qs_ref[...])
            put(jnp.stack([dk, dv]).astype(BF16))

        @pl.when(live_ref[kb] == 0)
        def _():
            put(jnp.zeros((2, KB, HD), BF16))

        return carry

    lax.fori_loop(0, n_kb, step, 0)
    for h in range(SHARE):
        dq_ref[:, pl.ds(h * HD, HD)] = (
            (dqt_ref[:, h * rows : (h + 1) * rows] * SCALE).T.astype(BF16)
        )


def back_call(group, live, pos, proj, x1, x2, w, adv, o, inv, q, k, v, p, n_kb, n_send):
    rows = q.shape[0]
    wide = SHARE * HD
    return call(
        functools.partial(back_kernel, n_kb, n_send, group * SHARE),
        (live, pos, proj, x1, x2, w, adv, o, inv, q, k, v, p),
        [SMEM, SMEM] + [VMEM] * 11,
        [
            ((rows, wide), BF16),
            ((max(n_send, 1), 2, KB, HD), BF16),
            ((n_kb - n_send, 2, KB, HD), BF16),
        ],
        scratch=[
            pltpu.VMEM((SHARE * rows, 2 * HD), BF16),
            pltpu.VMEM((SHARE * rows, HD), BF16),
            pltpu.VMEM((KB, SHARE * rows), BF16),
            pltpu.VMEM((HD, SHARE * rows), F32),
        ],
        flops=10 * SHARE * rows * n_kb * KB * HD,
        size=SHARE * rows * n_kb * KB * 2,
    )


def middle_kernel(me_ref, got_ref, keep_ref, base_ref, x_ref, y_ref, d_ref):
    me = me_ref[0]
    core, side, roll = me & 1, (me >> 1) & 1, me >= 4
    here = keep_ref[side].astype(F32) + got_ref[side].astype(F32)
    there = keep_ref[1 - side].astype(F32) + got_ref[1 - side].astype(F32)
    y_ref[...] = here.astype(BF16)
    d_ref[...] = there.astype(BF16)
    got = got_ref[2].astype(F32)
    late = (jnp.full(got.shape, core) == 1)

    @pl.when(roll)
    def _():
        x_ref[...] = (keep_ref[2].astype(F32) + jnp.where(late, got, 0.0)).astype(BF16)
        base_ref[...] = keep_ref[3].astype(F32) + jnp.where(late, 0.0, got)

    @pl.when(jnp.logical_not(roll))
    def _():
        x_ref[...] = there.astype(BF16)
        base_ref[...] = here


def last_kernel(groups, *refs):
    dk_ref, dv_ref = refs[-2:]
    for g in range(groups):
        base, x, y, d = refs[4 * g : 4 * g + 4]
        total = base[...] + x[...].astype(F32) + y[...].astype(F32) + d[...].astype(F32)
        dk_ref[:, g * HD : (g + 1) * HD] = (total[0] * SCALE).astype(BF16)
        dv_ref[:, g * HD : (g + 1) * HD] = total[1].astype(BF16)


def project_kernel(shard_ref, *refs):
    out_ref = refs[-1]
    pairs = (len(refs) - 1) // 2
    acc = dot_nt(refs[0][...], refs[pairs][...])
    for i in range(1, pairs):
        acc += dot_nt(refs[i][...], refs[pairs + i][...])
    out_ref[...] = acc


def project_add_kernel(shard_ref, acc_ref, *refs):
    project_kernel(shard_ref, *refs)
    refs[-1][...] += acc_ref[...]


def project_call(shards_of, xs, weight, acc=None):
    rows, depth = xs[0].shape
    wide = weight.shape[0]
    block = 512
    count = len(xs)
    tile = pl.BlockSpec((rows, block), lambda n, s: (0, n))
    return pl.pallas_call(
        project_kernel if acc is None else project_add_kernel,
        grid_spec=pltpu.PrefetchScalarGridSpec(
            num_scalar_prefetch=1,
            grid=(wide // block,),
            in_specs=([] if acc is None else [tile])
            + [pl.BlockSpec((rows, depth), lambda n, s: (0, 0))] * count
            + [pl.BlockSpec((block, depth), lambda n, s, i=i: (n, s[i])) for i in range(count)],
            out_specs=tile,
        ),
        out_shape=jax.ShapeDtypeStruct((rows, wide), F32),
        compiler_params=pltpu.CompilerParams(vmem_limit_bytes=VMEM_LIMIT),
        cost_estimate=pl.CostEstimate(
            flops=2 * rows * wide * depth * count,
            bytes_accessed=2 * wide * depth * count,
            transcendentals=0,
        ),
    )(shards_of, *([] if acc is None else [acc]), *xs, *([weight] * count))


def key_window(tok_rows, total):
    span = (total - total // 2) // ROLLOUTS
    reach = 3 * span + TILE + JITTER
    reach = reach // TILE * TILE
    return -(-reach // tok_rows)


def shards(
    upstream, advantage, out_weight, query_heads, key_heads, value_heads, segment_ids, tile_mask
):
    rows = query_heads.shape[0]
    n_ctx = lax.axis_size("ctx")
    n_tp = lax.axis_size("tp")
    total = rows * n_ctx
    prompt = total // 2
    groups = key_heads.shape[1] // HD
    me = lax.axis_index("ctx").astype(jnp.int32)
    z = lax.axis_index("tp").astype(jnp.int32)
    per = rows // KB
    back = key_window(rows, total)
    prompt_kb = prompt // KB
    n_kb = prompt_kb + (back + 1) * per
    fast = n_ctx == 8 and n_tp == 4 and per == 1 and back == 2
    own = jnp.concatenate([key_heads, value_heads], axis=1)

    def hop(value, pairs):
        return lax.ppermute(value, "tp", pairs)

    def flip(value, bit, pairs=None):
        return lax.ppermute(value, "ctx", pairs or [(i, i ^ bit) for i in range(n_ctx)])

    if fast:
        near = jnp.stack([own] + [flip(own, d) for d in (2, 4, 6)])
        far = flip(near, 1)
        up_b = hop(upstream, [(0, 2), (2, 0), (1, 3), (3, 1)])
        up_a = hop(upstream, [(0, 1), (1, 0), (2, 3), (3, 2)])
        up_c = hop(upstream, [(1, 2), (2, 1)])
        up_d = hop(up_b, [(1, 0), (2, 3)])
    else:
        near = lax.all_gather(own, "ctx", axis=0)
        near = far = near.reshape(n_ctx * per, KB, 2 * groups * HD)

    bias, live = mask_call(me, segment_ids, tile_mask, rows, n_kb, prompt, back)
    block = jnp.arange(n_kb, dtype=jnp.int32)
    holder = jnp.where(
        block < prompt_kb,
        block // per,
        jnp.where(me * rows >= prompt, me - back + (block - prompt_kb) // per, me),
    )
    if fast:
        away = holder ^ me
        slots = away // 2 + (away % 2) * 4
        core = me & 1
        pos = jnp.where(
            block < 4,
            jnp.where(block % 2 == core, 3 + block // 2, block // 2),
            jnp.array([0, 0, 0, 0, 5, 2, 6], jnp.int32),
        )
        n_send = 3
        x1, x2, shard = up_c, up_d, z ^ 3
        first = project_call(z[None], [upstream], out_weight)
        acc = project_call(jnp.stack([z ^ 1, z ^ 2]), [up_a, up_b], out_weight, first)
    else:
        slots = holder * per + block % per
        pos = block
        n_send = 0
        whole = lax.all_gather(upstream, "tp", axis=0)
        shard = z
        acc = jnp.zeros((rows, out_weight.shape[0]), F32)
        for i in range(n_tp - 1):
            other = (z + 1 + i) % n_tp
            x = lax.dynamic_index_in_dim(whole, other, 0, keepdims=False)
            acc = project_call(other[None], [x], out_weight, acc)
        x1, x2 = upstream, jnp.zeros_like(upstream)
    depth = upstream.shape[1]
    w_last = lax.dynamic_slice_in_dim(out_weight, shard * depth, depth, 1)

    probs, attn, inv, keys, values = probs_call(
        slots.astype(jnp.int32), query_heads, near, far, bias, groups, n_kb
    )
    outs = [
        back_call(
            g, live, pos.astype(jnp.int32), acc, x1, x2, w_last, advantage[:, None], attn, inv,
            query_heads, keys, values, probs, n_kb, n_send,
        )
        for g in range(groups)
    ]
    grad_queries = jnp.concatenate([dq for dq, _, _ in outs], axis=1)

    if fast:
        final = []
        shape = (2, KB, HD)
        for _, send, keep in outs:
            base, to_x, to_y, to_d = call(
                middle_kernel,
                (me[None], flip(send, 1), keep),
                [SMEM, VMEM, VMEM],
                [(shape, F32), (shape, BF16), (shape, BF16), (shape, BF16)],
            )
            by_y = flip(to_y, 4, [(4, 0), (5, 1), (6, 2), (7, 3)])
            by_d = flip(to_d, 6, [(4, 2), (5, 3), (6, 0), (7, 1)])
            by_x = flip(to_x, 2, [(0, 2), (2, 0), (1, 3), (3, 1), (6, 4), (7, 5)])
            final += [base, by_x, by_y, by_d]
        grad_keys, grad_values = call(
            functools.partial(last_kernel, groups),
            final,
            [VMEM] * len(final),
            [((rows, groups * HD), BF16)] * 2,
        )
        return grad_queries, grad_keys, grad_values

    win = (back + 1) * rows
    win_start = jnp.maximum(me - back, 0) * rows
    part = jnp.concatenate([keep for _, _, keep in outs], axis=3).astype(F32)
    part = part.transpose(0, 2, 1, 3).reshape(prompt + win, 2, groups * HD)
    full = jnp.zeros((total, 2, groups * HD), F32).at[:prompt].set(part[:prompt])
    old = lax.dynamic_slice_in_dim(full, win_start, win, 0)
    full = lax.dynamic_update_slice_in_dim(full, old + part[prompt:], win_start, 0)
    reduced = lax.psum_scatter(full, "ctx", scatter_dimension=0, tiled=True)
    return (
        grad_queries,
        (reduced[:, 0] * SCALE).astype(BF16),
        reduced[:, 1].astype(BF16),
    )


def solution(mesh):
    placed = (
        P("ctx", "tp"),
        P("ctx"),
        P("tp", None),
        P("ctx", "tp"),
        P("ctx", "tp"),
        P("ctx", "tp"),
        P(),
        P("ctx", None),
    )
    return jax.shard_map(
        shards,
        mesh=mesh,
        in_specs=placed,
        out_specs=(P("ctx", "tp"), P("ctx", "tp"), P("ctx", "tp")),
        check_vma=False,
    )
```

time: 330 us -> 118 us (0.36)
  waiting for transfers between devices: 172 us -> 16.1 us
  matrix products: 66.6 us -> 0 us
  Pallas kernels: 0 us -> 51.2 us
  other arithmetic: 35.1 us -> 3.06 us
  starting transfers between devices: 0.15 us -> 27.1 us
  between operations: 14.1 us -> 0.94 us
  loops' own time: 12.3 us -> 0 us
  local copies, waits for them, and re-layouts: 26.4 us -> 18.9 us
    reduce_scatter x1 -> x0, waiting for transfers between devices: 124 us -> none  [shards(): lax.psum_scatter(partial_all, 'ctx', scatter_dimension=0, tiled=True)]
    dot_general x29 -> x0, matrix products: 66.6 us -> none  [the longest x4 20.4 us: forward_compute(): jnp.dot(probs, value_block, precision=HIGHEST)]
    pallas_call x0 -> x9, Pallas kernels: none -> 51.2 us  [the longest x7 42.5 us: call(): pl.pallas_call(kernel, in_specs=in_specs, out_specs=out_specs or [VMEM] *...]
    all_gather x3 -> x0, waiting for transfers between devices: 45.9 us -> none  [the longest x1 24.1 us: shards(): lax.all_gather(value_heads, 'ctx', axis=0, tiled=True)]
    ppermute x0 -> x16, starting transfers between devices: none -> 27.1 us  [the longest x12 16.3 us: flip(): lax.ppermute(value, 'ctx', pairs or [(i, i ^ bit) for i in range(n_ctx)])]
    ppermute x0 -> x16, waiting for transfers between devices: none -> 16.1 us  [the longest x12 13.7 us: flip(): lax.ppermute(value, 'ctx', pairs or [(i, i ^ bit) for i in range(n_ctx)])]
    reduce_or x16 -> x0, other arithmetic: 14.9 us -> none  [the longest x8 7.52 us: joint_step(): jnp.any(visible)]
    another operation x20 -> x0, loops' own time: 12.3 us -> none  [the longest x2 5.75 us: shards(): lax.fori_loop(0, block_count, forward_step, start_state)]
  transfers between devices with their start and end apart: 4 -> 16, of which waited for: 3 -> 7; matrix products, arithmetic and copies ran while one was open for 17% -> 5% of each run, Pallas kernels for 0% -> 37%
where the time goes in v2:
time: 118 us; the launch traced here: 117 us
  Pallas kernels  51.2 us (43%)
  starting transfers between devices  27.1 us (23%)
  local copies, waits for them, and re-layouts  18.9 us (16%)
  waiting for transfers between devices  16.1 us (14%)
  other arithmetic  3.06 us (3%)
    pallas_call x7, Pallas kernels, call(): pl.pallas_call(kernel, in_specs=in_specs, out_specs=out_specs or [VMEM] *...  42.5 us
    ppermute x12, starting transfers between devices, flip(): lax.ppermute(value, 'ctx', pairs or [(i, i ^ bit) for i in range(n_ctx)])  16.3 us
    unnamed x15, local copies, waits for them, and re-layouts  14.9 us
    ppermute x12, waiting for transfers between devices, flip(): lax.ppermute(value, 'ctx', pairs or [(i, i ^ bit) for i in range(n_ctx)])  13.7 us
    ppermute x4, starting transfers between devices, hop(): return lax.ppermute(value, 'tp', pairs)  10.8 us
    pallas_call x2, Pallas kernels, project_call(): pl.pallas_call(project_kernel if acc is None else project_add_kernel, gri...  8.7 us
    dynamic_slice x1, local copies, waits for them, and re-layouts, shards(): w_last = lax.dynamic_slice_in_dim(out_weight, shard * depth, depth, 1)  2.92 us
  transfers between devices with their start and end apart: 16, of which 7 were waited for; matrix products, arithmetic and copies ran while one was open for 5% of the time, Pallas kernels for 37%

profile of v2, /device:TPU:10, one launch (start us, length us, event | category | flops | bytes accessed | tf_op | source)
XLA Modules:
  0.0 117.2 jit_solution(16228822211066385169)
XLA Ops:
  0.6 0.0 copy-start.3
  0.7 1.0 constant_dynamic-update-slice_fusion.1
  1.6 0.9 constant_dynamic-update-slice_fusion
  2.6 0.6 collective-permute-start.4
  3.2 1.5 %collective-permute-start.5 = (bf16[256,512]{1,0:T(8,128)(2,1)S(1)}, bf16[256,512]{1,0:T(8,128)(2,1)}, u32[]{:S(2)}, u32[]{:S(2)}) collective-permute-start(bf16[256,512]{1,0:T(8,128)(2,1)S(1)} %constant_dynamic-update-slice_fusion), channel_id=1, source_target_pairs={{0,16},{4,20},{8,24},{12,28},{16,0},{20,4},{24,8},{28,12},{1,17},{... | collective-permute-start | bytes 786440 | tf_op jit(solution)/shard_map/ppermute | solution.py:370
  4.7 1.4 %collective-permute-start.6 = (bf16[256,512]{1,0:T(8,128)(2,1)S(1)}, bf16[256,512]{1,0:T(8,128)(2,1)}, u32[]{:S(2)}, u32[]{:S(2)}) collective-permute-start(bf16[256,512]{1,0:T(8,128)(2,1)S(1)} %constant_dynamic-update-slice_fusion), channel_id=1, source_target_pairs={{0,24},{4,28},{8,16},{12,20},{16,8},{20,12},{24,0},{28,4},{1,25},{... | collective-permute-start | bytes 786440 | tf_op jit(solution)/shard_map/ppermute | solution.py:370
  6.1 2.6 %collective-permute-start.1 = (bf16[256,1280]{1,0:T(8,128)(2,1)}, bf16[256,1280]{1,0:T(8,128)(2,1)S(1)}, u32[]{:S(2)}, u32[]{:S(2)}) collective-permute-start(bf16[256,1280]{1,0:T(8,128)(2,1)} %refs_0_.1), channel_id=1, source_target_pairs={{0,2},{2,0},{1,3},{3,1},{4,6},{6,4},{5,7},{7,5},{8,10},{10,8},{9,1... | collective-permute-start | bytes 1966088 | tf_op jit(solution)/shard_map/ppermute | solution.py:367
  8.7 0.4 collective-permute-start
  9.2 0.7 compare_select_fusion.5.pos_ref
  9.9 2.1 %collective-permute-done.4 = bf16[256,512]{1,0:T(8,128)(2,1)} collective-permute-done((bf16[256,512]{1,0:T(8,128)(2,1)S(1)}, bf16[256,512]{1,0:T(8,128)(2,1)}, u32[]{:S(2)}, u32[]{:S(2)}) %collective-permute-start.4) | collective-permute-done | bytes 262176 | tf_op jit(solution)/shard_map/ppermute | solution.py:370
  11.9 3.5 %collective-permute-start.2 = (bf16[256,1280]{1,0:T(8,128)(2,1)}, bf16[256,1280]{1,0:T(8,128)(2,1)S(1)}, u32[]{:S(2)}, u32[]{:S(2)}) collective-permute-start(bf16[256,1280]{1,0:T(8,128)(2,1)} %refs_0_.1), channel_id=1, source_target_pairs={{1,2},{2,1},{5,6},{6,5},{9,10},{10,9},{13,14},{14,13},{17,18},{18,... | collective-permute-start | bytes 1966088 | tf_op jit(solution)/shard_map/ppermute | solution.py:367
  15.4 0.2 collective-permute-done.5
  15.6 1.7 %collective-permute-done.6 = bf16[256,512]{1,0:T(8,128)(2,1)} collective-permute-done((bf16[256,512]{1,0:T(8,128)(2,1)S(1)}, bf16[256,512]{1,0:T(8,128)(2,1)}, u32[]{:S(2)}, u32[]{:S(2)}) %collective-permute-start.6) | collective-permute-done | bytes 262176 | tf_op jit(solution)/shard_map/ppermute | solution.py:370
  17.4 1.2 %pad_maximum_fusion.near_ref = bf16[4,256,512]{2,1,0:T(8,128)(2,1)S(1)} fusion(bf16[1,256,512]{2,1,0:T(8,128)(2,1)} %bitcast.9, bf16[1,256,512]{2,1,0:T(8,128)(2,1)} %bitcast.8, bf16[1,256,512]{2,1,0:T(8,128)(2,1)} %bitcast.7, bf16[1,256,512]{2,1,0:T(8,128)(2,1)S(1)} %bitcast.11), kind=kLoop, calls=%fused_computation | loop fusion | flops 1572864 | bytes 2097152 | tf_op jit(solution)/shard_map/stack | solution.py:373
  18.6 0.1 collective-permute-start.7
  18.7 0.1 pad_add_fusion.shard_ref
  18.8 0.1 copy.12.adv_ref
  18.9 2.3 %shard_map.112 = (f32[7,256,256]{2,1,0:T(8,128)S(1)}, s32[7]{0:T(128)S(1)}) custom-call(s32[1]{0:T(128)} %bitcast.me_ref, s32[8,1,256]{2,1,0:T(1,128)S(1)} %bitcast.10, s32[2,16]{1,0:T(2,128)S(1)} %copy-done.5), custom_call_target="tpu_custom_call" | custom-call | bytes 1835008 | tf_op jit(solution)/shard_map/pallas_call | solution.py:44
  21.2 0.0 copy-start
  21.3 7.0 %copy-done = bf16[2048,5120]{1,0:T(8,128)(2,1)S(1)} copy-done((bf16[2048,5120]{1,0:T(8,128)(2,1)S(1)}, bf16[2048,5120]{1,0:T(8,128)(2,1)}, u32[]{:S(2)}) %copy-start) | copy-done | bytes 20971544
  28.2 2.7 %shard_map.113.acc_ref = f32[256,2048]{1,0:T(8,128)S(1)} custom-call(s32[1]{0:T(128)} %bitcast.4.shard_ref, bf16[256,1280]{1,0:T(8,128)(2,1)S(1)} %copy-done.3, bf16[2048,5120]{1,0:T(8,128)(2,1)S(1)} %copy-done), custom_call_target="tpu_custom_call" | custom-call | flops 1342177280 | bytes 5242880 | tf_op jit(solution)/shard_map/pallas_call | solution.py:321
  30.9 0.0 copy-start.2
  30.9 2.9 %constant_dynamic-slice_fusion.w_ref = bf16[2048,1280]{1,0:T(8,128)(2,1)S(1)} fusion(bf16[2048,5120]{1,0:T(8,128)(2,1)} %refs_3_.1, s32[]{:T(128)S(6)} %select_n.49), kind=kLoop, calls=%fused_computation.20 | loop fusion | bytes 10485764 | tf_op jit(solution)/shard_map/dynamic_slice | solution.py:416
  33.9 2.3 %collective-permute-done.1.refs_1_ = bf16[256,1280]{1,0:T(8,128)(2,1)S(1)} collective-permute-done((bf16[256,1280]{1,0:T(8,128)(2,1)}, bf16[256,1280]{1,0:T(8,128)(2,1)S(1)}, u32[]{:S(2)}, u32[]{:S(2)}) %collective-permute-start.1) | collective-permute-done | bytes 655392 | tf_op jit(solution)/shard_map/ppermute | solution.py:367
  36.2 4.3 %collective-permute-start.3 = (bf16[256,1280]{1,0:T(8,128)(2,1)S(1)}, bf16[256,1280]{1,0:T(8,128)(2,1)S(1)}, u32[]{:S(2)}, u32[]{:S(2)}) collective-permute-start(bf16[256,1280]{1,0:T(8,128)(2,1)S(1)} %collective-permute-done.1.refs_1_), channel_id=1, source_target_pairs={{1,0},{2,3},{5,4},{6,7},{9,8},{10,11},{13,12},{14,15},{17,16},{18,... | collective-permute-start | bytes 1966088 | tf_op jit(solution)/shard_map/ppermute | solution.py:367
  40.5 0.0 copy-start.1
  40.5 7.0 %copy-done.1 = bf16[2048,5120]{1,0:T(8,128)(2,1)S(1)} copy-done((bf16[2048,5120]{1,0:T(8,128)(2,1)S(1)}, bf16[2048,5120]{1,0:T(8,128)(2,1)}, u32[]{:S(2)}) %copy-start.1) | copy-done | bytes 20971544
  47.5 6.0 %shard_map.114.proj_ref = f32[256,2048]{1,0:T(8,128)S(1)} custom-call(s32[2]{0:T(128)S(1)} %pad_add_fusion.shard_ref, f32[256,2048]{1,0:T(8,128)S(1)} %shard_map.113.acc_ref, bf16[256,1280]{1,0:T(8,128)(2,1)} %collective-permute-done.refs_0_, bf16[256,1280]{1,0:T(8,128)(2,1)S(1)} %collective-permute-done.1.refs_1_, bf16[2048,5120]{1,0:T(8,128)(2,1)S(1)} %copy-done.1, ...), custom_call_target="tpu_custom_call" | custom-call | flops 2684354560 | bytes 10485760 | tf_op jit(solution)/shard_map/pallas_call | solution.py:321
  53.5 0.0 collective-permute-done.7.far_ref
  53.5 25.6 %shard_map.115 = (bf16[2,1792,2048]{2,1,0:T(8,128)(2,1)S(1)}, f32[256,2048]{1,0:T(8,128)S(1)}, f32[256,128]{1,0:T(8,128)S(1)}, bf16[2,1792,128]{2,1,0:T(8,128)(2,1)S(1)}, bf16[2,1792,128]{2,1,0:T(8,128)(2,1)S(1)}) custom-call(s32[7]{0:T(128)S(1)} %fusion.1.slot_ref, bf16[256,2048]{1,0:T(8,128)(2,1)S(1)} %copy-done.2, ...), custom_call_target="tpu_custom_call" | custom-call | flops 5637144576 | bytes 14680064 | tf_op jit(solution)/shard_map/pallas_call | solution.py:44
  79.1 0.0 collective-permute-done.2.x1_ref
  79.1 6.7 %shard_map.117 = (bf16[256,1024]{1,0:T(8,128)(2,1)S(1)}, bf16[3,2,256,128]{3,2,1,0:T(8,128)(2,1)S(1)}, bf16[4,2,256,128]{3,2,1,0:T(8,128)(2,1)S(1)}) custom-call(s32[7]{0:T(128)S(1)} %get-tuple-element.26.live_ref, s32[7]{0:T(128)S(1)} %compare_select_fusion.5.pos_ref, f32[256,2048]{1,0:T(8,128)S(1)} %shard_map.114.proj_ref, ...), custom_call_target="tpu_custom_call" | custom-call | flops 4697620480 | bytes 7340032 | tf_op jit(solution)/shard_map/pallas_call | solution.py:44
  85.9 0.1 collective-permute-start.12
  85.9 6.9 %shard_map.116 = (bf16[256,1024]{1,0:T(8,128)(2,1)S(1)}, bf16[3,2,256,128]{3,2,1,0:T(8,128)(2,1)S(1)}, bf16[4,2,256,128]{3,2,1,0:T(8,128)(2,1)S(1)}) custom-call(s32[7]{0:T(128)S(1)} %get-tuple-element.26.live_ref, s32[7]{0:T(128)S(1)} %compare_select_fusion.5.pos_ref, f32[256,2048]{1,0:T(8,128)S(1)} %shard_map.114.proj_ref, ...), custom_call_target="tpu_custom_call" | custom-call | flops 4697620480 | bytes 7340032 | tf_op jit(solution)/shard_map/pallas_call | solution.py:44
  92.8 1.7 %collective-permute-start.8 = (bf16[3,2,256,128]{3,2,1,0:T(8,128)(2,1)S(1)}, bf16[3,2,256,128]{3,2,1,0:T(8,128)(2,1)S(1)}, u32[]{:S(2)}, u32[]{:S(2)}) collective-permute-start(bf16[3,2,256,128]{3,2,1,0:T(8,128)(2,1)S(1)} %get-tuple-element.35), channel_id=1, source_target_pairs={{0,4},{4,0},{8,12},{12,8},{16,20},{20,16},{24,28},{28,24},{1,5},{5... | collective-permute-start | bytes 1179656 | tf_op jit(solution)/shard_map/ppermute | solution.py:370
  94.5 0.1 shard_map.119
  94.6 1.9 %collective-permute-start.13 = (bf16[2,256,128]{2,1,0:T(8,128)(2,1)S(1)}, bf16[2,256,128]{2,1,0:T(8,128)(2,1)S(1)}, u32[]{:S(2)}, u32[]{:S(2)}) collective-permute-start(bf16[2,256,128]{2,1,0:T(8,128)(2,1)S(1)} %get-tuple-element.44), channel_id=1, source_target_pairs={{0,8},{8,0},{4,12},{12,4},{24,16},{28,20},{1,9},{9,1},{5,13},{13,5... | collective-permute-start | bytes 393224 | tf_op jit(solution)/shard_map/ppermute | solution.py:370
  96.5 1.3 %collective-permute-start.14 = (bf16[2,256,128]{2,1,0:T(8,128)(2,1)S(1)}, bf16[2,256,128]{2,1,0:T(8,128)(2,1)S(1)}, u32[]{:S(2)}, u32[]{:S(2)}) collective-permute-start(bf16[2,256,128]{2,1,0:T(8,128)(2,1)S(1)} %get-tuple-element.45), channel_id=1, source_target_pairs={{16,0},{20,4},{24,8},{28,12},{17,1},{21,5},{25,9},{29,13},{18,2},{... | collective-permute-start | bytes 393224 | tf_op jit(solution)/shard_map/ppermute | solution.py:370
  97.8 1.3 %collective-permute-start.15 = (bf16[2,256,128]{2,1,0:T(8,128)(2,1)S(1)}, bf16[2,256,128]{2,1,0:T(8,128)(2,1)S(1)}, u32[]{:S(2)}, u32[]{:S(2)}) collective-permute-start(bf16[2,256,128]{2,1,0:T(8,128)(2,1)S(1)} %get-tuple-element.46), channel_id=1, source_target_pairs={{16,8},{20,12},{24,0},{28,4},{17,9},{21,13},{25,1},{29,5},{18,10},... | collective-permute-start | bytes 393224 | tf_op jit(solution)/shard_map/ppermute | solution.py:370
  99.1 0.1 shard_map.118
  99.2 1.3 %collective-permute-start.10 = (bf16[2,256,128]{2,1,0:T(8,128)(2,1)S(1)}, bf16[2,256,128]{2,1,0:T(8,128)(2,1)S(1)}, u32[]{:S(2)}, u32[]{:S(2)}) collective-permute-start(bf16[2,256,128]{2,1,0:T(8,128)(2,1)S(1)} %get-tuple-element.39), channel_id=1, source_target_pairs={{16,0},{20,4},{24,8},{28,12},{17,1},{21,5},{25,9},{29,13},{18,2},{... | collective-permute-start | bytes 393224 | tf_op jit(solution)/shard_map/ppermute | solution.py:370
  100.5 1.3 %collective-permute-start.11 = (bf16[2,256,128]{2,1,0:T(8,128)(2,1)S(1)}, bf16[2,256,128]{2,1,0:T(8,128)(2,1)S(1)}, u32[]{:S(2)}, u32[]{:S(2)}) collective-permute-start(bf16[2,256,128]{2,1,0:T(8,128)(2,1)S(1)} %get-tuple-element.40), channel_id=1, source_target_pairs={{16,8},{20,12},{24,0},{28,4},{17,9},{21,13},{25,1},{29,5},{18,10},... | collective-permute-start | bytes 393224 | tf_op jit(solution)/shard_map/ppermute | solution.py:370
  101.8 0.1 collective-permute-done.13.refs_5_
  101.9 3.9 %collective-permute-start.9 = (bf16[2,256,128]{2,1,0:T(8,128)(2,1)S(1)}, bf16[2,256,128]{2,1,0:T(8,128)(2,1)S(1)}, u32[]{:S(2)}, u32[]{:S(2)}) collective-permute-start(bf16[2,256,128]{2,1,0:T(8,128)(2,1)S(1)} %get-tuple-element.38), channel_id=1, source_target_pairs={{0,8},{8,0},{4,12},{12,4},{24,16},{28,20},{1,9},{9,1},{5,13},{13,5... | collective-permute-start | bytes 393224 | tf_op jit(solution)/shard_map/ppermute | solution.py:370
  105.8 1.1 pad_maximum_fusion.1
  106.8 7.0 %collective-permute-done.14.refs_6_ = bf16[2,256,128]{2,1,0:T(8,128)(2,1)S(1)} collective-permute-done((bf16[2,256,128]{2,1,0:T(8,128)(2,1)S(1)}, bf16[2,256,128]{2,1,0:T(8,128)(2,1)S(1)}, u32[]{:S(2)}, u32[]{:S(2)}) %collective-permute-start.14) | collective-permute-done | bytes 131104 | tf_op jit(solution)/shard_map/ppermute | solution.py:370
  113.9 2.5 %collective-permute-done.10.refs_2_ = bf16[2,256,128]{2,1,0:T(8,128)(2,1)S(1)} collective-permute-done((bf16[2,256,128]{2,1,0:T(8,128)(2,1)S(1)}, bf16[2,256,128]{2,1,0:T(8,128)(2,1)S(1)}, u32[]{:S(2)}, u32[]{:S(2)}) %collective-permute-start.10) | collective-permute-done | bytes 131104 | tf_op jit(solution)/shard_map/ppermute | solution.py:370
  116.4 0.8 shard_map.120
  (16 shorter events, 0.1 us)
Async XLA Ops:
  0.6 20.6 %copy-start.3 = (bf16[256,1280]{1,0:T(8,128)(2,1)S(1)}, bf16[256,1280]{1,0:T(8,128)(2,1)}, u32[]{:S(2)}) copy-start(bf16[256,1280]{1,0:T(8,128)(2,1)} %refs_0_.1) | copy-start | bytes 1966084
  0.6 18.1 %copy-start.6 = (f32[256]{0:T(256)S(1)}, f32[256]{0:T(256)}, u32[]{:S(2)}) copy-start(f32[256]{0:T(256)} %param.10) | copy-start | bytes 3076
  0.7 18.3 %copy-start.4 = (s32[2048]{0:T(1024)S(1)}, s32[2048]{0:T(1024)}, u32[]{:S(2)}) copy-start(s32[2048]{0:T(1024)} %param.15) | copy-start | bytes 24580
  0.7 18.3 %copy-start.5 = (s32[2,16]{1,0:T(2,128)S(1)}, s32[2,16]{1,0:T(2,128)}, u32[]{:S(2)}) copy-start(s32[2,16]{1,0:T(2,128)} %tile_ref.1) | copy-start | bytes 388
  2.6 9.4 %collective-permute-start.4 = (bf16[256,512]{1,0:T(8,128)(2,1)S(1)}, bf16[256,512]{1,0:T(8,128)(2,1)}, u32[]{:S(2)}, u32[]{:S(2)}) collective-permute-start(bf16[256,512]{1,0:T(8,128)(2,1)S(1)} %constant_dynamic-update-slice_fusion), channel_id=1, source_target_pairs={{0,8},{4,12},{8,0},{12,4},{16,24},{20,28},{24,16},{28,20},{1,9},{5... | collective-permute-start | bytes 786440 | tf_op jit(solution)/shard_map/ppermute | solution.py:370
  3.2 12.5 %collective-permute-start.5 = (bf16[256,512]{1,0:T(8,128)(2,1)S(1)}, bf16[256,512]{1,0:T(8,128)(2,1)}, u32[]{:S(2)}, u32[]{:S(2)}) collective-permute-start(bf16[256,512]{1,0:T(8,128)(2,1)S(1)} %constant_dynamic-update-slice_fusion), channel_id=1, source_target_pairs={{0,16},{4,20},{8,24},{12,28},{16,0},{20,4},{24,8},{28,12},{1,17},{... | collective-permute-start | bytes 786440 | tf_op jit(solution)/shard_map/ppermute | solution.py:370
  4.7 12.7 %collective-permute-start.6 = (bf16[256,512]{1,0:T(8,128)(2,1)S(1)}, bf16[256,512]{1,0:T(8,128)(2,1)}, u32[]{:S(2)}, u32[]{:S(2)}) collective-permute-start(bf16[256,512]{1,0:T(8,128)(2,1)S(1)} %constant_dynamic-update-slice_fusion), channel_id=1, source_target_pairs={{0,24},{4,28},{8,16},{12,20},{16,8},{20,12},{24,0},{28,4},{1,25},{... | collective-permute-start | bytes 786440 | tf_op jit(solution)/shard_map/ppermute | solution.py:370
  6.1 30.1 %collective-permute-start.1 = (bf16[256,1280]{1,0:T(8,128)(2,1)}, bf16[256,1280]{1,0:T(8,128)(2,1)S(1)}, u32[]{:S(2)}, u32[]{:S(2)}) collective-permute-start(bf16[256,1280]{1,0:T(8,128)(2,1)} %refs_0_.1), channel_id=1, source_target_pairs={{0,2},{2,0},{1,3},{3,1},{4,6},{6,4},{5,7},{7,5},{8,10},{10,8},{9,1... | collective-permute-start | bytes 1966088 | tf_op jit(solution)/shard_map/ppermute | solution.py:367
  8.7 31.8 %collective-permute-start = (bf16[256,1280]{1,0:T(8,128)(2,1)}, bf16[256,1280]{1,0:T(8,128)(2,1)}, u32[]{:S(2)}, u32[]{:S(2)}) collective-permute-start(bf16[256,1280]{1,0:T(8,128)(2,1)} %refs_0_.1), channel_id=1, source_target_pairs={{0,1},{1,0},{2,3},{3,2},{4,5},{5,4},{6,7},{7,6},{8,9},{9,8},{10,11... | collective-permute-start | bytes 1966088 | tf_op jit(solution)/shard_map/ppermute | solution.py:367
  11.9 67.2 %collective-permute-start.2 = (bf16[256,1280]{1,0:T(8,128)(2,1)}, bf16[256,1280]{1,0:T(8,128)(2,1)S(1)}, u32[]{:S(2)}, u32[]{:S(2)}) collective-permute-start(bf16[256,1280]{1,0:T(8,128)(2,1)} %refs_0_.1), channel_id=1, source_target_pairs={{1,2},{2,1},{5,6},{6,5},{9,10},{10,9},{13,14},{14,13},{17,18},{18,... | collective-permute-start | bytes 1966088 | tf_op jit(solution)/shard_map/ppermute | solution.py:367
  18.6 34.9 %collective-permute-start.7 = (bf16[4,256,512]{2,1,0:T(8,128)(2,1)S(1)}, bf16[4,256,512]{2,1,0:T(8,128)(2,1)}, u32[]{:S(2)}, u32[]{:S(2)}) collective-permute-start(bf16[4,256,512]{2,1,0:T(8,128)(2,1)S(1)} %pad_maximum_fusion.near_ref), channel_id=1, source_target_pairs={{0,4},{4,0},{8,12},{12,8},{16,20},{20,16},{24,28},{28,24},{1,5},{5... | collective-permute-start | bytes 3145736 | tf_op jit(solution)/shard_map/ppermute | solution.py:370
  21.2 7.0 %copy-start = (bf16[2048,5120]{1,0:T(8,128)(2,1)S(1)}, bf16[2048,5120]{1,0:T(8,128)(2,1)}, u32[]{:S(2)}) copy-start(bf16[2048,5120]{1,0:T(8,128)(2,1)} %refs_3_.1) | copy-start | bytes 62914564
  30.9 22.6 %copy-start.2 = (bf16[256,2048]{1,0:T(8,128)(2,1)S(1)}, bf16[256,2048]{1,0:T(8,128)(2,1)}, u32[]{:S(2)}) copy-start(bf16[256,2048]{1,0:T(8,128)(2,1)} %q_ref.5) | copy-start | bytes 3145732
  36.2 42.9 %collective-permute-start.3 = (bf16[256,1280]{1,0:T(8,128)(2,1)S(1)}, bf16[256,1280]{1,0:T(8,128)(2,1)S(1)}, u32[]{:S(2)}, u32[]{:S(2)}) collective-permute-start(bf16[256,1280]{1,0:T(8,128)(2,1)S(1)} %collective-permute-done.1.refs_1_), channel_id=1, source_target_pairs={{1,0},{2,3},{5,4},{6,7},{9,8},{10,11},{13,12},{14,15},{17,16},{18,... | collective-permute-start | bytes 1966088 | tf_op jit(solution)/shard_map/ppermute | solution.py:367
  40.5 7.0 %copy-start.1 = (bf16[2048,5120]{1,0:T(8,128)(2,1)S(1)}, bf16[2048,5120]{1,0:T(8,128)(2,1)}, u32[]{:S(2)}) copy-start(bf16[2048,5120]{1,0:T(8,128)(2,1)} %refs_3_.1) | copy-start | bytes 62914564
  85.9 8.6 %collective-permute-start.12 = (bf16[3,2,256,128]{3,2,1,0:T(8,128)(2,1)S(1)}, bf16[3,2,256,128]{3,2,1,0:T(8,128)(2,1)S(1)}, u32[]{:S(2)}, u32[]{:S(2)}) collective-permute-start(bf16[3,2,256,128]{3,2,1,0:T(8,128)(2,1)S(1)} %get-tuple-element.41), channel_id=1, source_target_pairs={{0,4},{4,0},{8,12},{12,8},{16,20},{20,16},{24,28},{28,24},{1,5},{5... | collective-permute-start | bytes 1179656 | tf_op jit(solution)/shard_map/ppermute | solution.py:370
  92.8 6.3 %collective-permute-start.8 = (bf16[3,2,256,128]{3,2,1,0:T(8,128)(2,1)S(1)}, bf16[3,2,256,128]{3,2,1,0:T(8,128)(2,1)S(1)}, u32[]{:S(2)}, u32[]{:S(2)}) collective-permute-start(bf16[3,2,256,128]{3,2,1,0:T(8,128)(2,1)S(1)} %get-tuple-element.35), channel_id=1, source_target_pairs={{0,4},{4,0},{8,12},{12,8},{16,20},{20,16},{24,28},{28,24},{1,5},{5... | collective-permute-start | bytes 1179656 | tf_op jit(solution)/shard_map/ppermute | solution.py:370
  94.6 7.3 %collective-permute-start.13 = (bf16[2,256,128]{2,1,0:T(8,128)(2,1)S(1)}, bf16[2,256,128]{2,1,0:T(8,128)(2,1)S(1)}, u32[]{:S(2)}, u32[]{:S(2)}) collective-permute-start(bf16[2,256,128]{2,1,0:T(8,128)(2,1)S(1)} %get-tuple-element.44), channel_id=1, source_target_pairs={{0,8},{8,0},{4,12},{12,4},{24,16},{28,20},{1,9},{9,1},{5,13},{13,5... | collective-permute-start | bytes 393224 | tf_op jit(solution)/shard_map/ppermute | solution.py:370
  96.5 17.4 %collective-permute-start.14 = (bf16[2,256,128]{2,1,0:T(8,128)(2,1)S(1)}, bf16[2,256,128]{2,1,0:T(8,128)(2,1)S(1)}, u32[]{:S(2)}, u32[]{:S(2)}) collective-permute-start(bf16[2,256,128]{2,1,0:T(8,128)(2,1)S(1)} %get-tuple-element.45), channel_id=1, source_target_pairs={{16,0},{20,4},{24,8},{28,12},{17,1},{21,5},{25,9},{29,13},{18,2},{... | collective-permute-start | bytes 393224 | tf_op jit(solution)/shard_map/ppermute | solution.py:370
  97.8 16.1 %collective-permute-start.15 = (bf16[2,256,128]{2,1,0:T(8,128)(2,1)S(1)}, bf16[2,256,128]{2,1,0:T(8,128)(2,1)S(1)}, u32[]{:S(2)}, u32[]{:S(2)}) collective-permute-start(bf16[2,256,128]{2,1,0:T(8,128)(2,1)S(1)} %get-tuple-element.46), channel_id=1, source_target_pairs={{16,8},{20,12},{24,0},{28,4},{17,9},{21,13},{25,1},{29,5},{18,10},... | collective-permute-start | bytes 393224 | tf_op jit(solution)/shard_map/ppermute | solution.py:370
  99.2 17.2 %collective-permute-start.10 = (bf16[2,256,128]{2,1,0:T(8,128)(2,1)S(1)}, bf16[2,256,128]{2,1,0:T(8,128)(2,1)S(1)}, u32[]{:S(2)}, u32[]{:S(2)}) collective-permute-start(bf16[2,256,128]{2,1,0:T(8,128)(2,1)S(1)} %get-tuple-element.39), channel_id=1, source_target_pairs={{16,0},{20,4},{24,8},{28,12},{17,1},{21,5},{25,9},{29,13},{18,2},{... | collective-permute-start | bytes 393224 | tf_op jit(solution)/shard_map/ppermute | solution.py:370
  100.5 15.9 %collective-permute-start.11 = (bf16[2,256,128]{2,1,0:T(8,128)(2,1)S(1)}, bf16[2,256,128]{2,1,0:T(8,128)(2,1)S(1)}, u32[]{:S(2)}, u32[]{:S(2)}) collective-permute-start(bf16[2,256,128]{2,1,0:T(8,128)(2,1)S(1)} %get-tuple-element.40), channel_id=1, source_target_pairs={{16,8},{20,12},{24,0},{28,4},{17,9},{21,13},{25,1},{29,5},{18,10},... | collective-permute-start | bytes 393224 | tf_op jit(solution)/shard_map/ppermute | solution.py:370
  101.9 14.5 %collective-permute-start.9 = (bf16[2,256,128]{2,1,0:T(8,128)(2,1)S(1)}, bf16[2,256,128]{2,1,0:T(8,128)(2,1)S(1)}, u32[]{:S(2)}, u32[]{:S(2)}) collective-permute-start(bf16[2,256,128]{2,1,0:T(8,128)(2,1)S(1)} %get-tuple-element.38), channel_id=1, source_target_pairs={{0,8},{8,0},{4,12},{12,4},{24,16},{28,20},{1,9},{9,1},{5,13},{13,5... | collective-permute-start | bytes 393224 | tf_op jit(solution)/shard_map/ppermute | solution.py:370

commit v3 on v2

--- a/solution.py
+++ b/solution.py
@@ -16,7 +16,7 @@
 ROLLOUTS = 8
 JITTER = 64
 KB = 256
-VMEM_LIMIT = 24 << 20
+VMEM_LIMIT = 20 << 20
 SCALE = 1.0 / math.sqrt(HD)
 LOG2E = 1.4426950408889634
 F32 = jnp.float32
@@ -45,7 +45,9 @@
         kernel,
         in_specs=in_specs,
         out_specs=out_specs or [VMEM] * len(outs),
-        out_shape=[jax.ShapeDtypeStruct(shape, dtype) for shape, dtype in outs],
+        out_shape=[
+            out if isinstance(out, pl.MemoryRef) else jax.ShapeDtypeStruct(*out) for out in outs
+        ],
         scratch_shapes=list(scratch),
         compiler_params=pltpu.CompilerParams(vmem_limit_bytes=VMEM_LIMIT),
         cost_estimate=pl.CostEstimate(flops=flops, bytes_accessed=size, transcendentals=exps),
@@ -94,23 +96,22 @@
 
 
 def probs_kernel(
-    n_kb, groups, slot_ref, q_ref, near_ref, far_ref, bias_ref,
-    p_ref, o_ref, inv_ref, k_ref, v_ref, kx_ref, vt_ref, s_ref,
+    n_kb, group, groups, slot_ref, q_ref, near_ref, far_ref, bias_ref,
+    p_ref, o_ref, inv_ref, k_ref, v_ref, kx_ref, vt_ref, s_ref, t_ref, a_ref, b_ref, sems,
 ):
     rows = q_ref.shape[0]
     per = rows // KB
     n_near = near_ref.shape[0]
     lane = lax.broadcasted_iota(jnp.int32, (KB, HD), 1)
     inv_ref[...] = jnp.zeros_like(inv_ref)
-    vt_ref[:, HD:, :] = jnp.ones((groups, 16, n_kb * KB), BF16)
+    vt_ref[HD:, :] = jnp.ones((16, n_kb * KB), BF16)
     for kb in range(n_kb):
         slot = slot_ref[kb]
         keys = pl.ds(kb * KB, KB)
 
         def place(source, index):
-            for g in range(groups):
-                k_ref[g, keys, :] = source[index, :, g * HD : (g + 1) * HD]
-                v_ref[g, keys, :] = source[index, :, (groups + g) * HD : (groups + g + 1) * HD]
+            k_ref[keys, :] = source[index, :, group * HD : (group + 1) * HD]
+            v_ref[keys, :] = source[index, :, (groups + group) * HD : (groups + group + 1) * HD]
 
         @pl.when(slot < n_near)
         def _():
@@ -120,60 +121,86 @@
         def _():
             place(far_ref, slot - n_near)
 
-    for g in range(groups):
-        for kb in range(n_kb):
-            keys = pl.ds(kb * KB, KB)
-            k = k_ref[g, keys, :]
-            kx_ref[g, keys, :HD] = k
-            kx_ref[g, keys, HD:] = k
-            vt_ref[g, :HD, keys] = v_ref[g, keys, :].T
-
-    def step(i, carry):
-        head, r = i // per, i % per
-        g, h = head // SHARE, head % SHARE
-        cols = at((h * per + r) * KB, KB)
-        here = at(r * KB, KB)
-        q = q_ref[here, at(head * HD, HD)].astype(F32) * (SCALE * LOG2E)
+    for kb in range(n_kb):
+        keys = pl.ds(kb * KB, KB)
+        k = k_ref[keys, :]
+        kx_ref[keys, :HD] = k
+        kx_ref[keys, HD:] = k
+        vt_ref[:HD, keys] = v_ref[keys, :].T
+
+    count = SHARE * per
+
+    def places(i):
+        h, r = i // per, i % per
+        return h, at(r * KB, KB), at((h * per + r) * KB, KB)
+
+    def score(i, s_ref):
+        h, here, _ = places(i)
+        q = q_ref[here, at((group * SHARE + h) * HD, HD)].astype(F32) * (SCALE * LOG2E)
         q_hi = q.astype(BF16)
         q_lo = (q - q_hi.astype(F32)).astype(BF16)
         qx = jnp.concatenate([q_hi, q_lo], axis=1)
-        s_ref[...] = dot_nt(kx_ref[g], qx) + bias_ref[:, :, here].reshape(n_kb * KB, KB)
-        top = jnp.max(s_ref[...], axis=0, keepdims=True)
-        p_ref[g, :, cols] = jnp.exp2(s_ref[...] - top).astype(BF16)
-        acc = dot(vt_ref[g], p_ref[g, :, cols])
+        s = dot_nt(kx_ref[...], qx) + bias_ref[:, :, here].reshape(n_kb * KB, KB)
+        s_ref[...] = s
+        return jnp.max(s, axis=0, keepdims=True)
+
+    def out(i, e_ref, sem):
+        return pltpu.make_async_copy(e_ref, p_ref.at[:, places(i)[2]], sem)
+
+    def soften(i, s_ref, top, e_ref, sem):
+        h, here, cols = places(i)
+        e = jnp.exp2(s_ref[...] - top).astype(BF16)
+
+        @pl.when(i >= 2)
+        def _():
+            out(i - 2, e_ref, sem).wait()
+
+        e_ref[...] = e
+        out(i, e_ref, sem).start()
+        acc = dot(vt_ref[...], e)
         inv = 1.0 / acc[HD : HD + 1, :]
-        o_ref[here, at(head * HD, HD)] = (acc[:HD] * inv).T
-        inv_ref[here, :] += jnp.where(lane == head, jnp.broadcast_to(inv, (HD, KB)).T, 0.0)
-        return carry
-
-    lax.fori_loop(0, groups * SHARE * per, step, 0, unroll=UNROLL)
-
-
-UNROLL = 2
-
-
-def probs_call(slots, q, near, far, bias, groups, n_kb):
+        o_ref[here, at(h * HD, HD)] = (acc[:HD] * inv).T
+        inv_ref[here, :] += jnp.where(lane == h, jnp.broadcast_to(inv, (HD, KB)).T, 0.0)
+
+    def step(j, top):
+        later = score(2 * j + 1, t_ref)
+        soften(2 * j, s_ref, top, a_ref, sems.at[0])
+        top = score(jnp.minimum(2 * j + 2, count - 1), s_ref)
+        soften(2 * j + 1, t_ref, later, b_ref, sems.at[1])
+        return top
+
+    lax.fori_loop(0, count // 2, step, score(0, s_ref))
+    out(count - 2, a_ref, sems.at[0]).wait()
+    out(count - 1, b_ref, sems.at[1]).wait()
+
+
+def probs_call(group, groups, slots, q, near, far, bias, n_kb):
     rows = q.shape[0]
     keys = n_kb * KB
     return call(
-        functools.partial(probs_kernel, n_kb, groups),
+        functools.partial(probs_kernel, n_kb, group, groups),
         (slots, q, near, far, bias),
         [SMEM, VMEM, VMEM, VMEM, VMEM],
         [
-            ((groups, keys, SHARE * rows), BF16),
-            ((rows, groups * SHARE * HD), F32),
+            pltpu.HBM((keys, SHARE * rows), BF16),
+            ((rows, SHARE * HD), F32),
             ((rows, HD), F32),
-            ((groups, keys, HD), BF16),
-            ((groups, keys, HD), BF16),
+            ((keys, HD), BF16),
+            ((keys, HD), BF16),
         ],
         scratch=[
-            pltpu.VMEM((groups, keys, 2 * HD), BF16),
-            pltpu.VMEM((groups, HD + 16, keys), BF16),
+            pltpu.VMEM((keys, 2 * HD), BF16),
+            pltpu.VMEM((HD + 16, keys), BF16),
             pltpu.VMEM((keys, KB), F32),
+            pltpu.VMEM((keys, KB), F32),
+            pltpu.VMEM((keys, KB), BF16),
+            pltpu.VMEM((keys, KB), BF16),
+            pltpu.SemaphoreType.DMA((2,)),
         ],
-        flops=6 * groups * SHARE * rows * keys * HD,
-        size=groups * SHARE * rows * keys * 2,
-        exps=groups * SHARE * rows * keys,
+        out_specs=[pl.BlockSpec(memory_space=pltpu.HBM)] + [VMEM] * 4,
+        flops=6 * SHARE * rows * keys * HD,
+        size=SHARE * rows * keys * 2,
+        exps=SHARE * rows * keys,
     )
 
 
@@ -183,7 +210,6 @@
     dq_ref, send_ref, keep_ref, dox_ref, qs_ref, ds_ref, dqt_ref,
 ):
     rows = proj_ref.shape[0]
-    group = first // SHARE
     lane = lax.broadcasted_iota(jnp.int32, (rows, HD), 1)
     minus = jnp.where(lax.broadcasted_iota(jnp.int32, (KB, HD), 1) < 3, -1.0, 0.0).astype(BF16)
     x = x1_ref[...] + x2_ref[...]
@@ -192,10 +218,10 @@
         head = first + h
         cols = pl.ds(head * HD, HD)
         here = pl.ds(h * rows, rows)
-        inv = inv_ref[:, head : head + 1]
+        inv = inv_ref[:, h : h + 1]
         proj = proj_ref[:, cols] + dot_nt(x, w_ref[cols, :])
         grad = (proj * (adv_ref[...] * inv)).astype(BF16)
-        delta = jnp.sum(grad.astype(F32) * o_ref[:, cols], axis=1, keepdims=True)
+        delta = jnp.sum(grad.astype(F32) * o_ref[:, h * HD : (h + 1) * HD], axis=1, keepdims=True)
         one = delta.astype(BF16).astype(F32)
         two = (delta - one).astype(BF16).astype(F32)
         three = delta - one - two
@@ -221,13 +247,13 @@
         @pl.when(live_ref[kb] != 0)
         def _():
             keys = at(kb * KB, KB)
-            vx = jnp.concatenate([v_ref[group, keys, :], minus], axis=1)
-            kt = k_ref[group, keys, :].T
-            dv = dot(p_ref[group, keys, :], dox_ref[:, :HD])
+            vx = jnp.concatenate([v_ref[keys, :], minus], axis=1)
+            kt = k_ref[keys, :].T
+            dv = dot(p_ref[keys, :], dox_ref[:, :HD])
             for h in range(SHARE * rows // KB):
                 here = pl.ds(h * KB, KB)
                 dp = dot_nt(vx, dox_ref[here, :])
-                ds_ref[:, here] = (p_ref[group, keys, here].astype(F32) * dp).astype(BF16)
+                ds_ref[:, here] = (p_ref[keys, here].astype(F32) * dp).astype(BF16)
             dqt_ref[...] += dot(kt, ds_ref[...])
             dk = dot(ds_ref[...], qs_ref[...])
             put(jnp.stack([dk, dv]).astype(BF16))
@@ -362,6 +388,7 @@
     n_kb = prompt_kb + (back + 1) * per
     fast = n_ctx == 8 and n_tp == 4 and per == 1 and back == 2
     own = jnp.concatenate([key_heads, value_heads], axis=1)
+    weight = pltpu.with_memory_space_constraint(out_weight, pltpu.HBM)
 
     def hop(value, pairs):
         return lax.ppermute(value, "tp", pairs)
@@ -374,8 +401,6 @@
         far = flip(near, 1)
         up_b = hop(upstream, [(0, 2), (2, 0), (1, 3), (3, 1)])
         up_a = hop(upstream, [(0, 1), (1, 0), (2, 3), (3, 2)])
-        up_c = hop(upstream, [(1, 2), (2, 1)])
-        up_d = hop(up_b, [(1, 0), (2, 3)])
     else:
         near = lax.all_gather(own, "ctx", axis=0)
         near = far = near.reshape(n_ctx * per, KB, 2 * groups * HD)
@@ -397,9 +422,8 @@
             jnp.array([0, 0, 0, 0, 5, 2, 6], jnp.int32),
         )
         n_send = 3
-        x1, x2, shard = up_c, up_d, z ^ 3
-        first = project_call(z[None], [upstream], out_weight)
-        acc = project_call(jnp.stack([z ^ 1, z ^ 2]), [up_a, up_b], out_weight, first)
+        shard = z ^ 3
+        acc = project_call(z[None], [upstream], weight)
     else:
         slots = holder * per + block % per
         pos = block
@@ -410,21 +434,35 @@
         for i in range(n_tp - 1):
             other = (z + 1 + i) % n_tp
             x = lax.dynamic_index_in_dim(whole, other, 0, keepdims=False)
-            acc = project_call(other[None], [x], out_weight, acc)
+            acc = project_call(other[None], [x], weight, acc)
         x1, x2 = upstream, jnp.zeros_like(upstream)
     depth = upstream.shape[1]
     w_last = lax.dynamic_slice_in_dim(out_weight, shard * depth, depth, 1)
 
-    probs, attn, inv, keys, values = probs_call(
-        slots.astype(jnp.int32), query_heads, near, far, bias, groups, n_kb
-    )
-    outs = [
-        back_call(
-            g, live, pos.astype(jnp.int32), acc, x1, x2, w_last, advantage[:, None], attn, inv,
-            query_heads, keys, values, probs, n_kb, n_send,
+    slots = slots.astype(jnp.int32)
+    soft = [list(probs_call(0, groups, slots, query_heads, near, far, bias, n_kb))]
+    if fast:
+        up_b, later, head = lax.optimization_barrier((up_b, upstream, soft[0][2]))
+        soft[0][2] = head
+        up_c = hop(later, [(1, 2), (2, 1)])
+        up_d = hop(up_b, [(1, 0), (2, 3)])
+        x1, x2 = up_c, up_d
+    soft += [
+        list(probs_call(g, groups, slots, query_heads, near, far, bias, n_kb))
+        for g in range(1, groups)
+    ]
+    if fast:
+        acc, soft[-1][2] = lax.optimization_barrier((acc, soft[-1][2]))
+        acc = project_call(jnp.stack([z ^ 1, z ^ 2]), [up_a, up_b], weight, acc)
+    outs = []
+    for g in range(groups):
+        probs, attn, inv, keys, values = soft[g]
+        outs.append(
+            back_call(
+                g, live, pos.astype(jnp.int32), acc, x1, x2, w_last, advantage[:, None], attn,
+                inv, query_heads, keys, values, probs, n_kb, n_send,
+            )
         )
-        for g in range(groups)
-    ]
     grad_queries = jnp.concatenate([dq for dq, _, _ in outs], axis=1)
 
     if fast:

time: 118 us -> 122 us (1.034)
  waiting for transfers between devices: 16.1 us -> 25.5 us
  local copies, waits for them, and re-layouts: 18.9 us -> 9.76 us
  Pallas kernels: 51.2 us -> 56.9 us
  other arithmetic: 3.06 us -> 1.3 us
    unnamed x15 -> x45, local copies, waits for them, and re-layouts: 14.9 us -> 3.53 us
    ppermute x12, waiting for transfers between devices: 13.7 us -> 20.8 us  [flip(): lax.ppermute(value, 'ctx', pairs or [(i, i ^ bit) for i in range(n_ctx)])]
    pallas_call x2, Pallas kernels: 8.7 us -> 13.2 us  [project_call(): pl.pallas_call(project_kernel if acc is None else project_add_kernel, gri...]
    ppermute x4, waiting for transfers between devices: 2.35 us -> 4.69 us  [hop(): return lax.ppermute(value, 'tp', pairs)]
    dynamic_slice x1, local copies, waits for them, and re-layouts: 2.92 us -> 5.17 us  [shards(): w_last = lax.dynamic_slice_in_dim(out_weight, shard * depth, depth, 1)]
    pallas_call x7 -> x8, Pallas kernels: 42.5 us -> 43.7 us  [call(): pl.pallas_call(kernel, in_specs=in_specs, out_specs=out_specs or [VMEM] *...]
  transfers between devices with their start and end apart: 16 -> 16, of which waited for: 7 -> 7; matrix products, arithmetic and copies ran while one was open for 5% -> 5% of each run, Pallas kernels for 37% -> 40%
where the time goes in v3:
time: 122 us
  Pallas kernels  56.9 us (47%)
  starting transfers between devices  27.4 us (22%)
  waiting for transfers between devices  25.5 us (21%)
  local copies, waits for them, and re-layouts  9.76 us (8%)
  other arithmetic  1.3 us (1%)
    pallas_call x8, Pallas kernels, call(): pl.pallas_call(kernel, in_specs=in_specs, out_specs=out_specs or [VMEM] *...  43.7 us
    ppermute x12, waiting for transfers between devices, flip(): lax.ppermute(value, 'ctx', pairs or [(i, i ^ bit) for i in range(n_ctx)])  20.8 us
    ppermute x12, starting transfers between devices, flip(): lax.ppermute(value, 'ctx', pairs or [(i, i ^ bit) for i in range(n_ctx)])  16.5 us
    pallas_call x2, Pallas kernels, project_call(): pl.pallas_call(project_kernel if acc is None else project_add_kernel, gri...  13.2 us
    ppermute x4, starting transfers between devices, hop(): return lax.ppermute(value, 'tp', pairs)  10.9 us
    dynamic_slice x1, local copies, waits for them, and re-layouts, shards(): w_last = lax.dynamic_slice_in_dim(out_weight, shard * depth, depth, 1)  5.17 us
    ppermute x4, waiting for transfers between devices, hop(): return lax.ppermute(value, 'tp', pairs)  4.69 us
    unnamed x45, local copies, waits for them, and re-layouts  3.53 us
  transfers between devices with their start and end apart: 16, of which 7 were waited for; matrix products, arithmetic and copies ran while one was open for 5% of the time, Pallas kernels for 40%

profile of v3, /device:TPU:10, one launch (start us, length us, event | category | flops | bytes accessed | tf_op | source)
XLA Modules:
  0.0 121.9 jit_solution(5602174390531491312)
XLA Ops:
  0.6 0.9 constant_dynamic-update-slice_fusion.1
  1.5 0.9 constant_dynamic-update-slice_fusion
  2.5 0.6 collective-permute-start
  3.1 1.5 %collective-permute-start.1 = (bf16[256,512]{1,0:T(8,128)(2,1)S(1)}, bf16[256,512]{1,0:T(8,128)(2,1)S(1)}, u32[]{:S(2)}, u32[]{:S(2)}) collective-permute-start(bf16[256,512]{1,0:T(8,128)(2,1)S(1)} %constant_dynamic-update-slice_fusion), channel_id=1, source_target_pairs={{0,16},{4,20},{8,24},{12,28},{16,0},{20,4},{24,8},{28,12},{1,17},{... | collective-permute-start | bytes 786440 | tf_op jit(solution)/shard_map/ppermute | solution.py:397
  4.6 1.4 %collective-permute-start.2 = (bf16[256,512]{1,0:T(8,128)(2,1)S(1)}, bf16[256,512]{1,0:T(8,128)(2,1)S(1)}, u32[]{:S(2)}, u32[]{:S(2)}) collective-permute-start(bf16[256,512]{1,0:T(8,128)(2,1)S(1)} %constant_dynamic-update-slice_fusion), channel_id=1, source_target_pairs={{0,24},{4,28},{8,16},{12,20},{16,8},{20,12},{24,0},{28,4},{1,25},{... | collective-permute-start | bytes 786440 | tf_op jit(solution)/shard_map/ppermute | solution.py:397
  6.0 5.7 %collective-permute-done = bf16[256,512]{1,0:T(8,128)(2,1)S(1)} collective-permute-done((bf16[256,512]{1,0:T(8,128)(2,1)S(1)}, bf16[256,512]{1,0:T(8,128)(2,1)S(1)}, u32[]{:S(2)}, u32[]{:S(2)}) %collective-permute-start) | collective-permute-done | bytes 262176 | tf_op jit(solution)/shard_map/ppermute | solution.py:397
  11.7 3.8 %collective-permute-done.1 = bf16[256,512]{1,0:T(8,128)(2,1)S(1)} collective-permute-done((bf16[256,512]{1,0:T(8,128)(2,1)S(1)}, bf16[256,512]{1,0:T(8,128)(2,1)S(1)}, u32[]{:S(2)}, u32[]{:S(2)}) %collective-permute-start.1) | collective-permute-done | bytes 262176 | tf_op jit(solution)/shard_map/ppermute | solution.py:397
  15.5 1.6 %collective-permute-done.2 = bf16[256,512]{1,0:T(8,128)(2,1)S(1)} collective-permute-done((bf16[256,512]{1,0:T(8,128)(2,1)S(1)}, bf16[256,512]{1,0:T(8,128)(2,1)S(1)}, u32[]{:S(2)}, u32[]{:S(2)}) %collective-permute-start.2) | collective-permute-done | bytes 262176 | tf_op jit(solution)/shard_map/ppermute | solution.py:397
  17.2 0.1 pad_maximum_fusion.near_ref
  17.3 0.0 copy-start.3
  17.3 0.1 collective-permute-start.3
  17.4 2.7 %collective-permute-start.5 = (bf16[256,1280]{1,0:T(8,128)(2,1)}, bf16[256,1280]{1,0:T(8,128)(2,1)}, u32[]{:S(2)}, u32[]{:S(2)}) collective-permute-start(bf16[256,1280]{1,0:T(8,128)(2,1)} %refs_0_.1), channel_id=1, source_target_pairs={{0,2},{2,0},{1,3},{3,1},{4,6},{6,4},{5,7},{7,5},{8,10},{10,8},{9,1... | collective-permute-start | bytes 1966088 | tf_op jit(solution)/shard_map/ppermute | solution.py:394
  20.0 0.4 collective-permute-start.4
  20.5 5.2 %constant_dynamic-slice_fusion.w_ref = bf16[2048,1280]{1,0:T(8,128)(2,1)} fusion(bf16[2048,5120]{1,0:T(8,128)(2,1)} %refs_3_.1, s32[]{:T(128)S(6)} %select_n.54), kind=kLoop, calls=%fused_computation.20 | loop fusion | bytes 10485764 | tf_op jit(solution)/shard_map/dynamic_slice | solution.py:440
  25.7 2.3 %shard_map.112 = (f32[7,256,256]{2,1,0:T(8,128)S(1)}, s32[7]{0:T(128)S(1)}) custom-call(s32[1]{0:T(128)} %bitcast.me_ref, s32[8,1,256]{2,1,0:T(1,128)S(1)} %bitcast.16, s32[2,16]{1,0:T(2,128)S(1)} %copy-done.11), custom_call_target="tpu_custom_call" | custom-call | bytes 1835008 | tf_op jit(solution)/shard_map/pallas_call | solution.py:44
  28.1 0.0 collective-permute-done.3.far_ref
  28.1 13.6 %shard_map.115 = (bf16[1792,2048]{1,0:T(8,128)(2,1)}, f32[256,1024]{1,0:T(8,128)S(1)}, f32[256,128]{1,0:T(8,128)S(1)}, bf16[1792,128]{1,0:T(8,128)(2,1)S(1)}, bf16[1792,128]{1,0:T(8,128)(2,1)S(1)}) custom-call(s32[7]{0:T(128)S(1)} %fusion.1.slot_ref, bf16[256,2048]{1,0:T(8,128)(2,1)S(1)} %copy-done, bf16[4,256,512]{2,1,0:T(8,128)(2,1)S(1)} %pad_maximum_fusion.near_ref, ...), custom_call_target="tpu_custom_call" | custom-call | flops 2818572288 | bytes 7340032 | tf_op jit(solution)/shard_map/pallas_call | solution.py:44
  41.7 1.0 copy-done.1
  42.7 0.8 copy-done.6
  43.4 0.8 copy-done.8
  44.2 4.7 %collective-permute-done.5.refs_1_ = bf16[256,1280]{1,0:T(8,128)(2,1)} collective-permute-done((bf16[256,1280]{1,0:T(8,128)(2,1)}, bf16[256,1280]{1,0:T(8,128)(2,1)}, u32[]{:S(2)}, u32[]{:S(2)}) %collective-permute-start.5) | collective-permute-done | bytes 655392 | tf_op jit(solution)/shard_map/ppermute | solution.py:394
  48.9 3.4 %collective-permute-start.7 = (bf16[256,1280]{1,0:T(8,128)(2,1)}, bf16[256,1280]{1,0:T(8,128)(2,1)S(1)}, u32[]{:S(2)}, u32[]{:S(2)}) collective-permute-start(bf16[256,1280]{1,0:T(8,128)(2,1)} %collective-permute-done.5.refs_1_), channel_id=1, source_target_pairs={{1,0},{2,3},{5,4},{6,7},{9,8},{10,11},{13,12},{14,15},{17,16},{18,... | collective-permute-start | bytes 1966088 | tf_op jit(solution)/shard_map/ppermute | solution.py:394
  52.3 4.4 %collective-permute-start.6 = (bf16[256,1280]{1,0:T(8,128)(2,1)S(1)}, bf16[256,1280]{1,0:T(8,128)(2,1)S(1)}, u32[]{:S(2)}, u32[]{:S(2)}) collective-permute-start(bf16[256,1280]{1,0:T(8,128)(2,1)S(1)} %copy-done.5), channel_id=1, source_target_pairs={{1,2},{2,1},{5,6},{6,5},{9,10},{10,9},{13,14},{14,13},{17,18},{18,... | collective-permute-start | bytes 1966088 | tf_op jit(solution)/shard_map/ppermute | solution.py:394
  56.7 0.1 pad_add_fusion.shard_ref
  56.8 0.1 copy.12.adv_ref
  56.9 0.0 copy-start.4
  56.9 4.6 %shard_map.113.acc_ref = f32[256,2048]{1,0:T(8,128)S(1)} custom-call(s32[1]{0:T(128)} %bitcast.4.shard_ref, bf16[256,1280]{1,0:T(8,128)(2,1)S(1)} %copy-done.5, bf16[2048,5120]{1,0:T(8,128)(2,1)} %refs_3_.1), custom_call_target="tpu_custom_call" | custom-call | flops 1342177280 | bytes 5242880 | tf_op jit(solution)/shard_map/pallas_call | solution.py:347
  61.6 13.3 %shard_map.114 = (bf16[1792,2048]{1,0:T(8,128)(2,1)}, f32[256,1024]{1,0:T(8,128)S(1)}, f32[256,128]{1,0:T(8,128)S(1)}, bf16[1792,128]{1,0:T(8,128)(2,1)S(1)}, bf16[1792,128]{1,0:T(8,128)(2,1)S(1)}) custom-call(s32[7]{0:T(128)S(1)} %fusion.1.slot_ref, bf16[256,2048]{1,0:T(8,128)(2,1)S(1)} %copy-done, bf16[4,256,512]{2,1,0:T(8,128)(2,1)S(1)} %copy-done.4, ...), custom_call_target="tpu_custom_call" | custom-call | flops 2818572288 | bytes 7340032 | tf_op jit(solution)/shard_map/pallas_call | solution.py:44
  75.0 0.0 slice-start
  75.0 0.0 slice-start.5
  75.0 8.5 %shard_map.116.proj_ref = f32[256,2048]{1,0:T(8,128)S(1)} custom-call(s32[2]{0:T(128)S(1)} %pad_add_fusion.shard_ref, f32[256,2048]{1,0:T(8,128)S(1)} %shard_map.113.acc_ref, bf16[256,1280]{1,0:T(8,128)(2,1)} %collective-permute-done.4.refs_0_, bf16[256,1280]{1,0:T(8,128)(2,1)} %collective-permute-done.5.refs_1_, bf16[2048,5120]{1,0:T(8,128)(2,1)} %refs_3_.1, ...), custom_call_target="tpu_custom_call" | custom-call | flops 2684354560 | bytes 10485760 | tf_op jit(solution)/shard_map/pallas_call | solution.py:347
  83.7 6.8 %shard_map.118 = (bf16[256,1024]{1,0:T(8,128)(2,1)S(1)}, bf16[3,2,256,128]{3,2,1,0:T(8,128)(2,1)S(1)}, bf16[4,2,256,128]{3,2,1,0:T(8,128)(2,1)S(1)}) custom-call(s32[7]{0:T(128)S(1)} %get-tuple-element.36.live_ref, s32[7]{0:T(128)S(1)} %compare_select_fusion.5.pos_ref, f32[256,2048]{1,0:T(8,128)S(1)} %shard_map.116.proj_ref, ...), custom_call_target="tpu_custom_call" | custom-call | flops 4697620480 | bytes 7340032 | tf_op jit(solution)/shard_map/pallas_call | solution.py:44
  90.4 0.7 collective-permute-start.12
  91.2 6.8 %shard_map.117 = (bf16[256,1024]{1,0:T(8,128)(2,1)S(1)}, bf16[3,2,256,128]{3,2,1,0:T(8,128)(2,1)S(1)}, bf16[4,2,256,128]{3,2,1,0:T(8,128)(2,1)S(1)}) custom-call(s32[7]{0:T(128)S(1)} %get-tuple-element.36.live_ref, s32[7]{0:T(128)S(1)} %compare_select_fusion.5.pos_ref, f32[256,2048]{1,0:T(8,128)S(1)} %shard_map.116.proj_ref, ...), custom_call_target="tpu_custom_call" | custom-call | flops 4697620480 | bytes 7340032 | tf_op jit(solution)/shard_map/pallas_call | solution.py:44
  97.9 1.2 %collective-permute-start.8 = (bf16[3,2,256,128]{3,2,1,0:T(8,128)(2,1)S(1)}, bf16[3,2,256,128]{3,2,1,0:T(8,128)(2,1)S(1)}, u32[]{:S(2)}, u32[]{:S(2)}) collective-permute-start(bf16[3,2,256,128]{3,2,1,0:T(8,128)(2,1)S(1)} %get-tuple-element.55), channel_id=1, source_target_pairs={{0,4},{4,0},{8,12},{12,8},{16,20},{20,16},{24,28},{28,24},{1,5},{5... | collective-permute-start | bytes 1179656 | tf_op jit(solution)/shard_map/ppermute | solution.py:397
  99.2 0.1 shard_map.120
  99.3 1.9 %collective-permute-start.13 = (bf16[2,256,128]{2,1,0:T(8,128)(2,1)S(1)}, bf16[2,256,128]{2,1,0:T(8,128)(2,1)S(1)}, u32[]{:S(2)}, u32[]{:S(2)}) collective-permute-start(bf16[2,256,128]{2,1,0:T(8,128)(2,1)S(1)} %get-tuple-element.64), channel_id=1, source_target_pairs={{0,8},{8,0},{4,12},{12,4},{24,16},{28,20},{1,9},{9,1},{5,13},{13,5... | collective-permute-start | bytes 393224 | tf_op jit(solution)/shard_map/ppermute | solution.py:397
  101.2 1.3 %collective-permute-start.14 = (bf16[2,256,128]{2,1,0:T(8,128)(2,1)S(1)}, bf16[2,256,128]{2,1,0:T(8,128)(2,1)S(1)}, u32[]{:S(2)}, u32[]{:S(2)}) collective-permute-start(bf16[2,256,128]{2,1,0:T(8,128)(2,1)S(1)} %get-tuple-element.65), channel_id=1, source_target_pairs={{16,0},{20,4},{24,8},{28,12},{17,1},{21,5},{25,9},{29,13},{18,2},{... | collective-permute-start | bytes 393224 | tf_op jit(solution)/shard_map/ppermute | solution.py:397
  102.5 1.3 %collective-permute-start.15 = (bf16[2,256,128]{2,1,0:T(8,128)(2,1)S(1)}, bf16[2,256,128]{2,1,0:T(8,128)(2,1)S(1)}, u32[]{:S(2)}, u32[]{:S(2)}) collective-permute-start(bf16[2,256,128]{2,1,0:T(8,128)(2,1)S(1)} %get-tuple-element.66), channel_id=1, source_target_pairs={{16,8},{20,12},{24,0},{28,4},{17,9},{21,13},{25,1},{29,5},{18,10},... | collective-permute-start | bytes 393224 | tf_op jit(solution)/shard_map/ppermute | solution.py:397
  103.8 0.1 shard_map.119
  103.9 1.3 %collective-permute-start.10 = (bf16[2,256,128]{2,1,0:T(8,128)(2,1)S(1)}, bf16[2,256,128]{2,1,0:T(8,128)(2,1)S(1)}, u32[]{:S(2)}, u32[]{:S(2)}) collective-permute-start(bf16[2,256,128]{2,1,0:T(8,128)(2,1)S(1)} %get-tuple-element.59), channel_id=1, source_target_pairs={{16,0},{20,4},{24,8},{28,12},{17,1},{21,5},{25,9},{29,13},{18,2},{... | collective-permute-start | bytes 393224 | tf_op jit(solution)/shard_map/ppermute | solution.py:397
  105.2 1.3 %collective-permute-start.11 = (bf16[2,256,128]{2,1,0:T(8,128)(2,1)S(1)}, bf16[2,256,128]{2,1,0:T(8,128)(2,1)S(1)}, u32[]{:S(2)}, u32[]{:S(2)}) collective-permute-start(bf16[2,256,128]{2,1,0:T(8,128)(2,1)S(1)} %get-tuple-element.60), channel_id=1, source_target_pairs={{16,8},{20,12},{24,0},{28,4},{17,9},{21,13},{25,1},{29,5},{18,10},... | collective-permute-start | bytes 393224 | tf_op jit(solution)/shard_map/ppermute | solution.py:397
  106.5 0.1 collective-permute-done.13.refs_5_
  106.6 3.9 %collective-permute-start.9 = (bf16[2,256,128]{2,1,0:T(8,128)(2,1)S(1)}, bf16[2,256,128]{2,1,0:T(8,128)(2,1)S(1)}, u32[]{:S(2)}, u32[]{:S(2)}) collective-permute-start(bf16[2,256,128]{2,1,0:T(8,128)(2,1)S(1)} %get-tuple-element.58), channel_id=1, source_target_pairs={{0,8},{8,0},{4,12},{12,4},{24,16},{28,20},{1,9},{9,1},{5,13},{13,5... | collective-permute-start | bytes 393224 | tf_op jit(solution)/shard_map/ppermute | solution.py:397
  110.5 1.1 pad_maximum_fusion.1
  111.5 7.3 %collective-permute-done.14.refs_6_ = bf16[2,256,128]{2,1,0:T(8,128)(2,1)S(1)} collective-permute-done((bf16[2,256,128]{2,1,0:T(8,128)(2,1)S(1)}, bf16[2,256,128]{2,1,0:T(8,128)(2,1)S(1)}, u32[]{:S(2)}, u32[]{:S(2)}) %collective-permute-start.14) | collective-permute-done | bytes 131104 | tf_op jit(solution)/shard_map/ppermute | solution.py:397
  118.8 2.3 %collective-permute-done.10.refs_2_ = bf16[2,256,128]{2,1,0:T(8,128)(2,1)S(1)} collective-permute-done((bf16[2,256,128]{2,1,0:T(8,128)(2,1)S(1)}, bf16[2,256,128]{2,1,0:T(8,128)(2,1)S(1)}, u32[]{:S(2)}, u32[]{:S(2)}) %collective-permute-start.10) | collective-permute-done | bytes 131104 | tf_op jit(solution)/shard_map/ppermute | solution.py:397
  121.1 0.8 shard_map.121
  (50 shorter events, 0.1 us)
Async XLA Ops:
  2.5 9.3 %collective-permute-start = (bf16[256,512]{1,0:T(8,128)(2,1)S(1)}, bf16[256,512]{1,0:T(8,128)(2,1)S(1)}, u32[]{:S(2)}, u32[]{:S(2)}) collective-permute-start(bf16[256,512]{1,0:T(8,128)(2,1)S(1)} %constant_dynamic-update-slice_fusion), channel_id=1, source_target_pairs={{0,8},{4,12},{8,0},{12,4},{16,24},{20,28},{24,16},{28,20},{1,9},{5... | collective-permute-start | bytes 786440 | tf_op jit(solution)/shard_map/ppermute | solution.py:397
  3.1 12.5 %collective-permute-start.1 = (bf16[256,512]{1,0:T(8,128)(2,1)S(1)}, bf16[256,512]{1,0:T(8,128)(2,1)S(1)}, u32[]{:S(2)}, u32[]{:S(2)}) collective-permute-start(bf16[256,512]{1,0:T(8,128)(2,1)S(1)} %constant_dynamic-update-slice_fusion), channel_id=1, source_target_pairs={{0,16},{4,20},{8,24},{12,28},{16,0},{20,4},{24,8},{28,12},{1,17},{... | collective-permute-start | bytes 786440 | tf_op jit(solution)/shard_map/ppermute | solution.py:397
  4.6 12.6 %collective-permute-start.2 = (bf16[256,512]{1,0:T(8,128)(2,1)S(1)}, bf16[256,512]{1,0:T(8,128)(2,1)S(1)}, u32[]{:S(2)}, u32[]{:S(2)}) collective-permute-start(bf16[256,512]{1,0:T(8,128)(2,1)S(1)} %constant_dynamic-update-slice_fusion), channel_id=1, source_target_pairs={{0,24},{4,28},{8,16},{12,20},{16,8},{20,12},{24,0},{28,4},{1,25},{... | collective-permute-start | bytes 786440 | tf_op jit(solution)/shard_map/ppermute | solution.py:397
  17.3 10.8 %copy-start.3 = (bf16[4,256,512]{2,1,0:T(8,128)(2,1)}, bf16[4,256,512]{2,1,0:T(8,128)(2,1)S(1)}, u32[]{:S(2)}) copy-start(bf16[4,256,512]{2,1,0:T(8,128)(2,1)S(1)} %pad_maximum_fusion.near_ref) | copy-start | bytes 3145732
  17.3 10.8 %collective-permute-start.3 = (bf16[4,256,512]{2,1,0:T(8,128)(2,1)S(1)}, bf16[4,256,512]{2,1,0:T(8,128)(2,1)}, u32[]{:S(2)}, u32[]{:S(2)}) collective-permute-start(bf16[4,256,512]{2,1,0:T(8,128)(2,1)S(1)} %pad_maximum_fusion.near_ref), channel_id=1, source_target_pairs={{0,4},{4,0},{8,12},{12,8},{16,20},{20,16},{24,28},{28,24},{1,5},{5... | collective-permute-start | bytes 3145736 | tf_op jit(solution)/shard_map/ppermute | solution.py:397
  17.4 31.5 %collective-permute-start.5 = (bf16[256,1280]{1,0:T(8,128)(2,1)}, bf16[256,1280]{1,0:T(8,128)(2,1)}, u32[]{:S(2)}, u32[]{:S(2)}) collective-permute-start(bf16[256,1280]{1,0:T(8,128)(2,1)} %refs_0_.1), channel_id=1, source_target_pairs={{0,2},{2,0},{1,3},{3,1},{4,6},{6,4},{5,7},{7,5},{8,10},{10,8},{9,1... | collective-permute-start | bytes 1966088 | tf_op jit(solution)/shard_map/ppermute | solution.py:394
  20.0 55.0 %collective-permute-start.4 = (bf16[256,1280]{1,0:T(8,128)(2,1)}, bf16[256,1280]{1,0:T(8,128)(2,1)}, u32[]{:S(2)}, u32[]{:S(2)}) collective-permute-start(bf16[256,1280]{1,0:T(8,128)(2,1)} %refs_0_.1), channel_id=1, source_target_pairs={{0,1},{1,0},{2,3},{3,2},{4,5},{5,4},{6,7},{7,6},{8,9},{9,8},{10,11... | collective-permute-start | bytes 1966088 | tf_op jit(solution)/shard_map/ppermute | solution.py:394
  20.5 5.2 %copy-start.10 = (s32[2048]{0:T(1024)S(1)}, s32[2048]{0:T(1024)}, u32[]{:S(2)}) copy-start(s32[2048]{0:T(1024)} %param.15) | copy-start | bytes 24580
  20.5 5.2 %copy-start.11 = (s32[2,16]{1,0:T(2,128)S(1)}, s32[2,16]{1,0:T(2,128)}, u32[]{:S(2)}) copy-start(s32[2,16]{1,0:T(2,128)} %tile_ref.1) | copy-start | bytes 388
  20.5 7.5 %copy-start.15 = (s32[7]{0:T(128)S(1)}, s32[7]{0:T(128)}, u32[]{:S(2)}) copy-start(s32[7]{0:T(128)} %constant.88.clone) | copy-start | bytes 88
  20.5 7.6 %copy-start = (bf16[256,2048]{1,0:T(8,128)(2,1)S(1)}, bf16[256,2048]{1,0:T(8,128)(2,1)}, u32[]{:S(2)}) copy-start(bf16[256,2048]{1,0:T(8,128)(2,1)} %q_ref.7) | copy-start | bytes 3145732
  25.7 26.6 %copy-start.5 = (bf16[256,1280]{1,0:T(8,128)(2,1)S(1)}, bf16[256,1280]{1,0:T(8,128)(2,1)}, u32[]{:S(2)}) copy-start(bf16[256,1280]{1,0:T(8,128)(2,1)} %refs_0_.1) | copy-start | bytes 1966084
  25.7 31.1 %copy-start.14 = (f32[256]{0:T(256)S(1)}, f32[256]{0:T(256)}, u32[]{:S(2)}) copy-start(f32[256]{0:T(256)} %param.10) | copy-start | bytes 3076
  28.0 28.8 %copy-start.12 = (f32[7,256,256]{2,1,0:T(8,128)}, f32[7,256,256]{2,1,0:T(8,128)S(1)}, u32[]{:S(2)}) copy-start(f32[7,256,256]{2,1,0:T(8,128)S(1)} %get-tuple-element.37.bias_ref) | copy-start | bytes 5505028
  41.6 1.0 copy-start.1
  42.7 0.8 copy-start.6
  43.4 0.8 copy-start.8
  48.9 34.7 %collective-permute-start.7 = (bf16[256,1280]{1,0:T(8,128)(2,1)}, bf16[256,1280]{1,0:T(8,128)(2,1)S(1)}, u32[]{:S(2)}, u32[]{:S(2)}) collective-permute-start(bf16[256,1280]{1,0:T(8,128)(2,1)} %collective-permute-done.5.refs_1_), channel_id=1, source_target_pairs={{1,0},{2,3},{5,4},{6,7},{9,8},{10,11},{13,12},{14,15},{17,16},{18,... | collective-permute-start | bytes 1966088 | tf_op jit(solution)/shard_map/ppermute | solution.py:394
  52.3 31.3 %collective-permute-start.6 = (bf16[256,1280]{1,0:T(8,128)(2,1)S(1)}, bf16[256,1280]{1,0:T(8,128)(2,1)S(1)}, u32[]{:S(2)}, u32[]{:S(2)}) collective-permute-start(bf16[256,1280]{1,0:T(8,128)(2,1)S(1)} %copy-done.5), channel_id=1, source_target_pairs={{1,2},{2,1},{5,6},{6,5},{9,10},{10,9},{13,14},{14,13},{17,18},{18,... | collective-permute-start | bytes 1966088 | tf_op jit(solution)/shard_map/ppermute | solution.py:394
  56.9 4.7 %copy-start.4 = (bf16[4,256,512]{2,1,0:T(8,128)(2,1)S(1)}, bf16[4,256,512]{2,1,0:T(8,128)(2,1)}, u32[]{:S(2)}) copy-start(bf16[4,256,512]{2,1,0:T(8,128)(2,1)} %copy-done.3) | copy-start | bytes 3145732
  56.9 4.7 %copy-start.13 = (f32[7,256,256]{2,1,0:T(8,128)S(1)}, f32[7,256,256]{2,1,0:T(8,128)}, u32[]{:S(2)}) copy-start(f32[7,256,256]{2,1,0:T(8,128)} %copy-done.12) | copy-start | bytes 5505028
  61.6 29.5 %slice-start.2 = ((s8[7340032]{0:T(1024)(128)(4,1)}), s8[4194304]{0:T(1024)(128)(4,1)S(1)}, s32[]{:S(2)}) async-start(s8[7340032]{0:T(1024)(128)(4,1)} %bitcast.12), calls=%async_computation.2 | async-start | bytes 8388608
  75.0 8.6 %slice-start = ((s8[5242880]{0:T(1024)(128)(4,1)}), s8[4194304]{0:T(1024)(128)(4,1)S(1)}, s32[]{:S(2)}) async-start(s8[5242880]{0:T(1024)(128)(4,1)} %bitcast.10), calls=%async_computation | async-start | bytes 8388608
  75.0 8.6 %slice-start.4 = ((s8[7340032]{0:T(1024)(128)(4,1)}), s8[4194304]{0:T(1024)(128)(4,1)S(1)}, s32[]{:S(2)}) async-start(s8[7340032]{0:T(1024)(128)(4,1)} %bitcast.14), calls=%async_computation.4 | async-start | bytes 8388608
  75.0 8.6 %slice-start.1 = ((s8[5242880]{0:T(1024)(128)(4,1)}), s8[1048576]{0:T(1024)(128)(4,1)S(1)}, s32[]{:S(2)}) async-start(s8[5242880]{0:T(1024)(128)(4,1)} %bitcast.10), calls=%async_computation.1 | async-start | bytes 2097152
  75.0 8.6 %slice-start.5 = ((s8[7340032]{0:T(1024)(128)(4,1)}), s8[3145728]{0:T(1024)(128)(4,1)S(1)}, s32[]{:S(2)}) async-start(s8[7340032]{0:T(1024)(128)(4,1)} %bitcast.14), calls=%async_computation.5 | async-start | bytes 6291456
  75.0 16.1 %slice-start.3 = ((s8[7340032]{0:T(1024)(128)(4,1)}), s8[3145728]{0:T(1024)(128)(4,1)S(1)}, s32[]{:S(2)}) async-start(s8[7340032]{0:T(1024)(128)(4,1)} %bitcast.12), calls=%async_computation.3 | async-start | bytes 6291456
  83.6 7.5 %copy-start.2 = (f32[256,1024]{1,0:T(8,128)S(1)}, f32[256,1024]{1,0:T(8,128)}, u32[]{:S(2)}) copy-start(f32[256,1024]{1,0:T(8,128)} %copy-done.1) | copy-start | bytes 3145732
  83.6 7.5 %copy-start.7 = (bf16[1792,128]{1,0:T(8,128)(2,1)S(1)}, bf16[1792,128]{1,0:T(8,128)(2,1)}, u32[]{:S(2)}) copy-start(bf16[1792,128]{1,0:T(8,128)(2,1)} %copy-done.6) | copy-start | bytes 1376260
  83.6 7.5 %copy-start.9 = (bf16[1792,128]{1,0:T(8,128)(2,1)S(1)}, bf16[1792,128]{1,0:T(8,128)(2,1)}, u32[]{:S(2)}) copy-start(bf16[1792,128]{1,0:T(8,128)(2,1)} %copy-done.8) | copy-start | bytes 1376260
  90.4 8.7 %collective-permute-start.12 = (bf16[3,2,256,128]{3,2,1,0:T(8,128)(2,1)S(1)}, bf16[3,2,256,128]{3,2,1,0:T(8,128)(2,1)S(1)}, u32[]{:S(2)}, u32[]{:S(2)}) collective-permute-start(bf16[3,2,256,128]{3,2,1,0:T(8,128)(2,1)S(1)} %get-tuple-element.61), channel_id=1, source_target_pairs={{0,4},{4,0},{8,12},{12,8},{16,20},{20,16},{24,28},{28,24},{1,5},{5... | collective-permute-start | bytes 1179656 | tf_op jit(solution)/shard_map/ppermute | solution.py:397
  97.9 5.9 %collective-permute-start.8 = (bf16[3,2,256,128]{3,2,1,0:T(8,128)(2,1)S(1)}, bf16[3,2,256,128]{3,2,1,0:T(8,128)(2,1)S(1)}, u32[]{:S(2)}, u32[]{:S(2)}) collective-permute-start(bf16[3,2,256,128]{3,2,1,0:T(8,128)(2,1)S(1)} %get-tuple-element.55), channel_id=1, source_target_pairs={{0,4},{4,0},{8,12},{12,8},{16,20},{20,16},{24,28},{28,24},{1,5},{5... | collective-permute-start | bytes 1179656 | tf_op jit(solution)/shard_map/ppermute | solution.py:397
  99.3 7.3 %collective-permute-start.13 = (bf16[2,256,128]{2,1,0:T(8,128)(2,1)S(1)}, bf16[2,256,128]{2,1,0:T(8,128)(2,1)S(1)}, u32[]{:S(2)}, u32[]{:S(2)}) collective-permute-start(bf16[2,256,128]{2,1,0:T(8,128)(2,1)S(1)} %get-tuple-element.64), channel_id=1, source_target_pairs={{0,8},{8,0},{4,12},{12,4},{24,16},{28,20},{1,9},{9,1},{5,13},{13,5... | collective-permute-start | bytes 393224 | tf_op jit(solution)/shard_map/ppermute | solution.py:397
  101.2 17.6 %collective-permute-start.14 = (bf16[2,256,128]{2,1,0:T(8,128)(2,1)S(1)}, bf16[2,256,128]{2,1,0:T(8,128)(2,1)S(1)}, u32[]{:S(2)}, u32[]{:S(2)}) collective-permute-start(bf16[2,256,128]{2,1,0:T(8,128)(2,1)S(1)} %get-tuple-element.65), channel_id=1, source_target_pairs={{16,0},{20,4},{24,8},{28,12},{17,1},{21,5},{25,9},{29,13},{18,2},{... | collective-permute-start | bytes 393224 | tf_op jit(solution)/shard_map/ppermute | solution.py:397
  102.5 16.3 %collective-permute-start.15 = (bf16[2,256,128]{2,1,0:T(8,128)(2,1)S(1)}, bf16[2,256,128]{2,1,0:T(8,128)(2,1)S(1)}, u32[]{:S(2)}, u32[]{:S(2)}) collective-permute-start(bf16[2,256,128]{2,1,0:T(8,128)(2,1)S(1)} %get-tuple-element.66), channel_id=1, source_target_pairs={{16,8},{20,12},{24,0},{28,4},{17,9},{21,13},{25,1},{29,5},{18,10},... | collective-permute-start | bytes 393224 | tf_op jit(solution)/shard_map/ppermute | solution.py:397
  103.9 17.2 %collective-permute-start.10 = (bf16[2,256,128]{2,1,0:T(8,128)(2,1)S(1)}, bf16[2,256,128]{2,1,0:T(8,128)(2,1)S(1)}, u32[]{:S(2)}, u32[]{:S(2)}) collective-permute-start(bf16[2,256,128]{2,1,0:T(8,128)(2,1)S(1)} %get-tuple-element.59), channel_id=1, source_target_pairs={{16,0},{20,4},{24,8},{28,12},{17,1},{21,5},{25,9},{29,13},{18,2},{... | collective-permute-start | bytes 393224 | tf_op jit(solution)/shard_map/ppermute | solution.py:397
  105.2 15.9 %collective-permute-start.11 = (bf16[2,256,128]{2,1,0:T(8,128)(2,1)S(1)}, bf16[2,256,128]{2,1,0:T(8,128)(2,1)S(1)}, u32[]{:S(2)}, u32[]{:S(2)}) collective-permute-start(bf16[2,256,128]{2,1,0:T(8,128)(2,1)S(1)} %get-tuple-element.60), channel_id=1, source_target_pairs={{16,8},{20,12},{24,0},{28,4},{17,9},{21,13},{25,1},{29,5},{18,10},... | collective-permute-start | bytes 393224 | tf_op jit(solution)/shard_map/ppermute | solution.py:397
  106.6 14.5 %collective-permute-start.9 = (bf16[2,256,128]{2,1,0:T(8,128)(2,1)S(1)}, bf16[2,256,128]{2,1,0:T(8,128)(2,1)S(1)}, u32[]{:S(2)}, u32[]{:S(2)}) collective-permute-start(bf16[2,256,128]{2,1,0:T(8,128)(2,1)S(1)} %get-tuple-element.58), channel_id=1, source_target_pairs={{0,8},{8,0},{4,12},{12,4},{24,16},{28,20},{1,9},{9,1},{5,13},{13,5... | collective-permute-start | bytes 393224 | tf_op jit(solution)/shard_map/ppermute | solution.py:397

commit v4 on v3

--- a/solution.py
+++ b/solution.py
@@ -16,7 +16,7 @@
 ROLLOUTS = 8
 JITTER = 64
 KB = 256
-VMEM_LIMIT = 20 << 20
+VMEM_LIMIT = 26 << 20
 SCALE = 1.0 / math.sqrt(HD)
 LOG2E = 1.4426950408889634
 F32 = jnp.float32
@@ -97,21 +97,20 @@
 
 def probs_kernel(
     n_kb, group, groups, slot_ref, q_ref, near_ref, far_ref, bias_ref,
-    p_ref, o_ref, inv_ref, k_ref, v_ref, kx_ref, vt_ref, s_ref, t_ref, a_ref, b_ref, sems,
+    p_ref, o_ref, k_ref, v_ref,
+    ks_ref, vs_ref, kx_ref, vt_ref, s_ref, t_ref, pa_ref, pb_ref, oa_ref, ob_ref, sems,
 ):
     rows = q_ref.shape[0]
     per = rows // KB
     n_near = near_ref.shape[0]
-    lane = lax.broadcasted_iota(jnp.int32, (KB, HD), 1)
-    inv_ref[...] = jnp.zeros_like(inv_ref)
     vt_ref[HD:, :] = jnp.ones((16, n_kb * KB), BF16)
     for kb in range(n_kb):
         slot = slot_ref[kb]
         keys = pl.ds(kb * KB, KB)
 
         def place(source, index):
-            k_ref[keys, :] = source[index, :, group * HD : (group + 1) * HD]
-            v_ref[keys, :] = source[index, :, (groups + group) * HD : (groups + group + 1) * HD]
+            ks_ref[keys, :] = source[index, :, group * HD : (group + 1) * HD]
+            vs_ref[keys, :] = source[index, :, (groups + group) * HD : (groups + group + 1) * HD]
 
         @pl.when(slot < n_near)
         def _():
@@ -121,21 +120,21 @@
         def _():
             place(far_ref, slot - n_near)
 
+    keep_k = pltpu.make_async_copy(ks_ref, k_ref, sems.at[4])
+    keep_v = pltpu.make_async_copy(vs_ref, v_ref, sems.at[5])
+    keep_k.start()
+    keep_v.start()
     for kb in range(n_kb):
         keys = pl.ds(kb * KB, KB)
-        k = k_ref[keys, :]
+        k = ks_ref[keys, :]
         kx_ref[keys, :HD] = k
         kx_ref[keys, HD:] = k
-        vt_ref[:HD, keys] = v_ref[keys, :].T
+        vt_ref[:HD, keys] = vs_ref[keys, :].T
 
     count = SHARE * per
 
-    def places(i):
-        h, r = i // per, i % per
-        return h, at(r * KB, KB), at((h * per + r) * KB, KB)
-
     def score(i, s_ref):
-        h, here, _ = places(i)
+        h, here = i // per, at((i % per) * KB, KB)
         q = q_ref[here, at((group * SHARE + h) * HD, HD)].astype(F32) * (SCALE * LOG2E)
         q_hi = q.astype(BF16)
         q_lo = (q - q_hi.astype(F32)).astype(BF16)
@@ -144,93 +143,109 @@
         s_ref[...] = s
         return jnp.max(s, axis=0, keepdims=True)
 
-    def out(i, e_ref, sem):
-        return pltpu.make_async_copy(e_ref, p_ref.at[:, places(i)[2]], sem)
-
-    def soften(i, s_ref, top, e_ref, sem):
-        h, here, cols = places(i)
+    def out(i, side):
+        p_side, o_side = ((pa_ref, oa_ref), (pb_ref, ob_ref))[side]
+        return (
+            pltpu.make_async_copy(p_side, p_ref.at[i], sems.at[side]),
+            pltpu.make_async_copy(o_side, o_ref.at[i], sems.at[2 + side]),
+        )
+
+    def soften(i, s_ref, top, side):
+        p_side, o_side = ((pa_ref, oa_ref), (pb_ref, ob_ref))[side]
         e = jnp.exp2(s_ref[...] - top).astype(BF16)
 
         @pl.when(i >= 2)
         def _():
-            out(i - 2, e_ref, sem).wait()
-
-        e_ref[...] = e
-        out(i, e_ref, sem).start()
+            for copy in out(i - 2, side):
+                copy.wait()
+
+        p_side[...] = e
         acc = dot(vt_ref[...], e)
         inv = 1.0 / acc[HD : HD + 1, :]
-        o_ref[here, at(h * HD, HD)] = (acc[:HD] * inv).T
-        inv_ref[here, :] += jnp.where(lane == h, jnp.broadcast_to(inv, (HD, KB)).T, 0.0)
+        o_side[:, :HD] = (acc[:HD] * inv).T
+        o_side[:, HD:] = jnp.broadcast_to(inv, (HD, KB)).T
+        for copy in out(i, side):
+            copy.start()
 
     def step(j, top):
         later = score(2 * j + 1, t_ref)
-        soften(2 * j, s_ref, top, a_ref, sems.at[0])
+        soften(2 * j, s_ref, top, 0)
         top = score(jnp.minimum(2 * j + 2, count - 1), s_ref)
-        soften(2 * j + 1, t_ref, later, b_ref, sems.at[1])
+        soften(2 * j + 1, t_ref, later, 1)
         return top
 
     lax.fori_loop(0, count // 2, step, score(0, s_ref))
-    out(count - 2, a_ref, sems.at[0]).wait()
-    out(count - 1, b_ref, sems.at[1]).wait()
+    for side in range(2):
+        for copy in out(count - 2 + side, side):
+            copy.wait()
+    keep_k.wait()
+    keep_v.wait()
+
+
+HBM = pl.BlockSpec(memory_space=pltpu.HBM)
 
 
 def probs_call(group, groups, slots, q, near, far, bias, n_kb):
     rows = q.shape[0]
     keys = n_kb * KB
+    blocks = SHARE * rows // KB
     return call(
         functools.partial(probs_kernel, n_kb, group, groups),
         (slots, q, near, far, bias),
         [SMEM, VMEM, VMEM, VMEM, VMEM],
         [
-            pltpu.HBM((keys, SHARE * rows), BF16),
-            ((rows, SHARE * HD), F32),
-            ((rows, HD), F32),
-            ((keys, HD), BF16),
-            ((keys, HD), BF16),
+            pltpu.HBM((blocks, keys, KB), BF16),
+            pltpu.HBM((blocks, KB, 2 * HD), F32),
+            pltpu.HBM((keys, HD), BF16),
+            pltpu.HBM((keys, HD), BF16),
         ],
         scratch=[
+            pltpu.VMEM((keys, HD), BF16),
+            pltpu.VMEM((keys, HD), BF16),
             pltpu.VMEM((keys, 2 * HD), BF16),
             pltpu.VMEM((HD + 16, keys), BF16),
             pltpu.VMEM((keys, KB), F32),
             pltpu.VMEM((keys, KB), F32),
             pltpu.VMEM((keys, KB), BF16),
             pltpu.VMEM((keys, KB), BF16),
-            pltpu.SemaphoreType.DMA((2,)),
+            pltpu.VMEM((KB, 2 * HD), F32),
+            pltpu.VMEM((KB, 2 * HD), F32),
+            pltpu.SemaphoreType.DMA((6,)),
         ],
-        out_specs=[pl.BlockSpec(memory_space=pltpu.HBM)] + [VMEM] * 4,
-        flops=6 * SHARE * rows * keys * HD,
-        size=SHARE * rows * keys * 2,
-        exps=SHARE * rows * keys,
+        out_specs=[HBM] * 4,
     )
 
 
 def back_kernel(
     n_kb, n_send, first, live_ref, pos_ref, proj_ref, x1_ref, x2_ref, w_ref, adv_ref, o_ref,
-    inv_ref, q_ref, k_ref, v_ref, p_ref,
+    q_ref, k_ref, v_ref, p_ref,
     dq_ref, send_ref, keep_ref, dox_ref, qs_ref, ds_ref, dqt_ref,
 ):
     rows = proj_ref.shape[0]
-    lane = lax.broadcasted_iota(jnp.int32, (rows, HD), 1)
-    minus = jnp.where(lax.broadcasted_iota(jnp.int32, (KB, HD), 1) < 3, -1.0, 0.0).astype(BF16)
+    per = rows // KB
+    lane = lax.broadcasted_iota(jnp.int32, (KB, HD), 1)
+    minus = jnp.where(lane < 3, -1.0, 0.0).astype(BF16)
     x = x1_ref[...] + x2_ref[...]
     dqt_ref[...] = jnp.zeros_like(dqt_ref)
     for h in range(SHARE):
-        head = first + h
-        cols = pl.ds(head * HD, HD)
-        here = pl.ds(h * rows, rows)
-        inv = inv_ref[:, h : h + 1]
-        proj = proj_ref[:, cols] + dot_nt(x, w_ref[cols, :])
-        grad = (proj * (adv_ref[...] * inv)).astype(BF16)
-        delta = jnp.sum(grad.astype(F32) * o_ref[:, h * HD : (h + 1) * HD], axis=1, keepdims=True)
-        one = delta.astype(BF16).astype(F32)
-        two = (delta - one).astype(BF16).astype(F32)
-        three = delta - one - two
-        ext = jnp.where(
-            lane == 0, one, jnp.where(lane == 1, two, jnp.where(lane == 2, three, 0.0))
-        )
-        dox_ref[here, :HD] = grad
-        dox_ref[here, HD:] = ext.astype(BF16)
-        qs_ref[here, :] = q_ref[:, cols]
+        cols = pl.ds((first + h) * HD, HD)
+        fresh = dot_nt(x, w_ref[cols, :])
+        for r in range(per):
+            part = slice(r * KB, (r + 1) * KB)
+            here = pl.ds((h * per + r) * KB, KB)
+            out = o_ref[h * per + r]
+            proj = proj_ref[part, cols] + fresh[part]
+            grad = (proj * (adv_ref[part, :] * out[:, HD:])).astype(BF16)
+            delta = jnp.sum(grad.astype(F32) * out[:, :HD], axis=1, keepdims=True)
+            one = delta.astype(BF16).astype(F32)
+            two = (delta - one).astype(BF16).astype(F32)
+            three = delta - one - two
+            ext = jnp.where(
+                lane == 0, one, jnp.where(lane == 1, two, jnp.where(lane == 2, three, 0.0))
+            )
+            dox_ref[here, :HD] = grad
+            dox_ref[here, HD:] = ext.astype(BF16)
+            qs_ref[here, :] = q_ref[part, cols]
 
     def step(kb, carry):
         pos = pos_ref[kb]
@@ -249,11 +264,12 @@
             keys = at(kb * KB, KB)
             vx = jnp.concatenate([v_ref[keys, :], minus], axis=1)
             kt = k_ref[keys, :].T
-            dv = dot(p_ref[keys, :], dox_ref[:, :HD])
-            for h in range(SHARE * rows // KB):
-                here = pl.ds(h * KB, KB)
+            p = jnp.concatenate([p_ref[i, keys, :] for i in range(SHARE * per)], axis=1)
+            dv = dot(p, dox_ref[:, :HD])
+            for i in range(SHARE * per):
+                here = pl.ds(i * KB, KB)
                 dp = dot_nt(vx, dox_ref[here, :])
-                ds_ref[:, here] = (p_ref[keys, here].astype(F32) * dp).astype(BF16)
+                ds_ref[:, here] = (p_ref[i, keys, :].astype(F32) * dp).astype(BF16)
             dqt_ref[...] += dot(kt, ds_ref[...])
             dk = dot(ds_ref[...], qs_ref[...])
             put(jnp.stack([dk, dv]).astype(BF16))
@@ -271,15 +287,14 @@
         )
 
 
-def back_call(group, live, pos, proj, x1, x2, w, adv, o, inv, q, k, v, p, n_kb, n_send):
+def back_call(group, live, pos, proj, x1, x2, w, adv, o, q, k, v, p, n_kb, n_send):
     rows = q.shape[0]
-    wide = SHARE * HD
     return call(
         functools.partial(back_kernel, n_kb, n_send, group * SHARE),
-        (live, pos, proj, x1, x2, w, adv, o, inv, q, k, v, p),
-        [SMEM, SMEM] + [VMEM] * 11,
+        (live, pos, proj, x1, x2, w, adv, o, q, k, v, p),
+        [SMEM, SMEM] + [VMEM] * 10,
         [
-            ((rows, wide), BF16),
+            ((rows, SHARE * HD), BF16),
             ((max(n_send, 1), 2, KB, HD), BF16),
             ((n_kb - n_send, 2, KB, HD), BF16),
         ],
@@ -289,8 +304,6 @@
             pltpu.VMEM((KB, SHARE * rows), BF16),
             pltpu.VMEM((HD, SHARE * rows), F32),
         ],
-        flops=10 * SHARE * rows * n_kb * KB * HD,
-        size=SHARE * rows * n_kb * KB * 2,
     )
 
 
@@ -398,9 +411,9 @@
 
     if fast:
         near = jnp.stack([own] + [flip(own, d) for d in (2, 4, 6)])
-        far = flip(near, 1)
-        up_b = hop(upstream, [(0, 2), (2, 0), (1, 3), (3, 1)])
-        up_a = hop(upstream, [(0, 1), (1, 0), (2, 3), (3, 2)])
+        ends, middle, out = [(0, 1), (1, 0), (2, 3), (3, 2)], [(1, 2), (2, 1)], [(1, 0), (2, 3)]
+        up_a = hop(upstream, ends)
+        up_c = hop(upstream, middle)
     else:
         near = lax.all_gather(own, "ctx", axis=0)
         near = far = near.reshape(n_ctx * per, KB, 2 * groups * HD)
@@ -422,7 +435,8 @@
             jnp.array([0, 0, 0, 0, 5, 2, 6], jnp.int32),
         )
         n_send = 3
-        shard = z ^ 3
+        half = z // 2
+        second, shard = 2 - half, 3 - 3 * half
         acc = project_call(z[None], [upstream], weight)
     else:
         slots = holder * per + block % per
@@ -440,27 +454,32 @@
     w_last = lax.dynamic_slice_in_dim(out_weight, shard * depth, depth, 1)
 
     slots = slots.astype(jnp.int32)
+    if fast:
+        near, bias, w_last, acc, up_a, up_c = lax.optimization_barrier(
+            (near, bias, w_last, acc, up_a, up_c)
+        )
+        far = flip(near, 1)
+        up_e = hop(up_a, middle)
+        up_f = hop(up_c, out)
     soft = [list(probs_call(0, groups, slots, query_heads, near, far, bias, n_kb))]
     if fast:
-        up_b, later, head = lax.optimization_barrier((up_b, upstream, soft[0][2]))
-        soft[0][2] = head
-        up_c = hop(later, [(1, 2), (2, 1)])
-        up_d = hop(up_b, [(1, 0), (2, 3)])
-        x1, x2 = up_c, up_d
+        up_e, soft[0][2] = lax.optimization_barrier((up_e, soft[0][2]))
+        up_d = hop(up_e, out)
+        x1, x2 = up_d, up_e
     soft += [
         list(probs_call(g, groups, slots, query_heads, near, far, bias, n_kb))
         for g in range(1, groups)
     ]
     if fast:
         acc, soft[-1][2] = lax.optimization_barrier((acc, soft[-1][2]))
-        acc = project_call(jnp.stack([z ^ 1, z ^ 2]), [up_a, up_b], weight, acc)
+        acc = project_call(jnp.stack([z ^ 1, second]), [up_a, up_c + up_f], weight, acc)
     outs = []
     for g in range(groups):
-        probs, attn, inv, keys, values = soft[g]
+        probs, attn, keys, values = soft[g]
         outs.append(
             back_call(
                 g, live, pos.astype(jnp.int32), acc, x1, x2, w_last, advantage[:, None], attn,
-                inv, query_heads, keys, values, probs, n_kb, n_send,
+                query_heads, keys, values, probs, n_kb, n_send,
             )
         )
     grad_queries = jnp.concatenate([dq for dq, _, _ in outs], axis=1)

time: 122 us -> 114 us (0.934)
  waiting for transfers between devices: 25.5 us -> 10.7 us
  local copies, waits for them, and re-layouts: 9.76 us -> 15.1 us
  other arithmetic: 1.3 us -> 4.21 us
  Pallas kernels: 56.9 us -> 54.7 us
    ppermute x12, waiting for transfers between devices: 20.8 us -> 9.37 us  [flip(): lax.ppermute(value, 'ctx', pairs or [(i, i ^ bit) for i in range(n_ctx)])]
    unnamed x45 -> x51, local copies, waits for them, and re-layouts: 3.53 us -> 8.93 us
    ppermute x4 -> x5, waiting for transfers between devices: 4.69 us -> 1.31 us  [hop(): return lax.ppermute(value, 'tp', pairs)]
    pallas_call x8, Pallas kernels: 43.7 us -> 42.1 us  [call(): pl.pallas_call(kernel, in_specs=in_specs, out_specs=out_specs or [VMEM] *...]
    add x0 -> x1, other arithmetic: none -> 1.55 us  [shards(): up_c + up_f]
    another operation x1, other arithmetic: 0.13 us -> 1.5 us  [shards(): near = jnp.stack([own] + [flip(own, d) for d in (2, 4, 6)])]
    ppermute x4 -> x5, starting transfers between devices: 10.9 us -> 11.3 us  [hop(): return lax.ppermute(value, 'tp', pairs)]
  transfers between devices with their start and end apart: 16 -> 17, of which waited for: 7 -> 3; matrix products, arithmetic and copies ran while one was open for 5% -> 8% of each run, Pallas kernels for 40% -> 41%
where the time goes in v4:
time: 114 us
  Pallas kernels  54.7 us (48%)
  starting transfers between devices  28 us (25%)
  local copies, waits for them, and re-layouts  15.1 us (13%)
  waiting for transfers between devices  10.7 us (9%)
  other arithmetic  4.21 us (4%)
    pallas_call x8, Pallas kernels, call(): pl.pallas_call(kernel, in_specs=in_specs, out_specs=out_specs or [VMEM] *...  42.1 us
    ppermute x12, starting transfers between devices, flip(): lax.ppermute(value, 'ctx', pairs or [(i, i ^ bit) for i in range(n_ctx)])  16.7 us
    pallas_call x2, Pallas kernels, project_call(): pl.pallas_call(project_kernel if acc is None else project_add_kernel, gri...  12.6 us
    ppermute x5, starting transfers between devices, hop(): return lax.ppermute(value, 'tp', pairs)  11.3 us
    ppermute x12, waiting for transfers between devices, flip(): lax.ppermute(value, 'ctx', pairs or [(i, i ^ bit) for i in range(n_ctx)])  9.37 us
    unnamed x51, local copies, waits for them, and re-layouts  8.93 us
    dynamic_slice x1, local copies, waits for them, and re-layouts, shards(): w_last = lax.dynamic_slice_in_dim(out_weight, shard * depth, depth, 1)  5.14 us
  transfers between devices with their start and end apart: 17, of which 3 were waited for; matrix products, arithmetic and copies ran while one was open for 8% of the time, Pallas kernels for 41%

profile of v4, /device:TPU:10, one launch (start us, length us, event | category | flops | bytes accessed | tf_op | source)
XLA Modules:
  0.0 113.8 jit_solution(571465398032312795)
XLA Ops:
  0.6 0.9 constant_dynamic-update-slice_fusion.1
  1.5 0.9 constant_dynamic-update-slice_fusion
  2.5 1.6 %collective-permute-start.2 = (bf16[256,512]{1,0:T(8,128)(2,1)S(1)}, bf16[256,512]{1,0:T(8,128)(2,1)S(1)}, u32[]{:S(2)}, u32[]{:S(2)}) collective-permute-start(bf16[256,512]{1,0:T(8,128)(2,1)S(1)} %constant_dynamic-update-slice_fusion), channel_id=1, source_target_pairs={{0,24},{4,28},{8,16},{12,20},{16,8},{20,12},{24,0},{28,4},{1,25},{... | collective-permute-start | bytes 786440 | tf_op jit(solution)/shard_map/ppermute | solution.py:410
  4.0 0.5 collective-permute-start.1
  4.5 1.5 %collective-permute-start = (bf16[256,512]{1,0:T(8,128)(2,1)S(1)}, bf16[256,512]{1,0:T(8,128)(2,1)S(1)}, u32[]{:S(2)}, u32[]{:S(2)}) collective-permute-start(bf16[256,512]{1,0:T(8,128)(2,1)S(1)} %constant_dynamic-update-slice_fusion), channel_id=1, source_target_pairs={{0,8},{4,12},{8,0},{12,4},{16,24},{20,28},{24,16},{28,20},{1,9},{5... | collective-permute-start | bytes 786440 | tf_op jit(solution)/shard_map/ppermute | solution.py:410
  6.0 0.4 collective-permute-start.3
  6.5 4.6 %collective-permute-start.4 = (bf16[256,1280]{1,0:T(8,128)(2,1)}, bf16[256,1280]{1,0:T(8,128)(2,1)}, u32[]{:S(2)}, u32[]{:S(2)}) collective-permute-start(bf16[256,1280]{1,0:T(8,128)(2,1)} %refs_0_.1), channel_id=1, source_target_pairs={{1,2},{2,1},{5,6},{6,5},{9,10},{10,9},{13,14},{14,13},{17,18},{18,... | collective-permute-start | bytes 1966088 | tf_op jit(solution)/shard_map/ppermute | solution.py:407
  11.1 0.0 copy-start.16
  11.1 5.1 %constant_dynamic-slice_fusion.w_ref = bf16[2048,1280]{1,0:T(8,128)(2,1)} fusion(bf16[2048,5120]{1,0:T(8,128)(2,1)} %refs_3_.1, s32[]{:T(128)S(6)} %select_n.54), kind=kLoop, calls=%fused_computation.20 | loop fusion | bytes 10485764 | tf_op jit(solution)/shard_map/dynamic_slice | solution.py:454
  16.3 2.3 %shard_map.112 = (f32[7,256,256]{2,1,0:T(8,128)S(1)}, s32[7]{0:T(128)S(1)}) custom-call(s32[1]{0:T(128)} %bitcast.me_ref, s32[8,1,256]{2,1,0:T(1,128)S(1)} %bitcast.14, s32[2,16]{1,0:T(2,128)S(1)} %copy-done.17), custom_call_target="tpu_custom_call" | custom-call | bytes 1835008 | tf_op jit(solution)/shard_map/pallas_call | solution.py:44
  18.6 1.3 %copy-done.3 = f32[7,256,256]{2,1,0:T(8,128)} copy-done((f32[7,256,256]{2,1,0:T(8,128)}, f32[7,256,256]{2,1,0:T(8,128)S(1)}, u32[]{:S(2)}) %copy-start.3) | copy-done | bytes 1835032
  19.9 4.5 %shard_map.113.acc_ref = f32[256,2048]{1,0:T(8,128)S(1)} custom-call(s32[1]{0:T(128)} %bitcast.8.shard_ref, bf16[256,1280]{1,0:T(8,128)(2,1)S(1)} %copy-done.9, bf16[2048,5120]{1,0:T(8,128)(2,1)} %refs_3_.1), custom_call_target="tpu_custom_call" | custom-call | flops 1342177280 | bytes 5242880 | tf_op jit(solution)/shard_map/pallas_call | solution.py:360
  24.4 0.0 copy-start
  24.5 0.0 copy-start.18
  24.5 0.7 copy-done.18
  25.2 1.5 %pad_maximum_fusion.near_ref = bf16[4,256,512]{2,1,0:T(8,128)(2,1)S(1)} fusion(bf16[1,256,512]{2,1,0:T(8,128)(2,1)S(1)} %bitcast.16, bf16[1,256,512]{2,1,0:T(8,128)(2,1)S(1)} %bitcast.17, bf16[1,256,512]{2,1,0:T(8,128)(2,1)} %bitcast.18, bf16[1,256,512]{2,1,0:T(8,128)(2,1)S(1)} %bitcast.15), kind=kLoop, calls=%fused_computation | loop fusion | flops 1572864 | bytes 2097152 | tf_op jit(solution)/shard_map/stack | solution.py:413
  26.7 0.8 copy-done.10
  27.5 1.9 %collective-permute-start.7 = (bf16[256,1280]{1,0:T(8,128)(2,1)}, bf16[256,1280]{1,0:T(8,128)(2,1)}, u32[]{:S(2)}, u32[]{:S(2)}) collective-permute-start(bf16[256,1280]{1,0:T(8,128)(2,1)} %copy-done.10), channel_id=1, source_target_pairs={{1,2},{2,1},{5,6},{6,5},{9,10},{10,9},{13,14},{14,13},{17,18},{18,... | collective-permute-start | bytes 1966088 | tf_op jit(solution)/shard_map/ppermute | solution.py:407
  29.4 2.2 %collective-permute-start.6 = (bf16[256,1280]{1,0:T(8,128)(2,1)}, bf16[256,1280]{1,0:T(8,128)(2,1)}, u32[]{:S(2)}, u32[]{:S(2)}) collective-permute-start(bf16[256,1280]{1,0:T(8,128)(2,1)} %collective-permute-done.4), channel_id=1, source_target_pairs={{1,0},{2,3},{5,4},{6,7},{9,8},{10,11},{13,12},{14,15},{17,16},{18,... | collective-permute-start | bytes 1966088 | tf_op jit(solution)/shard_map/ppermute | solution.py:407
  31.7 1.5 %copy-done.4 = f32[7,256,256]{2,1,0:T(8,128)S(1)} copy-done((f32[7,256,256]{2,1,0:T(8,128)S(1)}, f32[7,256,256]{2,1,0:T(8,128)}, u32[]{:S(2)}) %copy-start.4) | copy-done | bytes 1835032
  33.2 12.4 %shard_map.116 = (bf16[8,1792,256]{2,1,0:T(8,128)(2,1)}, f32[8,256,256]{2,1,0:T(8,128)}, bf16[1792,128]{1,0:T(8,128)(2,1)}, bf16[1792,128]{1,0:T(8,128)(2,1)}) custom-call(s32[7]{0:T(128)S(1)} %fusion.1.slot_ref, bf16[256,2048]{1,0:T(8,128)(2,1)S(1)} %copy-done, bf16[4,256,512]{2,1,0:T(8,128)(2,1)S(1)} %pad_maximum_fusion.near_ref, ...), custom_call_target="tpu_custom_call" | custom-call | tf_op jit(solution)/shard_map/pallas_call | solution.py:44
  45.6 1.3 %collective-permute-done.7.x2_ref = bf16[256,1280]{1,0:T(8,128)(2,1)} collective-permute-done((bf16[256,1280]{1,0:T(8,128)(2,1)}, bf16[256,1280]{1,0:T(8,128)(2,1)}, u32[]{:S(2)}, u32[]{:S(2)}) %collective-permute-start.7) | collective-permute-done | bytes 655392 | tf_op jit(solution)/shard_map/ppermute | solution.py:407
  46.9 2.1 %collective-permute-start.8 = (bf16[256,1280]{1,0:T(8,128)(2,1)}, bf16[256,1280]{1,0:T(8,128)(2,1)}, u32[]{:S(2)}, u32[]{:S(2)}) collective-permute-start(bf16[256,1280]{1,0:T(8,128)(2,1)} %collective-permute-done.7.x2_ref), channel_id=1, source_target_pairs={{1,0},{2,3},{5,4},{6,7},{9,8},{10,11},{13,12},{14,15},{17,16},{18,... | collective-permute-start | bytes 1966088 | tf_op jit(solution)/shard_map/ppermute | solution.py:407
  49.0 0.1 copy.12.adv_ref
  49.2 0.1 pad_add_fusion.shard_ref
  49.2 1.6 %add.44.refs_1_ = bf16[256,1280]{1,0:T(8,128)(2,1)S(1)} add(bf16[256,1280]{1,0:T(8,128)(2,1)} %collective-permute-done.4, bf16[256,1280]{1,0:T(8,128)(2,1)} %collective-permute-done.6) | non-fusion elementwise | flops 327680 | bytes 1966080 | tf_op jit(solution)/shard_map/add | solution.py:475
  50.8 0.2 copy-done.5
  51.0 12.5 %shard_map.114 = (bf16[8,1792,256]{2,1,0:T(8,128)(2,1)}, f32[8,256,256]{2,1,0:T(8,128)}, bf16[1792,128]{1,0:T(8,128)(2,1)}, bf16[1792,128]{1,0:T(8,128)(2,1)}) custom-call(s32[7]{0:T(128)S(1)} %fusion.1.slot_ref, bf16[256,2048]{1,0:T(8,128)(2,1)S(1)} %copy-done, bf16[4,256,512]{2,1,0:T(8,128)(2,1)S(1)} %pad_maximum_fusion.near_ref, ...), custom_call_target="tpu_custom_call" | custom-call | tf_op jit(solution)/shard_map/pallas_call | solution.py:44
  63.6 8.1 %shard_map.115.proj_ref = f32[256,2048]{1,0:T(8,128)S(1)} custom-call(s32[2]{0:T(128)S(1)} %pad_add_fusion.shard_ref, f32[256,2048]{1,0:T(8,128)S(1)} %copy-done.2, bf16[256,1280]{1,0:T(8,128)(2,1)S(1)} %copy-done.11, bf16[256,1280]{1,0:T(8,128)(2,1)S(1)} %add.44.refs_1_, bf16[2048,5120]{1,0:T(8,128)(2,1)} %refs_3_.1, bf16[2048,5120]{1,0:T(8,128)(2,1)} %refs_3_.1), custom_call_target="tpu_custom_call" | custom-call | flops 2684354560 | bytes 10485760 | tf_op jit(solution)/shard_map/pallas_call | solution.py:360
  71.8 0.2 copy-done.7
  72.0 0.1 copy-done.13
  72.1 7.1 %shard_map.117 = (bf16[256,1024]{1,0:T(8,128)(2,1)S(1)}, bf16[3,2,256,128]{3,2,1,0:T(8,128)(2,1)S(1)}, bf16[4,2,256,128]{3,2,1,0:T(8,128)(2,1)S(1)}) custom-call(s32[7]{0:T(128)S(1)} %get-tuple-element.39.live_ref, s32[7]{0:T(128)S(1)} %compare_select_fusion.5.pos_ref, f32[256,2048]{1,0:T(8,128)S(1)} %shard_map.115.proj_ref, ...), custom_call_target="tpu_custom_call" | custom-call | tf_op jit(solution)/shard_map/pallas_call | solution.py:44
  79.2 0.9 collective-permute-start.9
  80.1 3.1 %copy-done.6 = bf16[8,1792,256]{2,1,0:T(8,128)(2,1)S(1)} copy-done((bf16[8,1792,256]{2,1,0:T(8,128)(2,1)S(1)}, bf16[8,1792,256]{2,1,0:T(8,128)(2,1)}, u32[]{:S(2)}) %copy-start.6) | copy-done | bytes 7340056
  83.2 6.9 %shard_map.118 = (bf16[256,1024]{1,0:T(8,128)(2,1)S(1)}, bf16[3,2,256,128]{3,2,1,0:T(8,128)(2,1)S(1)}, bf16[4,2,256,128]{3,2,1,0:T(8,128)(2,1)S(1)}) custom-call(s32[7]{0:T(128)S(1)} %get-tuple-element.39.live_ref, s32[7]{0:T(128)S(1)} %compare_select_fusion.5.pos_ref, f32[256,2048]{1,0:T(8,128)S(1)} %shard_map.115.proj_ref, ...), custom_call_target="tpu_custom_call" | custom-call | tf_op jit(solution)/shard_map/pallas_call | solution.py:44
  90.1 1.2 %collective-permute-start.13 = (bf16[3,2,256,128]{3,2,1,0:T(8,128)(2,1)S(1)}, bf16[3,2,256,128]{3,2,1,0:T(8,128)(2,1)S(1)}, u32[]{:S(2)}, u32[]{:S(2)}) collective-permute-start(bf16[3,2,256,128]{3,2,1,0:T(8,128)(2,1)S(1)} %get-tuple-element.67), channel_id=1, source_target_pairs={{0,4},{4,0},{8,12},{12,8},{16,20},{20,16},{24,28},{28,24},{1,5},{5... | collective-permute-start | bytes 1179656 | tf_op jit(solution)/shard_map/ppermute | solution.py:410
  91.3 0.1 shard_map.119
  91.4 1.9 %collective-permute-start.10 = (bf16[2,256,128]{2,1,0:T(8,128)(2,1)S(1)}, bf16[2,256,128]{2,1,0:T(8,128)(2,1)S(1)}, u32[]{:S(2)}, u32[]{:S(2)}) collective-permute-start(bf16[2,256,128]{2,1,0:T(8,128)(2,1)S(1)} %get-tuple-element.64), channel_id=1, source_target_pairs={{0,8},{8,0},{4,12},{12,4},{24,16},{28,20},{1,9},{9,1},{5,13},{13,5... | collective-permute-start | bytes 393224 | tf_op jit(solution)/shard_map/ppermute | solution.py:410
  93.4 1.3 %collective-permute-start.11 = (bf16[2,256,128]{2,1,0:T(8,128)(2,1)S(1)}, bf16[2,256,128]{2,1,0:T(8,128)(2,1)S(1)}, u32[]{:S(2)}, u32[]{:S(2)}) collective-permute-start(bf16[2,256,128]{2,1,0:T(8,128)(2,1)S(1)} %get-tuple-element.65), channel_id=1, source_target_pairs={{16,0},{20,4},{24,8},{28,12},{17,1},{21,5},{25,9},{29,13},{18,2},{... | collective-permute-start | bytes 393224 | tf_op jit(solution)/shard_map/ppermute | solution.py:410
  94.7 1.3 %collective-permute-start.12 = (bf16[2,256,128]{2,1,0:T(8,128)(2,1)S(1)}, bf16[2,256,128]{2,1,0:T(8,128)(2,1)S(1)}, u32[]{:S(2)}, u32[]{:S(2)}) collective-permute-start(bf16[2,256,128]{2,1,0:T(8,128)(2,1)S(1)} %get-tuple-element.66), channel_id=1, source_target_pairs={{16,8},{20,12},{24,0},{28,4},{17,9},{21,13},{25,1},{29,5},{18,10},... | collective-permute-start | bytes 393224 | tf_op jit(solution)/shard_map/ppermute | solution.py:410
  96.0 0.1 shard_map.120
  96.1 3.9 %collective-permute-start.14 = (bf16[2,256,128]{2,1,0:T(8,128)(2,1)S(1)}, bf16[2,256,128]{2,1,0:T(8,128)(2,1)S(1)}, u32[]{:S(2)}, u32[]{:S(2)}) collective-permute-start(bf16[2,256,128]{2,1,0:T(8,128)(2,1)S(1)} %get-tuple-element.70), channel_id=1, source_target_pairs={{0,8},{8,0},{4,12},{12,4},{24,16},{28,20},{1,9},{9,1},{5,13},{13,5... | collective-permute-start | bytes 393224 | tf_op jit(solution)/shard_map/ppermute | solution.py:410
  100.0 1.3 %collective-permute-start.15 = (bf16[2,256,128]{2,1,0:T(8,128)(2,1)S(1)}, bf16[2,256,128]{2,1,0:T(8,128)(2,1)S(1)}, u32[]{:S(2)}, u32[]{:S(2)}) collective-permute-start(bf16[2,256,128]{2,1,0:T(8,128)(2,1)S(1)} %get-tuple-element.71), channel_id=1, source_target_pairs={{16,0},{20,4},{24,8},{28,12},{17,1},{21,5},{25,9},{29,13},{18,2},{... | collective-permute-start | bytes 393224 | tf_op jit(solution)/shard_map/ppermute | solution.py:410
  101.3 1.3 %collective-permute-start.16 = (bf16[2,256,128]{2,1,0:T(8,128)(2,1)S(1)}, bf16[2,256,128]{2,1,0:T(8,128)(2,1)S(1)}, u32[]{:S(2)}, u32[]{:S(2)}) collective-permute-start(bf16[2,256,128]{2,1,0:T(8,128)(2,1)S(1)} %get-tuple-element.72), channel_id=1, source_target_pairs={{16,8},{20,12},{24,0},{28,4},{17,9},{21,13},{25,1},{29,5},{18,10},... | collective-permute-start | bytes 393224 | tf_op jit(solution)/shard_map/ppermute | solution.py:410
  102.6 1.1 pad_maximum_fusion.1
  103.7 7.0 %collective-permute-done.11.refs_2_ = bf16[2,256,128]{2,1,0:T(8,128)(2,1)S(1)} collective-permute-done((bf16[2,256,128]{2,1,0:T(8,128)(2,1)S(1)}, bf16[2,256,128]{2,1,0:T(8,128)(2,1)S(1)}, u32[]{:S(2)}, u32[]{:S(2)}) %collective-permute-start.11) | collective-permute-done | bytes 131104 | tf_op jit(solution)/shard_map/ppermute | solution.py:410
  110.7 2.3 %collective-permute-done.15.refs_6_ = bf16[2,256,128]{2,1,0:T(8,128)(2,1)S(1)} collective-permute-done((bf16[2,256,128]{2,1,0:T(8,128)(2,1)S(1)}, bf16[2,256,128]{2,1,0:T(8,128)(2,1)S(1)}, u32[]{:S(2)}, u32[]{:S(2)}) %collective-permute-start.15) | collective-permute-done | bytes 131104 | tf_op jit(solution)/shard_map/ppermute | solution.py:410
  113.0 0.8 shard_map.121
  (58 shorter events, 0.1 us)
Async XLA Ops:
  2.5 22.0 %collective-permute-start.2 = (bf16[256,512]{1,0:T(8,128)(2,1)S(1)}, bf16[256,512]{1,0:T(8,128)(2,1)S(1)}, u32[]{:S(2)}, u32[]{:S(2)}) collective-permute-start(bf16[256,512]{1,0:T(8,128)(2,1)S(1)} %constant_dynamic-update-slice_fusion), channel_id=1, source_target_pairs={{0,24},{4,28},{8,16},{12,20},{16,8},{20,12},{24,0},{28,4},{1,25},{... | collective-permute-start | bytes 786440 | tf_op jit(solution)/shard_map/ppermute | solution.py:410
  4.0 20.4 %collective-permute-start.1 = (bf16[256,512]{1,0:T(8,128)(2,1)S(1)}, bf16[256,512]{1,0:T(8,128)(2,1)S(1)}, u32[]{:S(2)}, u32[]{:S(2)}) collective-permute-start(bf16[256,512]{1,0:T(8,128)(2,1)S(1)} %constant_dynamic-update-slice_fusion), channel_id=1, source_target_pairs={{0,16},{4,20},{8,24},{12,28},{16,0},{20,4},{24,8},{28,12},{1,17},{... | collective-permute-start | bytes 786440 | tf_op jit(solution)/shard_map/ppermute | solution.py:410
  4.5 19.9 %collective-permute-start = (bf16[256,512]{1,0:T(8,128)(2,1)S(1)}, bf16[256,512]{1,0:T(8,128)(2,1)S(1)}, u32[]{:S(2)}, u32[]{:S(2)}) collective-permute-start(bf16[256,512]{1,0:T(8,128)(2,1)S(1)} %constant_dynamic-update-slice_fusion), channel_id=1, source_target_pairs={{0,8},{4,12},{8,0},{12,4},{16,24},{20,28},{24,16},{28,20},{1,9},{5... | collective-permute-start | bytes 786440 | tf_op jit(solution)/shard_map/ppermute | solution.py:410
  6.0 20.7 %collective-permute-start.3 = (bf16[256,1280]{1,0:T(8,128)(2,1)}, bf16[256,1280]{1,0:T(8,128)(2,1)S(1)}, u32[]{:S(2)}, u32[]{:S(2)}) collective-permute-start(bf16[256,1280]{1,0:T(8,128)(2,1)} %refs_0_.1), channel_id=1, source_target_pairs={{0,1},{1,0},{2,3},{3,2},{4,5},{5,4},{6,7},{7,6},{8,9},{9,8},{10,11... | collective-permute-start | bytes 1966088 | tf_op jit(solution)/shard_map/ppermute | solution.py:407
  6.5 20.2 %collective-permute-start.4 = (bf16[256,1280]{1,0:T(8,128)(2,1)}, bf16[256,1280]{1,0:T(8,128)(2,1)}, u32[]{:S(2)}, u32[]{:S(2)}) collective-permute-start(bf16[256,1280]{1,0:T(8,128)(2,1)} %refs_0_.1), channel_id=1, source_target_pairs={{1,2},{2,1},{5,6},{6,5},{9,10},{10,9},{13,14},{14,13},{17,18},{18,... | collective-permute-start | bytes 1966088 | tf_op jit(solution)/shard_map/ppermute | solution.py:407
  11.1 5.2 %copy-start.16 = (s32[2048]{0:T(1024)S(1)}, s32[2048]{0:T(1024)}, u32[]{:S(2)}) copy-start(s32[2048]{0:T(1024)} %param.15) | copy-start | bytes 24580
  11.1 5.2 %copy-start.17 = (s32[2,16]{1,0:T(2,128)S(1)}, s32[2,16]{1,0:T(2,128)}, u32[]{:S(2)}) copy-start(s32[2,16]{1,0:T(2,128)} %tile_ref.1) | copy-start | bytes 388
  11.1 8.8 %copy-start.9 = (bf16[256,1280]{1,0:T(8,128)(2,1)S(1)}, bf16[256,1280]{1,0:T(8,128)(2,1)}, u32[]{:S(2)}) copy-start(bf16[256,1280]{1,0:T(8,128)(2,1)} %refs_0_.1) | copy-start | bytes 1966084
  18.6 1.3 %copy-start.3 = (f32[7,256,256]{2,1,0:T(8,128)}, f32[7,256,256]{2,1,0:T(8,128)S(1)}, u32[]{:S(2)}) copy-start(f32[7,256,256]{2,1,0:T(8,128)S(1)} %get-tuple-element.43.bias_ref) | copy-start | bytes 5505028
  24.4 2.3 %copy-start.1 = (f32[256,2048]{1,0:T(8,128)}, f32[256,2048]{1,0:T(8,128)S(1)}, u32[]{:S(2)}) copy-start(f32[256,2048]{1,0:T(8,128)S(1)} %shard_map.113.acc_ref) | copy-start | bytes 6291460
  24.4 7.3 %copy-start = (bf16[256,2048]{1,0:T(8,128)(2,1)S(1)}, bf16[256,2048]{1,0:T(8,128)(2,1)}, u32[]{:S(2)}) copy-start(bf16[256,2048]{1,0:T(8,128)(2,1)} %q_ref.7) | copy-start | bytes 3145732
  24.5 0.7 copy-start.18
  26.7 0.8 copy-start.10
  27.5 4.1 %collective-permute-start.5 = (bf16[4,256,512]{2,1,0:T(8,128)(2,1)S(1)}, bf16[4,256,512]{2,1,0:T(8,128)(2,1)S(1)}, u32[]{:S(2)}, u32[]{:S(2)}) collective-permute-start(bf16[4,256,512]{2,1,0:T(8,128)(2,1)S(1)} %pad_maximum_fusion.near_ref), channel_id=1, source_target_pairs={{0,4},{4,0},{8,12},{12,8},{16,20},{20,16},{24,28},{28,24},{1,5},{5... | collective-permute-start | bytes 3145736 | tf_op jit(solution)/shard_map/ppermute | solution.py:410
  27.5 19.3 %collective-permute-start.7 = (bf16[256,1280]{1,0:T(8,128)(2,1)}, bf16[256,1280]{1,0:T(8,128)(2,1)}, u32[]{:S(2)}, u32[]{:S(2)}) collective-permute-start(bf16[256,1280]{1,0:T(8,128)(2,1)} %copy-done.10), channel_id=1, source_target_pairs={{1,2},{2,1},{5,6},{6,5},{9,10},{10,9},{13,14},{14,13},{17,18},{18,... | collective-permute-start | bytes 1966088 | tf_op jit(solution)/shard_map/ppermute | solution.py:407
  29.4 19.8 %collective-permute-start.6 = (bf16[256,1280]{1,0:T(8,128)(2,1)}, bf16[256,1280]{1,0:T(8,128)(2,1)}, u32[]{:S(2)}, u32[]{:S(2)}) collective-permute-start(bf16[256,1280]{1,0:T(8,128)(2,1)} %collective-permute-done.4), channel_id=1, source_target_pairs={{1,0},{2,3},{5,4},{6,7},{9,8},{10,11},{13,12},{14,15},{17,16},{18,... | collective-permute-start | bytes 1966088 | tf_op jit(solution)/shard_map/ppermute | solution.py:407
  31.7 1.5 %copy-start.4 = (f32[7,256,256]{2,1,0:T(8,128)S(1)}, f32[7,256,256]{2,1,0:T(8,128)}, u32[]{:S(2)}) copy-start(f32[7,256,256]{2,1,0:T(8,128)} %copy-done.3) | copy-start | bytes 5505028
  33.2 15.8 %copy-start.19 = (f32[256]{0:T(256)S(1)}, f32[256]{0:T(256)}, u32[]{:S(2)}) copy-start(f32[256]{0:T(256)} %param.10) | copy-start | bytes 3076
  33.2 16.0 %copy-start.20 = (s32[7]{0:T(128)S(1)}, s32[7]{0:T(128)}, u32[]{:S(2)}) copy-start(s32[7]{0:T(128)} %constant.97.clone) | copy-start | bytes 88
  46.9 24.9 %collective-permute-start.8 = (bf16[256,1280]{1,0:T(8,128)(2,1)}, bf16[256,1280]{1,0:T(8,128)(2,1)}, u32[]{:S(2)}, u32[]{:S(2)}) collective-permute-start(bf16[256,1280]{1,0:T(8,128)(2,1)} %collective-permute-done.7.x2_ref), channel_id=1, source_target_pairs={{1,0},{2,3},{5,4},{6,7},{9,8},{10,11},{13,12},{14,15},{17,16},{18,... | collective-permute-start | bytes 1966088 | tf_op jit(solution)/shard_map/ppermute | solution.py:407
  49.1 1.9 %copy-start.5 = (f32[7,256,256]{2,1,0:T(8,128)S(1)}, f32[7,256,256]{2,1,0:T(8,128)}, u32[]{:S(2)}) copy-start(f32[7,256,256]{2,1,0:T(8,128)} %copy-done.3) | copy-start | bytes 5505028
  51.0 12.5 %copy-start.2 = (f32[256,2048]{1,0:T(8,128)S(1)}, f32[256,2048]{1,0:T(8,128)}, u32[]{:S(2)}) copy-start(f32[256,2048]{1,0:T(8,128)} %copy-done.1) | copy-start | bytes 6291460
  51.0 12.5 %copy-start.11 = (bf16[256,1280]{1,0:T(8,128)(2,1)S(1)}, bf16[256,1280]{1,0:T(8,128)(2,1)}, u32[]{:S(2)}) copy-start(bf16[256,1280]{1,0:T(8,128)(2,1)} %copy-done.10) | copy-start | bytes 1966084
  63.6 8.2 %slice-start = ((s8[5242880]{0:T(1024)(128)(4,1)}), s8[4194304]{0:T(1024)(128)(4,1)S(1)}, s32[]{:S(2)}) async-start(s8[5242880]{0:T(1024)(128)(4,1)} %bitcast.10), calls=%async_computation | async-start | bytes 8388608
  63.6 8.2 %slice-start.2 = ((s8[7340032]{0:T(1024)(128)(4,1)}), s8[4194304]{0:T(1024)(128)(4,1)S(1)}, s32[]{:S(2)}) async-start(s8[7340032]{0:T(1024)(128)(4,1)} %bitcast.12), calls=%async_computation.2 | async-start | bytes 8388608
  63.6 8.2 %slice-start.1 = ((s8[5242880]{0:T(1024)(128)(4,1)}), s8[1048576]{0:T(1024)(128)(4,1)S(1)}, s32[]{:S(2)}) async-start(s8[5242880]{0:T(1024)(128)(4,1)} %bitcast.10), calls=%async_computation.1 | async-start | bytes 2097152
  63.6 8.2 %slice-start.3 = ((s8[7340032]{0:T(1024)(128)(4,1)}), s8[3145728]{0:T(1024)(128)(4,1)S(1)}, s32[]{:S(2)}) async-start(s8[7340032]{0:T(1024)(128)(4,1)} %bitcast.12), calls=%async_computation.3 | async-start | bytes 6291456
  63.6 8.4 %copy-start.7 = (f32[8,256,256]{2,1,0:T(8,128)S(1)}, f32[8,256,256]{2,1,0:T(8,128)}, u32[]{:S(2)}) copy-start(f32[8,256,256]{2,1,0:T(8,128)} %get-tuple-element.51.o_ref) | copy-start | bytes 6291460
  63.6 8.4 %copy-start.12 = (bf16[1792,128]{1,0:T(8,128)(2,1)S(1)}, bf16[1792,128]{1,0:T(8,128)(2,1)}, u32[]{:S(2)}) copy-start(bf16[1792,128]{1,0:T(8,128)(2,1)} %get-tuple-element.52.k_ref) | copy-start | bytes 1376260
  63.6 8.5 %copy-start.13 = (bf16[1792,128]{1,0:T(8,128)(2,1)S(1)}, bf16[1792,128]{1,0:T(8,128)(2,1)}, u32[]{:S(2)}) copy-start(bf16[1792,128]{1,0:T(8,128)(2,1)} %get-tuple-element.53.v_ref) | copy-start | bytes 1376260
  72.1 8.0 %copy-start.8 = (f32[8,256,256]{2,1,0:T(8,128)S(1)}, f32[8,256,256]{2,1,0:T(8,128)}, u32[]{:S(2)}) copy-start(f32[8,256,256]{2,1,0:T(8,128)} %get-tuple-element.56.o_ref) | copy-start | bytes 6291460
  72.1 8.0 %copy-start.14 = (bf16[1792,128]{1,0:T(8,128)(2,1)S(1)}, bf16[1792,128]{1,0:T(8,128)(2,1)}, u32[]{:S(2)}) copy-start(bf16[1792,128]{1,0:T(8,128)(2,1)} %get-tuple-element.57.k_ref) | copy-start | bytes 1376260
  72.1 8.0 %copy-start.15 = (bf16[1792,128]{1,0:T(8,128)(2,1)S(1)}, bf16[1792,128]{1,0:T(8,128)(2,1)}, u32[]{:S(2)}) copy-start(bf16[1792,128]{1,0:T(8,128)(2,1)} %get-tuple-element.58.v_ref) | copy-start | bytes 1376260
  79.2 12.1 %collective-permute-start.9 = (bf16[3,2,256,128]{3,2,1,0:T(8,128)(2,1)S(1)}, bf16[3,2,256,128]{3,2,1,0:T(8,128)(2,1)S(1)}, u32[]{:S(2)}, u32[]{:S(2)}) collective-permute-start(bf16[3,2,256,128]{3,2,1,0:T(8,128)(2,1)S(1)} %get-tuple-element.61), channel_id=1, source_target_pairs={{0,4},{4,0},{8,12},{12,8},{16,20},{20,16},{24,28},{28,24},{1,5},{5... | collective-permute-start | bytes 1179656 | tf_op jit(solution)/shard_map/ppermute | solution.py:410
  80.1 3.1 %copy-start.6 = (bf16[8,1792,256]{2,1,0:T(8,128)(2,1)S(1)}, bf16[8,1792,256]{2,1,0:T(8,128)(2,1)}, u32[]{:S(2)}) copy-start(bf16[8,1792,256]{2,1,0:T(8,128)(2,1)} %get-tuple-element.59.p_ref) | copy-start | bytes 22020100
  90.1 5.8 %collective-permute-start.13 = (bf16[3,2,256,128]{3,2,1,0:T(8,128)(2,1)S(1)}, bf16[3,2,256,128]{3,2,1,0:T(8,128)(2,1)S(1)}, u32[]{:S(2)}, u32[]{:S(2)}) collective-permute-start(bf16[3,2,256,128]{3,2,1,0:T(8,128)(2,1)S(1)} %get-tuple-element.67), channel_id=1, source_target_pairs={{0,4},{4,0},{8,12},{12,8},{16,20},{20,16},{24,28},{28,24},{1,5},{5... | collective-permute-start | bytes 1179656 | tf_op jit(solution)/shard_map/ppermute | solution.py:410
  91.4 9.9 %collective-permute-start.10 = (bf16[2,256,128]{2,1,0:T(8,128)(2,1)S(1)}, bf16[2,256,128]{2,1,0:T(8,128)(2,1)S(1)}, u32[]{:S(2)}, u32[]{:S(2)}) collective-permute-start(bf16[2,256,128]{2,1,0:T(8,128)(2,1)S(1)} %get-tuple-element.64), channel_id=1, source_target_pairs={{0,8},{8,0},{4,12},{12,4},{24,16},{28,20},{1,9},{9,1},{5,13},{13,5... | collective-permute-start | bytes 393224 | tf_op jit(solution)/shard_map/ppermute | solution.py:410
  93.4 17.3 %collective-permute-start.11 = (bf16[2,256,128]{2,1,0:T(8,128)(2,1)S(1)}, bf16[2,256,128]{2,1,0:T(8,128)(2,1)S(1)}, u32[]{:S(2)}, u32[]{:S(2)}) collective-permute-start(bf16[2,256,128]{2,1,0:T(8,128)(2,1)S(1)} %get-tuple-element.65), channel_id=1, source_target_pairs={{16,0},{20,4},{24,8},{28,12},{17,1},{21,5},{25,9},{29,13},{18,2},{... | collective-permute-start | bytes 393224 | tf_op jit(solution)/shard_map/ppermute | solution.py:410
  94.7 16.1 %collective-permute-start.12 = (bf16[2,256,128]{2,1,0:T(8,128)(2,1)S(1)}, bf16[2,256,128]{2,1,0:T(8,128)(2,1)S(1)}, u32[]{:S(2)}, u32[]{:S(2)}) collective-permute-start(bf16[2,256,128]{2,1,0:T(8,128)(2,1)S(1)} %get-tuple-element.66), channel_id=1, source_target_pairs={{16,8},{20,12},{24,0},{28,4},{17,9},{21,13},{25,1},{29,5},{18,10},... | collective-permute-start | bytes 393224 | tf_op jit(solution)/shard_map/ppermute | solution.py:410
  96.1 14.6 %collective-permute-start.14 = (bf16[2,256,128]{2,1,0:T(8,128)(2,1)S(1)}, bf16[2,256,128]{2,1,0:T(8,128)(2,1)S(1)}, u32[]{:S(2)}, u32[]{:S(2)}) collective-permute-start(bf16[2,256,128]{2,1,0:T(8,128)(2,1)S(1)} %get-tuple-element.70), channel_id=1, source_target_pairs={{0,8},{8,0},{4,12},{12,4},{24,16},{28,20},{1,9},{9,1},{5,13},{13,5... | collective-permute-start | bytes 393224 | tf_op jit(solution)/shard_map/ppermute | solution.py:410
  100.0 13.0 %collective-permute-start.15 = (bf16[2,256,128]{2,1,0:T(8,128)(2,1)S(1)}, bf16[2,256,128]{2,1,0:T(8,128)(2,1)S(1)}, u32[]{:S(2)}, u32[]{:S(2)}) collective-permute-start(bf16[2,256,128]{2,1,0:T(8,128)(2,1)S(1)} %get-tuple-element.71), channel_id=1, source_target_pairs={{16,0},{20,4},{24,8},{28,12},{17,1},{21,5},{25,9},{29,13},{18,2},{... | collective-permute-start | bytes 393224 | tf_op jit(solution)/shard_map/ppermute | solution.py:410
  101.3 11.7 %collective-permute-start.16 = (bf16[2,256,128]{2,1,0:T(8,128)(2,1)S(1)}, bf16[2,256,128]{2,1,0:T(8,128)(2,1)S(1)}, u32[]{:S(2)}, u32[]{:S(2)}) collective-permute-start(bf16[2,256,128]{2,1,0:T(8,128)(2,1)S(1)} %get-tuple-element.72), channel_id=1, source_target_pairs={{16,8},{20,12},{24,0},{28,4},{17,9},{21,13},{25,1},{29,5},{18,10},... | collective-permute-start | bytes 393224 | tf_op jit(solution)/shard_map/ppermute | solution.py:410

commit v5 on v4

--- a/solution.py
+++ b/solution.py
@@ -16,6 +16,9 @@
 ROLLOUTS = 8
 JITTER = 64
 KB = 256
+CHUNK = 1
+WB = 512
+AHEAD = 2
 VMEM_LIMIT = 26 << 20
 SCALE = 1.0 / math.sqrt(HD)
 LOG2E = 1.4426950408889634
@@ -34,6 +37,7 @@
 
 SMEM = pl.BlockSpec(memory_space=pltpu.SMEM)
 VMEM = pl.BlockSpec(memory_space=pltpu.VMEM)
+HBM = pl.BlockSpec(memory_space=pltpu.HBM)
 
 
 def at(start, size):
@@ -59,12 +63,12 @@
     per = rows // KB
     me = me_ref[0]
     row_start = me * rows
-    win_kb = jnp.maximum(me - back, 0) * per
     key_at = lax.broadcasted_iota(jnp.int32, (KB, KB), 0)
     query_at = lax.broadcasted_iota(jnp.int32, (KB, KB), 1)
     for kb in range(n_kb):
         window = kb >= prompt // KB
-        block = win_kb + (kb - prompt // KB) if window else kb
+        age, sub = divmod(kb - prompt // KB, per)
+        block = jnp.maximum(me - age, 0) * per + sub if window else kb
         key_pos = block * KB + key_at
         seg_k = jnp.broadcast_to(seg_ref[block], (KB, KB)).T
         some = jnp.int32(0)
@@ -96,9 +100,9 @@
 
 
 def probs_kernel(
-    n_kb, group, groups, slot_ref, q_ref, near_ref, far_ref, bias_ref,
-    p_ref, o_ref, k_ref, v_ref,
-    ks_ref, vs_ref, kx_ref, vt_ref, s_ref, t_ref, pa_ref, pb_ref, oa_ref, ob_ref, sems,
+    n_kb, group, groups, slot_ref, shard_ref, w_ref, q_ref, near_ref, far_ref, bias_ref,
+    p_ref, o_ref, k_ref, v_ref, wl_ref,
+    ks_ref, vs_ref, kx_ref, vt_ref, s_ref, t_ref, ps_ref, os_ref, ws_ref, sems,
 ):
     rows = q_ref.shape[0]
     per = rows // KB
@@ -120,8 +124,19 @@
         def _():
             place(far_ref, slot - n_near)
 
-    keep_k = pltpu.make_async_copy(ks_ref, k_ref, sems.at[4])
-    keep_v = pltpu.make_async_copy(vs_ref, v_ref, sems.at[5])
+    depth = wl_ref.shape[1]
+    wide = SHARE * HD
+    keep_w = pltpu.make_async_copy(
+        w_ref.at[
+            pl.ds(group * wide, wide), pl.ds(pl.multiple_of(shard_ref[0] * depth, HD), depth)
+        ],
+        ws_ref,
+        sems.at[10],
+    )
+    pass_w = pltpu.make_async_copy(ws_ref, wl_ref, sems.at[11])
+    keep_w.start()
+    keep_k = pltpu.make_async_copy(ks_ref, k_ref, sems.at[8])
+    keep_v = pltpu.make_async_copy(vs_ref, v_ref, sems.at[9])
     keep_k.start()
     keep_v.start()
     for kb in range(n_kb):
@@ -143,61 +158,65 @@
         s_ref[...] = s
         return jnp.max(s, axis=0, keepdims=True)
 
-    def out(i, side):
-        p_side, o_side = ((pa_ref, oa_ref), (pb_ref, ob_ref))[side]
+    def out(j, side):
+        at_side = (j % 2) * 2 + side
+        i = 2 * j + side
         return (
-            pltpu.make_async_copy(p_side, p_ref.at[i], sems.at[side]),
-            pltpu.make_async_copy(o_side, o_ref.at[i], sems.at[2 + side]),
+            pltpu.make_async_copy(ps_ref.at[at_side], p_ref.at[i], sems.at[at_side]),
+            pltpu.make_async_copy(os_ref.at[at_side], o_ref.at[i], sems.at[4 + at_side]),
         )
 
-    def soften(i, s_ref, top, side):
-        p_side, o_side = ((pa_ref, oa_ref), (pb_ref, ob_ref))[side]
+    def soften(j, s_ref, top, side):
+        at_side = (j % 2) * 2 + side
         e = jnp.exp2(s_ref[...] - top).astype(BF16)
-
-        @pl.when(i >= 2)
-        def _():
-            for copy in out(i - 2, side):
-                copy.wait()
-
-        p_side[...] = e
+        ps_ref[at_side] = e
         acc = dot(vt_ref[...], e)
         inv = 1.0 / acc[HD : HD + 1, :]
-        o_side[:, :HD] = (acc[:HD] * inv).T
-        o_side[:, HD:] = jnp.broadcast_to(inv, (HD, KB)).T
-        for copy in out(i, side):
+        os_ref[at_side, :, :HD] = (acc[:HD] * inv).T
+        os_ref[at_side, :, HD:] = jnp.broadcast_to(inv, (HD, KB)).T
+
+    def step(j, top):
+        @pl.when(j == 1)
+        def _():
+            keep_w.wait()
+            pass_w.start()
+
+        @pl.when(j >= 2)
+        def _():
+            for copy in out(j - 2, 0) + out(j - 2, 1):
+                copy.wait()
+
+        later = score(2 * j + 1, t_ref)
+        soften(j, s_ref, top, 0)
+        top = score(jnp.minimum(2 * j + 2, count - 1), s_ref)
+        soften(j, t_ref, later, 1)
+        for copy in out(j, 0) + out(j, 1):
             copy.start()
-
-    def step(j, top):
-        later = score(2 * j + 1, t_ref)
-        soften(2 * j, s_ref, top, 0)
-        top = score(jnp.minimum(2 * j + 2, count - 1), s_ref)
-        soften(2 * j + 1, t_ref, later, 1)
         return top
 
     lax.fori_loop(0, count // 2, step, score(0, s_ref))
-    for side in range(2):
-        for copy in out(count - 2 + side, side):
+    for j in range(max(count // 2 - 2, 0), count // 2):
+        for copy in out(j, 0) + out(j, 1):
             copy.wait()
     keep_k.wait()
     keep_v.wait()
-
-
-HBM = pl.BlockSpec(memory_space=pltpu.HBM)
-
-
-def probs_call(group, groups, slots, q, near, far, bias, n_kb):
+    pass_w.wait()
+
+
+def probs_call(group, groups, slots, shard, weight, depth, q, near, far, bias, n_kb):
     rows = q.shape[0]
     keys = n_kb * KB
     blocks = SHARE * rows // KB
     return call(
         functools.partial(probs_kernel, n_kb, group, groups),
-        (slots, q, near, far, bias),
-        [SMEM, VMEM, VMEM, VMEM, VMEM],
+        (slots, shard, weight, q, near, far, bias),
+        [SMEM, SMEM, HBM] + [VMEM] * 4,
         [
             pltpu.HBM((blocks, keys, KB), BF16),
             pltpu.HBM((blocks, KB, 2 * HD), F32),
             pltpu.HBM((keys, HD), BF16),
             pltpu.HBM((keys, HD), BF16),
+            pltpu.HBM((SHARE * HD, depth), BF16),
         ],
         scratch=[
             pltpu.VMEM((keys, HD), BF16),
@@ -206,19 +225,18 @@
             pltpu.VMEM((HD + 16, keys), BF16),
             pltpu.VMEM((keys, KB), F32),
             pltpu.VMEM((keys, KB), F32),
-            pltpu.VMEM((keys, KB), BF16),
-            pltpu.VMEM((keys, KB), BF16),
-            pltpu.VMEM((KB, 2 * HD), F32),
-            pltpu.VMEM((KB, 2 * HD), F32),
-            pltpu.SemaphoreType.DMA((6,)),
-        ],
-        out_specs=[HBM] * 4,
+            pltpu.VMEM((4, keys, KB), BF16),
+            pltpu.VMEM((4, KB, 2 * HD), F32),
+            pltpu.VMEM((SHARE * HD, depth), BF16),
+            pltpu.SemaphoreType.DMA((12,)),
+        ],
+        out_specs=[HBM] * 5,
     )
 
 
 def back_kernel(
-    n_kb, n_send, first, live_ref, pos_ref, proj_ref, x1_ref, x2_ref, w_ref, adv_ref, o_ref,
-    q_ref, k_ref, v_ref, p_ref,
+    n_kb, n_send, first, live_ref, pos_ref, proj_ref, x1_ref, x2_ref, w_ref, adv_ref,
+    o_ref, q_ref, k_ref, v_ref, p_ref,
     dq_ref, send_ref, keep_ref, dox_ref, qs_ref, ds_ref, dqt_ref,
 ):
     rows = proj_ref.shape[0]
@@ -229,7 +247,7 @@
     dqt_ref[...] = jnp.zeros_like(dqt_ref)
     for h in range(SHARE):
         cols = pl.ds((first + h) * HD, HD)
-        fresh = dot_nt(x, w_ref[cols, :])
+        fresh = dot_nt(x, w_ref[h * HD : (h + 1) * HD, :])
         for r in range(per):
             part = slice(r * KB, (r + 1) * KB)
             here = pl.ds((h * per + r) * KB, KB)
@@ -247,40 +265,46 @@
             dox_ref[here, HD:] = ext.astype(BF16)
             qs_ref[here, :] = q_ref[part, cols]
 
-    def step(kb, carry):
+    def put(kb, value):
         pos = pos_ref[kb]
 
-        def put(value):
-            @pl.when(pos < n_send)
-            def _():
-                send_ref[pos] = value
-
-            @pl.when(pos >= n_send)
-            def _():
-                keep_ref[pos - n_send] = value
-
-        @pl.when(live_ref[kb] != 0)
-        def _():
-            keys = at(kb * KB, KB)
-            vx = jnp.concatenate([v_ref[keys, :], minus], axis=1)
-            kt = k_ref[keys, :].T
+        @pl.when(pos < n_send)
+        def _():
+            send_ref[pos] = value
+
+        @pl.when(pos >= n_send)
+        def _():
+            keep_ref[pos - n_send] = value
+
+    def chunk(start, count):
+        keys = pl.ds(start * KB, count * KB)
+        blocks = range(start, start + count)
+        live = functools.reduce(jnp.bitwise_or, [live_ref[kb] for kb in blocks])
+
+        @pl.when(live != 0)
+        def _():
+            vx = jnp.concatenate(
+                [v_ref[keys, :], jnp.concatenate([minus] * count, axis=0)], axis=1
+            )
             p = jnp.concatenate([p_ref[i, keys, :] for i in range(SHARE * per)], axis=1)
             dv = dot(p, dox_ref[:, :HD])
             for i in range(SHARE * per):
                 here = pl.ds(i * KB, KB)
                 dp = dot_nt(vx, dox_ref[here, :])
-                ds_ref[:, here] = (p_ref[i, keys, :].astype(F32) * dp).astype(BF16)
-            dqt_ref[...] += dot(kt, ds_ref[...])
-            dk = dot(ds_ref[...], qs_ref[...])
-            put(jnp.stack([dk, dv]).astype(BF16))
-
-        @pl.when(live_ref[kb] == 0)
-        def _():
-            put(jnp.zeros((2, KB, HD), BF16))
-
-        return carry
-
-    lax.fori_loop(0, n_kb, step, 0)
+                ds_ref[: count * KB, here] = (p_ref[i, keys, :].astype(F32) * dp).astype(BF16)
+            dqt_ref[...] += dot(k_ref[keys, :].T, ds_ref[: count * KB, :])
+            dk = dot(ds_ref[: count * KB, :], qs_ref[...])
+            for j, kb in enumerate(blocks):
+                part = slice(j * KB, (j + 1) * KB)
+                put(kb, jnp.stack([dk[part], dv[part]]).astype(BF16))
+
+        @pl.when(live == 0)
+        def _():
+            for kb in blocks:
+                put(kb, jnp.zeros((2, KB, HD), BF16))
+
+    for start in range(0, n_kb, CHUNK):
+        chunk(start, min(CHUNK, n_kb - start))
     for h in range(SHARE):
         dq_ref[:, pl.ds(h * HD, HD)] = (
             (dqt_ref[:, h * rows : (h + 1) * rows] * SCALE).T.astype(BF16)
@@ -292,7 +316,7 @@
     return call(
         functools.partial(back_kernel, n_kb, n_send, group * SHARE),
         (live, pos, proj, x1, x2, w, adv, o, q, k, v, p),
-        [SMEM, SMEM] + [VMEM] * 10,
+        [SMEM] * 2 + [VMEM] * 10,
         [
             ((rows, SHARE * HD), BF16),
             ((max(n_send, 1), 2, KB, HD), BF16),
@@ -301,7 +325,7 @@
         scratch=[
             pltpu.VMEM((SHARE * rows, 2 * HD), BF16),
             pltpu.VMEM((SHARE * rows, HD), BF16),
-            pltpu.VMEM((KB, SHARE * rows), BF16),
+            pltpu.VMEM((CHUNK * KB, SHARE * rows), BF16),
             pltpu.VMEM((HD, SHARE * rows), F32),
         ],
     )
@@ -337,44 +361,59 @@
         dv_ref[:, g * HD : (g + 1) * HD] = total[1].astype(BF16)
 
 
-def project_kernel(shard_ref, *refs):
-    out_ref = refs[-1]
-    pairs = (len(refs) - 1) // 2
-    acc = dot_nt(refs[0][...], refs[pairs][...])
-    for i in range(1, pairs):
-        acc += dot_nt(refs[i][...], refs[pairs + i][...])
-    out_ref[...] = acc
-
-
-def project_add_kernel(shard_ref, acc_ref, *refs):
-    project_kernel(shard_ref, *refs)
-    refs[-1][...] += acc_ref[...]
-
-
-def project_call(shards_of, xs, weight, acc=None):
+def project_kernel(count, added, halves, shard_ref, w_ref, *refs):
+    xs, refs = refs[:count], refs[count:]
+    if added:
+        acc_ref, refs = refs[0], refs[1:]
+    values = [x[...] for x in xs]
+    if halves:
+        values[-1] = values[-1] + refs[0][...]
+        refs = refs[1:]
+    out_ref, held_ref, sems = refs
+    depth = xs[0].shape[1]
+    blocks = w_ref.shape[0] // WB
+
+    def fetch(i, n):
+        return pltpu.make_async_copy(
+            w_ref.at[pl.ds(n * WB, WB), pl.ds(pl.multiple_of(shard_ref[i] * depth, HD), depth)],
+            held_ref.at[i, n],
+            sems.at[i, n],
+        )
+
+    def start(n):
+        for i in range(count):
+            fetch(i, n).start()
+
+    for n in range(min(AHEAD, blocks)):
+        start(n)
+    for n in range(blocks):
+        here = slice(n * WB, (n + 1) * WB)
+        total = acc_ref[:, here] if added else None
+        for i in range(count):
+            fetch(i, n).wait()
+        if n + AHEAD < blocks:
+            start(n + AHEAD)
+        for i in range(count):
+            part = dot_nt(values[i], held_ref[i, n])
+            total = part if total is None else total + part
+        out_ref[:, here] = total
+
+
+def project_call(shards_of, xs, weight, acc=None, rest=None):
     rows, depth = xs[0].shape
     wide = weight.shape[0]
-    block = 512
     count = len(xs)
-    tile = pl.BlockSpec((rows, block), lambda n, s: (0, n))
-    return pl.pallas_call(
-        project_kernel if acc is None else project_add_kernel,
-        grid_spec=pltpu.PrefetchScalarGridSpec(
-            num_scalar_prefetch=1,
-            grid=(wide // block,),
-            in_specs=([] if acc is None else [tile])
-            + [pl.BlockSpec((rows, depth), lambda n, s: (0, 0))] * count
-            + [pl.BlockSpec((block, depth), lambda n, s, i=i: (n, s[i])) for i in range(count)],
-            out_specs=tile,
-        ),
-        out_shape=jax.ShapeDtypeStruct((rows, wide), F32),
-        compiler_params=pltpu.CompilerParams(vmem_limit_bytes=VMEM_LIMIT),
-        cost_estimate=pl.CostEstimate(
-            flops=2 * rows * wide * depth * count,
-            bytes_accessed=2 * wide * depth * count,
-            transcendentals=0,
-        ),
-    )(shards_of, *([] if acc is None else [acc]), *xs, *([weight] * count))
+    added, halves = acc is not None, rest is not None
+    return call(
+        functools.partial(project_kernel, count, added, halves),
+        (shards_of, weight, *xs, *([acc] if added else []), *([rest] if halves else [])),
+        [SMEM, HBM] + [VMEM] * (count + added + halves),
+        [((rows, wide), F32)],
+        scratch=[
+            pltpu.VMEM((count, wide // WB, WB, depth), BF16),
+            pltpu.SemaphoreType.DMA((count, wide // WB)),
+        ],
+    )[0]
 
 
 def key_window(tok_rows, total):
@@ -423,7 +462,7 @@
     holder = jnp.where(
         block < prompt_kb,
         block // per,
-        jnp.where(me * rows >= prompt, me - back + (block - prompt_kb) // per, me),
+        jnp.where(me * rows >= prompt, me - (block - prompt_kb) // per, me),
     )
     if fast:
         away = holder ^ me
@@ -432,7 +471,7 @@
         pos = jnp.where(
             block < 4,
             jnp.where(block % 2 == core, 3 + block // 2, block // 2),
-            jnp.array([0, 0, 0, 0, 5, 2, 6], jnp.int32),
+            jnp.array([0, 0, 0, 0, 6, 2, 5], jnp.int32),
         )
         n_send = 3
         half = z // 2
@@ -450,32 +489,29 @@
             x = lax.dynamic_index_in_dim(whole, other, 0, keepdims=False)
             acc = project_call(other[None], [x], weight, acc)
         x1, x2 = upstream, jnp.zeros_like(upstream)
+
+    slots = slots.astype(jnp.int32)
     depth = upstream.shape[1]
-    w_last = lax.dynamic_slice_in_dim(out_weight, shard * depth, depth, 1)
-
-    slots = slots.astype(jnp.int32)
     if fast:
-        near, bias, w_last, acc, up_a, up_c = lax.optimization_barrier(
-            (near, bias, w_last, acc, up_a, up_c)
-        )
+        near, bias, acc, up_a, up_c = lax.optimization_barrier((near, bias, acc, up_a, up_c))
         far = flip(near, 1)
         up_e = hop(up_a, middle)
         up_f = hop(up_c, out)
-    soft = [list(probs_call(0, groups, slots, query_heads, near, far, bias, n_kb))]
+    soft = [list(probs_call(0, groups, slots, shard[None], weight, depth, query_heads, near, far, bias, n_kb))]
     if fast:
         up_e, soft[0][2] = lax.optimization_barrier((up_e, soft[0][2]))
         up_d = hop(up_e, out)
         x1, x2 = up_d, up_e
     soft += [
-        list(probs_call(g, groups, slots, query_heads, near, far, bias, n_kb))
+        list(probs_call(g, groups, slots, shard[None], weight, depth, query_heads, near, far, bias, n_kb))
         for g in range(1, groups)
     ]
     if fast:
         acc, soft[-1][2] = lax.optimization_barrier((acc, soft[-1][2]))
-        acc = project_call(jnp.stack([z ^ 1, second]), [up_a, up_c + up_f], weight, acc)
+        acc = project_call(jnp.stack([z ^ 1, second]), [up_a, up_c], weight, acc, up_f)
     outs = []
     for g in range(groups):
-        probs, attn, keys, values = soft[g]
+        probs, attn, keys, values, w_last = soft[g]
         outs.append(
             back_call(
                 g, live, pos.astype(jnp.int32), acc, x1, x2, w_last, advantage[:, None], attn,
@@ -510,9 +546,10 @@
     win_start = jnp.maximum(me - back, 0) * rows
     part = jnp.concatenate([keep for _, _, keep in outs], axis=3).astype(F32)
     part = part.transpose(0, 2, 1, 3).reshape(prompt + win, 2, groups * HD)
+    rear = part[prompt:].reshape(back + 1, rows, 2, groups * HD)[::-1].reshape(win, 2, -1)
     full = jnp.zeros((total, 2, groups * HD), F32).at[:prompt].set(part[:prompt])
     old = lax.dynamic_slice_in_dim(full, win_start, win, 0)
-    full = lax.dynamic_update_slice_in_dim(full, old + part[prompt:], win_start, 0)
+    full = lax.dynamic_update_slice_in_dim(full, old + rear, win_start, 0)
     reduced = lax.psum_scatter(full, "ctx", scatter_dimension=0, tiled=True)
     return (
         grad_queries,

time: 114 us -> 106 us (0.930)
  local copies, waits for them, and re-layouts: 15.1 us -> 9.13 us
  Pallas kernels: 54.7 us -> 49.4 us
  waiting for transfers between devices: 10.7 us -> 15.3 us
  other arithmetic: 4.21 us -> 2.48 us
    pallas_call x2 -> x0, Pallas kernels: 12.6 us -> none  [project_call(): pl.pallas_call(project_kernel if acc is None else project_add_kernel, gri...]
    pallas_call x8 -> x10, Pallas kernels: 42.1 us -> 49.4 us  [call(): pl.pallas_call(kernel, in_specs=in_specs, out_specs=out_specs or [VMEM] *...]
    dynamic_slice x1 -> x0, local copies, waits for them, and re-layouts: 5.14 us -> none  [shards(): w_last = lax.dynamic_slice_in_dim(out_weight, shard * depth, depth, 1)]
    ppermute x5, waiting for transfers between devices: 1.31 us -> 3.83 us  [hop(): return lax.ppermute(value, 'tp', pairs)]
    ppermute x12, waiting for transfers between devices: 9.37 us -> 11.4 us  [flip(): lax.ppermute(value, 'ctx', pairs or [(i, i ^ bit) for i in range(n_ctx)])]
    add x1 -> x0, other arithmetic: 1.55 us -> none  [shards(): up_c + up_f]
    unnamed x51 -> x57, local copies, waits for them, and re-layouts: 8.93 us -> 8.08 us
  transfers between devices with their start and end apart: 17 -> 17, of which waited for: 3 -> 5; matrix products, arithmetic and copies ran while one was open for 8% -> 4% of each run, Pallas kernels for 41% -> 39%
where the time goes in v5:
time: 106 us
  Pallas kernels  49.4 us (47%)
  starting transfers between devices  28.4 us (27%)
  waiting for transfers between devices  15.3 us (14%)
  local copies, waits for them, and re-layouts  9.13 us (9%)
  other arithmetic  2.48 us (2%)
  between operations  1.13 us (1%)
    pallas_call x10, Pallas kernels, call(): pl.pallas_call(kernel, in_specs=in_specs, out_specs=out_specs or [VMEM] *...  49.4 us
    ppermute x12, starting transfers between devices, flip(): lax.ppermute(value, 'ctx', pairs or [(i, i ^ bit) for i in range(n_ctx)])  16.8 us
    ppermute x5, starting transfers between devices, hop(): return lax.ppermute(value, 'tp', pairs)  11.6 us
    ppermute x12, waiting for transfers between devices, flip(): lax.ppermute(value, 'ctx', pairs or [(i, i ^ bit) for i in range(n_ctx)])  11.4 us
    unnamed x57, local copies, waits for them, and re-layouts  8.08 us
    ppermute x5, waiting for transfers between devices, hop(): return lax.ppermute(value, 'tp', pairs)  3.83 us
  transfers between devices with their start and end apart: 17, of which 5 were waited for; matrix products, arithmetic and copies ran while one was open for 4% of the time, Pallas kernels for 39%

profile of v5, /device:TPU:10, one launch (start us, length us, event | category | flops | bytes accessed | tf_op | source)
XLA Modules:
  0.0 105.8 jit_solution(10590712191842714813)
XLA Ops:
  0.6 0.5 collective-permute-start.3
  1.1 4.6 %collective-permute-start.4 = (bf16[256,1280]{1,0:T(8,128)(2,1)}, bf16[256,1280]{1,0:T(8,128)(2,1)S(1)}, u32[]{:S(2)}, u32[]{:S(2)}) collective-permute-start(bf16[256,1280]{1,0:T(8,128)(2,1)} %refs_0_.1), channel_id=1, source_target_pairs={{1,2},{2,1},{5,6},{6,5},{9,10},{10,9},{13,14},{14,13},{17,18},{18,... | collective-permute-start | bytes 1966088 | tf_op jit(solution)/shard_map/ppermute | solution.py:446
  5.8 0.9 constant_dynamic-update-slice_fusion.1
  6.7 0.9 constant_dynamic-update-slice_fusion
  7.6 0.0 copy-start.21
  7.6 1.6 %collective-permute-start.2 = (bf16[256,512]{1,0:T(8,128)(2,1)S(1)}, bf16[256,512]{1,0:T(8,128)(2,1)}, u32[]{:S(2)}, u32[]{:S(2)}) collective-permute-start(bf16[256,512]{1,0:T(8,128)(2,1)S(1)} %constant_dynamic-update-slice_fusion), channel_id=1, source_target_pairs={{0,24},{4,28},{8,16},{12,20},{16,8},{20,12},{24,0},{28,4},{1,25},{... | collective-permute-start | bytes 786440 | tf_op jit(solution)/shard_map/ppermute | solution.py:449
  9.2 0.5 collective-permute-start.1
  9.7 1.5 %collective-permute-start = (bf16[256,512]{1,0:T(8,128)(2,1)S(1)}, bf16[256,512]{1,0:T(8,128)(2,1)}, u32[]{:S(2)}, u32[]{:S(2)}) collective-permute-start(bf16[256,512]{1,0:T(8,128)(2,1)S(1)} %constant_dynamic-update-slice_fusion), channel_id=1, source_target_pairs={{0,8},{4,12},{8,0},{12,4},{16,24},{20,28},{24,16},{28,20},{1,9},{5... | collective-permute-start | bytes 786440 | tf_op jit(solution)/shard_map/ppermute | solution.py:449
  11.2 1.1 %copy-done.10 = bf16[256,1280]{1,0:T(8,128)(2,1)S(1)} copy-done((bf16[256,1280]{1,0:T(8,128)(2,1)S(1)}, bf16[256,1280]{1,0:T(8,128)(2,1)}, u32[]{:S(2)}) %copy-start.10) | copy-done | bytes 655384
  12.2 3.9 %shard_map.113.refs_2_ = f32[256,2048]{1,0:T(8,128)S(1)} custom-call(s32[1]{0:T(128)} %bitcast.8.shard_ref, bf16[2048,5120]{1,0:T(8,128)(2,1)} %w_ref.7, bf16[256,1280]{1,0:T(8,128)(2,1)S(1)} %copy-done.10), custom_call_target="tpu_custom_call" | custom-call | tf_op jit(solution)/shard_map/pallas_call | solution.py:48
  16.1 1.3 %copy-done.1 = f32[256,2048]{1,0:T(8,128)} copy-done((f32[256,2048]{1,0:T(8,128)}, f32[256,2048]{1,0:T(8,128)S(1)}, u32[]{:S(2)}) %copy-start.1) | copy-done | bytes 2097176
  17.5 2.3 %shard_map.112 = (f32[7,256,256]{2,1,0:T(8,128)S(1)}, s32[7]{0:T(128)S(1)}) custom-call(s32[1]{0:T(128)} %bitcast.me_ref, s32[8,1,256]{2,1,0:T(1,128)S(1)} %bitcast.15, s32[2,16]{1,0:T(2,128)S(1)} %copy-done.20), custom_call_target="tpu_custom_call" | custom-call | bytes 1835008 | tf_op jit(solution)/shard_map/pallas_call | solution.py:48
  19.8 0.0 collective-permute-done.2
  19.8 2.0 %collective-permute-done.1 = bf16[256,512]{1,0:T(8,128)(2,1)} collective-permute-done((bf16[256,512]{1,0:T(8,128)(2,1)S(1)}, bf16[256,512]{1,0:T(8,128)(2,1)}, u32[]{:S(2)}, u32[]{:S(2)}) %collective-permute-start.1) | collective-permute-done | bytes 262176 | tf_op jit(solution)/shard_map/ppermute | solution.py:449
  21.8 0.1 collective-permute-done
  21.9 1.3 %pad_maximum_fusion.near_ref = bf16[4,256,512]{2,1,0:T(8,128)(2,1)S(1)} fusion(bf16[1,256,512]{2,1,0:T(8,128)(2,1)} %bitcast.7, bf16[1,256,512]{2,1,0:T(8,128)(2,1)} %bitcast.6, bf16[1,256,512]{2,1,0:T(8,128)(2,1)} %bitcast.5, bf16[1,256,512]{2,1,0:T(8,128)(2,1)} %bitcast.16), kind=kLoop, calls=%fused_computation | loop fusion | flops 1572864 | bytes 2097152 | tf_op jit(solution)/shard_map/stack | solution.py:452
  23.2 0.0 collective-permute-done.3.refs_0_
  23.2 0.0 copy-start.11
  23.2 0.8 copy-done.11
  24.1 0.8 copy-done.13
  24.9 0.0 collective-permute-start.5
  24.9 2.2 %collective-permute-start.7 = (bf16[256,1280]{1,0:T(8,128)(2,1)}, bf16[256,1280]{1,0:T(8,128)(2,1)}, u32[]{:S(2)}, u32[]{:S(2)}) collective-permute-start(bf16[256,1280]{1,0:T(8,128)(2,1)} %copy-done.11), channel_id=1, source_target_pairs={{1,2},{2,1},{5,6},{6,5},{9,10},{10,9},{13,14},{14,13},{17,18},{18,... | collective-permute-start | bytes 1966088 | tf_op jit(solution)/shard_map/ppermute | solution.py:446
  27.1 2.2 %collective-permute-start.6 = (bf16[256,1280]{1,0:T(8,128)(2,1)}, bf16[256,1280]{1,0:T(8,128)(2,1)}, u32[]{:S(2)}, u32[]{:S(2)}) collective-permute-start(bf16[256,1280]{1,0:T(8,128)(2,1)} %copy-done.13), channel_id=1, source_target_pairs={{1,0},{2,3},{5,4},{6,7},{9,8},{10,11},{13,12},{14,15},{17,16},{18,... | collective-permute-start | bytes 1966088 | tf_op jit(solution)/shard_map/ppermute | solution.py:446
  29.3 1.5 %copy-done.4 = f32[7,256,256]{2,1,0:T(8,128)S(1)} copy-done((f32[7,256,256]{2,1,0:T(8,128)S(1)}, f32[7,256,256]{2,1,0:T(8,128)}, u32[]{:S(2)}) %copy-start.4) | copy-done | bytes 1835032
  30.8 9.6 %shard_map.116 = (bf16[8,1792,256]{2,1,0:T(8,128)(2,1)}, f32[8,256,256]{2,1,0:T(8,128)}, bf16[1792,128]{1,0:T(8,128)(2,1)}, bf16[1792,128]{1,0:T(8,128)(2,1)}, bf16[1024,1280]{1,0:T(8,128)(2,1)}) custom-call(s32[7]{0:T(128)S(1)} %fusion.1.slot_ref, s32[1]{0:T(128)} %bitcast.9.shard_ref, bf16[2048,5120]{1,0:T(8,128)(2,1)} %w_ref.7, ...), custom_call_target="tpu_custom_call" | custom-call | tf_op jit(solution)/shard_map/pallas_call | solution.py:48
  40.4 3.8 %collective-permute-done.7.x2_ref = bf16[256,1280]{1,0:T(8,128)(2,1)} collective-permute-done((bf16[256,1280]{1,0:T(8,128)(2,1)}, bf16[256,1280]{1,0:T(8,128)(2,1)}, u32[]{:S(2)}, u32[]{:S(2)}) %collective-permute-start.7) | collective-permute-done | bytes 655392 | tf_op jit(solution)/shard_map/ppermute | solution.py:446
  44.2 2.1 %collective-permute-start.8 = (bf16[256,1280]{1,0:T(8,128)(2,1)}, bf16[256,1280]{1,0:T(8,128)(2,1)}, u32[]{:S(2)}, u32[]{:S(2)}) collective-permute-start(bf16[256,1280]{1,0:T(8,128)(2,1)} %collective-permute-done.7.x2_ref), channel_id=1, source_target_pairs={{1,0},{2,3},{5,4},{6,7},{9,8},{10,11},{13,12},{14,15},{17,16},{18,... | collective-permute-start | bytes 1966088 | tf_op jit(solution)/shard_map/ppermute | solution.py:446
  46.4 0.1 copy.12.adv_ref
  46.5 0.1 pad_add_fusion.shard_ref
  46.6 1.5 %copy-done.5 = f32[7,256,256]{2,1,0:T(8,128)S(1)} copy-done((f32[7,256,256]{2,1,0:T(8,128)S(1)}, f32[7,256,256]{2,1,0:T(8,128)}, u32[]{:S(2)}) %copy-start.5) | copy-done | bytes 1835032
  48.1 9.8 %shard_map.114 = (bf16[8,1792,256]{2,1,0:T(8,128)(2,1)}, f32[8,256,256]{2,1,0:T(8,128)}, bf16[1792,128]{1,0:T(8,128)(2,1)}, bf16[1792,128]{1,0:T(8,128)(2,1)}, bf16[1024,1280]{1,0:T(8,128)(2,1)}) custom-call(s32[7]{0:T(128)S(1)} %fusion.1.slot_ref, s32[1]{0:T(128)} %bitcast.9.shard_ref, bf16[2048,5120]{1,0:T(8,128)(2,1)} %w_ref.7, ...), custom_call_target="tpu_custom_call" | custom-call | tf_op jit(solution)/shard_map/pallas_call | solution.py:48
  58.1 8.2 %shard_map.115.proj_ref = f32[256,2048]{1,0:T(8,128)S(1)} custom-call(s32[2]{0:T(128)S(1)} %pad_add_fusion.shard_ref, bf16[2048,5120]{1,0:T(8,128)(2,1)} %w_ref.7, bf16[256,1280]{1,0:T(8,128)(2,1)S(1)} %copy-done.12, bf16[256,1280]{1,0:T(8,128)(2,1)S(1)} %copy-done.14, f32[256,2048]{1,0:T(8,128)S(1)} %copy-done.2, ...), custom_call_target="tpu_custom_call" | custom-call | tf_op jit(solution)/shard_map/pallas_call | solution.py:48
  66.5 7.5 %shard_map.117 = (bf16[256,1024]{1,0:T(8,128)(2,1)S(1)}, bf16[3,2,256,128]{3,2,1,0:T(8,128)(2,1)S(1)}, bf16[4,2,256,128]{3,2,1,0:T(8,128)(2,1)S(1)}) custom-call(s32[7]{0:T(128)S(1)} %get-tuple-element.40.live_ref, s32[7]{0:T(128)S(1)} %compare_select_fusion.5.pos_ref, f32[256,2048]{1,0:T(8,128)S(1)} %shard_map.115.proj_ref, ...), custom_call_target="tpu_custom_call" | custom-call | tf_op jit(solution)/shard_map/pallas_call | solution.py:48
  73.9 0.9 collective-permute-start.9
  74.9 7.1 %shard_map.118 = (bf16[256,1024]{1,0:T(8,128)(2,1)S(1)}, bf16[3,2,256,128]{3,2,1,0:T(8,128)(2,1)S(1)}, bf16[4,2,256,128]{3,2,1,0:T(8,128)(2,1)S(1)}) custom-call(s32[7]{0:T(128)S(1)} %get-tuple-element.40.live_ref, s32[7]{0:T(128)S(1)} %compare_select_fusion.5.pos_ref, f32[256,2048]{1,0:T(8,128)S(1)} %shard_map.115.proj_ref, ...), custom_call_target="tpu_custom_call" | custom-call | tf_op jit(solution)/shard_map/pallas_call | solution.py:48
  82.0 1.3 %collective-permute-start.13 = (bf16[3,2,256,128]{3,2,1,0:T(8,128)(2,1)S(1)}, bf16[3,2,256,128]{3,2,1,0:T(8,128)(2,1)S(1)}, u32[]{:S(2)}, u32[]{:S(2)}) collective-permute-start(bf16[3,2,256,128]{3,2,1,0:T(8,128)(2,1)S(1)} %get-tuple-element.69), channel_id=1, source_target_pairs={{0,4},{4,0},{8,12},{12,8},{16,20},{20,16},{24,28},{28,24},{1,5},{5... | collective-permute-start | bytes 1179656 | tf_op jit(solution)/shard_map/ppermute | solution.py:449
  83.3 0.1 shard_map.119
  83.4 1.9 %collective-permute-start.10 = (bf16[2,256,128]{2,1,0:T(8,128)(2,1)S(1)}, bf16[2,256,128]{2,1,0:T(8,128)(2,1)S(1)}, u32[]{:S(2)}, u32[]{:S(2)}) collective-permute-start(bf16[2,256,128]{2,1,0:T(8,128)(2,1)S(1)} %get-tuple-element.66), channel_id=1, source_target_pairs={{0,8},{8,0},{4,12},{12,4},{24,16},{28,20},{1,9},{9,1},{5,13},{13,5... | collective-permute-start | bytes 393224 | tf_op jit(solution)/shard_map/ppermute | solution.py:449
  85.3 1.3 %collective-permute-start.11 = (bf16[2,256,128]{2,1,0:T(8,128)(2,1)S(1)}, bf16[2,256,128]{2,1,0:T(8,128)(2,1)S(1)}, u32[]{:S(2)}, u32[]{:S(2)}) collective-permute-start(bf16[2,256,128]{2,1,0:T(8,128)(2,1)S(1)} %get-tuple-element.67), channel_id=1, source_target_pairs={{16,0},{20,4},{24,8},{28,12},{17,1},{21,5},{25,9},{29,13},{18,2},{... | collective-permute-start | bytes 393224 | tf_op jit(solution)/shard_map/ppermute | solution.py:449
  86.6 1.3 %collective-permute-start.12 = (bf16[2,256,128]{2,1,0:T(8,128)(2,1)S(1)}, bf16[2,256,128]{2,1,0:T(8,128)(2,1)S(1)}, u32[]{:S(2)}, u32[]{:S(2)}) collective-permute-start(bf16[2,256,128]{2,1,0:T(8,128)(2,1)S(1)} %get-tuple-element.68), channel_id=1, source_target_pairs={{16,8},{20,12},{24,0},{28,4},{17,9},{21,13},{25,1},{29,5},{18,10},... | collective-permute-start | bytes 393224 | tf_op jit(solution)/shard_map/ppermute | solution.py:449
  87.9 0.1 shard_map.120
  88.0 3.9 %collective-permute-start.14 = (bf16[2,256,128]{2,1,0:T(8,128)(2,1)S(1)}, bf16[2,256,128]{2,1,0:T(8,128)(2,1)S(1)}, u32[]{:S(2)}, u32[]{:S(2)}) collective-permute-start(bf16[2,256,128]{2,1,0:T(8,128)(2,1)S(1)} %get-tuple-element.72), channel_id=1, source_target_pairs={{0,8},{8,0},{4,12},{12,4},{24,16},{28,20},{1,9},{9,1},{5,13},{13,5... | collective-permute-start | bytes 393224 | tf_op jit(solution)/shard_map/ppermute | solution.py:449
  91.9 1.3 %collective-permute-start.15 = (bf16[2,256,128]{2,1,0:T(8,128)(2,1)S(1)}, bf16[2,256,128]{2,1,0:T(8,128)(2,1)S(1)}, u32[]{:S(2)}, u32[]{:S(2)}) collective-permute-start(bf16[2,256,128]{2,1,0:T(8,128)(2,1)S(1)} %get-tuple-element.73), channel_id=1, source_target_pairs={{16,0},{20,4},{24,8},{28,12},{17,1},{21,5},{25,9},{29,13},{18,2},{... | collective-permute-start | bytes 393224 | tf_op jit(solution)/shard_map/ppermute | solution.py:449
  93.2 1.3 %collective-permute-start.16 = (bf16[2,256,128]{2,1,0:T(8,128)(2,1)S(1)}, bf16[2,256,128]{2,1,0:T(8,128)(2,1)S(1)}, u32[]{:S(2)}, u32[]{:S(2)}) collective-permute-start(bf16[2,256,128]{2,1,0:T(8,128)(2,1)S(1)} %get-tuple-element.74), channel_id=1, source_target_pairs={{16,8},{20,12},{24,0},{28,4},{17,9},{21,13},{25,1},{29,5},{18,10},... | collective-permute-start | bytes 393224 | tf_op jit(solution)/shard_map/ppermute | solution.py:449
  94.5 1.1 %pad_maximum_fusion.1 = bf16[256,2048]{1,0:T(8,128)(2,1)} fusion(bf16[256,1024]{1,0:T(8,128)(2,1)S(1)} %get-tuple-element.62, bf16[256,1024]{1,0:T(8,128)(2,1)S(1)} %get-tuple-element.56), kind=kLoop, calls=%fused_computation.1 | loop fusion | flops 2097152 | bytes 2097152 | tf_op jit(solution)/shard_map/concatenate | solution.py:521
  95.6 7.0 %collective-permute-done.11.refs_2_ = bf16[2,256,128]{2,1,0:T(8,128)(2,1)S(1)} collective-permute-done((bf16[2,256,128]{2,1,0:T(8,128)(2,1)S(1)}, bf16[2,256,128]{2,1,0:T(8,128)(2,1)S(1)}, u32[]{:S(2)}, u32[]{:S(2)}) %collective-permute-start.11) | collective-permute-done | bytes 131104 | tf_op jit(solution)/shard_map/ppermute | solution.py:449
  102.7 2.3 %collective-permute-done.15.refs_6_ = bf16[2,256,128]{2,1,0:T(8,128)(2,1)S(1)} collective-permute-done((bf16[2,256,128]{2,1,0:T(8,128)(2,1)S(1)}, bf16[2,256,128]{2,1,0:T(8,128)(2,1)S(1)}, u32[]{:S(2)}, u32[]{:S(2)}) %collective-permute-start.15) | collective-permute-done | bytes 131104 | tf_op jit(solution)/shard_map/ppermute | solution.py:449
  105.0 0.8 shard_map.121
  (62 shorter events, 0.1 us)
Async XLA Ops:
  0.6 22.6 %collective-permute-start.3 = (bf16[256,1280]{1,0:T(8,128)(2,1)}, bf16[256,1280]{1,0:T(8,128)(2,1)S(1)}, u32[]{:S(2)}, u32[]{:S(2)}) collective-permute-start(bf16[256,1280]{1,0:T(8,128)(2,1)} %refs_0_.1), channel_id=1, source_target_pairs={{0,1},{1,0},{2,3},{3,2},{4,5},{5,4},{6,7},{7,6},{8,9},{9,8},{10,11... | collective-permute-start | bytes 1966088 | tf_op jit(solution)/shard_map/ppermute | solution.py:446
  1.1 22.1 %collective-permute-start.4 = (bf16[256,1280]{1,0:T(8,128)(2,1)}, bf16[256,1280]{1,0:T(8,128)(2,1)S(1)}, u32[]{:S(2)}, u32[]{:S(2)}) collective-permute-start(bf16[256,1280]{1,0:T(8,128)(2,1)} %refs_0_.1), channel_id=1, source_target_pairs={{1,2},{2,1},{5,6},{6,5},{9,10},{10,9},{13,14},{14,13},{17,18},{18,... | collective-permute-start | bytes 1966088 | tf_op jit(solution)/shard_map/ppermute | solution.py:446
  7.6 8.5 %copy-start.21 = (bf16[256,512]{1,0:T(8,128)(2,1)}, bf16[256,512]{1,0:T(8,128)(2,1)S(1)}, u32[]{:S(2)}) copy-start(bf16[256,512]{1,0:T(8,128)(2,1)S(1)} %constant_dynamic-update-slice_fusion) | copy-start | bytes 786436
  7.6 12.2 %collective-permute-start.2 = (bf16[256,512]{1,0:T(8,128)(2,1)S(1)}, bf16[256,512]{1,0:T(8,128)(2,1)}, u32[]{:S(2)}, u32[]{:S(2)}) collective-permute-start(bf16[256,512]{1,0:T(8,128)(2,1)S(1)} %constant_dynamic-update-slice_fusion), channel_id=1, source_target_pairs={{0,24},{4,28},{8,16},{12,20},{16,8},{20,12},{24,0},{28,4},{1,25},{... | collective-permute-start | bytes 786440 | tf_op jit(solution)/shard_map/ppermute | solution.py:449
  9.2 12.6 %collective-permute-start.1 = (bf16[256,512]{1,0:T(8,128)(2,1)S(1)}, bf16[256,512]{1,0:T(8,128)(2,1)}, u32[]{:S(2)}, u32[]{:S(2)}) collective-permute-start(bf16[256,512]{1,0:T(8,128)(2,1)S(1)} %constant_dynamic-update-slice_fusion), channel_id=1, source_target_pairs={{0,16},{4,20},{8,24},{12,28},{16,0},{20,4},{24,8},{28,12},{1,17},{... | collective-permute-start | bytes 786440 | tf_op jit(solution)/shard_map/ppermute | solution.py:449
  9.7 12.2 %collective-permute-start = (bf16[256,512]{1,0:T(8,128)(2,1)S(1)}, bf16[256,512]{1,0:T(8,128)(2,1)}, u32[]{:S(2)}, u32[]{:S(2)}) collective-permute-start(bf16[256,512]{1,0:T(8,128)(2,1)S(1)} %constant_dynamic-update-slice_fusion), channel_id=1, source_target_pairs={{0,8},{4,12},{8,0},{12,4},{16,24},{20,28},{24,16},{28,20},{1,9},{5... | collective-permute-start | bytes 786440 | tf_op jit(solution)/shard_map/ppermute | solution.py:449
  11.2 1.1 %copy-start.10 = (bf16[256,1280]{1,0:T(8,128)(2,1)S(1)}, bf16[256,1280]{1,0:T(8,128)(2,1)}, u32[]{:S(2)}) copy-start(bf16[256,1280]{1,0:T(8,128)(2,1)} %refs_0_.1) | copy-start | bytes 1966084
  12.2 5.2 %copy-start.19 = (s32[2048]{0:T(1024)S(1)}, s32[2048]{0:T(1024)}, u32[]{:S(2)}) copy-start(s32[2048]{0:T(1024)} %param.15) | copy-start | bytes 24580
  12.2 5.2 %copy-start.20 = (s32[2,16]{1,0:T(2,128)S(1)}, s32[2,16]{1,0:T(2,128)}, u32[]{:S(2)}) copy-start(s32[2,16]{1,0:T(2,128)} %tile_ref.1) | copy-start | bytes 388
  16.1 1.3 %copy-start.1 = (f32[256,2048]{1,0:T(8,128)}, f32[256,2048]{1,0:T(8,128)S(1)}, u32[]{:S(2)}) copy-start(f32[256,2048]{1,0:T(8,128)S(1)} %shard_map.113.refs_2_) | copy-start | bytes 6291460
  17.5 11.8 %copy-start = (bf16[256,2048]{1,0:T(8,128)(2,1)S(1)}, bf16[256,2048]{1,0:T(8,128)(2,1)}, u32[]{:S(2)}) copy-start(bf16[256,2048]{1,0:T(8,128)(2,1)} %q_ref.7) | copy-start | bytes 3145732
  19.8 3.4 %copy-start.3 = (f32[7,256,256]{2,1,0:T(8,128)}, f32[7,256,256]{2,1,0:T(8,128)S(1)}, u32[]{:S(2)}) copy-start(f32[7,256,256]{2,1,0:T(8,128)S(1)} %get-tuple-element.46.bias_ref) | copy-start | bytes 5505028
  23.2 0.8 copy-start.11
  24.1 0.8 copy-start.13
  24.9 4.4 %collective-permute-start.5 = (bf16[4,256,512]{2,1,0:T(8,128)(2,1)S(1)}, bf16[4,256,512]{2,1,0:T(8,128)(2,1)S(1)}, u32[]{:S(2)}, u32[]{:S(2)}) collective-permute-start(bf16[4,256,512]{2,1,0:T(8,128)(2,1)S(1)} %pad_maximum_fusion.near_ref), channel_id=1, source_target_pairs={{0,4},{4,0},{8,12},{12,8},{16,20},{20,16},{24,28},{28,24},{1,5},{5... | collective-permute-start | bytes 3145736 | tf_op jit(solution)/shard_map/ppermute | solution.py:449
  24.9 19.3 %collective-permute-start.7 = (bf16[256,1280]{1,0:T(8,128)(2,1)}, bf16[256,1280]{1,0:T(8,128)(2,1)}, u32[]{:S(2)}, u32[]{:S(2)}) collective-permute-start(bf16[256,1280]{1,0:T(8,128)(2,1)} %copy-done.11), channel_id=1, source_target_pairs={{1,2},{2,1},{5,6},{6,5},{9,10},{10,9},{13,14},{14,13},{17,18},{18,... | collective-permute-start | bytes 1966088 | tf_op jit(solution)/shard_map/ppermute | solution.py:446
  27.1 30.9 %collective-permute-start.6 = (bf16[256,1280]{1,0:T(8,128)(2,1)}, bf16[256,1280]{1,0:T(8,128)(2,1)}, u32[]{:S(2)}, u32[]{:S(2)}) collective-permute-start(bf16[256,1280]{1,0:T(8,128)(2,1)} %copy-done.13), channel_id=1, source_target_pairs={{1,0},{2,3},{5,4},{6,7},{9,8},{10,11},{13,12},{14,15},{17,16},{18,... | collective-permute-start | bytes 1966088 | tf_op jit(solution)/shard_map/ppermute | solution.py:446
  29.3 1.5 %copy-start.4 = (f32[7,256,256]{2,1,0:T(8,128)S(1)}, f32[7,256,256]{2,1,0:T(8,128)}, u32[]{:S(2)}) copy-start(f32[7,256,256]{2,1,0:T(8,128)} %copy-done.3) | copy-start | bytes 5505028
  30.8 15.6 %copy-start.22 = (f32[256]{0:T(256)S(1)}, f32[256]{0:T(256)}, u32[]{:S(2)}) copy-start(f32[256]{0:T(256)} %param.10) | copy-start | bytes 3076
  30.8 15.8 %copy-start.23 = (s32[7]{0:T(128)S(1)}, s32[7]{0:T(128)}, u32[]{:S(2)}) copy-start(s32[7]{0:T(128)} %constant.90.clone) | copy-start | bytes 88
  44.2 22.1 %collective-permute-start.8 = (bf16[256,1280]{1,0:T(8,128)(2,1)}, bf16[256,1280]{1,0:T(8,128)(2,1)}, u32[]{:S(2)}, u32[]{:S(2)}) collective-permute-start(bf16[256,1280]{1,0:T(8,128)(2,1)} %collective-permute-done.7.x2_ref), channel_id=1, source_target_pairs={{1,0},{2,3},{5,4},{6,7},{9,8},{10,11},{13,12},{14,15},{17,16},{18,... | collective-permute-start | bytes 1966088 | tf_op jit(solution)/shard_map/ppermute | solution.py:446
  46.6 1.5 %copy-start.5 = (f32[7,256,256]{2,1,0:T(8,128)S(1)}, f32[7,256,256]{2,1,0:T(8,128)}, u32[]{:S(2)}) copy-start(f32[7,256,256]{2,1,0:T(8,128)} %copy-done.3) | copy-start | bytes 5505028
  48.1 9.9 %copy-start.2 = (f32[256,2048]{1,0:T(8,128)S(1)}, f32[256,2048]{1,0:T(8,128)}, u32[]{:S(2)}) copy-start(f32[256,2048]{1,0:T(8,128)} %copy-done.1) | copy-start | bytes 6291460
  48.1 9.9 %copy-start.12 = (bf16[256,1280]{1,0:T(8,128)(2,1)S(1)}, bf16[256,1280]{1,0:T(8,128)(2,1)}, u32[]{:S(2)}) copy-start(bf16[256,1280]{1,0:T(8,128)(2,1)} %copy-done.11) | copy-start | bytes 1966084
  48.1 9.9 %copy-start.14 = (bf16[256,1280]{1,0:T(8,128)(2,1)S(1)}, bf16[256,1280]{1,0:T(8,128)(2,1)}, u32[]{:S(2)}) copy-start(bf16[256,1280]{1,0:T(8,128)(2,1)} %copy-done.13) | copy-start | bytes 1966084
  58.0 8.4 %slice-start = ((s8[7340032]{0:T(1024)(128)(4,1)}), s8[4194304]{0:T(1024)(128)(4,1)S(1)}, s32[]{:S(2)}) async-start(s8[7340032]{0:T(1024)(128)(4,1)} %bitcast.11), calls=%async_computation | async-start | bytes 8388608
  58.0 8.4 %slice-start.1 = ((s8[7340032]{0:T(1024)(128)(4,1)}), s8[3145728]{0:T(1024)(128)(4,1)S(1)}, s32[]{:S(2)}) async-start(s8[7340032]{0:T(1024)(128)(4,1)} %bitcast.11), calls=%async_computation.1 | async-start | bytes 6291456
  58.0 8.4 %copy-start.6 = (bf16[1024,1280]{1,0:T(8,128)(2,1)S(1)}, bf16[1024,1280]{1,0:T(8,128)(2,1)}, u32[]{:S(2)}) copy-start(bf16[1024,1280]{1,0:T(8,128)(2,1)} %get-tuple-element.51.w_ref) | copy-start | bytes 7864324
  58.0 8.4 %copy-start.8 = (f32[8,256,256]{2,1,0:T(8,128)S(1)}, f32[8,256,256]{2,1,0:T(8,128)}, u32[]{:S(2)}) copy-start(f32[8,256,256]{2,1,0:T(8,128)} %get-tuple-element.52.o_ref) | copy-start | bytes 6291460
  58.0 8.4 %copy-start.15 = (bf16[1792,128]{1,0:T(8,128)(2,1)S(1)}, bf16[1792,128]{1,0:T(8,128)(2,1)}, u32[]{:S(2)}) copy-start(bf16[1792,128]{1,0:T(8,128)(2,1)} %get-tuple-element.53.k_ref) | copy-start | bytes 1376260
  58.0 8.4 %copy-start.16 = (bf16[1792,128]{1,0:T(8,128)(2,1)S(1)}, bf16[1792,128]{1,0:T(8,128)(2,1)}, u32[]{:S(2)}) copy-start(bf16[1792,128]{1,0:T(8,128)(2,1)} %get-tuple-element.54.v_ref) | copy-start | bytes 1376260
  66.3 8.5 %slice-start.2 = ((s8[7340032]{0:T(1024)(128)(4,1)}), s8[4194304]{0:T(1024)(128)(4,1)S(1)}, s32[]{:S(2)}) async-start(s8[7340032]{0:T(1024)(128)(4,1)} %bitcast.13), calls=%async_computation.2 | async-start | bytes 8388608
  66.4 8.5 %slice-start.3 = ((s8[7340032]{0:T(1024)(128)(4,1)}), s8[3145728]{0:T(1024)(128)(4,1)S(1)}, s32[]{:S(2)}) async-start(s8[7340032]{0:T(1024)(128)(4,1)} %bitcast.13), calls=%async_computation.3 | async-start | bytes 6291456
  66.4 8.5 %copy-start.7 = (bf16[1024,1280]{1,0:T(8,128)(2,1)S(1)}, bf16[1024,1280]{1,0:T(8,128)(2,1)}, u32[]{:S(2)}) copy-start(bf16[1024,1280]{1,0:T(8,128)(2,1)} %get-tuple-element.57.w_ref) | copy-start | bytes 7864324
  66.4 8.4 %copy-start.9 = (f32[8,256,256]{2,1,0:T(8,128)S(1)}, f32[8,256,256]{2,1,0:T(8,128)}, u32[]{:S(2)}) copy-start(f32[8,256,256]{2,1,0:T(8,128)} %get-tuple-element.58.o_ref) | copy-start | bytes 6291460
  66.4 8.4 %copy-start.17 = (bf16[1792,128]{1,0:T(8,128)(2,1)S(1)}, bf16[1792,128]{1,0:T(8,128)(2,1)}, u32[]{:S(2)}) copy-start(bf16[1792,128]{1,0:T(8,128)(2,1)} %get-tuple-element.59.k_ref) | copy-start | bytes 1376260
  66.4 8.4 %copy-start.18 = (bf16[1792,128]{1,0:T(8,128)(2,1)S(1)}, bf16[1792,128]{1,0:T(8,128)(2,1)}, u32[]{:S(2)}) copy-start(bf16[1792,128]{1,0:T(8,128)(2,1)} %get-tuple-element.60.v_ref) | copy-start | bytes 1376260
  73.9 9.3 %collective-permute-start.9 = (bf16[3,2,256,128]{3,2,1,0:T(8,128)(2,1)S(1)}, bf16[3,2,256,128]{3,2,1,0:T(8,128)(2,1)S(1)}, u32[]{:S(2)}, u32[]{:S(2)}) collective-permute-start(bf16[3,2,256,128]{3,2,1,0:T(8,128)(2,1)S(1)} %get-tuple-element.63), channel_id=1, source_target_pairs={{0,4},{4,0},{8,12},{12,8},{16,20},{20,16},{24,28},{28,24},{1,5},{5... | collective-permute-start | bytes 1179656 | tf_op jit(solution)/shard_map/ppermute | solution.py:449
  82.0 5.9 %collective-permute-start.13 = (bf16[3,2,256,128]{3,2,1,0:T(8,128)(2,1)S(1)}, bf16[3,2,256,128]{3,2,1,0:T(8,128)(2,1)S(1)}, u32[]{:S(2)}, u32[]{:S(2)}) collective-permute-start(bf16[3,2,256,128]{3,2,1,0:T(8,128)(2,1)S(1)} %get-tuple-element.69), channel_id=1, source_target_pairs={{0,4},{4,0},{8,12},{12,8},{16,20},{20,16},{24,28},{28,24},{1,5},{5... | collective-permute-start | bytes 1179656 | tf_op jit(solution)/shard_map/ppermute | solution.py:449
  83.4 9.9 %collective-permute-start.10 = (bf16[2,256,128]{2,1,0:T(8,128)(2,1)S(1)}, bf16[2,256,128]{2,1,0:T(8,128)(2,1)S(1)}, u32[]{:S(2)}, u32[]{:S(2)}) collective-permute-start(bf16[2,256,128]{2,1,0:T(8,128)(2,1)S(1)} %get-tuple-element.66), channel_id=1, source_target_pairs={{0,8},{8,0},{4,12},{12,4},{24,16},{28,20},{1,9},{9,1},{5,13},{13,5... | collective-permute-start | bytes 393224 | tf_op jit(solution)/shard_map/ppermute | solution.py:449
  85.3 17.4 %collective-permute-start.11 = (bf16[2,256,128]{2,1,0:T(8,128)(2,1)S(1)}, bf16[2,256,128]{2,1,0:T(8,128)(2,1)S(1)}, u32[]{:S(2)}, u32[]{:S(2)}) collective-permute-start(bf16[2,256,128]{2,1,0:T(8,128)(2,1)S(1)} %get-tuple-element.67), channel_id=1, source_target_pairs={{16,0},{20,4},{24,8},{28,12},{17,1},{21,5},{25,9},{29,13},{18,2},{... | collective-permute-start | bytes 393224 | tf_op jit(solution)/shard_map/ppermute | solution.py:449
  86.6 16.1 %collective-permute-start.12 = (bf16[2,256,128]{2,1,0:T(8,128)(2,1)S(1)}, bf16[2,256,128]{2,1,0:T(8,128)(2,1)S(1)}, u32[]{:S(2)}, u32[]{:S(2)}) collective-permute-start(bf16[2,256,128]{2,1,0:T(8,128)(2,1)S(1)} %get-tuple-element.68), channel_id=1, source_target_pairs={{16,8},{20,12},{24,0},{28,4},{17,9},{21,13},{25,1},{29,5},{18,10},... | collective-permute-start | bytes 393224 | tf_op jit(solution)/shard_map/ppermute | solution.py:449
  88.0 14.6 %collective-permute-start.14 = (bf16[2,256,128]{2,1,0:T(8,128)(2,1)S(1)}, bf16[2,256,128]{2,1,0:T(8,128)(2,1)S(1)}, u32[]{:S(2)}, u32[]{:S(2)}) collective-permute-start(bf16[2,256,128]{2,1,0:T(8,128)(2,1)S(1)} %get-tuple-element.72), channel_id=1, source_target_pairs={{0,8},{8,0},{4,12},{12,4},{24,16},{28,20},{1,9},{9,1},{5,13},{13,5... | collective-permute-start | bytes 393224 | tf_op jit(solution)/shard_map/ppermute | solution.py:449
  91.9 13.0 %collective-permute-start.15 = (bf16[2,256,128]{2,1,0:T(8,128)(2,1)S(1)}, bf16[2,256,128]{2,1,0:T(8,128)(2,1)S(1)}, u32[]{:S(2)}, u32[]{:S(2)}) collective-permute-start(bf16[2,256,128]{2,1,0:T(8,128)(2,1)S(1)} %get-tuple-element.73), channel_id=1, source_target_pairs={{16,0},{20,4},{24,8},{28,12},{17,1},{21,5},{25,9},{29,13},{18,2},{... | collective-permute-start | bytes 393224 | tf_op jit(solution)/shard_map/ppermute | solution.py:449
  93.2 11.7 %collective-permute-start.16 = (bf16[2,256,128]{2,1,0:T(8,128)(2,1)S(1)}, bf16[2,256,128]{2,1,0:T(8,128)(2,1)S(1)}, u32[]{:S(2)}, u32[]{:S(2)}) collective-permute-start(bf16[2,256,128]{2,1,0:T(8,128)(2,1)S(1)} %get-tuple-element.74), channel_id=1, source_target_pairs={{16,8},{20,12},{24,0},{28,4},{17,9},{21,13},{25,1},{29,5},{18,10},... | collective-permute-start | bytes 393224 | tf_op jit(solution)/shard_map/ppermute | solution.py:449

commit v6 on v5

--- a/solution.py
+++ b/solution.py
@@ -56,6 +56,17 @@
         compiler_params=pltpu.CompilerParams(vmem_limit_bytes=VMEM_LIMIT),
         cost_estimate=pl.CostEstimate(flops=flops, bytes_accessed=size, transcendentals=exps),
     )(*ins)
+
+
+def join_kernel(k_ref, v_ref, out_ref):
+    width = k_ref.shape[1]
+    out_ref[:, :width] = k_ref[...]
+    out_ref[:, width:] = v_ref[...]
+
+
+def stack_kernel(*refs):
+    for i, ref in enumerate(refs[:-1]):
+        refs[-1][i] = ref[...]
 
 
 def mask_kernel(n_kb, prompt, back, total, me_ref, seg_ref, tile_ref, bias_ref, live_ref):
@@ -235,7 +246,7 @@
 
 
 def back_kernel(
-    n_kb, n_send, first, live_ref, pos_ref, proj_ref, x1_ref, x2_ref, w_ref, adv_ref,
+    n_kb, n_send, first, live_ref, pos_ref, edge_ref, proj_ref, x1_ref, x2_ref, w_ref, adv_ref,
     o_ref, q_ref, k_ref, v_ref, p_ref,
     dq_ref, send_ref, keep_ref, dox_ref, qs_ref, ds_ref, dqt_ref,
 ):
@@ -243,8 +254,9 @@
     per = rows // KB
     lane = lax.broadcasted_iota(jnp.int32, (KB, HD), 1)
     minus = jnp.where(lane < 3, -1.0, 0.0).astype(BF16)
-    x = x1_ref[...] + x2_ref[...]
+    x = choose(edge_ref[0], x1_ref[...], x2_ref[...])
     dqt_ref[...] = jnp.zeros_like(dqt_ref)
+    adv = jnp.broadcast_to(adv_ref[...], (HD, rows)).T
     for h in range(SHARE):
         cols = pl.ds((first + h) * HD, HD)
         fresh = dot_nt(x, w_ref[h * HD : (h + 1) * HD, :])
@@ -253,7 +265,7 @@
             here = pl.ds((h * per + r) * KB, KB)
             out = o_ref[h * per + r]
             proj = proj_ref[part, cols] + fresh[part]
-            grad = (proj * (adv_ref[part, :] * out[:, HD:])).astype(BF16)
+            grad = (proj * (adv[part] * out[:, HD:])).astype(BF16)
             delta = jnp.sum(grad.astype(F32) * out[:, :HD], axis=1, keepdims=True)
             one = delta.astype(BF16).astype(F32)
             two = (delta - one).astype(BF16).astype(F32)
@@ -311,12 +323,12 @@
         )
 
 
-def back_call(group, live, pos, proj, x1, x2, w, adv, o, q, k, v, p, n_kb, n_send):
+def back_call(group, live, pos, edge, proj, x1, x2, w, adv, o, q, k, v, p, n_kb, n_send):
     rows = q.shape[0]
     return call(
         functools.partial(back_kernel, n_kb, n_send, group * SHARE),
-        (live, pos, proj, x1, x2, w, adv, o, q, k, v, p),
-        [SMEM] * 2 + [VMEM] * 10,
+        (live, pos, edge, proj, x1, x2, w, adv, o, q, k, v, p),
+        [SMEM] * 3 + [VMEM] * 10,
         [
             ((rows, SHARE * HD), BF16),
             ((max(n_send, 1), 2, KB, HD), BF16),
@@ -352,13 +364,20 @@
         base_ref[...] = here
 
 
-def last_kernel(groups, *refs):
+def last_kernel(groups, me_ref, *refs):
     dk_ref, dv_ref = refs[-2:]
+    me = jnp.full((2, KB, HD), me_ref[0])
+    across, beside = me < 4, me < 6
     for g in range(groups):
         base, x, y, d = refs[4 * g : 4 * g + 4]
-        total = base[...] + x[...].astype(F32) + y[...].astype(F32) + d[...].astype(F32)
+        total = base[...] + jnp.where(beside, x[...].astype(F32), 0.0)
+        total += jnp.where(across, y[...].astype(F32) + d[...].astype(F32), 0.0)
         dk_ref[:, g * HD : (g + 1) * HD] = (total[0] * SCALE).astype(BF16)
         dv_ref[:, g * HD : (g + 1) * HD] = total[1].astype(BF16)
+
+
+def choose(flag, first, second):
+    return jnp.where(jnp.full(first.shape, flag) != 0, first, second)
 
 
 def project_kernel(count, added, halves, shard_ref, w_ref, *refs):
@@ -367,7 +386,7 @@
         acc_ref, refs = refs[0], refs[1:]
     values = [x[...] for x in xs]
     if halves:
-        values[-1] = values[-1] + refs[0][...]
+        values[-1] = choose(shard_ref[count], refs[0][...], values[-1])
         refs = refs[1:]
     out_ref, held_ref, sems = refs
     depth = xs[0].shape[1]
@@ -439,18 +458,20 @@
     prompt_kb = prompt // KB
     n_kb = prompt_kb + (back + 1) * per
     fast = n_ctx == 8 and n_tp == 4 and per == 1 and back == 2
-    own = jnp.concatenate([key_heads, value_heads], axis=1)
+    shape = (rows, 2 * groups * HD)
+    own = call(join_kernel, (key_heads, value_heads), [VMEM] * 2, [(shape, BF16)])[0]
     weight = pltpu.with_memory_space_constraint(out_weight, pltpu.HBM)
 
     def hop(value, pairs):
         return lax.ppermute(value, "tp", pairs)
 
-    def flip(value, bit, pairs=None):
-        return lax.ppermute(value, "ctx", pairs or [(i, i ^ bit) for i in range(n_ctx)])
+    def flip(value, bit):
+        return lax.ppermute(value, "ctx", [(i, i ^ bit) for i in range(n_ctx)])
 
     if fast:
-        near = jnp.stack([own] + [flip(own, d) for d in (2, 4, 6)])
-        ends, middle, out = [(0, 1), (1, 0), (2, 3), (3, 2)], [(1, 2), (2, 1)], [(1, 0), (2, 3)]
+        pieces = [own] + [flip(own, d) for d in (2, 4, 6)]
+        near = call(stack_kernel, pieces, [VMEM] * 4, [((4,) + shape, BF16)])[0]
+        ends, middle = [(0, 1), (1, 0), (2, 3), (3, 2)], [(1, 2), (2, 1), (0, 0), (3, 3)]
         up_a = hop(upstream, ends)
         up_c = hop(upstream, middle)
     else:
@@ -474,7 +495,7 @@
             jnp.array([0, 0, 0, 0, 6, 2, 5], jnp.int32),
         )
         n_send = 3
-        half = z // 2
+        half, edge = z // 2, (z % 3 == 0).astype(jnp.int32)
         second, shard = 2 - half, 3 - 3 * half
         acc = project_call(z[None], [upstream], weight)
     else:
@@ -488,19 +509,20 @@
             other = (z + 1 + i) % n_tp
             x = lax.dynamic_index_in_dim(whole, other, 0, keepdims=False)
             acc = project_call(other[None], [x], weight, acc)
-        x1, x2 = upstream, jnp.zeros_like(upstream)
+        x1, x2, edge = upstream, upstream, jnp.int32(1)
 
     slots = slots.astype(jnp.int32)
     depth = upstream.shape[1]
     if fast:
-        near, bias, acc, up_a, up_c = lax.optimization_barrier((near, bias, acc, up_a, up_c))
+        up_a, up_c, bias, acc = lax.optimization_barrier((up_a, up_c, bias, acc))
+        up_e = hop(up_a, middle)
+        up_f = hop(up_c, ends)
+        near, up_a = lax.optimization_barrier((near, up_a))
         far = flip(near, 1)
-        up_e = hop(up_a, middle)
-        up_f = hop(up_c, out)
     soft = [list(probs_call(0, groups, slots, shard[None], weight, depth, query_heads, near, far, bias, n_kb))]
     if fast:
         up_e, soft[0][2] = lax.optimization_barrier((up_e, soft[0][2]))
-        up_d = hop(up_e, out)
+        up_d = hop(up_e, ends)
         x1, x2 = up_d, up_e
     soft += [
         list(probs_call(g, groups, slots, shard[None], weight, depth, query_heads, near, far, bias, n_kb))
@@ -508,13 +530,13 @@
     ]
     if fast:
         acc, soft[-1][2] = lax.optimization_barrier((acc, soft[-1][2]))
-        acc = project_call(jnp.stack([z ^ 1, second]), [up_a, up_c], weight, acc, up_f)
+        acc = project_call(jnp.stack([z ^ 1, second, edge]), [up_a, up_c], weight, acc, up_f)
     outs = []
     for g in range(groups):
         probs, attn, keys, values, w_last = soft[g]
         outs.append(
             back_call(
-                g, live, pos.astype(jnp.int32), acc, x1, x2, w_last, advantage[:, None], attn,
+                g, live, pos.astype(jnp.int32), edge[None], acc, x1, x2, w_last, advantage[None, :], attn,
                 query_heads, keys, values, probs, n_kb, n_send,
             )
         )
@@ -530,14 +552,14 @@
                 [SMEM, VMEM, VMEM],
                 [(shape, F32), (shape, BF16), (shape, BF16), (shape, BF16)],
             )
-            by_y = flip(to_y, 4, [(4, 0), (5, 1), (6, 2), (7, 3)])
-            by_d = flip(to_d, 6, [(4, 2), (5, 3), (6, 0), (7, 1)])
-            by_x = flip(to_x, 2, [(0, 2), (2, 0), (1, 3), (3, 1), (6, 4), (7, 5)])
+            by_y = flip(to_y, 4)
+            by_d = flip(to_d, 6)
+            by_x = flip(to_x, 2)
             final += [base, by_x, by_y, by_d]
         grad_keys, grad_values = call(
             functools.partial(last_kernel, groups),
-            final,
-            [VMEM] * len(final),
+            [me[None]] + final,
+            [SMEM] + [VMEM] * len(final),
             [((rows, groups * HD), BF16)] * 2,
         )
         return grad_queries, grad_keys, grad_values

time: 106 us -> 106 us (level)
  the two profiles are of different devices: /device:TPU:10 before, /device:TPU:0 now
where the time goes in v6:
time: 106 us; the launch traced here: 105 us
  Pallas kernels  43.8 us (41%)
  starting transfers between devices  41.4 us (39%)
  local copies, waits for them, and re-layouts  11 us (10%)
  waiting for transfers between devices  6.7 us (6%)
  other arithmetic  1.15 us (1%)
    pallas_call x12, Pallas kernels, call(): pl.pallas_call(kernel, in_specs=in_specs, out_specs=out_specs or [VMEM] *...  43.8 us
    ppermute x12, starting transfers between devices, flip(): return lax.ppermute(value, 'ctx', [(i, i ^ bit) for i in range(n_ctx)])  23.2 us
    ppermute x5, starting transfers between devices, hop(): return lax.ppermute(value, 'tp', pairs)  18.2 us
    unnamed x58, local copies, waits for them, and re-layouts  11 us
    ppermute x12, waiting for transfers between devices, flip(): return lax.ppermute(value, 'ctx', [(i, i ^ bit) for i in range(n_ctx)])  6.68 us
  transfers between devices with their start and end apart: 17, of which 6 were waited for; matrix products, arithmetic and copies ran while one was open for 1% of the time, Pallas kernels for 36%

profile of v6, /device:TPU:0, one launch (start us, length us, event | category | flops | bytes accessed | tf_op | source)
XLA Modules:
  0.0 105.2 jit_solution(2435164365573081359)
XLA Ops:
  0.6 3.1 %collective-permute-start.3 = (bf16[256,1280]{1,0:T(8,128)(2,1)}, bf16[256,1280]{1,0:T(8,128)(2,1)S(1)}, u32[]{:S(2)}, u32[]{:S(2)}) collective-permute-start(bf16[256,1280]{1,0:T(8,128)(2,1)} %refs_0_.1), channel_id=1, source_target_pairs={{0,1},{1,0},{2,3},{3,2},{4,5},{5,4},{6,7},{7,6},{8,9},{9,8},{10,11... | collective-permute-start | bytes 1966088 | tf_op jit(solution)/shard_map/ppermute | solution.py:466
  3.7 6.5 %collective-permute-start.4 = (bf16[256,1280]{1,0:T(8,128)(2,1)}, bf16[256,1280]{1,0:T(8,128)(2,1)}, u32[]{:S(2)}, u32[]{:S(2)}) collective-permute-start(bf16[256,1280]{1,0:T(8,128)(2,1)} %refs_0_.1), channel_id=1, source_target_pairs={{1,2},{2,1},{0,0},{3,3},{5,6},{6,5},{4,4},{7,7},{9,10},{10,9},{8,8... | collective-permute-start | bytes 1966088 | tf_op jit(solution)/shard_map/ppermute | solution.py:466
  10.2 0.9 copy-done.19
  11.1 0.9 copy-done.20
  12.0 1.6 %collective-permute-start = (bf16[256,512]{1,0:T(8,128)(2,1)S(1)}, bf16[256,512]{1,0:T(8,128)(2,1)S(1)}, u32[]{:S(2)}, u32[]{:S(2)}) collective-permute-start(bf16[256,512]{1,0:T(8,128)(2,1)S(1)} %shard_map.113.refs_0_), channel_id=1, source_target_pairs={{0,8},{4,12},{8,0},{12,4},{16,24},{20,28},{24,16},{28,20},{1,9},{5... | collective-permute-start | bytes 786440 | tf_op jit(solution)/shard_map/ppermute | solution.py:469
  13.6 1.5 %collective-permute-start.1 = (bf16[256,512]{1,0:T(8,128)(2,1)S(1)}, bf16[256,512]{1,0:T(8,128)(2,1)S(1)}, u32[]{:S(2)}, u32[]{:S(2)}) collective-permute-start(bf16[256,512]{1,0:T(8,128)(2,1)S(1)} %shard_map.113.refs_0_), channel_id=1, source_target_pairs={{0,16},{4,20},{8,24},{12,28},{16,0},{20,4},{24,8},{28,12},{1,17},{... | collective-permute-start | bytes 786440 | tf_op jit(solution)/shard_map/ppermute | solution.py:469
  15.1 0.5 collective-permute-start.2
  15.6 1.1 %copy-done.10 = bf16[256,1280]{1,0:T(8,128)(2,1)S(1)} copy-done((bf16[256,1280]{1,0:T(8,128)(2,1)S(1)}, bf16[256,1280]{1,0:T(8,128)(2,1)}, u32[]{:S(2)}) %copy-start.10) | copy-done | bytes 655384
  16.7 3.9 %shard_map.115.refs_2_ = f32[256,2048]{1,0:T(8,128)S(1)} custom-call(s32[1]{0:T(128)} %bitcast.5.shard_ref, bf16[2048,5120]{1,0:T(8,128)(2,1)} %w_ref.7, bf16[256,1280]{1,0:T(8,128)(2,1)S(1)} %copy-done.10), custom_call_target="tpu_custom_call" | custom-call | tf_op jit(solution)/shard_map/pallas_call | solution.py:48
  20.6 1.3 %copy-done.1 = f32[256,2048]{1,0:T(8,128)} copy-done((f32[256,2048]{1,0:T(8,128)}, f32[256,2048]{1,0:T(8,128)S(1)}, u32[]{:S(2)}) %copy-start.1) | copy-done | bytes 2097176
  21.9 2.3 %shard_map.112 = (f32[7,256,256]{2,1,0:T(8,128)S(1)}, s32[7]{0:T(128)S(1)}) custom-call(s32[1]{0:T(128)} %bitcast.me_ref, s32[8,1,256]{2,1,0:T(1,128)S(1)} %bitcast.12, s32[2,16]{1,0:T(2,128)S(1)} %copy-done.23), custom_call_target="tpu_custom_call" | custom-call | bytes 1835008 | tf_op jit(solution)/shard_map/pallas_call | solution.py:48
  24.2 1.2 %copy-done.3 = f32[7,256,256]{2,1,0:T(8,128)} copy-done((f32[7,256,256]{2,1,0:T(8,128)}, f32[7,256,256]{2,1,0:T(8,128)S(1)}, u32[]{:S(2)}) %copy-start.3) | copy-done | bytes 1835032
  25.5 0.0 collective-permute-done.refs_1_
  25.5 1.3 %collective-permute-done.1.refs_2_ = bf16[256,512]{1,0:T(8,128)(2,1)S(1)} collective-permute-done((bf16[256,512]{1,0:T(8,128)(2,1)S(1)}, bf16[256,512]{1,0:T(8,128)(2,1)S(1)}, u32[]{:S(2)}, u32[]{:S(2)}) %collective-permute-start.1) | collective-permute-done | bytes 262176 | tf_op jit(solution)/shard_map/ppermute | solution.py:469
  26.7 0.7 copy-done.17
  27.4 0.9 copy-done.18
  28.4 0.1 shard_map.114.near_ref
  28.4 0.0 copy-start.11
  28.5 0.8 copy-done.11
  29.3 6.5 %collective-permute-start.7 = (bf16[256,1280]{1,0:T(8,128)(2,1)}, bf16[256,1280]{1,0:T(8,128)(2,1)}, u32[]{:S(2)}, u32[]{:S(2)}) collective-permute-start(bf16[256,1280]{1,0:T(8,128)(2,1)} %copy-done.11), channel_id=1, source_target_pairs={{1,2},{2,1},{0,0},{3,3},{5,6},{6,5},{4,4},{7,7},{9,10},{10,9},{8,8... | collective-permute-start | bytes 1966088 | tf_op jit(solution)/shard_map/ppermute | solution.py:466
  35.8 0.1 collective-permute-start.6
  35.9 1.5 %copy-done.4 = f32[7,256,256]{2,1,0:T(8,128)S(1)} copy-done((f32[7,256,256]{2,1,0:T(8,128)S(1)}, f32[7,256,256]{2,1,0:T(8,128)}, u32[]{:S(2)}) %copy-start.4) | copy-done | bytes 1835032
  37.4 9.2 %shard_map.118 = (bf16[8,1792,256]{2,1,0:T(8,128)(2,1)}, f32[8,256,256]{2,1,0:T(8,128)}, bf16[1792,128]{1,0:T(8,128)(2,1)}, bf16[1792,128]{1,0:T(8,128)(2,1)}, bf16[1024,1280]{1,0:T(8,128)(2,1)}) custom-call(s32[7]{0:T(128)S(1)} %fusion.1.slot_ref, s32[1]{0:T(128)} %bitcast.6.shard_ref, bf16[2048,5120]{1,0:T(8,128)(2,1)} %w_ref.7, ...), custom_call_target="tpu_custom_call" | custom-call | tf_op jit(solution)/shard_map/pallas_call | solution.py:48
  46.6 2.1 %collective-permute-start.8 = (bf16[256,1280]{1,0:T(8,128)(2,1)}, bf16[256,1280]{1,0:T(8,128)(2,1)}, u32[]{:S(2)}, u32[]{:S(2)}) collective-permute-start(bf16[256,1280]{1,0:T(8,128)(2,1)} %collective-permute-done.7.x2_ref), channel_id=1, source_target_pairs={{0,1},{1,0},{2,3},{3,2},{4,5},{5,4},{6,7},{7,6},{8,9},{9,8},{10,11... | collective-permute-start | bytes 1966088 | tf_op jit(solution)/shard_map/ppermute | solution.py:466
  48.7 0.1 pad_add_fusion.shard_ref
  48.8 1.5 %copy-done.5 = f32[7,256,256]{2,1,0:T(8,128)S(1)} copy-done((f32[7,256,256]{2,1,0:T(8,128)S(1)}, f32[7,256,256]{2,1,0:T(8,128)}, u32[]{:S(2)}) %copy-start.5) | copy-done | bytes 1835032
  50.3 9.3 %shard_map.116 = (bf16[8,1792,256]{2,1,0:T(8,128)(2,1)}, f32[8,256,256]{2,1,0:T(8,128)}, bf16[1792,128]{1,0:T(8,128)(2,1)}, bf16[1792,128]{1,0:T(8,128)(2,1)}, bf16[1024,1280]{1,0:T(8,128)(2,1)}) custom-call(s32[7]{0:T(128)S(1)} %fusion.1.slot_ref, s32[1]{0:T(128)} %bitcast.6.shard_ref, bf16[2048,5120]{1,0:T(8,128)(2,1)} %w_ref.7, ...), custom_call_target="tpu_custom_call" | custom-call | tf_op jit(solution)/shard_map/pallas_call | solution.py:48
  59.7 0.0 copy-start.22
  59.7 8.5 %shard_map.117.proj_ref = f32[256,2048]{1,0:T(8,128)S(1)} custom-call(s32[3]{0:T(128)S(1)} %pad_add_fusion.shard_ref, bf16[2048,5120]{1,0:T(8,128)(2,1)} %w_ref.7, bf16[256,1280]{1,0:T(8,128)(2,1)S(1)} %copy-done.12, bf16[256,1280]{1,0:T(8,128)(2,1)} %collective-permute-done.4.refs_1_, f32[256,2048]{1,0:T(8,128)S(1)} %copy-done.2, ...), custom_call_target="tpu_custom_call" | custom-call | tf_op jit(solution)/shard_map/pallas_call | solution.py:48
  68.4 4.9 %shard_map.119 = (bf16[256,1024]{1,0:T(8,128)(2,1)S(1)}, bf16[3,2,256,128]{3,2,1,0:T(8,128)(2,1)S(1)}, bf16[4,2,256,128]{3,2,1,0:T(8,128)(2,1)S(1)}) custom-call(s32[7]{0:T(128)S(1)} %get-tuple-element.41.live_ref, s32[7]{0:T(128)S(1)} %compare_select_fusion.5.pos_ref, s32[1]{0:T(128)} %bitcast.2.edge_ref, f32[256,2048]{1,0:T(8,128)S(1)} %shard_map.117.proj_ref, ...), custom_call_target="tpu_custom_call" | custom-call | tf_op jit(solution)/shard_map/pallas_call | solution.py:48
  73.3 1.1 %collective-permute-start.9 = (bf16[3,2,256,128]{3,2,1,0:T(8,128)(2,1)S(1)}, bf16[3,2,256,128]{3,2,1,0:T(8,128)(2,1)S(1)}, u32[]{:S(2)}, u32[]{:S(2)}) collective-permute-start(bf16[3,2,256,128]{3,2,1,0:T(8,128)(2,1)S(1)} %get-tuple-element.65), channel_id=1, source_target_pairs={{0,4},{4,0},{8,12},{12,8},{16,20},{20,16},{24,28},{28,24},{1,5},{5... | collective-permute-start | bytes 1179656 | tf_op jit(solution)/shard_map/ppermute | solution.py:469
  74.5 4.6 %shard_map.120 = (bf16[256,1024]{1,0:T(8,128)(2,1)S(1)}, bf16[3,2,256,128]{3,2,1,0:T(8,128)(2,1)S(1)}, bf16[4,2,256,128]{3,2,1,0:T(8,128)(2,1)S(1)}) custom-call(s32[7]{0:T(128)S(1)} %get-tuple-element.41.live_ref, s32[7]{0:T(128)S(1)} %compare_select_fusion.5.pos_ref, s32[1]{0:T(128)} %bitcast.2.edge_ref, f32[256,2048]{1,0:T(8,128)S(1)} %shard_map.117.proj_ref, ...), custom_call_target="tpu_custom_call" | custom-call | tf_op jit(solution)/shard_map/pallas_call | solution.py:48
  79.1 1.2 %collective-permute-start.13 = (bf16[3,2,256,128]{3,2,1,0:T(8,128)(2,1)S(1)}, bf16[3,2,256,128]{3,2,1,0:T(8,128)(2,1)S(1)}, u32[]{:S(2)}, u32[]{:S(2)}) collective-permute-start(bf16[3,2,256,128]{3,2,1,0:T(8,128)(2,1)S(1)} %get-tuple-element.71), channel_id=1, source_target_pairs={{0,4},{4,0},{8,12},{12,8},{16,20},{20,16},{24,28},{28,24},{1,5},{5... | collective-permute-start | bytes 1179656 | tf_op jit(solution)/shard_map/ppermute | solution.py:469
  80.3 0.1 shard_map.121
  80.4 5.8 %collective-permute-start.10 = (bf16[2,256,128]{2,1,0:T(8,128)(2,1)S(1)}, bf16[2,256,128]{2,1,0:T(8,128)(2,1)S(1)}, u32[]{:S(2)}, u32[]{:S(2)}) collective-permute-start(bf16[2,256,128]{2,1,0:T(8,128)(2,1)S(1)} %get-tuple-element.68), channel_id=1, source_target_pairs={{0,8},{4,12},{8,0},{12,4},{16,24},{20,28},{24,16},{28,20},{1,9},{5... | collective-permute-start | bytes 393224 | tf_op jit(solution)/shard_map/ppermute | solution.py:469
  86.2 5.9 %collective-permute-start.11 = (bf16[2,256,128]{2,1,0:T(8,128)(2,1)S(1)}, bf16[2,256,128]{2,1,0:T(8,128)(2,1)S(1)}, u32[]{:S(2)}, u32[]{:S(2)}) collective-permute-start(bf16[2,256,128]{2,1,0:T(8,128)(2,1)S(1)} %get-tuple-element.69), channel_id=1, source_target_pairs={{0,16},{4,20},{8,24},{12,28},{16,0},{20,4},{24,8},{28,12},{1,17},{... | collective-permute-start | bytes 393224 | tf_op jit(solution)/shard_map/ppermute | solution.py:469
  92.0 0.4 collective-permute-start.12
  92.4 0.1 shard_map.122
  92.5 1.1 %collective-permute-start.14 = (bf16[2,256,128]{2,1,0:T(8,128)(2,1)S(1)}, bf16[2,256,128]{2,1,0:T(8,128)(2,1)S(1)}, u32[]{:S(2)}, u32[]{:S(2)}) collective-permute-start(bf16[2,256,128]{2,1,0:T(8,128)(2,1)S(1)} %get-tuple-element.74), channel_id=1, source_target_pairs={{0,8},{4,12},{8,0},{12,4},{16,24},{20,28},{24,16},{28,20},{1,9},{5... | collective-permute-start | bytes 393224 | tf_op jit(solution)/shard_map/ppermute | solution.py:469
  93.7 2.1 %collective-permute-start.15 = (bf16[2,256,128]{2,1,0:T(8,128)(2,1)S(1)}, bf16[2,256,128]{2,1,0:T(8,128)(2,1)S(1)}, u32[]{:S(2)}, u32[]{:S(2)}) collective-permute-start(bf16[2,256,128]{2,1,0:T(8,128)(2,1)S(1)} %get-tuple-element.75), channel_id=1, source_target_pairs={{0,16},{4,20},{8,24},{12,28},{16,0},{20,4},{24,8},{28,12},{1,17},{... | collective-permute-start | bytes 393224 | tf_op jit(solution)/shard_map/ppermute | solution.py:469
  95.8 2.1 %collective-permute-start.16 = (bf16[2,256,128]{2,1,0:T(8,128)(2,1)S(1)}, bf16[2,256,128]{2,1,0:T(8,128)(2,1)S(1)}, u32[]{:S(2)}, u32[]{:S(2)}) collective-permute-start(bf16[2,256,128]{2,1,0:T(8,128)(2,1)S(1)} %get-tuple-element.76), channel_id=1, source_target_pairs={{0,24},{4,28},{8,16},{12,20},{16,8},{20,12},{24,0},{28,4},{1,25},{... | collective-permute-start | bytes 393224 | tf_op jit(solution)/shard_map/ppermute | solution.py:469
  97.8 1.1 %pad_maximum_fusion = bf16[256,2048]{1,0:T(8,128)(2,1)} fusion(bf16[256,1024]{1,0:T(8,128)(2,1)S(1)} %get-tuple-element.64, bf16[256,1024]{1,0:T(8,128)(2,1)S(1)} %get-tuple-element.58), kind=kLoop, calls=%fused_computation | loop fusion | flops 2097152 | bytes 2097152 | tf_op jit(solution)/shard_map/concatenate | solution.py:543
  98.9 0.4 collective-permute-done.11.refs_2_
  99.3 0.2 collective-permute-done.12.refs_3_
  99.5 1.2 %collective-permute-done.14.refs_5_ = bf16[2,256,128]{2,1,0:T(8,128)(2,1)S(1)} collective-permute-done((bf16[2,256,128]{2,1,0:T(8,128)(2,1)S(1)}, bf16[2,256,128]{2,1,0:T(8,128)(2,1)S(1)}, u32[]{:S(2)}, u32[]{:S(2)}) %collective-permute-start.14) | collective-permute-done | bytes 131104 | tf_op jit(solution)/shard_map/ppermute | solution.py:469
  100.7 2.5 %collective-permute-done.15.refs_6_ = bf16[2,256,128]{2,1,0:T(8,128)(2,1)S(1)} collective-permute-done((bf16[2,256,128]{2,1,0:T(8,128)(2,1)S(1)}, bf16[2,256,128]{2,1,0:T(8,128)(2,1)S(1)}, u32[]{:S(2)}, u32[]{:S(2)}) %collective-permute-start.15) | collective-permute-done | bytes 131104 | tf_op jit(solution)/shard_map/ppermute | solution.py:469
  103.2 1.2 %collective-permute-done.16.refs_7_ = bf16[2,256,128]{2,1,0:T(8,128)(2,1)S(1)} collective-permute-done((bf16[2,256,128]{2,1,0:T(8,128)(2,1)S(1)}, bf16[2,256,128]{2,1,0:T(8,128)(2,1)S(1)}, u32[]{:S(2)}, u32[]{:S(2)}) %collective-permute-start.16) | collective-permute-done | bytes 131104 | tf_op jit(solution)/shard_map/ppermute | solution.py:469
  104.3 0.8 shard_map.123
  (62 shorter events, 0.2 us)
Async XLA Ops:
  0.6 27.8 %collective-permute-start.3 = (bf16[256,1280]{1,0:T(8,128)(2,1)}, bf16[256,1280]{1,0:T(8,128)(2,1)S(1)}, u32[]{:S(2)}, u32[]{:S(2)}) collective-permute-start(bf16[256,1280]{1,0:T(8,128)(2,1)} %refs_0_.1), channel_id=1, source_target_pairs={{0,1},{1,0},{2,3},{3,2},{4,5},{5,4},{6,7},{7,6},{8,9},{9,8},{10,11... | collective-permute-start | bytes 1966088 | tf_op jit(solution)/shard_map/ppermute | solution.py:466
  3.7 24.7 %collective-permute-start.4 = (bf16[256,1280]{1,0:T(8,128)(2,1)}, bf16[256,1280]{1,0:T(8,128)(2,1)}, u32[]{:S(2)}, u32[]{:S(2)}) collective-permute-start(bf16[256,1280]{1,0:T(8,128)(2,1)} %refs_0_.1), channel_id=1, source_target_pairs={{1,2},{2,1},{0,0},{3,3},{5,6},{6,5},{4,4},{7,7},{9,10},{10,9},{8,8... | collective-permute-start | bytes 1966088 | tf_op jit(solution)/shard_map/ppermute | solution.py:466
  10.2 0.9 copy-start.19
  11.1 0.9 copy-start.20
  12.0 13.4 %collective-permute-start = (bf16[256,512]{1,0:T(8,128)(2,1)S(1)}, bf16[256,512]{1,0:T(8,128)(2,1)S(1)}, u32[]{:S(2)}, u32[]{:S(2)}) collective-permute-start(bf16[256,512]{1,0:T(8,128)(2,1)S(1)} %shard_map.113.refs_0_), channel_id=1, source_target_pairs={{0,8},{4,12},{8,0},{12,4},{16,24},{20,28},{24,16},{28,20},{1,9},{5... | collective-permute-start | bytes 786440 | tf_op jit(solution)/shard_map/ppermute | solution.py:469
  13.6 13.1 %collective-permute-start.1 = (bf16[256,512]{1,0:T(8,128)(2,1)S(1)}, bf16[256,512]{1,0:T(8,128)(2,1)S(1)}, u32[]{:S(2)}, u32[]{:S(2)}) collective-permute-start(bf16[256,512]{1,0:T(8,128)(2,1)S(1)} %shard_map.113.refs_0_), channel_id=1, source_target_pairs={{0,16},{4,20},{8,24},{12,28},{16,0},{20,4},{24,8},{28,12},{1,17},{... | collective-permute-start | bytes 786440 | tf_op jit(solution)/shard_map/ppermute | solution.py:469
  15.1 11.6 %collective-permute-start.2 = (bf16[256,512]{1,0:T(8,128)(2,1)S(1)}, bf16[256,512]{1,0:T(8,128)(2,1)S(1)}, u32[]{:S(2)}, u32[]{:S(2)}) collective-permute-start(bf16[256,512]{1,0:T(8,128)(2,1)S(1)} %shard_map.113.refs_0_), channel_id=1, source_target_pairs={{0,24},{4,28},{8,16},{12,20},{16,8},{20,12},{24,0},{28,4},{1,25},{... | collective-permute-start | bytes 786440 | tf_op jit(solution)/shard_map/ppermute | solution.py:469
  15.6 1.1 %copy-start.10 = (bf16[256,1280]{1,0:T(8,128)(2,1)S(1)}, bf16[256,1280]{1,0:T(8,128)(2,1)}, u32[]{:S(2)}) copy-start(bf16[256,1280]{1,0:T(8,128)(2,1)} %refs_0_.1) | copy-start | bytes 1966084
  16.7 5.2 %copy-start.21 = (s32[2048]{0:T(1024)S(1)}, s32[2048]{0:T(1024)}, u32[]{:S(2)}) copy-start(s32[2048]{0:T(1024)} %param.15) | copy-start | bytes 24580
  16.7 5.2 %copy-start.23 = (s32[2,16]{1,0:T(2,128)S(1)}, s32[2,16]{1,0:T(2,128)}, u32[]{:S(2)}) copy-start(s32[2,16]{1,0:T(2,128)} %tile_ref.1) | copy-start | bytes 388
  20.6 1.3 %copy-start.1 = (f32[256,2048]{1,0:T(8,128)}, f32[256,2048]{1,0:T(8,128)S(1)}, u32[]{:S(2)}) copy-start(f32[256,2048]{1,0:T(8,128)S(1)} %shard_map.115.refs_2_) | copy-start | bytes 6291460
  21.9 14.0 %copy-start = (bf16[256,2048]{1,0:T(8,128)(2,1)S(1)}, bf16[256,2048]{1,0:T(8,128)(2,1)}, u32[]{:S(2)}) copy-start(bf16[256,2048]{1,0:T(8,128)(2,1)} %q_ref.7) | copy-start | bytes 3145732
  24.2 1.2 %copy-start.3 = (f32[7,256,256]{2,1,0:T(8,128)}, f32[7,256,256]{2,1,0:T(8,128)S(1)}, u32[]{:S(2)}) copy-start(f32[7,256,256]{2,1,0:T(8,128)S(1)} %get-tuple-element.48.bias_ref) | copy-start | bytes 5505028
  26.7 0.7 copy-start.17
  27.4 0.9 copy-start.18
  28.4 0.8 copy-start.11
  29.3 6.6 %collective-permute-start.5 = (bf16[4,256,512]{2,1,0:T(8,128)(2,1)S(1)}, bf16[4,256,512]{2,1,0:T(8,128)(2,1)S(1)}, u32[]{:S(2)}, u32[]{:S(2)}) collective-permute-start(bf16[4,256,512]{2,1,0:T(8,128)(2,1)S(1)} %shard_map.114.near_ref), channel_id=1, source_target_pairs={{0,4},{4,0},{8,12},{12,8},{16,20},{20,16},{24,28},{28,24},{1,5},{5... | collective-permute-start | bytes 3145736 | tf_op jit(solution)/shard_map/ppermute | solution.py:469
  29.3 17.3 %collective-permute-start.7 = (bf16[256,1280]{1,0:T(8,128)(2,1)}, bf16[256,1280]{1,0:T(8,128)(2,1)}, u32[]{:S(2)}, u32[]{:S(2)}) collective-permute-start(bf16[256,1280]{1,0:T(8,128)(2,1)} %copy-done.11), channel_id=1, source_target_pairs={{1,2},{2,1},{0,0},{3,3},{5,6},{6,5},{4,4},{7,7},{9,10},{10,9},{8,8... | collective-permute-start | bytes 1966088 | tf_op jit(solution)/shard_map/ppermute | solution.py:466
  35.8 23.9 %collective-permute-start.6 = (bf16[256,1280]{1,0:T(8,128)(2,1)}, bf16[256,1280]{1,0:T(8,128)(2,1)}, u32[]{:S(2)}, u32[]{:S(2)}) collective-permute-start(bf16[256,1280]{1,0:T(8,128)(2,1)} %collective-permute-done.4.refs_1_), channel_id=1, source_target_pairs={{0,1},{1,0},{2,3},{3,2},{4,5},{5,4},{6,7},{7,6},{8,9},{9,8},{10,11... | collective-permute-start | bytes 1966088 | tf_op jit(solution)/shard_map/ppermute | solution.py:466
  35.9 1.5 %copy-start.4 = (f32[7,256,256]{2,1,0:T(8,128)S(1)}, f32[7,256,256]{2,1,0:T(8,128)}, u32[]{:S(2)}) copy-start(f32[7,256,256]{2,1,0:T(8,128)} %copy-done.3) | copy-start | bytes 5505028
  37.4 11.3 %copy-start.24 = (s32[7]{0:T(128)S(1)}, s32[7]{0:T(128)}, u32[]{:S(2)}) copy-start(s32[7]{0:T(128)} %constant.98.clone) | copy-start | bytes 88
  46.6 21.6 %collective-permute-start.8 = (bf16[256,1280]{1,0:T(8,128)(2,1)}, bf16[256,1280]{1,0:T(8,128)(2,1)}, u32[]{:S(2)}, u32[]{:S(2)}) collective-permute-start(bf16[256,1280]{1,0:T(8,128)(2,1)} %collective-permute-done.7.x2_ref), channel_id=1, source_target_pairs={{0,1},{1,0},{2,3},{3,2},{4,5},{5,4},{6,7},{7,6},{8,9},{9,8},{10,11... | collective-permute-start | bytes 1966088 | tf_op jit(solution)/shard_map/ppermute | solution.py:466
  48.8 1.5 %copy-start.5 = (f32[7,256,256]{2,1,0:T(8,128)S(1)}, f32[7,256,256]{2,1,0:T(8,128)}, u32[]{:S(2)}) copy-start(f32[7,256,256]{2,1,0:T(8,128)} %copy-done.3) | copy-start | bytes 5505028
  50.3 9.4 %copy-start.2 = (f32[256,2048]{1,0:T(8,128)S(1)}, f32[256,2048]{1,0:T(8,128)}, u32[]{:S(2)}) copy-start(f32[256,2048]{1,0:T(8,128)} %copy-done.1) | copy-start | bytes 6291460
  50.3 9.4 %copy-start.12 = (bf16[256,1280]{1,0:T(8,128)(2,1)S(1)}, bf16[256,1280]{1,0:T(8,128)(2,1)}, u32[]{:S(2)}) copy-start(bf16[256,1280]{1,0:T(8,128)(2,1)} %copy-done.11) | copy-start | bytes 1966084
  59.6 8.6 %slice-start = ((s8[7340032]{0:T(1024)(128)(4,1)}), s8[4194304]{0:T(1024)(128)(4,1)S(1)}, s32[]{:S(2)}) async-start(s8[7340032]{0:T(1024)(128)(4,1)} %bitcast.8), calls=%async_computation | async-start | bytes 8388608
  59.6 8.6 %slice-start.1 = ((s8[7340032]{0:T(1024)(128)(4,1)}), s8[3145728]{0:T(1024)(128)(4,1)S(1)}, s32[]{:S(2)}) async-start(s8[7340032]{0:T(1024)(128)(4,1)} %bitcast.8), calls=%async_computation.1 | async-start | bytes 6291456
  59.6 8.6 %copy-start.6 = (bf16[1024,1280]{1,0:T(8,128)(2,1)S(1)}, bf16[1024,1280]{1,0:T(8,128)(2,1)}, u32[]{:S(2)}) copy-start(bf16[1024,1280]{1,0:T(8,128)(2,1)} %get-tuple-element.53.w_ref) | copy-start | bytes 7864324
  59.6 8.6 %copy-start.8 = (f32[8,256,256]{2,1,0:T(8,128)S(1)}, f32[8,256,256]{2,1,0:T(8,128)}, u32[]{:S(2)}) copy-start(f32[8,256,256]{2,1,0:T(8,128)} %get-tuple-element.54.o_ref) | copy-start | bytes 6291460
  59.7 8.6 %copy-start.13 = (bf16[1792,128]{1,0:T(8,128)(2,1)S(1)}, bf16[1792,128]{1,0:T(8,128)(2,1)}, u32[]{:S(2)}) copy-start(bf16[1792,128]{1,0:T(8,128)(2,1)} %get-tuple-element.55.k_ref) | copy-start | bytes 1376260
  59.7 8.6 %copy-start.14 = (bf16[1792,128]{1,0:T(8,128)(2,1)S(1)}, bf16[1792,128]{1,0:T(8,128)(2,1)}, u32[]{:S(2)}) copy-start(bf16[1792,128]{1,0:T(8,128)(2,1)} %get-tuple-element.56.v_ref) | copy-start | bytes 1376260
  59.7 8.6 %copy-start.22 = (f32[256]{0:T(256)S(1)}, f32[256]{0:T(256)}, u32[]{:S(2)}) copy-start(f32[256]{0:T(256)} %param.10) | copy-start | bytes 3076
  68.2 6.2 %slice-start.2 = ((s8[7340032]{0:T(1024)(128)(4,1)}), s8[4194304]{0:T(1024)(128)(4,1)S(1)}, s32[]{:S(2)}) async-start(s8[7340032]{0:T(1024)(128)(4,1)} %bitcast.10), calls=%async_computation.2 | async-start | bytes 8388608
  68.3 6.1 %slice-start.3 = ((s8[7340032]{0:T(1024)(128)(4,1)}), s8[3145728]{0:T(1024)(128)(4,1)S(1)}, s32[]{:S(2)}) async-start(s8[7340032]{0:T(1024)(128)(4,1)} %bitcast.10), calls=%async_computation.3 | async-start | bytes 6291456
  68.3 6.1 %copy-start.7 = (bf16[1024,1280]{1,0:T(8,128)(2,1)S(1)}, bf16[1024,1280]{1,0:T(8,128)(2,1)}, u32[]{:S(2)}) copy-start(bf16[1024,1280]{1,0:T(8,128)(2,1)} %get-tuple-element.59.w_ref) | copy-start | bytes 7864324
  68.4 6.1 %copy-start.9 = (f32[8,256,256]{2,1,0:T(8,128)S(1)}, f32[8,256,256]{2,1,0:T(8,128)}, u32[]{:S(2)}) copy-start(f32[8,256,256]{2,1,0:T(8,128)} %get-tuple-element.60.o_ref) | copy-start | bytes 6291460
  68.4 6.1 %copy-start.15 = (bf16[1792,128]{1,0:T(8,128)(2,1)S(1)}, bf16[1792,128]{1,0:T(8,128)(2,1)}, u32[]{:S(2)}) copy-start(bf16[1792,128]{1,0:T(8,128)(2,1)} %get-tuple-element.61.k_ref) | copy-start | bytes 1376260
  68.4 6.1 %copy-start.16 = (bf16[1792,128]{1,0:T(8,128)(2,1)S(1)}, bf16[1792,128]{1,0:T(8,128)(2,1)}, u32[]{:S(2)}) copy-start(bf16[1792,128]{1,0:T(8,128)(2,1)} %get-tuple-element.62.v_ref) | copy-start | bytes 1376260
  73.3 7.0 %collective-permute-start.9 = (bf16[3,2,256,128]{3,2,1,0:T(8,128)(2,1)S(1)}, bf16[3,2,256,128]{3,2,1,0:T(8,128)(2,1)S(1)}, u32[]{:S(2)}, u32[]{:S(2)}) collective-permute-start(bf16[3,2,256,128]{3,2,1,0:T(8,128)(2,1)S(1)} %get-tuple-element.65), channel_id=1, source_target_pairs={{0,4},{4,0},{8,12},{12,8},{16,20},{20,16},{24,28},{28,24},{1,5},{5... | collective-permute-start | bytes 1179656 | tf_op jit(solution)/shard_map/ppermute | solution.py:469
  79.1 13.3 %collective-permute-start.13 = (bf16[3,2,256,128]{3,2,1,0:T(8,128)(2,1)S(1)}, bf16[3,2,256,128]{3,2,1,0:T(8,128)(2,1)S(1)}, u32[]{:S(2)}, u32[]{:S(2)}) collective-permute-start(bf16[3,2,256,128]{3,2,1,0:T(8,128)(2,1)S(1)} %get-tuple-element.71), channel_id=1, source_target_pairs={{0,4},{4,0},{8,12},{12,8},{16,20},{20,16},{24,28},{28,24},{1,5},{5... | collective-permute-start | bytes 1179656 | tf_op jit(solution)/shard_map/ppermute | solution.py:469
  80.4 15.3 %collective-permute-start.10 = (bf16[2,256,128]{2,1,0:T(8,128)(2,1)S(1)}, bf16[2,256,128]{2,1,0:T(8,128)(2,1)S(1)}, u32[]{:S(2)}, u32[]{:S(2)}) collective-permute-start(bf16[2,256,128]{2,1,0:T(8,128)(2,1)S(1)} %get-tuple-element.68), channel_id=1, source_target_pairs={{0,8},{4,12},{8,0},{12,4},{16,24},{20,28},{24,16},{28,20},{1,9},{5... | collective-permute-start | bytes 393224 | tf_op jit(solution)/shard_map/ppermute | solution.py:469
  86.2 13.1 %collective-permute-start.11 = (bf16[2,256,128]{2,1,0:T(8,128)(2,1)S(1)}, bf16[2,256,128]{2,1,0:T(8,128)(2,1)S(1)}, u32[]{:S(2)}, u32[]{:S(2)}) collective-permute-start(bf16[2,256,128]{2,1,0:T(8,128)(2,1)S(1)} %get-tuple-element.69), channel_id=1, source_target_pairs={{0,16},{4,20},{8,24},{12,28},{16,0},{20,4},{24,8},{28,12},{1,17},{... | collective-permute-start | bytes 393224 | tf_op jit(solution)/shard_map/ppermute | solution.py:469
  92.0 7.5 %collective-permute-start.12 = (bf16[2,256,128]{2,1,0:T(8,128)(2,1)S(1)}, bf16[2,256,128]{2,1,0:T(8,128)(2,1)S(1)}, u32[]{:S(2)}, u32[]{:S(2)}) collective-permute-start(bf16[2,256,128]{2,1,0:T(8,128)(2,1)S(1)} %get-tuple-element.70), channel_id=1, source_target_pairs={{0,24},{4,28},{8,16},{12,20},{16,8},{20,12},{24,0},{28,4},{1,25},{... | collective-permute-start | bytes 393224 | tf_op jit(solution)/shard_map/ppermute | solution.py:469
  92.5 8.1 %collective-permute-start.14 = (bf16[2,256,128]{2,1,0:T(8,128)(2,1)S(1)}, bf16[2,256,128]{2,1,0:T(8,128)(2,1)S(1)}, u32[]{:S(2)}, u32[]{:S(2)}) collective-permute-start(bf16[2,256,128]{2,1,0:T(8,128)(2,1)S(1)} %get-tuple-element.74), channel_id=1, source_target_pairs={{0,8},{4,12},{8,0},{12,4},{16,24},{20,28},{24,16},{28,20},{1,9},{5... | collective-permute-start | bytes 393224 | tf_op jit(solution)/shard_map/ppermute | solution.py:469
  93.7 9.5 %collective-permute-start.15 = (bf16[2,256,128]{2,1,0:T(8,128)(2,1)S(1)}, bf16[2,256,128]{2,1,0:T(8,128)(2,1)S(1)}, u32[]{:S(2)}, u32[]{:S(2)}) collective-permute-start(bf16[2,256,128]{2,1,0:T(8,128)(2,1)S(1)} %get-tuple-element.75), channel_id=1, source_target_pairs={{0,16},{4,20},{8,24},{12,28},{16,0},{20,4},{24,8},{28,12},{1,17},{... | collective-permute-start | bytes 393224 | tf_op jit(solution)/shard_map/ppermute | solution.py:469
  95.8 8.6 %collective-permute-start.16 = (bf16[2,256,128]{2,1,0:T(8,128)(2,1)S(1)}, bf16[2,256,128]{2,1,0:T(8,128)(2,1)S(1)}, u32[]{:S(2)}, u32[]{:S(2)}) collective-permute-start(bf16[2,256,128]{2,1,0:T(8,128)(2,1)S(1)} %get-tuple-element.76), channel_id=1, source_target_pairs={{0,24},{4,28},{8,16},{12,20},{16,8},{20,12},{24,0},{28,4},{1,25},{... | collective-permute-start | bytes 393224 | tf_op jit(solution)/shard_map/ppermute | solution.py:469

commit v7 on v6

--- a/solution.py
+++ b/solution.py
@@ -58,10 +58,16 @@
     )(*ins)
 
 
-def join_kernel(k_ref, v_ref, out_ref):
+def join_kernel(k_ref, v_ref, out_ref, sems):
     width = k_ref.shape[1]
-    out_ref[:, :width] = k_ref[...]
-    out_ref[:, width:] = v_ref[...]
+    copies = [
+        pltpu.make_async_copy(ref, out_ref.at[:, i * width : (i + 1) * width], sems.at[i])
+        for i, ref in enumerate((k_ref, v_ref))
+    ]
+    for copy in copies:
+        copy.start()
+    for copy in copies:
+        copy.wait()
 
 
 def stack_kernel(*refs):
@@ -459,7 +465,13 @@
     n_kb = prompt_kb + (back + 1) * per
     fast = n_ctx == 8 and n_tp == 4 and per == 1 and back == 2
     shape = (rows, 2 * groups * HD)
-    own = call(join_kernel, (key_heads, value_heads), [VMEM] * 2, [(shape, BF16)])[0]
+    own = call(
+        join_kernel,
+        [pltpu.with_memory_space_constraint(x, pltpu.HBM) for x in (key_heads, value_heads)],
+        [HBM] * 2,
+        [(shape, BF16)],
+        scratch=[pltpu.SemaphoreType.DMA((2,))],
+    )[0]
     weight = pltpu.with_memory_space_constraint(out_weight, pltpu.HBM)
 
     def hop(value, pairs):
@@ -471,7 +483,7 @@
     if fast:
         pieces = [own] + [flip(own, d) for d in (2, 4, 6)]
         near = call(stack_kernel, pieces, [VMEM] * 4, [((4,) + shape, BF16)])[0]
-        ends, middle = [(0, 1), (1, 0), (2, 3), (3, 2)], [(1, 2), (2, 1), (0, 0), (3, 3)]
+        ends, middle = [(0, 1), (1, 0), (2, 3), (3, 2)], [(1, 2), (2, 1)]
         up_a = hop(upstream, ends)
         up_c = hop(upstream, middle)
     else:

time: 106 us -> 103 us (0.972)
  local copies, waits for them, and re-layouts: 11 us -> 9.2 us
  starting transfers between devices: 41.4 us -> 39.7 us
    unnamed x58 -> x54, local copies, waits for them, and re-layouts: 11 us -> 9.2 us
    ppermute x5, starting transfers between devices: 18.2 us -> 16.5 us  [hop(): return lax.ppermute(value, 'tp', pairs)]
  transfers between devices with their start and end apart: 17 -> 17, of which waited for: 6 -> 5; matrix products, arithmetic and copies ran while one was open for 1% -> 1% of each run, Pallas kernels for 36% -> 38%
where the time goes in v7:
time: 103 us; the launch traced here: 102 us
  Pallas kernels  44.8 us (43%)
  starting transfers between devices  39.7 us (39%)
  local copies, waits for them, and re-layouts  9.2 us (9%)
  waiting for transfers between devices  6.26 us (6%)
  other arithmetic  1.15 us (1%)
    pallas_call x12, Pallas kernels, call(): pl.pallas_call(kernel, in_specs=in_specs, out_specs=out_specs or [VMEM] *...  44.8 us
    ppermute x12, starting transfers between devices, flip(): return lax.ppermute(value, 'ctx', [(i, i ^ bit) for i in range(n_ctx)])  23.2 us
    ppermute x5, starting transfers between devices, hop(): return lax.ppermute(value, 'tp', pairs)  16.5 us
    unnamed x54, local copies, waits for them, and re-layouts  9.2 us
    ppermute x12, waiting for transfers between devices, flip(): return lax.ppermute(value, 'ctx', [(i, i ^ bit) for i in range(n_ctx)])  6.25 us
  transfers between devices with their start and end apart: 17, of which 5 were waited for; matrix products, arithmetic and copies ran while one was open for 1% of the time, Pallas kernels for 38%

profile of v7, /device:TPU:0, one launch (start us, length us, event | category | flops | bytes accessed | tf_op | source)
XLA Modules:
  0.0 102.2 jit_solution(1774504299440009122)
XLA Ops:
  0.6 3.1 %collective-permute-start.3 = (bf16[256,1280]{1,0:T(8,128)(2,1)}, bf16[256,1280]{1,0:T(8,128)(2,1)S(1)}, u32[]{:S(2)}, u32[]{:S(2)}) collective-permute-start(bf16[256,1280]{1,0:T(8,128)(2,1)} %refs_0_.1), channel_id=1, source_target_pairs={{0,1},{1,0},{2,3},{3,2},{4,5},{5,4},{6,7},{7,6},{8,9},{9,8},{10,11... | collective-permute-start | bytes 1966088 | tf_op jit(solution)/shard_map/ppermute | solution.py:478
  3.7 1.5 %collective-permute-start.4 = (bf16[256,1280]{1,0:T(8,128)(2,1)}, bf16[256,1280]{1,0:T(8,128)(2,1)}, u32[]{:S(2)}, u32[]{:S(2)}) collective-permute-start(bf16[256,1280]{1,0:T(8,128)(2,1)} %refs_0_.1), channel_id=1, source_target_pairs={{1,2},{2,1},{5,6},{6,5},{9,10},{10,9},{13,14},{14,13},{17,18},{18,... | collective-permute-start | bytes 1966088 | tf_op jit(solution)/shard_map/ppermute | solution.py:478
  5.2 1.0 shard_map.113.refs_0_
  6.2 1.6 %collective-permute-start = (bf16[256,512]{1,0:T(8,128)(2,1)S(1)}, bf16[256,512]{1,0:T(8,128)(2,1)S(1)}, u32[]{:S(2)}, u32[]{:S(2)}) collective-permute-start(bf16[256,512]{1,0:T(8,128)(2,1)S(1)} %shard_map.113.refs_0_), channel_id=1, source_target_pairs={{0,8},{4,12},{8,0},{12,4},{16,24},{20,28},{24,16},{28,20},{1,9},{5... | collective-permute-start | bytes 786440 | tf_op jit(solution)/shard_map/ppermute | solution.py:481
  7.8 1.5 %collective-permute-start.1 = (bf16[256,512]{1,0:T(8,128)(2,1)S(1)}, bf16[256,512]{1,0:T(8,128)(2,1)S(1)}, u32[]{:S(2)}, u32[]{:S(2)}) collective-permute-start(bf16[256,512]{1,0:T(8,128)(2,1)S(1)} %shard_map.113.refs_0_), channel_id=1, source_target_pairs={{0,16},{4,20},{8,24},{12,28},{16,0},{20,4},{24,8},{28,12},{1,17},{... | collective-permute-start | bytes 786440 | tf_op jit(solution)/shard_map/ppermute | solution.py:481
  9.3 0.5 collective-permute-start.2
  9.8 1.1 %copy-done.10 = bf16[256,1280]{1,0:T(8,128)(2,1)S(1)} copy-done((bf16[256,1280]{1,0:T(8,128)(2,1)S(1)}, bf16[256,1280]{1,0:T(8,128)(2,1)}, u32[]{:S(2)}) %copy-start.10) | copy-done | bytes 655384
  10.9 3.9 %shard_map.115.refs_2_ = f32[256,2048]{1,0:T(8,128)S(1)} custom-call(s32[1]{0:T(128)} %bitcast.5.shard_ref, bf16[2048,5120]{1,0:T(8,128)(2,1)} %w_ref.7, bf16[256,1280]{1,0:T(8,128)(2,1)S(1)} %copy-done.10), custom_call_target="tpu_custom_call" | custom-call | tf_op jit(solution)/shard_map/pallas_call | solution.py:48
  14.8 1.3 %copy-done.1 = f32[256,2048]{1,0:T(8,128)} copy-done((f32[256,2048]{1,0:T(8,128)}, f32[256,2048]{1,0:T(8,128)S(1)}, u32[]{:S(2)}) %copy-start.1) | copy-done | bytes 2097176
  16.1 2.3 %shard_map.112 = (f32[7,256,256]{2,1,0:T(8,128)S(1)}, s32[7]{0:T(128)S(1)}) custom-call(s32[1]{0:T(128)} %bitcast.me_ref, s32[8,1,256]{2,1,0:T(1,128)S(1)} %bitcast.12, s32[2,16]{1,0:T(2,128)S(1)} %copy-done.21), custom_call_target="tpu_custom_call" | custom-call | bytes 1835008 | tf_op jit(solution)/shard_map/pallas_call | solution.py:48
  18.4 1.2 %copy-done.3 = f32[7,256,256]{2,1,0:T(8,128)} copy-done((f32[7,256,256]{2,1,0:T(8,128)}, f32[7,256,256]{2,1,0:T(8,128)S(1)}, u32[]{:S(2)}) %copy-start.3) | copy-done | bytes 1835032
  19.6 0.0 collective-permute-done.refs_1_
  19.6 1.2 %collective-permute-done.1.refs_2_ = bf16[256,512]{1,0:T(8,128)(2,1)S(1)} collective-permute-done((bf16[256,512]{1,0:T(8,128)(2,1)S(1)}, bf16[256,512]{1,0:T(8,128)(2,1)S(1)}, u32[]{:S(2)}, u32[]{:S(2)}) %collective-permute-start.1) | collective-permute-done | bytes 262176 | tf_op jit(solution)/shard_map/ppermute | solution.py:481
  20.9 0.0 collective-permute-done.2.refs_3_
  20.9 0.7 copy-done.17
  21.6 0.9 copy-done.18
  22.5 0.1 shard_map.114.near_ref
  22.6 0.0 collective-permute-done.3.refs_0_
  22.6 0.0 copy-start.11
  22.6 0.8 copy-done.11
  23.5 0.0 collective-permute-start.5
  23.5 1.5 %collective-permute-start.7 = (bf16[256,1280]{1,0:T(8,128)(2,1)}, bf16[256,1280]{1,0:T(8,128)(2,1)}, u32[]{:S(2)}, u32[]{:S(2)}) collective-permute-start(bf16[256,1280]{1,0:T(8,128)(2,1)} %copy-done.11), channel_id=1, source_target_pairs={{1,2},{2,1},{5,6},{6,5},{9,10},{10,9},{13,14},{14,13},{17,18},{18,... | collective-permute-start | bytes 1966088 | tf_op jit(solution)/shard_map/ppermute | solution.py:478
  25.0 4.0 %collective-permute-start.6 = (bf16[256,1280]{1,0:T(8,128)(2,1)}, bf16[256,1280]{1,0:T(8,128)(2,1)}, u32[]{:S(2)}, u32[]{:S(2)}) collective-permute-start(bf16[256,1280]{1,0:T(8,128)(2,1)} %collective-permute-done.4.refs_1_), channel_id=1, source_target_pairs={{0,1},{1,0},{2,3},{3,2},{4,5},{5,4},{6,7},{7,6},{8,9},{9,8},{10,11... | collective-permute-start | bytes 1966088 | tf_op jit(solution)/shard_map/ppermute | solution.py:478
  29.0 1.5 %copy-done.4 = f32[7,256,256]{2,1,0:T(8,128)S(1)} copy-done((f32[7,256,256]{2,1,0:T(8,128)S(1)}, f32[7,256,256]{2,1,0:T(8,128)}, u32[]{:S(2)}) %copy-start.4) | copy-done | bytes 1835032
  30.6 9.2 %shard_map.118 = (bf16[8,1792,256]{2,1,0:T(8,128)(2,1)}, f32[8,256,256]{2,1,0:T(8,128)}, bf16[1792,128]{1,0:T(8,128)(2,1)}, bf16[1792,128]{1,0:T(8,128)(2,1)}, bf16[1024,1280]{1,0:T(8,128)(2,1)}) custom-call(s32[7]{0:T(128)S(1)} %fusion.1.slot_ref, s32[1]{0:T(128)} %bitcast.6.shard_ref, bf16[2048,5120]{1,0:T(8,128)(2,1)} %w_ref.7, ...), custom_call_target="tpu_custom_call" | custom-call | tf_op jit(solution)/shard_map/pallas_call | solution.py:48
  39.8 6.3 %collective-permute-start.8 = (bf16[256,1280]{1,0:T(8,128)(2,1)}, bf16[256,1280]{1,0:T(8,128)(2,1)}, u32[]{:S(2)}, u32[]{:S(2)}) collective-permute-start(bf16[256,1280]{1,0:T(8,128)(2,1)} %collective-permute-done.7.x2_ref), channel_id=1, source_target_pairs={{0,1},{1,0},{2,3},{3,2},{4,5},{5,4},{6,7},{7,6},{8,9},{9,8},{10,11... | collective-permute-start | bytes 1966088 | tf_op jit(solution)/shard_map/ppermute | solution.py:478
  46.1 0.1 pad_add_fusion.shard_ref
  46.2 1.5 %copy-done.5 = f32[7,256,256]{2,1,0:T(8,128)S(1)} copy-done((f32[7,256,256]{2,1,0:T(8,128)S(1)}, f32[7,256,256]{2,1,0:T(8,128)}, u32[]{:S(2)}) %copy-start.5) | copy-done | bytes 1835032
  47.7 9.3 %shard_map.116 = (bf16[8,1792,256]{2,1,0:T(8,128)(2,1)}, f32[8,256,256]{2,1,0:T(8,128)}, bf16[1792,128]{1,0:T(8,128)(2,1)}, bf16[1792,128]{1,0:T(8,128)(2,1)}, bf16[1024,1280]{1,0:T(8,128)(2,1)}) custom-call(s32[7]{0:T(128)S(1)} %fusion.1.slot_ref, s32[1]{0:T(128)} %bitcast.6.shard_ref, bf16[2048,5120]{1,0:T(8,128)(2,1)} %w_ref.7, ...), custom_call_target="tpu_custom_call" | custom-call | tf_op jit(solution)/shard_map/pallas_call | solution.py:48
  57.1 0.0 copy-start.20
  57.1 8.5 %shard_map.117.proj_ref = f32[256,2048]{1,0:T(8,128)S(1)} custom-call(s32[3]{0:T(128)S(1)} %pad_add_fusion.shard_ref, bf16[2048,5120]{1,0:T(8,128)(2,1)} %w_ref.7, bf16[256,1280]{1,0:T(8,128)(2,1)S(1)} %copy-done.12, bf16[256,1280]{1,0:T(8,128)(2,1)} %collective-permute-done.4.refs_1_, f32[256,2048]{1,0:T(8,128)S(1)} %copy-done.2, ...), custom_call_target="tpu_custom_call" | custom-call | tf_op jit(solution)/shard_map/pallas_call | solution.py:48
  65.8 4.9 %shard_map.119 = (bf16[256,1024]{1,0:T(8,128)(2,1)S(1)}, bf16[3,2,256,128]{3,2,1,0:T(8,128)(2,1)S(1)}, bf16[4,2,256,128]{3,2,1,0:T(8,128)(2,1)S(1)}) custom-call(s32[7]{0:T(128)S(1)} %get-tuple-element.41.live_ref, s32[7]{0:T(128)S(1)} %compare_select_fusion.5.pos_ref, s32[1]{0:T(128)} %bitcast.2.edge_ref, f32[256,2048]{1,0:T(8,128)S(1)} %shard_map.117.proj_ref, ...), custom_call_target="tpu_custom_call" | custom-call | tf_op jit(solution)/shard_map/pallas_call | solution.py:48
  70.7 0.6 collective-permute-start.9
  71.4 4.6 %shard_map.120 = (bf16[256,1024]{1,0:T(8,128)(2,1)S(1)}, bf16[3,2,256,128]{3,2,1,0:T(8,128)(2,1)S(1)}, bf16[4,2,256,128]{3,2,1,0:T(8,128)(2,1)S(1)}) custom-call(s32[7]{0:T(128)S(1)} %get-tuple-element.41.live_ref, s32[7]{0:T(128)S(1)} %compare_select_fusion.5.pos_ref, s32[1]{0:T(128)} %bitcast.2.edge_ref, f32[256,2048]{1,0:T(8,128)S(1)} %shard_map.117.proj_ref, ...), custom_call_target="tpu_custom_call" | custom-call | tf_op jit(solution)/shard_map/pallas_call | solution.py:48
  76.0 1.2 %collective-permute-start.13 = (bf16[3,2,256,128]{3,2,1,0:T(8,128)(2,1)S(1)}, bf16[3,2,256,128]{3,2,1,0:T(8,128)(2,1)S(1)}, u32[]{:S(2)}, u32[]{:S(2)}) collective-permute-start(bf16[3,2,256,128]{3,2,1,0:T(8,128)(2,1)S(1)} %get-tuple-element.71), channel_id=1, source_target_pairs={{0,4},{4,0},{8,12},{12,8},{16,20},{20,16},{24,28},{28,24},{1,5},{5... | collective-permute-start | bytes 1179656 | tf_op jit(solution)/shard_map/ppermute | solution.py:481
  77.2 0.1 shard_map.121
  77.3 5.8 %collective-permute-start.10 = (bf16[2,256,128]{2,1,0:T(8,128)(2,1)S(1)}, bf16[2,256,128]{2,1,0:T(8,128)(2,1)S(1)}, u32[]{:S(2)}, u32[]{:S(2)}) collective-permute-start(bf16[2,256,128]{2,1,0:T(8,128)(2,1)S(1)} %get-tuple-element.68), channel_id=1, source_target_pairs={{0,8},{4,12},{8,0},{12,4},{16,24},{20,28},{24,16},{28,20},{1,9},{5... | collective-permute-start | bytes 393224 | tf_op jit(solution)/shard_map/ppermute | solution.py:481
  83.1 6.4 %collective-permute-start.11 = (bf16[2,256,128]{2,1,0:T(8,128)(2,1)S(1)}, bf16[2,256,128]{2,1,0:T(8,128)(2,1)S(1)}, u32[]{:S(2)}, u32[]{:S(2)}) collective-permute-start(bf16[2,256,128]{2,1,0:T(8,128)(2,1)S(1)} %get-tuple-element.69), channel_id=1, source_target_pairs={{0,16},{4,20},{8,24},{12,28},{16,0},{20,4},{24,8},{28,12},{1,17},{... | collective-permute-start | bytes 393224 | tf_op jit(solution)/shard_map/ppermute | solution.py:481
  89.5 0.1 shard_map.122
  89.6 1.5 %collective-permute-start.14 = (bf16[2,256,128]{2,1,0:T(8,128)(2,1)S(1)}, bf16[2,256,128]{2,1,0:T(8,128)(2,1)S(1)}, u32[]{:S(2)}, u32[]{:S(2)}) collective-permute-start(bf16[2,256,128]{2,1,0:T(8,128)(2,1)S(1)} %get-tuple-element.74), channel_id=1, source_target_pairs={{0,8},{4,12},{8,0},{12,4},{16,24},{20,28},{24,16},{28,20},{1,9},{5... | collective-permute-start | bytes 393224 | tf_op jit(solution)/shard_map/ppermute | solution.py:481
  91.1 2.1 %collective-permute-start.15 = (bf16[2,256,128]{2,1,0:T(8,128)(2,1)S(1)}, bf16[2,256,128]{2,1,0:T(8,128)(2,1)S(1)}, u32[]{:S(2)}, u32[]{:S(2)}) collective-permute-start(bf16[2,256,128]{2,1,0:T(8,128)(2,1)S(1)} %get-tuple-element.75), channel_id=1, source_target_pairs={{0,16},{4,20},{8,24},{12,28},{16,0},{20,4},{24,8},{28,12},{1,17},{... | collective-permute-start | bytes 393224 | tf_op jit(solution)/shard_map/ppermute | solution.py:481
  93.2 2.1 %collective-permute-start.16 = (bf16[2,256,128]{2,1,0:T(8,128)(2,1)S(1)}, bf16[2,256,128]{2,1,0:T(8,128)(2,1)S(1)}, u32[]{:S(2)}, u32[]{:S(2)}) collective-permute-start(bf16[2,256,128]{2,1,0:T(8,128)(2,1)S(1)} %get-tuple-element.76), channel_id=1, source_target_pairs={{0,24},{4,28},{8,16},{12,20},{16,8},{20,12},{24,0},{28,4},{1,25},{... | collective-permute-start | bytes 393224 | tf_op jit(solution)/shard_map/ppermute | solution.py:481
  95.3 1.1 %pad_maximum_fusion = bf16[256,2048]{1,0:T(8,128)(2,1)} fusion(bf16[256,1024]{1,0:T(8,128)(2,1)S(1)} %get-tuple-element.64, bf16[256,1024]{1,0:T(8,128)(2,1)S(1)} %get-tuple-element.58), kind=kLoop, calls=%fused_computation | loop fusion | flops 2097152 | bytes 2097152 | tf_op jit(solution)/shard_map/concatenate | solution.py:555
  96.3 0.4 collective-permute-done.11.refs_2_
  96.7 0.1 collective-permute-done.12.refs_3_
  96.8 1.3 %collective-permute-done.14.refs_5_ = bf16[2,256,128]{2,1,0:T(8,128)(2,1)S(1)} collective-permute-done((bf16[2,256,128]{2,1,0:T(8,128)(2,1)S(1)}, bf16[2,256,128]{2,1,0:T(8,128)(2,1)S(1)}, u32[]{:S(2)}, u32[]{:S(2)}) %collective-permute-start.14) | collective-permute-done | bytes 131104 | tf_op jit(solution)/shard_map/ppermute | solution.py:481
  98.1 3.2 %collective-permute-done.15.refs_6_ = bf16[2,256,128]{2,1,0:T(8,128)(2,1)S(1)} collective-permute-done((bf16[2,256,128]{2,1,0:T(8,128)(2,1)S(1)}, bf16[2,256,128]{2,1,0:T(8,128)(2,1)S(1)}, u32[]{:S(2)}, u32[]{:S(2)}) %collective-permute-start.15) | collective-permute-done | bytes 131104 | tf_op jit(solution)/shard_map/ppermute | solution.py:481
  101.3 0.8 shard_map.123
  (58 shorter events, 0.1 us)
Async XLA Ops:
  0.6 22.0 %collective-permute-start.3 = (bf16[256,1280]{1,0:T(8,128)(2,1)}, bf16[256,1280]{1,0:T(8,128)(2,1)S(1)}, u32[]{:S(2)}, u32[]{:S(2)}) collective-permute-start(bf16[256,1280]{1,0:T(8,128)(2,1)} %refs_0_.1), channel_id=1, source_target_pairs={{0,1},{1,0},{2,3},{3,2},{4,5},{5,4},{6,7},{7,6},{8,9},{9,8},{10,11... | collective-permute-start | bytes 1966088 | tf_op jit(solution)/shard_map/ppermute | solution.py:478
  3.7 18.9 %collective-permute-start.4 = (bf16[256,1280]{1,0:T(8,128)(2,1)}, bf16[256,1280]{1,0:T(8,128)(2,1)}, u32[]{:S(2)}, u32[]{:S(2)}) collective-permute-start(bf16[256,1280]{1,0:T(8,128)(2,1)} %refs_0_.1), channel_id=1, source_target_pairs={{1,2},{2,1},{5,6},{6,5},{9,10},{10,9},{13,14},{14,13},{17,18},{18,... | collective-permute-start | bytes 1966088 | tf_op jit(solution)/shard_map/ppermute | solution.py:478
  6.2 13.4 %collective-permute-start = (bf16[256,512]{1,0:T(8,128)(2,1)S(1)}, bf16[256,512]{1,0:T(8,128)(2,1)S(1)}, u32[]{:S(2)}, u32[]{:S(2)}) collective-permute-start(bf16[256,512]{1,0:T(8,128)(2,1)S(1)} %shard_map.113.refs_0_), channel_id=1, source_target_pairs={{0,8},{4,12},{8,0},{12,4},{16,24},{20,28},{24,16},{28,20},{1,9},{5... | collective-permute-start | bytes 786440 | tf_op jit(solution)/shard_map/ppermute | solution.py:481
  7.8 13.1 %collective-permute-start.1 = (bf16[256,512]{1,0:T(8,128)(2,1)S(1)}, bf16[256,512]{1,0:T(8,128)(2,1)S(1)}, u32[]{:S(2)}, u32[]{:S(2)}) collective-permute-start(bf16[256,512]{1,0:T(8,128)(2,1)S(1)} %shard_map.113.refs_0_), channel_id=1, source_target_pairs={{0,16},{4,20},{8,24},{12,28},{16,0},{20,4},{24,8},{28,12},{1,17},{... | collective-permute-start | bytes 786440 | tf_op jit(solution)/shard_map/ppermute | solution.py:481
  9.3 11.6 %collective-permute-start.2 = (bf16[256,512]{1,0:T(8,128)(2,1)S(1)}, bf16[256,512]{1,0:T(8,128)(2,1)S(1)}, u32[]{:S(2)}, u32[]{:S(2)}) collective-permute-start(bf16[256,512]{1,0:T(8,128)(2,1)S(1)} %shard_map.113.refs_0_), channel_id=1, source_target_pairs={{0,24},{4,28},{8,16},{12,20},{16,8},{20,12},{24,0},{28,4},{1,25},{... | collective-permute-start | bytes 786440 | tf_op jit(solution)/shard_map/ppermute | solution.py:481
  9.8 1.1 %copy-start.10 = (bf16[256,1280]{1,0:T(8,128)(2,1)S(1)}, bf16[256,1280]{1,0:T(8,128)(2,1)}, u32[]{:S(2)}) copy-start(bf16[256,1280]{1,0:T(8,128)(2,1)} %refs_0_.1) | copy-start | bytes 1966084
  10.9 5.2 %copy-start.19 = (s32[2048]{0:T(1024)S(1)}, s32[2048]{0:T(1024)}, u32[]{:S(2)}) copy-start(s32[2048]{0:T(1024)} %param.15) | copy-start | bytes 24580
  10.9 5.2 %copy-start.21 = (s32[2,16]{1,0:T(2,128)S(1)}, s32[2,16]{1,0:T(2,128)}, u32[]{:S(2)}) copy-start(s32[2,16]{1,0:T(2,128)} %tile_ref.1) | copy-start | bytes 388
  14.7 1.3 %copy-start.1 = (f32[256,2048]{1,0:T(8,128)}, f32[256,2048]{1,0:T(8,128)S(1)}, u32[]{:S(2)}) copy-start(f32[256,2048]{1,0:T(8,128)S(1)} %shard_map.115.refs_2_) | copy-start | bytes 6291460
  16.1 13.0 %copy-start = (bf16[256,2048]{1,0:T(8,128)(2,1)S(1)}, bf16[256,2048]{1,0:T(8,128)(2,1)}, u32[]{:S(2)}) copy-start(bf16[256,2048]{1,0:T(8,128)(2,1)} %q_ref.7) | copy-start | bytes 3145732
  18.4 1.2 %copy-start.3 = (f32[7,256,256]{2,1,0:T(8,128)}, f32[7,256,256]{2,1,0:T(8,128)S(1)}, u32[]{:S(2)}) copy-start(f32[7,256,256]{2,1,0:T(8,128)S(1)} %get-tuple-element.48.bias_ref) | copy-start | bytes 5505028
  20.9 0.7 copy-start.17
  21.6 0.9 copy-start.18
  22.6 0.8 copy-start.11
  23.5 5.6 %collective-permute-start.5 = (bf16[4,256,512]{2,1,0:T(8,128)(2,1)S(1)}, bf16[4,256,512]{2,1,0:T(8,128)(2,1)S(1)}, u32[]{:S(2)}, u32[]{:S(2)}) collective-permute-start(bf16[4,256,512]{2,1,0:T(8,128)(2,1)S(1)} %shard_map.114.near_ref), channel_id=1, source_target_pairs={{0,4},{4,0},{8,12},{12,8},{16,20},{20,16},{24,28},{28,24},{1,5},{5... | collective-permute-start | bytes 3145736 | tf_op jit(solution)/shard_map/ppermute | solution.py:481
  23.5 16.3 %collective-permute-start.7 = (bf16[256,1280]{1,0:T(8,128)(2,1)}, bf16[256,1280]{1,0:T(8,128)(2,1)}, u32[]{:S(2)}, u32[]{:S(2)}) collective-permute-start(bf16[256,1280]{1,0:T(8,128)(2,1)} %copy-done.11), channel_id=1, source_target_pairs={{1,2},{2,1},{5,6},{6,5},{9,10},{10,9},{13,14},{14,13},{17,18},{18,... | collective-permute-start | bytes 1966088 | tf_op jit(solution)/shard_map/ppermute | solution.py:478
  25.0 32.1 %collective-permute-start.6 = (bf16[256,1280]{1,0:T(8,128)(2,1)}, bf16[256,1280]{1,0:T(8,128)(2,1)}, u32[]{:S(2)}, u32[]{:S(2)}) collective-permute-start(bf16[256,1280]{1,0:T(8,128)(2,1)} %collective-permute-done.4.refs_1_), channel_id=1, source_target_pairs={{0,1},{1,0},{2,3},{3,2},{4,5},{5,4},{6,7},{7,6},{8,9},{9,8},{10,11... | collective-permute-start | bytes 1966088 | tf_op jit(solution)/shard_map/ppermute | solution.py:478
  29.0 1.5 %copy-start.4 = (f32[7,256,256]{2,1,0:T(8,128)S(1)}, f32[7,256,256]{2,1,0:T(8,128)}, u32[]{:S(2)}) copy-start(f32[7,256,256]{2,1,0:T(8,128)} %copy-done.3) | copy-start | bytes 5505028
  30.5 15.6 %copy-start.22 = (s32[7]{0:T(128)S(1)}, s32[7]{0:T(128)}, u32[]{:S(2)}) copy-start(s32[7]{0:T(128)} %constant.98.clone) | copy-start | bytes 88
  39.8 25.9 %collective-permute-start.8 = (bf16[256,1280]{1,0:T(8,128)(2,1)}, bf16[256,1280]{1,0:T(8,128)(2,1)}, u32[]{:S(2)}, u32[]{:S(2)}) collective-permute-start(bf16[256,1280]{1,0:T(8,128)(2,1)} %collective-permute-done.7.x2_ref), channel_id=1, source_target_pairs={{0,1},{1,0},{2,3},{3,2},{4,5},{5,4},{6,7},{7,6},{8,9},{9,8},{10,11... | collective-permute-start | bytes 1966088 | tf_op jit(solution)/shard_map/ppermute | solution.py:478
  46.2 1.5 %copy-start.5 = (f32[7,256,256]{2,1,0:T(8,128)S(1)}, f32[7,256,256]{2,1,0:T(8,128)}, u32[]{:S(2)}) copy-start(f32[7,256,256]{2,1,0:T(8,128)} %copy-done.3) | copy-start | bytes 5505028
  47.7 9.4 %copy-start.2 = (f32[256,2048]{1,0:T(8,128)S(1)}, f32[256,2048]{1,0:T(8,128)}, u32[]{:S(2)}) copy-start(f32[256,2048]{1,0:T(8,128)} %copy-done.1) | copy-start | bytes 6291460
  47.7 9.4 %copy-start.12 = (bf16[256,1280]{1,0:T(8,128)(2,1)S(1)}, bf16[256,1280]{1,0:T(8,128)(2,1)}, u32[]{:S(2)}) copy-start(bf16[256,1280]{1,0:T(8,128)(2,1)} %copy-done.11) | copy-start | bytes 1966084
  57.0 8.6 %slice-start = ((s8[7340032]{0:T(1024)(128)(4,1)}), s8[4194304]{0:T(1024)(128)(4,1)S(1)}, s32[]{:S(2)}) async-start(s8[7340032]{0:T(1024)(128)(4,1)} %bitcast.8), calls=%async_computation | async-start | bytes 8388608
  57.0 8.6 %slice-start.1 = ((s8[7340032]{0:T(1024)(128)(4,1)}), s8[3145728]{0:T(1024)(128)(4,1)S(1)}, s32[]{:S(2)}) async-start(s8[7340032]{0:T(1024)(128)(4,1)} %bitcast.8), calls=%async_computation.1 | async-start | bytes 6291456
  57.0 8.6 %copy-start.6 = (bf16[1024,1280]{1,0:T(8,128)(2,1)S(1)}, bf16[1024,1280]{1,0:T(8,128)(2,1)}, u32[]{:S(2)}) copy-start(bf16[1024,1280]{1,0:T(8,128)(2,1)} %get-tuple-element.53.w_ref) | copy-start | bytes 7864324
  57.0 8.6 %copy-start.8 = (f32[8,256,256]{2,1,0:T(8,128)S(1)}, f32[8,256,256]{2,1,0:T(8,128)}, u32[]{:S(2)}) copy-start(f32[8,256,256]{2,1,0:T(8,128)} %get-tuple-element.54.o_ref) | copy-start | bytes 6291460
  57.1 8.6 %copy-start.13 = (bf16[1792,128]{1,0:T(8,128)(2,1)S(1)}, bf16[1792,128]{1,0:T(8,128)(2,1)}, u32[]{:S(2)}) copy-start(bf16[1792,128]{1,0:T(8,128)(2,1)} %get-tuple-element.55.k_ref) | copy-start | bytes 1376260
  57.1 8.6 %copy-start.14 = (bf16[1792,128]{1,0:T(8,128)(2,1)S(1)}, bf16[1792,128]{1,0:T(8,128)(2,1)}, u32[]{:S(2)}) copy-start(bf16[1792,128]{1,0:T(8,128)(2,1)} %get-tuple-element.56.v_ref) | copy-start | bytes 1376260
  57.1 8.6 %copy-start.20 = (f32[256]{0:T(256)S(1)}, f32[256]{0:T(256)}, u32[]{:S(2)}) copy-start(f32[256]{0:T(256)} %param.10) | copy-start | bytes 3076
  65.7 5.7 %slice-start.2 = ((s8[7340032]{0:T(1024)(128)(4,1)}), s8[4194304]{0:T(1024)(128)(4,1)S(1)}, s32[]{:S(2)}) async-start(s8[7340032]{0:T(1024)(128)(4,1)} %bitcast.10), calls=%async_computation.2 | async-start | bytes 8388608
  65.7 5.6 %slice-start.3 = ((s8[7340032]{0:T(1024)(128)(4,1)}), s8[3145728]{0:T(1024)(128)(4,1)S(1)}, s32[]{:S(2)}) async-start(s8[7340032]{0:T(1024)(128)(4,1)} %bitcast.10), calls=%async_computation.3 | async-start | bytes 6291456
  65.8 5.6 %copy-start.7 = (bf16[1024,1280]{1,0:T(8,128)(2,1)S(1)}, bf16[1024,1280]{1,0:T(8,128)(2,1)}, u32[]{:S(2)}) copy-start(bf16[1024,1280]{1,0:T(8,128)(2,1)} %get-tuple-element.59.w_ref) | copy-start | bytes 7864324
  65.8 5.6 %copy-start.9 = (f32[8,256,256]{2,1,0:T(8,128)S(1)}, f32[8,256,256]{2,1,0:T(8,128)}, u32[]{:S(2)}) copy-start(f32[8,256,256]{2,1,0:T(8,128)} %get-tuple-element.60.o_ref) | copy-start | bytes 6291460
  65.8 5.6 %copy-start.15 = (bf16[1792,128]{1,0:T(8,128)(2,1)S(1)}, bf16[1792,128]{1,0:T(8,128)(2,1)}, u32[]{:S(2)}) copy-start(bf16[1792,128]{1,0:T(8,128)(2,1)} %get-tuple-element.61.k_ref) | copy-start | bytes 1376260
  65.8 5.6 %copy-start.16 = (bf16[1792,128]{1,0:T(8,128)(2,1)S(1)}, bf16[1792,128]{1,0:T(8,128)(2,1)}, u32[]{:S(2)}) copy-start(bf16[1792,128]{1,0:T(8,128)(2,1)} %get-tuple-element.62.v_ref) | copy-start | bytes 1376260
  70.7 6.5 %collective-permute-start.9 = (bf16[3,2,256,128]{3,2,1,0:T(8,128)(2,1)S(1)}, bf16[3,2,256,128]{3,2,1,0:T(8,128)(2,1)S(1)}, u32[]{:S(2)}, u32[]{:S(2)}) collective-permute-start(bf16[3,2,256,128]{3,2,1,0:T(8,128)(2,1)S(1)} %get-tuple-element.65), channel_id=1, source_target_pairs={{0,4},{4,0},{8,12},{12,8},{16,20},{20,16},{24,28},{28,24},{1,5},{5... | collective-permute-start | bytes 1179656 | tf_op jit(solution)/shard_map/ppermute | solution.py:481
  76.0 13.5 %collective-permute-start.13 = (bf16[3,2,256,128]{3,2,1,0:T(8,128)(2,1)S(1)}, bf16[3,2,256,128]{3,2,1,0:T(8,128)(2,1)S(1)}, u32[]{:S(2)}, u32[]{:S(2)}) collective-permute-start(bf16[3,2,256,128]{3,2,1,0:T(8,128)(2,1)S(1)} %get-tuple-element.71), channel_id=1, source_target_pairs={{0,4},{4,0},{8,12},{12,8},{16,20},{20,16},{24,28},{28,24},{1,5},{5... | collective-permute-start | bytes 1179656 | tf_op jit(solution)/shard_map/ppermute | solution.py:481
  77.3 15.8 %collective-permute-start.10 = (bf16[2,256,128]{2,1,0:T(8,128)(2,1)S(1)}, bf16[2,256,128]{2,1,0:T(8,128)(2,1)S(1)}, u32[]{:S(2)}, u32[]{:S(2)}) collective-permute-start(bf16[2,256,128]{2,1,0:T(8,128)(2,1)S(1)} %get-tuple-element.68), channel_id=1, source_target_pairs={{0,8},{4,12},{8,0},{12,4},{16,24},{20,28},{24,16},{28,20},{1,9},{5... | collective-permute-start | bytes 393224 | tf_op jit(solution)/shard_map/ppermute | solution.py:481
  83.1 13.7 %collective-permute-start.11 = (bf16[2,256,128]{2,1,0:T(8,128)(2,1)S(1)}, bf16[2,256,128]{2,1,0:T(8,128)(2,1)S(1)}, u32[]{:S(2)}, u32[]{:S(2)}) collective-permute-start(bf16[2,256,128]{2,1,0:T(8,128)(2,1)S(1)} %get-tuple-element.69), channel_id=1, source_target_pairs={{0,16},{4,20},{8,24},{12,28},{16,0},{20,4},{24,8},{28,12},{1,17},{... | collective-permute-start | bytes 393224 | tf_op jit(solution)/shard_map/ppermute | solution.py:481
  89.5 7.4 %collective-permute-start.12 = (bf16[2,256,128]{2,1,0:T(8,128)(2,1)S(1)}, bf16[2,256,128]{2,1,0:T(8,128)(2,1)S(1)}, u32[]{:S(2)}, u32[]{:S(2)}) collective-permute-start(bf16[2,256,128]{2,1,0:T(8,128)(2,1)S(1)} %get-tuple-element.70), channel_id=1, source_target_pairs={{0,24},{4,28},{8,16},{12,20},{16,8},{20,12},{24,0},{28,4},{1,25},{... | collective-permute-start | bytes 393224 | tf_op jit(solution)/shard_map/ppermute | solution.py:481
  89.6 8.5 %collective-permute-start.14 = (bf16[2,256,128]{2,1,0:T(8,128)(2,1)S(1)}, bf16[2,256,128]{2,1,0:T(8,128)(2,1)S(1)}, u32[]{:S(2)}, u32[]{:S(2)}) collective-permute-start(bf16[2,256,128]{2,1,0:T(8,128)(2,1)S(1)} %get-tuple-element.74), channel_id=1, source_target_pairs={{0,8},{4,12},{8,0},{12,4},{16,24},{20,28},{24,16},{28,20},{1,9},{5... | collective-permute-start | bytes 393224 | tf_op jit(solution)/shard_map/ppermute | solution.py:481
  91.1 10.2 %collective-permute-start.15 = (bf16[2,256,128]{2,1,0:T(8,128)(2,1)S(1)}, bf16[2,256,128]{2,1,0:T(8,128)(2,1)S(1)}, u32[]{:S(2)}, u32[]{:S(2)}) collective-permute-start(bf16[2,256,128]{2,1,0:T(8,128)(2,1)S(1)} %get-tuple-element.75), channel_id=1, source_target_pairs={{0,16},{4,20},{8,24},{12,28},{16,0},{20,4},{24,8},{28,12},{1,17},{... | collective-permute-start | bytes 393224 | tf_op jit(solution)/shard_map/ppermute | solution.py:481
  93.2 8.1 %collective-permute-start.16 = (bf16[2,256,128]{2,1,0:T(8,128)(2,1)S(1)}, bf16[2,256,128]{2,1,0:T(8,128)(2,1)S(1)}, u32[]{:S(2)}, u32[]{:S(2)}) collective-permute-start(bf16[2,256,128]{2,1,0:T(8,128)(2,1)S(1)} %get-tuple-element.76), channel_id=1, source_target_pairs={{0,24},{4,28},{8,16},{12,20},{16,8},{20,12},{24,0},{28,4},{1,25},{... | collective-permute-start | bytes 393224 | tf_op jit(solution)/shard_map/ppermute | solution.py:481

commit v8 on v7

--- a/solution.py
+++ b/solution.py
@@ -483,7 +483,7 @@
     if fast:
         pieces = [own] + [flip(own, d) for d in (2, 4, 6)]
         near = call(stack_kernel, pieces, [VMEM] * 4, [((4,) + shape, BF16)])[0]
-        ends, middle = [(0, 1), (1, 0), (2, 3), (3, 2)], [(1, 2), (2, 1)]
+        ends, middle, out = [(0, 1), (1, 0), (2, 3), (3, 2)], [(1, 2), (2, 1)], [(1, 0), (2, 3)]
         up_a = hop(upstream, ends)
         up_c = hop(upstream, middle)
     else:
@@ -528,13 +528,13 @@
     if fast:
         up_a, up_c, bias, acc = lax.optimization_barrier((up_a, up_c, bias, acc))
         up_e = hop(up_a, middle)
-        up_f = hop(up_c, ends)
+        up_f = hop(up_c, out)
         near, up_a = lax.optimization_barrier((near, up_a))
         far = flip(near, 1)
     soft = [list(probs_call(0, groups, slots, shard[None], weight, depth, query_heads, near, far, bias, n_kb))]
     if fast:
         up_e, soft[0][2] = lax.optimization_barrier((up_e, soft[0][2]))
-        up_d = hop(up_e, ends)
+        up_d = hop(up_e, out)
         x1, x2 = up_d, up_e
     soft += [
         list(probs_call(g, groups, slots, shard[None], weight, depth, query_heads, near, far, bias, n_kb))

time: 103 us -> 102 us (level)
  the two profiles are of different devices: /device:TPU:0 before, /device:TPU:10 now
where the time goes in v8:
time: 102 us; the launch traced here: 101 us
  Pallas kernels  49.3 us (48%)
  starting transfers between devices  29.5 us (29%)
  waiting for transfers between devices  11.1 us (11%)
  local copies, waits for them, and re-layouts  9.2 us (9%)
  other arithmetic  1.15 us (1%)
  between operations  1.05 us (1%)
    pallas_call x12, Pallas kernels, call(): pl.pallas_call(kernel, in_specs=in_specs, out_specs=out_specs or [VMEM] *...  49.3 us
    ppermute x12, starting transfers between devices, flip(): return lax.ppermute(value, 'ctx', [(i, i ^ bit) for i in range(n_ctx)])  17.9 us
    ppermute x5, starting transfers between devices, hop(): return lax.ppermute(value, 'tp', pairs)  11.6 us
    unnamed x54, local copies, waits for them, and re-layouts  9.2 us
    ppermute x12, waiting for transfers between devices, flip(): return lax.ppermute(value, 'ctx', [(i, i ^ bit) for i in range(n_ctx)])  6.85 us
    ppermute x5, waiting for transfers between devices, hop(): return lax.ppermute(value, 'tp', pairs)  4.24 us
  transfers between devices with their start and end apart: 17, of which 7 were waited for; matrix products, arithmetic and copies ran while one was open for 1% of the time, Pallas kernels for 41%

profile of v8, /device:TPU:10, one launch (start us, length us, event | category | flops | bytes accessed | tf_op | source)
XLA Modules:
  0.0 101.3 jit_solution(3141460053931532109)
XLA Ops:
  0.6 0.5 collective-permute-start.3
  1.1 4.6 %collective-permute-start.4 = (bf16[256,1280]{1,0:T(8,128)(2,1)}, bf16[256,1280]{1,0:T(8,128)(2,1)}, u32[]{:S(2)}, u32[]{:S(2)}) collective-permute-start(bf16[256,1280]{1,0:T(8,128)(2,1)} %refs_0_.1), channel_id=1, source_target_pairs={{1,2},{2,1},{5,6},{6,5},{9,10},{10,9},{13,14},{14,13},{17,18},{18,... | collective-permute-start | bytes 1966088 | tf_op jit(solution)/shard_map/ppermute | solution.py:478
  5.8 1.0 shard_map.113.refs_0_
  6.7 0.6 collective-permute-start
  7.3 1.5 %collective-permute-start.1 = (bf16[256,512]{1,0:T(8,128)(2,1)S(1)}, bf16[256,512]{1,0:T(8,128)(2,1)S(1)}, u32[]{:S(2)}, u32[]{:S(2)}) collective-permute-start(bf16[256,512]{1,0:T(8,128)(2,1)S(1)} %shard_map.113.refs_0_), channel_id=1, source_target_pairs={{0,16},{4,20},{8,24},{12,28},{16,0},{20,4},{24,8},{28,12},{1,17},{... | collective-permute-start | bytes 786440 | tf_op jit(solution)/shard_map/ppermute | solution.py:481
  8.9 1.4 %collective-permute-start.2 = (bf16[256,512]{1,0:T(8,128)(2,1)S(1)}, bf16[256,512]{1,0:T(8,128)(2,1)S(1)}, u32[]{:S(2)}, u32[]{:S(2)}) collective-permute-start(bf16[256,512]{1,0:T(8,128)(2,1)S(1)} %shard_map.113.refs_0_), channel_id=1, source_target_pairs={{0,24},{4,28},{8,16},{12,20},{16,8},{20,12},{24,0},{28,4},{1,25},{... | collective-permute-start | bytes 786440 | tf_op jit(solution)/shard_map/ppermute | solution.py:481
  10.3 1.1 %copy-done.10 = bf16[256,1280]{1,0:T(8,128)(2,1)S(1)} copy-done((bf16[256,1280]{1,0:T(8,128)(2,1)S(1)}, bf16[256,1280]{1,0:T(8,128)(2,1)}, u32[]{:S(2)}) %copy-start.10) | copy-done | bytes 655384
  11.4 3.9 %shard_map.115.refs_2_ = f32[256,2048]{1,0:T(8,128)S(1)} custom-call(s32[1]{0:T(128)} %bitcast.5.shard_ref, bf16[2048,5120]{1,0:T(8,128)(2,1)} %w_ref.7, bf16[256,1280]{1,0:T(8,128)(2,1)S(1)} %copy-done.10), custom_call_target="tpu_custom_call" | custom-call | tf_op jit(solution)/shard_map/pallas_call | solution.py:48
  15.3 1.3 %copy-done.1 = f32[256,2048]{1,0:T(8,128)} copy-done((f32[256,2048]{1,0:T(8,128)}, f32[256,2048]{1,0:T(8,128)S(1)}, u32[]{:S(2)}) %copy-start.1) | copy-done | bytes 2097176
  16.6 2.3 %shard_map.112 = (f32[7,256,256]{2,1,0:T(8,128)S(1)}, s32[7]{0:T(128)S(1)}) custom-call(s32[1]{0:T(128)} %bitcast.me_ref, s32[8,1,256]{2,1,0:T(1,128)S(1)} %bitcast.12, s32[2,16]{1,0:T(2,128)S(1)} %copy-done.21), custom_call_target="tpu_custom_call" | custom-call | bytes 1835008 | tf_op jit(solution)/shard_map/pallas_call | solution.py:48
  18.9 1.2 %copy-done.3 = f32[7,256,256]{2,1,0:T(8,128)} copy-done((f32[7,256,256]{2,1,0:T(8,128)}, f32[7,256,256]{2,1,0:T(8,128)S(1)}, u32[]{:S(2)}) %copy-start.3) | copy-done | bytes 1835032
  20.2 0.7 collective-permute-done.2.refs_3_
  20.9 0.7 copy-done.17
  21.6 0.9 copy-done.18
  22.5 0.1 shard_map.114.near_ref
  22.6 0.0 collective-permute-done.3.refs_0_
  22.6 0.0 copy-start.11
  22.6 0.8 copy-done.11
  23.5 2.2 %collective-permute-start.7 = (bf16[256,1280]{1,0:T(8,128)(2,1)}, bf16[256,1280]{1,0:T(8,128)(2,1)}, u32[]{:S(2)}, u32[]{:S(2)}) collective-permute-start(bf16[256,1280]{1,0:T(8,128)(2,1)} %copy-done.11), channel_id=1, source_target_pairs={{1,2},{2,1},{5,6},{6,5},{9,10},{10,9},{13,14},{14,13},{17,18},{18,... | collective-permute-start | bytes 1966088 | tf_op jit(solution)/shard_map/ppermute | solution.py:478
  25.7 2.2 %collective-permute-start.6 = (bf16[256,1280]{1,0:T(8,128)(2,1)}, bf16[256,1280]{1,0:T(8,128)(2,1)}, u32[]{:S(2)}, u32[]{:S(2)}) collective-permute-start(bf16[256,1280]{1,0:T(8,128)(2,1)} %collective-permute-done.4.refs_1_), channel_id=1, source_target_pairs={{1,0},{2,3},{5,4},{6,7},{9,8},{10,11},{13,12},{14,15},{17,16},{18,... | collective-permute-start | bytes 1966088 | tf_op jit(solution)/shard_map/ppermute | solution.py:478
  27.9 1.5 %copy-done.4 = f32[7,256,256]{2,1,0:T(8,128)S(1)} copy-done((f32[7,256,256]{2,1,0:T(8,128)S(1)}, f32[7,256,256]{2,1,0:T(8,128)}, u32[]{:S(2)}) %copy-start.4) | copy-done | bytes 1835032
  29.4 9.2 %shard_map.118 = (bf16[8,1792,256]{2,1,0:T(8,128)(2,1)}, f32[8,256,256]{2,1,0:T(8,128)}, bf16[1792,128]{1,0:T(8,128)(2,1)}, bf16[1792,128]{1,0:T(8,128)(2,1)}, bf16[1024,1280]{1,0:T(8,128)(2,1)}) custom-call(s32[7]{0:T(128)S(1)} %fusion.1.slot_ref, s32[1]{0:T(128)} %bitcast.6.shard_ref, bf16[2048,5120]{1,0:T(8,128)(2,1)} %w_ref.7, ...), custom_call_target="tpu_custom_call" | custom-call | tf_op jit(solution)/shard_map/pallas_call | solution.py:48
  38.6 4.2 %collective-permute-done.7.x2_ref = bf16[256,1280]{1,0:T(8,128)(2,1)} collective-permute-done((bf16[256,1280]{1,0:T(8,128)(2,1)}, bf16[256,1280]{1,0:T(8,128)(2,1)}, u32[]{:S(2)}, u32[]{:S(2)}) %collective-permute-start.7) | collective-permute-done | bytes 655392 | tf_op jit(solution)/shard_map/ppermute | solution.py:478
  42.8 2.2 %collective-permute-start.8 = (bf16[256,1280]{1,0:T(8,128)(2,1)}, bf16[256,1280]{1,0:T(8,128)(2,1)}, u32[]{:S(2)}, u32[]{:S(2)}) collective-permute-start(bf16[256,1280]{1,0:T(8,128)(2,1)} %collective-permute-done.7.x2_ref), channel_id=1, source_target_pairs={{1,0},{2,3},{5,4},{6,7},{9,8},{10,11},{13,12},{14,15},{17,16},{18,... | collective-permute-start | bytes 1966088 | tf_op jit(solution)/shard_map/ppermute | solution.py:478
  45.0 0.1 pad_add_fusion.shard_ref
  45.0 1.5 %copy-done.5 = f32[7,256,256]{2,1,0:T(8,128)S(1)} copy-done((f32[7,256,256]{2,1,0:T(8,128)S(1)}, f32[7,256,256]{2,1,0:T(8,128)}, u32[]{:S(2)}) %copy-start.5) | copy-done | bytes 1835032
  46.5 9.3 %shard_map.116 = (bf16[8,1792,256]{2,1,0:T(8,128)(2,1)}, f32[8,256,256]{2,1,0:T(8,128)}, bf16[1792,128]{1,0:T(8,128)(2,1)}, bf16[1792,128]{1,0:T(8,128)(2,1)}, bf16[1024,1280]{1,0:T(8,128)(2,1)}) custom-call(s32[7]{0:T(128)S(1)} %fusion.1.slot_ref, s32[1]{0:T(128)} %bitcast.6.shard_ref, bf16[2048,5120]{1,0:T(8,128)(2,1)} %w_ref.7, ...), custom_call_target="tpu_custom_call" | custom-call | tf_op jit(solution)/shard_map/pallas_call | solution.py:48
  56.0 0.0 copy-start.20
  56.0 8.5 %shard_map.117.proj_ref = f32[256,2048]{1,0:T(8,128)S(1)} custom-call(s32[3]{0:T(128)S(1)} %pad_add_fusion.shard_ref, bf16[2048,5120]{1,0:T(8,128)(2,1)} %w_ref.7, bf16[256,1280]{1,0:T(8,128)(2,1)S(1)} %copy-done.12, bf16[256,1280]{1,0:T(8,128)(2,1)} %collective-permute-done.4.refs_1_, f32[256,2048]{1,0:T(8,128)S(1)} %copy-done.2, ...), custom_call_target="tpu_custom_call" | custom-call | tf_op jit(solution)/shard_map/pallas_call | solution.py:48
  64.7 7.2 %shard_map.119 = (bf16[256,1024]{1,0:T(8,128)(2,1)S(1)}, bf16[3,2,256,128]{3,2,1,0:T(8,128)(2,1)S(1)}, bf16[4,2,256,128]{3,2,1,0:T(8,128)(2,1)S(1)}) custom-call(s32[7]{0:T(128)S(1)} %get-tuple-element.41.live_ref, s32[7]{0:T(128)S(1)} %compare_select_fusion.5.pos_ref, s32[1]{0:T(128)} %bitcast.2.edge_ref, f32[256,2048]{1,0:T(8,128)S(1)} %shard_map.117.proj_ref, ...), custom_call_target="tpu_custom_call" | custom-call | tf_op jit(solution)/shard_map/pallas_call | solution.py:48
  71.9 0.9 collective-permute-start.9
  72.8 6.8 %shard_map.120 = (bf16[256,1024]{1,0:T(8,128)(2,1)S(1)}, bf16[3,2,256,128]{3,2,1,0:T(8,128)(2,1)S(1)}, bf16[4,2,256,128]{3,2,1,0:T(8,128)(2,1)S(1)}) custom-call(s32[7]{0:T(128)S(1)} %get-tuple-element.41.live_ref, s32[7]{0:T(128)S(1)} %compare_select_fusion.5.pos_ref, s32[1]{0:T(128)} %bitcast.2.edge_ref, f32[256,2048]{1,0:T(8,128)S(1)} %shard_map.117.proj_ref, ...), custom_call_target="tpu_custom_call" | custom-call | tf_op jit(solution)/shard_map/pallas_call | solution.py:48
  79.6 1.2 %collective-permute-start.13 = (bf16[3,2,256,128]{3,2,1,0:T(8,128)(2,1)S(1)}, bf16[3,2,256,128]{3,2,1,0:T(8,128)(2,1)S(1)}, u32[]{:S(2)}, u32[]{:S(2)}) collective-permute-start(bf16[3,2,256,128]{3,2,1,0:T(8,128)(2,1)S(1)} %get-tuple-element.71), channel_id=1, source_target_pairs={{0,4},{4,0},{8,12},{12,8},{16,20},{20,16},{24,28},{28,24},{1,5},{5... | collective-permute-start | bytes 1179656 | tf_op jit(solution)/shard_map/ppermute | solution.py:481
  80.8 0.1 shard_map.121
  80.9 0.1 collective-permute-start.10
  81.0 6.8 %collective-permute-start.11 = (bf16[2,256,128]{2,1,0:T(8,128)(2,1)S(1)}, bf16[2,256,128]{2,1,0:T(8,128)(2,1)S(1)}, u32[]{:S(2)}, u32[]{:S(2)}) collective-permute-start(bf16[2,256,128]{2,1,0:T(8,128)(2,1)S(1)} %get-tuple-element.69), channel_id=1, source_target_pairs={{0,16},{4,20},{8,24},{12,28},{16,0},{20,4},{24,8},{28,12},{1,17},{... | collective-permute-start | bytes 393224 | tf_op jit(solution)/shard_map/ppermute | solution.py:481
  87.8 0.7 collective-permute-start.12
  88.6 0.1 shard_map.122
  88.7 0.8 collective-permute-start.14
  89.5 2.1 %collective-permute-start.15 = (bf16[2,256,128]{2,1,0:T(8,128)(2,1)S(1)}, bf16[2,256,128]{2,1,0:T(8,128)(2,1)S(1)}, u32[]{:S(2)}, u32[]{:S(2)}) collective-permute-start(bf16[2,256,128]{2,1,0:T(8,128)(2,1)S(1)} %get-tuple-element.75), channel_id=1, source_target_pairs={{0,16},{4,20},{8,24},{12,28},{16,0},{20,4},{24,8},{28,12},{1,17},{... | collective-permute-start | bytes 393224 | tf_op jit(solution)/shard_map/ppermute | solution.py:481
  91.5 1.7 %collective-permute-start.16 = (bf16[2,256,128]{2,1,0:T(8,128)(2,1)S(1)}, bf16[2,256,128]{2,1,0:T(8,128)(2,1)S(1)}, u32[]{:S(2)}, u32[]{:S(2)}) collective-permute-start(bf16[2,256,128]{2,1,0:T(8,128)(2,1)S(1)} %get-tuple-element.76), channel_id=1, source_target_pairs={{0,24},{4,28},{8,16},{12,20},{16,8},{20,12},{24,0},{28,4},{1,25},{... | collective-permute-start | bytes 393224 | tf_op jit(solution)/shard_map/ppermute | solution.py:481
  93.3 1.1 %pad_maximum_fusion = bf16[256,2048]{1,0:T(8,128)(2,1)} fusion(bf16[256,1024]{1,0:T(8,128)(2,1)S(1)} %get-tuple-element.64, bf16[256,1024]{1,0:T(8,128)(2,1)S(1)} %get-tuple-element.58), kind=kLoop, calls=%fused_computation | loop fusion | flops 2097152 | bytes 2097152 | tf_op jit(solution)/shard_map/concatenate | solution.py:555
  94.3 0.8 collective-permute-done.11.refs_2_
  95.1 0.6 collective-permute-done.12.refs_3_
  95.8 0.7 collective-permute-done.14.refs_5_
  96.5 2.4 %collective-permute-done.15.refs_6_ = bf16[2,256,128]{2,1,0:T(8,128)(2,1)S(1)} collective-permute-done((bf16[2,256,128]{2,1,0:T(8,128)(2,1)S(1)}, bf16[2,256,128]{2,1,0:T(8,128)(2,1)S(1)}, u32[]{:S(2)}, u32[]{:S(2)}) %collective-permute-start.15) | collective-permute-done | bytes 131104 | tf_op jit(solution)/shard_map/ppermute | solution.py:481
  98.9 1.5 %collective-permute-done.16.refs_7_ = bf16[2,256,128]{2,1,0:T(8,128)(2,1)S(1)} collective-permute-done((bf16[2,256,128]{2,1,0:T(8,128)(2,1)S(1)}, bf16[2,256,128]{2,1,0:T(8,128)(2,1)S(1)}, u32[]{:S(2)}, u32[]{:S(2)}) %collective-permute-start.16) | collective-permute-done | bytes 131104 | tf_op jit(solution)/shard_map/ppermute | solution.py:481
  100.5 0.8 shard_map.123
  (58 shorter events, 0.1 us)
Async XLA Ops:
  0.6 22.0 %collective-permute-start.3 = (bf16[256,1280]{1,0:T(8,128)(2,1)}, bf16[256,1280]{1,0:T(8,128)(2,1)S(1)}, u32[]{:S(2)}, u32[]{:S(2)}) collective-permute-start(bf16[256,1280]{1,0:T(8,128)(2,1)} %refs_0_.1), channel_id=1, source_target_pairs={{0,1},{1,0},{2,3},{3,2},{4,5},{5,4},{6,7},{7,6},{8,9},{9,8},{10,11... | collective-permute-start | bytes 1966088 | tf_op jit(solution)/shard_map/ppermute | solution.py:478
  1.1 21.5 %collective-permute-start.4 = (bf16[256,1280]{1,0:T(8,128)(2,1)}, bf16[256,1280]{1,0:T(8,128)(2,1)}, u32[]{:S(2)}, u32[]{:S(2)}) collective-permute-start(bf16[256,1280]{1,0:T(8,128)(2,1)} %refs_0_.1), channel_id=1, source_target_pairs={{1,2},{2,1},{5,6},{6,5},{9,10},{10,9},{13,14},{14,13},{17,18},{18,... | collective-permute-start | bytes 1966088 | tf_op jit(solution)/shard_map/ppermute | solution.py:478
  6.7 13.4 %collective-permute-start = (bf16[256,512]{1,0:T(8,128)(2,1)S(1)}, bf16[256,512]{1,0:T(8,128)(2,1)S(1)}, u32[]{:S(2)}, u32[]{:S(2)}) collective-permute-start(bf16[256,512]{1,0:T(8,128)(2,1)S(1)} %shard_map.113.refs_0_), channel_id=1, source_target_pairs={{0,8},{4,12},{8,0},{12,4},{16,24},{20,28},{24,16},{28,20},{1,9},{5... | collective-permute-start | bytes 786440 | tf_op jit(solution)/shard_map/ppermute | solution.py:481
  7.3 12.8 %collective-permute-start.1 = (bf16[256,512]{1,0:T(8,128)(2,1)S(1)}, bf16[256,512]{1,0:T(8,128)(2,1)S(1)}, u32[]{:S(2)}, u32[]{:S(2)}) collective-permute-start(bf16[256,512]{1,0:T(8,128)(2,1)S(1)} %shard_map.113.refs_0_), channel_id=1, source_target_pairs={{0,16},{4,20},{8,24},{12,28},{16,0},{20,4},{24,8},{28,12},{1,17},{... | collective-permute-start | bytes 786440 | tf_op jit(solution)/shard_map/ppermute | solution.py:481
  8.9 12.0 %collective-permute-start.2 = (bf16[256,512]{1,0:T(8,128)(2,1)S(1)}, bf16[256,512]{1,0:T(8,128)(2,1)S(1)}, u32[]{:S(2)}, u32[]{:S(2)}) collective-permute-start(bf16[256,512]{1,0:T(8,128)(2,1)S(1)} %shard_map.113.refs_0_), channel_id=1, source_target_pairs={{0,24},{4,28},{8,16},{12,20},{16,8},{20,12},{24,0},{28,4},{1,25},{... | collective-permute-start | bytes 786440 | tf_op jit(solution)/shard_map/ppermute | solution.py:481
  10.3 1.1 %copy-start.10 = (bf16[256,1280]{1,0:T(8,128)(2,1)S(1)}, bf16[256,1280]{1,0:T(8,128)(2,1)}, u32[]{:S(2)}) copy-start(bf16[256,1280]{1,0:T(8,128)(2,1)} %refs_0_.1) | copy-start | bytes 1966084
  11.4 5.2 %copy-start.19 = (s32[2048]{0:T(1024)S(1)}, s32[2048]{0:T(1024)}, u32[]{:S(2)}) copy-start(s32[2048]{0:T(1024)} %param.15) | copy-start | bytes 24580
  11.4 5.2 %copy-start.21 = (s32[2,16]{1,0:T(2,128)S(1)}, s32[2,16]{1,0:T(2,128)}, u32[]{:S(2)}) copy-start(s32[2,16]{1,0:T(2,128)} %tile_ref.1) | copy-start | bytes 388
  15.3 1.3 %copy-start.1 = (f32[256,2048]{1,0:T(8,128)}, f32[256,2048]{1,0:T(8,128)S(1)}, u32[]{:S(2)}) copy-start(f32[256,2048]{1,0:T(8,128)S(1)} %shard_map.115.refs_2_) | copy-start | bytes 6291460
  16.6 11.2 %copy-start = (bf16[256,2048]{1,0:T(8,128)(2,1)S(1)}, bf16[256,2048]{1,0:T(8,128)(2,1)}, u32[]{:S(2)}) copy-start(bf16[256,2048]{1,0:T(8,128)(2,1)} %q_ref.7) | copy-start | bytes 3145732
  18.9 1.2 %copy-start.3 = (f32[7,256,256]{2,1,0:T(8,128)}, f32[7,256,256]{2,1,0:T(8,128)S(1)}, u32[]{:S(2)}) copy-start(f32[7,256,256]{2,1,0:T(8,128)S(1)} %get-tuple-element.48.bias_ref) | copy-start | bytes 5505028
  20.9 0.7 copy-start.17
  21.6 0.9 copy-start.18
  22.6 0.8 copy-start.11
  23.5 4.4 %collective-permute-start.5 = (bf16[4,256,512]{2,1,0:T(8,128)(2,1)S(1)}, bf16[4,256,512]{2,1,0:T(8,128)(2,1)S(1)}, u32[]{:S(2)}, u32[]{:S(2)}) collective-permute-start(bf16[4,256,512]{2,1,0:T(8,128)(2,1)S(1)} %shard_map.114.near_ref), channel_id=1, source_target_pairs={{0,4},{4,0},{8,12},{12,8},{16,20},{20,16},{24,28},{28,24},{1,5},{5... | collective-permute-start | bytes 3145736 | tf_op jit(solution)/shard_map/ppermute | solution.py:481
  23.5 19.3 %collective-permute-start.7 = (bf16[256,1280]{1,0:T(8,128)(2,1)}, bf16[256,1280]{1,0:T(8,128)(2,1)}, u32[]{:S(2)}, u32[]{:S(2)}) collective-permute-start(bf16[256,1280]{1,0:T(8,128)(2,1)} %copy-done.11), channel_id=1, source_target_pairs={{1,2},{2,1},{5,6},{6,5},{9,10},{10,9},{13,14},{14,13},{17,18},{18,... | collective-permute-start | bytes 1966088 | tf_op jit(solution)/shard_map/ppermute | solution.py:478
  25.7 30.3 %collective-permute-start.6 = (bf16[256,1280]{1,0:T(8,128)(2,1)}, bf16[256,1280]{1,0:T(8,128)(2,1)}, u32[]{:S(2)}, u32[]{:S(2)}) collective-permute-start(bf16[256,1280]{1,0:T(8,128)(2,1)} %collective-permute-done.4.refs_1_), channel_id=1, source_target_pairs={{1,0},{2,3},{5,4},{6,7},{9,8},{10,11},{13,12},{14,15},{17,16},{18,... | collective-permute-start | bytes 1966088 | tf_op jit(solution)/shard_map/ppermute | solution.py:478
  27.9 1.5 %copy-start.4 = (f32[7,256,256]{2,1,0:T(8,128)S(1)}, f32[7,256,256]{2,1,0:T(8,128)}, u32[]{:S(2)}) copy-start(f32[7,256,256]{2,1,0:T(8,128)} %copy-done.3) | copy-start | bytes 5505028
  29.4 15.7 %copy-start.22 = (s32[7]{0:T(128)S(1)}, s32[7]{0:T(128)}, u32[]{:S(2)}) copy-start(s32[7]{0:T(128)} %constant.98.clone) | copy-start | bytes 88
  42.8 21.7 %collective-permute-start.8 = (bf16[256,1280]{1,0:T(8,128)(2,1)}, bf16[256,1280]{1,0:T(8,128)(2,1)}, u32[]{:S(2)}, u32[]{:S(2)}) collective-permute-start(bf16[256,1280]{1,0:T(8,128)(2,1)} %collective-permute-done.7.x2_ref), channel_id=1, source_target_pairs={{1,0},{2,3},{5,4},{6,7},{9,8},{10,11},{13,12},{14,15},{17,16},{18,... | collective-permute-start | bytes 1966088 | tf_op jit(solution)/shard_map/ppermute | solution.py:478
  45.0 1.5 %copy-start.5 = (f32[7,256,256]{2,1,0:T(8,128)S(1)}, f32[7,256,256]{2,1,0:T(8,128)}, u32[]{:S(2)}) copy-start(f32[7,256,256]{2,1,0:T(8,128)} %copy-done.3) | copy-start | bytes 5505028
  46.5 9.4 %copy-start.2 = (f32[256,2048]{1,0:T(8,128)S(1)}, f32[256,2048]{1,0:T(8,128)}, u32[]{:S(2)}) copy-start(f32[256,2048]{1,0:T(8,128)} %copy-done.1) | copy-start | bytes 6291460
  46.5 9.5 %copy-start.12 = (bf16[256,1280]{1,0:T(8,128)(2,1)S(1)}, bf16[256,1280]{1,0:T(8,128)(2,1)}, u32[]{:S(2)}) copy-start(bf16[256,1280]{1,0:T(8,128)(2,1)} %copy-done.11) | copy-start | bytes 1966084
  55.9 8.6 %slice-start = ((s8[7340032]{0:T(1024)(128)(4,1)}), s8[4194304]{0:T(1024)(128)(4,1)S(1)}, s32[]{:S(2)}) async-start(s8[7340032]{0:T(1024)(128)(4,1)} %bitcast.8), calls=%async_computation | async-start | bytes 8388608
  55.9 8.6 %slice-start.1 = ((s8[7340032]{0:T(1024)(128)(4,1)}), s8[3145728]{0:T(1024)(128)(4,1)S(1)}, s32[]{:S(2)}) async-start(s8[7340032]{0:T(1024)(128)(4,1)} %bitcast.8), calls=%async_computation.1 | async-start | bytes 6291456
  55.9 8.6 %copy-start.6 = (bf16[1024,1280]{1,0:T(8,128)(2,1)S(1)}, bf16[1024,1280]{1,0:T(8,128)(2,1)}, u32[]{:S(2)}) copy-start(bf16[1024,1280]{1,0:T(8,128)(2,1)} %get-tuple-element.53.w_ref) | copy-start | bytes 7864324
  55.9 8.6 %copy-start.8 = (f32[8,256,256]{2,1,0:T(8,128)S(1)}, f32[8,256,256]{2,1,0:T(8,128)}, u32[]{:S(2)}) copy-start(f32[8,256,256]{2,1,0:T(8,128)} %get-tuple-element.54.o_ref) | copy-start | bytes 6291460
  55.9 8.6 %copy-start.13 = (bf16[1792,128]{1,0:T(8,128)(2,1)S(1)}, bf16[1792,128]{1,0:T(8,128)(2,1)}, u32[]{:S(2)}) copy-start(bf16[1792,128]{1,0:T(8,128)(2,1)} %get-tuple-element.55.k_ref) | copy-start | bytes 1376260
  55.9 8.6 %copy-start.14 = (bf16[1792,128]{1,0:T(8,128)(2,1)S(1)}, bf16[1792,128]{1,0:T(8,128)(2,1)}, u32[]{:S(2)}) copy-start(bf16[1792,128]{1,0:T(8,128)(2,1)} %get-tuple-element.56.v_ref) | copy-start | bytes 1376260
  56.0 8.6 %copy-start.20 = (f32[256]{0:T(256)S(1)}, f32[256]{0:T(256)}, u32[]{:S(2)}) copy-start(f32[256]{0:T(256)} %param.10) | copy-start | bytes 3076
  64.5 8.2 %slice-start.2 = ((s8[7340032]{0:T(1024)(128)(4,1)}), s8[4194304]{0:T(1024)(128)(4,1)S(1)}, s32[]{:S(2)}) async-start(s8[7340032]{0:T(1024)(128)(4,1)} %bitcast.10), calls=%async_computation.2 | async-start | bytes 8388608
  64.6 8.1 %slice-start.3 = ((s8[7340032]{0:T(1024)(128)(4,1)}), s8[3145728]{0:T(1024)(128)(4,1)S(1)}, s32[]{:S(2)}) async-start(s8[7340032]{0:T(1024)(128)(4,1)} %bitcast.10), calls=%async_computation.3 | async-start | bytes 6291456
  64.6 8.1 %copy-start.7 = (bf16[1024,1280]{1,0:T(8,128)(2,1)S(1)}, bf16[1024,1280]{1,0:T(8,128)(2,1)}, u32[]{:S(2)}) copy-start(bf16[1024,1280]{1,0:T(8,128)(2,1)} %get-tuple-element.59.w_ref) | copy-start | bytes 7864324
  64.6 8.1 %copy-start.9 = (f32[8,256,256]{2,1,0:T(8,128)S(1)}, f32[8,256,256]{2,1,0:T(8,128)}, u32[]{:S(2)}) copy-start(f32[8,256,256]{2,1,0:T(8,128)} %get-tuple-element.60.o_ref) | copy-start | bytes 6291460
  64.6 8.1 %copy-start.15 = (bf16[1792,128]{1,0:T(8,128)(2,1)S(1)}, bf16[1792,128]{1,0:T(8,128)(2,1)}, u32[]{:S(2)}) copy-start(bf16[1792,128]{1,0:T(8,128)(2,1)} %get-tuple-element.61.k_ref) | copy-start | bytes 1376260
  64.7 8.1 %copy-start.16 = (bf16[1792,128]{1,0:T(8,128)(2,1)S(1)}, bf16[1792,128]{1,0:T(8,128)(2,1)}, u32[]{:S(2)}) copy-start(bf16[1792,128]{1,0:T(8,128)(2,1)} %get-tuple-element.62.v_ref) | copy-start | bytes 1376260
  71.9 9.0 %collective-permute-start.9 = (bf16[3,2,256,128]{3,2,1,0:T(8,128)(2,1)S(1)}, bf16[3,2,256,128]{3,2,1,0:T(8,128)(2,1)S(1)}, u32[]{:S(2)}, u32[]{:S(2)}) collective-permute-start(bf16[3,2,256,128]{3,2,1,0:T(8,128)(2,1)S(1)} %get-tuple-element.65), channel_id=1, source_target_pairs={{0,4},{4,0},{8,12},{12,8},{16,20},{20,16},{24,28},{28,24},{1,5},{5... | collective-permute-start | bytes 1179656 | tf_op jit(solution)/shard_map/ppermute | solution.py:481
  79.6 8.9 %collective-permute-start.13 = (bf16[3,2,256,128]{3,2,1,0:T(8,128)(2,1)S(1)}, bf16[3,2,256,128]{3,2,1,0:T(8,128)(2,1)S(1)}, u32[]{:S(2)}, u32[]{:S(2)}) collective-permute-start(bf16[3,2,256,128]{3,2,1,0:T(8,128)(2,1)S(1)} %get-tuple-element.71), channel_id=1, source_target_pairs={{0,4},{4,0},{8,12},{12,8},{16,20},{20,16},{24,28},{28,24},{1,5},{5... | collective-permute-start | bytes 1179656 | tf_op jit(solution)/shard_map/ppermute | solution.py:481
  80.9 10.6 %collective-permute-start.10 = (bf16[2,256,128]{2,1,0:T(8,128)(2,1)S(1)}, bf16[2,256,128]{2,1,0:T(8,128)(2,1)S(1)}, u32[]{:S(2)}, u32[]{:S(2)}) collective-permute-start(bf16[2,256,128]{2,1,0:T(8,128)(2,1)S(1)} %get-tuple-element.68), channel_id=1, source_target_pairs={{0,8},{4,12},{8,0},{12,4},{16,24},{20,28},{24,16},{28,20},{1,9},{5... | collective-permute-start | bytes 393224 | tf_op jit(solution)/shard_map/ppermute | solution.py:481
  81.0 14.1 %collective-permute-start.11 = (bf16[2,256,128]{2,1,0:T(8,128)(2,1)S(1)}, bf16[2,256,128]{2,1,0:T(8,128)(2,1)S(1)}, u32[]{:S(2)}, u32[]{:S(2)}) collective-permute-start(bf16[2,256,128]{2,1,0:T(8,128)(2,1)S(1)} %get-tuple-element.69), channel_id=1, source_target_pairs={{0,16},{4,20},{8,24},{12,28},{16,0},{20,4},{24,8},{28,12},{1,17},{... | collective-permute-start | bytes 393224 | tf_op jit(solution)/shard_map/ppermute | solution.py:481
  87.8 7.9 %collective-permute-start.12 = (bf16[2,256,128]{2,1,0:T(8,128)(2,1)S(1)}, bf16[2,256,128]{2,1,0:T(8,128)(2,1)S(1)}, u32[]{:S(2)}, u32[]{:S(2)}) collective-permute-start(bf16[2,256,128]{2,1,0:T(8,128)(2,1)S(1)} %get-tuple-element.70), channel_id=1, source_target_pairs={{0,24},{4,28},{8,16},{12,20},{16,8},{20,12},{24,0},{28,4},{1,25},{... | collective-permute-start | bytes 393224 | tf_op jit(solution)/shard_map/ppermute | solution.py:481
  88.7 7.8 %collective-permute-start.14 = (bf16[2,256,128]{2,1,0:T(8,128)(2,1)S(1)}, bf16[2,256,128]{2,1,0:T(8,128)(2,1)S(1)}, u32[]{:S(2)}, u32[]{:S(2)}) collective-permute-start(bf16[2,256,128]{2,1,0:T(8,128)(2,1)S(1)} %get-tuple-element.74), channel_id=1, source_target_pairs={{0,8},{4,12},{8,0},{12,4},{16,24},{20,28},{24,16},{28,20},{1,9},{5... | collective-permute-start | bytes 393224 | tf_op jit(solution)/shard_map/ppermute | solution.py:481
  89.5 9.5 %collective-permute-start.15 = (bf16[2,256,128]{2,1,0:T(8,128)(2,1)S(1)}, bf16[2,256,128]{2,1,0:T(8,128)(2,1)S(1)}, u32[]{:S(2)}, u32[]{:S(2)}) collective-permute-start(bf16[2,256,128]{2,1,0:T(8,128)(2,1)S(1)} %get-tuple-element.75), channel_id=1, source_target_pairs={{0,16},{4,20},{8,24},{12,28},{16,0},{20,4},{24,8},{28,12},{1,17},{... | collective-permute-start | bytes 393224 | tf_op jit(solution)/shard_map/ppermute | solution.py:481
  91.5 8.9 %collective-permute-start.16 = (bf16[2,256,128]{2,1,0:T(8,128)(2,1)S(1)}, bf16[2,256,128]{2,1,0:T(8,128)(2,1)S(1)}, u32[]{:S(2)}, u32[]{:S(2)}) collective-permute-start(bf16[2,256,128]{2,1,0:T(8,128)(2,1)S(1)} %get-tuple-element.76), channel_id=1, source_target_pairs={{0,24},{4,28},{8,16},{12,20},{16,8},{20,12},{24,0},{28,4},{1,25},{... | collective-permute-start | bytes 393224 | tf_op jit(solution)/shard_map/ppermute | solution.py:481

commit v9 on v8

--- a/solution.py
+++ b/solution.py
@@ -346,6 +346,8 @@
             pltpu.VMEM((CHUNK * KB, SHARE * rows), BF16),
             pltpu.VMEM((HD, SHARE * rows), F32),
         ],
+        flops=10 * SHARE * rows * n_kb * KB * HD,
+        size=SHARE * rows * n_kb * KB * 2,
     )
 
 
@@ -543,31 +545,29 @@
     if fast:
         acc, soft[-1][2] = lax.optimization_barrier((acc, soft[-1][2]))
         acc = project_call(jnp.stack([z ^ 1, second, edge]), [up_a, up_c], weight, acc, up_f)
-    outs = []
+    outs, final, turn = [], [], edge[None]
     for g in range(groups):
         probs, attn, keys, values, w_last = soft[g]
         outs.append(
             back_call(
-                g, live, pos.astype(jnp.int32), edge[None], acc, x1, x2, w_last, advantage[None, :], attn,
-                query_heads, keys, values, probs, n_kb, n_send,
+                g, live, pos.astype(jnp.int32), turn, acc, x1, x2, w_last, advantage[None, :],
+                attn, query_heads, keys, values, probs, n_kb, n_send,
             )
         )
-    grad_queries = jnp.concatenate([dq for dq, _, _ in outs], axis=1)
-
-    if fast:
-        final = []
-        shape = (2, KB, HD)
-        for _, send, keep in outs:
+        if fast:
+            block = (2, KB, HD)
+            send, *final = lax.optimization_barrier((outs[g][1], *final))
             base, to_x, to_y, to_d = call(
                 middle_kernel,
-                (me[None], flip(send, 1), keep),
+                (me[None], flip(send, 1), outs[g][2]),
                 [SMEM, VMEM, VMEM],
-                [(shape, F32), (shape, BF16), (shape, BF16), (shape, BF16)],
+                [(block, F32), (block, BF16), (block, BF16), (block, BF16)],
             )
-            by_y = flip(to_y, 4)
-            by_d = flip(to_d, 6)
-            by_x = flip(to_x, 2)
-            final += [base, by_x, by_y, by_d]
+            base, turn = lax.optimization_barrier((base, turn))
+            final += [base, flip(to_x, 2), flip(to_y, 4), flip(to_d, 6)]
+    grad_queries = jnp.concatenate([dq for dq, _, _ in outs], axis=1)
+
+    if fast:
         grad_keys, grad_values = call(
             functools.partial(last_kernel, groups),
             [me[None]] + final,

time: 102 us -> 103 us (level)
  waiting for transfers between devices: 11.1 us -> 12.9 us
    ppermute x12, waiting for transfers between devices: 6.85 us -> 8.66 us  [flip(): return lax.ppermute(value, 'ctx', [(i, i ^ bit) for i in range(n_ctx)])]
    unnamed x54 -> x52, local copies, waits for them, and re-layouts: 9.2 us -> 9.2 us
  transfers between devices with their start and end apart: 17 -> 17, of which waited for: 7 -> 6; matrix products, arithmetic and copies ran while one was open for 1% -> 1% of each run, Pallas kernels for 41% -> 40%
where the time goes in v9:
time: 103 us; the launch traced here: 102 us
  Pallas kernels  49.3 us (48%)
  starting transfers between devices  28.7 us (28%)
  waiting for transfers between devices  12.9 us (13%)
  local copies, waits for them, and re-layouts  9.2 us (9%)
  other arithmetic  1.15 us (1%)
  between operations  1.05 us (1%)
    pallas_call x12, Pallas kernels, call(): pl.pallas_call(kernel, in_specs=in_specs, out_specs=out_specs or [VMEM] *...  49.3 us
    ppermute x12, starting transfers between devices, flip(): return lax.ppermute(value, 'ctx', [(i, i ^ bit) for i in range(n_ctx)])  17.2 us
    ppermute x5, starting transfers between devices, hop(): return lax.ppermute(value, 'tp', pairs)  11.6 us
    unnamed x52, local copies, waits for them, and re-layouts  9.2 us
    ppermute x12, waiting for transfers between devices, flip(): return lax.ppermute(value, 'ctx', [(i, i ^ bit) for i in range(n_ctx)])  8.66 us
    ppermute x5, waiting for transfers between devices, hop(): return lax.ppermute(value, 'tp', pairs)  4.22 us
  transfers between devices with their start and end apart: 17, of which 6 were waited for; matrix products, arithmetic and copies ran while one was open for 1% of the time, Pallas kernels for 40%

profile of v9, /device:TPU:10, one launch (start us, length us, event | category | flops | bytes accessed | tf_op | source)
XLA Modules:
  0.0 102.3 jit_solution(2347378638256044964)
XLA Ops:
  0.6 0.5 collective-permute-start.3
  1.1 4.6 %collective-permute-start.4 = (bf16[256,1280]{1,0:T(8,128)(2,1)}, bf16[256,1280]{1,0:T(8,128)(2,1)}, u32[]{:S(2)}, u32[]{:S(2)}) collective-permute-start(bf16[256,1280]{1,0:T(8,128)(2,1)} %refs_0_.1), channel_id=1, source_target_pairs={{1,2},{2,1},{5,6},{6,5},{9,10},{10,9},{13,14},{14,13},{17,18},{18,... | collective-permute-start | bytes 1966088 | tf_op jit(solution)/shard_map/ppermute | solution.py:480
  5.8 1.0 shard_map.113.refs_0_
  6.7 0.6 collective-permute-start
  7.3 1.5 %collective-permute-start.1 = (bf16[256,512]{1,0:T(8,128)(2,1)S(1)}, bf16[256,512]{1,0:T(8,128)(2,1)S(1)}, u32[]{:S(2)}, u32[]{:S(2)}) collective-permute-start(bf16[256,512]{1,0:T(8,128)(2,1)S(1)} %shard_map.113.refs_0_), channel_id=1, source_target_pairs={{0,16},{4,20},{8,24},{12,28},{16,0},{20,4},{24,8},{28,12},{1,17},{... | collective-permute-start | bytes 786440 | tf_op jit(solution)/shard_map/ppermute | solution.py:483
  8.9 1.4 %collective-permute-start.2 = (bf16[256,512]{1,0:T(8,128)(2,1)S(1)}, bf16[256,512]{1,0:T(8,128)(2,1)S(1)}, u32[]{:S(2)}, u32[]{:S(2)}) collective-permute-start(bf16[256,512]{1,0:T(8,128)(2,1)S(1)} %shard_map.113.refs_0_), channel_id=1, source_target_pairs={{0,24},{4,28},{8,16},{12,20},{16,8},{20,12},{24,0},{28,4},{1,25},{... | collective-permute-start | bytes 786440 | tf_op jit(solution)/shard_map/ppermute | solution.py:483
  10.3 1.1 %copy-done.11 = bf16[256,1280]{1,0:T(8,128)(2,1)S(1)} copy-done((bf16[256,1280]{1,0:T(8,128)(2,1)S(1)}, bf16[256,1280]{1,0:T(8,128)(2,1)}, u32[]{:S(2)}) %copy-start.11) | copy-done | bytes 655384
  11.4 3.9 %shard_map.115.refs_2_ = f32[256,2048]{1,0:T(8,128)S(1)} custom-call(s32[1]{0:T(128)} %bitcast.5.shard_ref, bf16[2048,5120]{1,0:T(8,128)(2,1)} %w_ref.7, bf16[256,1280]{1,0:T(8,128)(2,1)S(1)} %copy-done.11), custom_call_target="tpu_custom_call" | custom-call | tf_op jit(solution)/shard_map/pallas_call | solution.py:48
  15.3 1.3 %copy-done.1 = f32[256,2048]{1,0:T(8,128)} copy-done((f32[256,2048]{1,0:T(8,128)}, f32[256,2048]{1,0:T(8,128)S(1)}, u32[]{:S(2)}) %copy-start.1) | copy-done | bytes 2097176
  16.6 2.3 %shard_map.112 = (f32[7,256,256]{2,1,0:T(8,128)S(1)}, s32[7]{0:T(128)S(1)}) custom-call(s32[1]{0:T(128)} %bitcast.me_ref, s32[8,1,256]{2,1,0:T(1,128)S(1)} %bitcast.10, s32[2,16]{1,0:T(2,128)S(1)} %copy-done.22), custom_call_target="tpu_custom_call" | custom-call | bytes 1835008 | tf_op jit(solution)/shard_map/pallas_call | solution.py:48
  19.0 1.2 %copy-done.3 = f32[7,256,256]{2,1,0:T(8,128)} copy-done((f32[7,256,256]{2,1,0:T(8,128)}, f32[7,256,256]{2,1,0:T(8,128)S(1)}, u32[]{:S(2)}) %copy-start.3) | copy-done | bytes 1835032
  20.2 0.7 collective-permute-done.2.refs_3_
  20.9 0.7 copy-done.18
  21.6 0.9 copy-done.19
  22.5 0.1 shard_map.114.near_ref
  22.6 0.0 collective-permute-done.3.refs_0_
  22.6 0.0 copy-start.12
  22.6 0.8 copy-done.12
  23.5 0.0 collective-permute-start.5
  23.5 2.2 %collective-permute-start.7 = (bf16[256,1280]{1,0:T(8,128)(2,1)}, bf16[256,1280]{1,0:T(8,128)(2,1)}, u32[]{:S(2)}, u32[]{:S(2)}) collective-permute-start(bf16[256,1280]{1,0:T(8,128)(2,1)} %copy-done.12), channel_id=1, source_target_pairs={{1,2},{2,1},{5,6},{6,5},{9,10},{10,9},{13,14},{14,13},{17,18},{18,... | collective-permute-start | bytes 1966088 | tf_op jit(solution)/shard_map/ppermute | solution.py:480
  25.7 2.2 %collective-permute-start.6 = (bf16[256,1280]{1,0:T(8,128)(2,1)}, bf16[256,1280]{1,0:T(8,128)(2,1)}, u32[]{:S(2)}, u32[]{:S(2)}) collective-permute-start(bf16[256,1280]{1,0:T(8,128)(2,1)} %collective-permute-done.4.refs_1_), channel_id=1, source_target_pairs={{1,0},{2,3},{5,4},{6,7},{9,8},{10,11},{13,12},{14,15},{17,16},{18,... | collective-permute-start | bytes 1966088 | tf_op jit(solution)/shard_map/ppermute | solution.py:480
  27.9 1.5 %copy-done.4 = f32[7,256,256]{2,1,0:T(8,128)S(1)} copy-done((f32[7,256,256]{2,1,0:T(8,128)S(1)}, f32[7,256,256]{2,1,0:T(8,128)}, u32[]{:S(2)}) %copy-start.4) | copy-done | bytes 1835032
  29.4 9.2 %shard_map.118 = (bf16[8,1792,256]{2,1,0:T(8,128)(2,1)}, f32[8,256,256]{2,1,0:T(8,128)}, bf16[1792,128]{1,0:T(8,128)(2,1)}, bf16[1792,128]{1,0:T(8,128)(2,1)}, bf16[1024,1280]{1,0:T(8,128)(2,1)}) custom-call(s32[7]{0:T(128)S(1)} %fusion.1.slot_ref, s32[1]{0:T(128)} %bitcast.6.shard_ref, bf16[2048,5120]{1,0:T(8,128)(2,1)} %w_ref.7, ...), custom_call_target="tpu_custom_call" | custom-call | tf_op jit(solution)/shard_map/pallas_call | solution.py:48
  38.6 4.2 %collective-permute-done.7.x2_ref = bf16[256,1280]{1,0:T(8,128)(2,1)} collective-permute-done((bf16[256,1280]{1,0:T(8,128)(2,1)}, bf16[256,1280]{1,0:T(8,128)(2,1)}, u32[]{:S(2)}, u32[]{:S(2)}) %collective-permute-start.7) | collective-permute-done | bytes 655392 | tf_op jit(solution)/shard_map/ppermute | solution.py:480
  42.8 2.1 %collective-permute-start.8 = (bf16[256,1280]{1,0:T(8,128)(2,1)}, bf16[256,1280]{1,0:T(8,128)(2,1)}, u32[]{:S(2)}, u32[]{:S(2)}) collective-permute-start(bf16[256,1280]{1,0:T(8,128)(2,1)} %collective-permute-done.7.x2_ref), channel_id=1, source_target_pairs={{1,0},{2,3},{5,4},{6,7},{9,8},{10,11},{13,12},{14,15},{17,16},{18,... | collective-permute-start | bytes 1966088 | tf_op jit(solution)/shard_map/ppermute | solution.py:480
  44.9 0.1 pad_add_fusion.shard_ref
  45.0 1.5 %copy-done.5 = f32[7,256,256]{2,1,0:T(8,128)S(1)} copy-done((f32[7,256,256]{2,1,0:T(8,128)S(1)}, f32[7,256,256]{2,1,0:T(8,128)}, u32[]{:S(2)}) %copy-start.5) | copy-done | bytes 1835032
  46.5 9.3 %shard_map.116 = (bf16[8,1792,256]{2,1,0:T(8,128)(2,1)}, f32[8,256,256]{2,1,0:T(8,128)}, bf16[1792,128]{1,0:T(8,128)(2,1)}, bf16[1792,128]{1,0:T(8,128)(2,1)}, bf16[1024,1280]{1,0:T(8,128)(2,1)}) custom-call(s32[7]{0:T(128)S(1)} %fusion.1.slot_ref, s32[1]{0:T(128)} %bitcast.6.shard_ref, bf16[2048,5120]{1,0:T(8,128)(2,1)} %w_ref.7, ...), custom_call_target="tpu_custom_call" | custom-call | tf_op jit(solution)/shard_map/pallas_call | solution.py:48
  55.9 0.0 copy-start.21
  56.0 8.5 %shard_map.117.proj_ref = f32[256,2048]{1,0:T(8,128)S(1)} custom-call(s32[3]{0:T(128)S(1)} %pad_add_fusion.shard_ref, bf16[2048,5120]{1,0:T(8,128)(2,1)} %w_ref.7, bf16[256,1280]{1,0:T(8,128)(2,1)S(1)} %copy-done.13, bf16[256,1280]{1,0:T(8,128)(2,1)} %collective-permute-done.4.refs_1_, f32[256,2048]{1,0:T(8,128)S(1)} %copy-done.2, ...), custom_call_target="tpu_custom_call" | custom-call | tf_op jit(solution)/shard_map/pallas_call | solution.py:48
  64.6 7.2 %shard_map.119 = (bf16[256,1024]{1,0:T(8,128)(2,1)S(1)}, bf16[3,2,256,128]{3,2,1,0:T(8,128)(2,1)S(1)}, bf16[4,2,256,128]{3,2,1,0:T(8,128)(2,1)S(1)}) custom-call(s32[7]{0:T(128)S(1)} %get-tuple-element.49.live_ref, s32[7]{0:T(128)S(1)} %compare_select_fusion.5.pos_ref, s32[1]{0:T(128)} %bitcast.2.edge_ref, f32[256,2048]{1,0:T(8,128)S(1)} %shard_map.117.proj_ref, ...), custom_call_target="tpu_custom_call" | custom-call | flops 4697620480 | bytes 7340032 | tf_op jit(solution)/shard_map/pallas_call | solution.py:48
  71.8 0.9 collective-permute-start.9
  72.7 1.3 %collective-permute-done.9.got_ref = bf16[3,2,256,128]{3,2,1,0:T(8,128)(2,1)S(1)} collective-permute-done((bf16[3,2,256,128]{3,2,1,0:T(8,128)(2,1)S(1)}, bf16[3,2,256,128]{3,2,1,0:T(8,128)(2,1)S(1)}, u32[]{:S(2)}, u32[]{:S(2)}) %collective-permute-start.9) | collective-permute-done | bytes 393248 | tf_op jit(solution)/shard_map/ppermute | solution.py:483
  74.1 0.1 shard_map.120
  74.2 0.1 collective-permute-start.10
  74.2 4.6 %collective-permute-start.11 = (bf16[2,256,128]{2,1,0:T(8,128)(2,1)S(1)}, bf16[2,256,128]{2,1,0:T(8,128)(2,1)S(1)}, u32[]{:S(2)}, u32[]{:S(2)}) collective-permute-start(bf16[2,256,128]{2,1,0:T(8,128)(2,1)S(1)} %get-tuple-element.80), channel_id=1, source_target_pairs={{0,16},{4,20},{8,24},{12,28},{16,0},{20,4},{24,8},{28,12},{1,17},{... | collective-permute-start | bytes 393224 | tf_op jit(solution)/shard_map/ppermute | solution.py:483
  78.8 0.6 collective-permute-start.12
  79.5 6.8 %shard_map.121 = (bf16[256,1024]{1,0:T(8,128)(2,1)S(1)}, bf16[3,2,256,128]{3,2,1,0:T(8,128)(2,1)S(1)}, bf16[4,2,256,128]{3,2,1,0:T(8,128)(2,1)S(1)}) custom-call(s32[7]{0:T(128)S(1)} %get-tuple-element.49.live_ref, s32[7]{0:T(128)S(1)} %compare_select_fusion.5.pos_ref, s32[1]{0:T(128)} %bitcast.2.edge_ref, f32[256,2048]{1,0:T(8,128)S(1)} %shard_map.117.proj_ref, ...), custom_call_target="tpu_custom_call" | custom-call | flops 4697620480 | bytes 7340032 | tf_op jit(solution)/shard_map/pallas_call | solution.py:48
  86.4 0.8 collective-permute-start.13
  87.1 1.3 %collective-permute-done.13.got_ref = bf16[3,2,256,128]{3,2,1,0:T(8,128)(2,1)S(1)} collective-permute-done((bf16[3,2,256,128]{3,2,1,0:T(8,128)(2,1)S(1)}, bf16[3,2,256,128]{3,2,1,0:T(8,128)(2,1)S(1)}, u32[]{:S(2)}, u32[]{:S(2)}) %collective-permute-start.13) | collective-permute-done | bytes 393248 | tf_op jit(solution)/shard_map/ppermute | solution.py:483
  88.5 0.1 shard_map.122
  88.6 0.2 collective-permute-start.14
  88.7 5.1 %collective-permute-start.15 = (bf16[2,256,128]{2,1,0:T(8,128)(2,1)S(1)}, bf16[2,256,128]{2,1,0:T(8,128)(2,1)S(1)}, u32[]{:S(2)}, u32[]{:S(2)}) collective-permute-start(bf16[2,256,128]{2,1,0:T(8,128)(2,1)S(1)} %get-tuple-element.91), channel_id=1, source_target_pairs={{0,16},{4,20},{8,24},{12,28},{16,0},{20,4},{24,8},{28,12},{1,17},{... | collective-permute-start | bytes 393224 | tf_op jit(solution)/shard_map/ppermute | solution.py:483
  93.8 1.4 %collective-permute-start.16 = (bf16[2,256,128]{2,1,0:T(8,128)(2,1)S(1)}, bf16[2,256,128]{2,1,0:T(8,128)(2,1)S(1)}, u32[]{:S(2)}, u32[]{:S(2)}) collective-permute-start(bf16[2,256,128]{2,1,0:T(8,128)(2,1)S(1)} %get-tuple-element.92), channel_id=1, source_target_pairs={{0,24},{4,28},{8,16},{12,20},{16,8},{20,12},{24,0},{28,4},{1,25},{... | collective-permute-start | bytes 393224 | tf_op jit(solution)/shard_map/ppermute | solution.py:483
  95.2 1.1 %pad_maximum_fusion = bf16[256,2048]{1,0:T(8,128)(2,1)} fusion(bf16[256,1024]{1,0:T(8,128)(2,1)S(1)} %get-tuple-element.76, bf16[256,1024]{1,0:T(8,128)(2,1)S(1)} %get-tuple-element.66), kind=kLoop, calls=%fused_computation | loop fusion | flops 2097152 | bytes 2097152 | tf_op jit(solution)/shard_map/concatenate | solution.py:568
  96.3 3.4 %collective-permute-done.15.refs_6_ = bf16[2,256,128]{2,1,0:T(8,128)(2,1)S(1)} collective-permute-done((bf16[2,256,128]{2,1,0:T(8,128)(2,1)S(1)}, bf16[2,256,128]{2,1,0:T(8,128)(2,1)S(1)}, u32[]{:S(2)}, u32[]{:S(2)}) %collective-permute-start.15) | collective-permute-done | bytes 131104 | tf_op jit(solution)/shard_map/ppermute | solution.py:483
  99.7 1.8 %collective-permute-done.16.refs_7_ = bf16[2,256,128]{2,1,0:T(8,128)(2,1)S(1)} collective-permute-done((bf16[2,256,128]{2,1,0:T(8,128)(2,1)S(1)}, bf16[2,256,128]{2,1,0:T(8,128)(2,1)S(1)}, u32[]{:S(2)}, u32[]{:S(2)}) %collective-permute-start.16) | collective-permute-done | bytes 131104 | tf_op jit(solution)/shard_map/ppermute | solution.py:483
  101.5 0.8 shard_map.123
  (55 shorter events, 0.1 us)
Async XLA Ops:
  0.6 22.0 %collective-permute-start.3 = (bf16[256,1280]{1,0:T(8,128)(2,1)}, bf16[256,1280]{1,0:T(8,128)(2,1)S(1)}, u32[]{:S(2)}, u32[]{:S(2)}) collective-permute-start(bf16[256,1280]{1,0:T(8,128)(2,1)} %refs_0_.1), channel_id=1, source_target_pairs={{0,1},{1,0},{2,3},{3,2},{4,5},{5,4},{6,7},{7,6},{8,9},{9,8},{10,11... | collective-permute-start | bytes 1966088 | tf_op jit(solution)/shard_map/ppermute | solution.py:480
  1.1 21.5 %collective-permute-start.4 = (bf16[256,1280]{1,0:T(8,128)(2,1)}, bf16[256,1280]{1,0:T(8,128)(2,1)}, u32[]{:S(2)}, u32[]{:S(2)}) collective-permute-start(bf16[256,1280]{1,0:T(8,128)(2,1)} %refs_0_.1), channel_id=1, source_target_pairs={{1,2},{2,1},{5,6},{6,5},{9,10},{10,9},{13,14},{14,13},{17,18},{18,... | collective-permute-start | bytes 1966088 | tf_op jit(solution)/shard_map/ppermute | solution.py:480
  6.7 13.4 %collective-permute-start = (bf16[256,512]{1,0:T(8,128)(2,1)S(1)}, bf16[256,512]{1,0:T(8,128)(2,1)S(1)}, u32[]{:S(2)}, u32[]{:S(2)}) collective-permute-start(bf16[256,512]{1,0:T(8,128)(2,1)S(1)} %shard_map.113.refs_0_), channel_id=1, source_target_pairs={{0,8},{4,12},{8,0},{12,4},{16,24},{20,28},{24,16},{28,20},{1,9},{5... | collective-permute-start | bytes 786440 | tf_op jit(solution)/shard_map/ppermute | solution.py:483
  7.3 12.8 %collective-permute-start.1 = (bf16[256,512]{1,0:T(8,128)(2,1)S(1)}, bf16[256,512]{1,0:T(8,128)(2,1)S(1)}, u32[]{:S(2)}, u32[]{:S(2)}) collective-permute-start(bf16[256,512]{1,0:T(8,128)(2,1)S(1)} %shard_map.113.refs_0_), channel_id=1, source_target_pairs={{0,16},{4,20},{8,24},{12,28},{16,0},{20,4},{24,8},{28,12},{1,17},{... | collective-permute-start | bytes 786440 | tf_op jit(solution)/shard_map/ppermute | solution.py:483
  8.9 12.0 %collective-permute-start.2 = (bf16[256,512]{1,0:T(8,128)(2,1)S(1)}, bf16[256,512]{1,0:T(8,128)(2,1)S(1)}, u32[]{:S(2)}, u32[]{:S(2)}) collective-permute-start(bf16[256,512]{1,0:T(8,128)(2,1)S(1)} %shard_map.113.refs_0_), channel_id=1, source_target_pairs={{0,24},{4,28},{8,16},{12,20},{16,8},{20,12},{24,0},{28,4},{1,25},{... | collective-permute-start | bytes 786440 | tf_op jit(solution)/shard_map/ppermute | solution.py:483
  10.3 1.1 %copy-start.11 = (bf16[256,1280]{1,0:T(8,128)(2,1)S(1)}, bf16[256,1280]{1,0:T(8,128)(2,1)}, u32[]{:S(2)}) copy-start(bf16[256,1280]{1,0:T(8,128)(2,1)} %refs_0_.1) | copy-start | bytes 1966084
  11.4 5.2 %copy-start.20 = (s32[2048]{0:T(1024)S(1)}, s32[2048]{0:T(1024)}, u32[]{:S(2)}) copy-start(s32[2048]{0:T(1024)} %param.15) | copy-start | bytes 24580
  11.4 5.2 %copy-start.22 = (s32[2,16]{1,0:T(2,128)S(1)}, s32[2,16]{1,0:T(2,128)}, u32[]{:S(2)}) copy-start(s32[2,16]{1,0:T(2,128)} %tile_ref.1) | copy-start | bytes 388
  15.3 1.4 %copy-start.1 = (f32[256,2048]{1,0:T(8,128)}, f32[256,2048]{1,0:T(8,128)S(1)}, u32[]{:S(2)}) copy-start(f32[256,2048]{1,0:T(8,128)S(1)} %shard_map.115.refs_2_) | copy-start | bytes 6291460
  16.6 11.2 %copy-start = (bf16[256,2048]{1,0:T(8,128)(2,1)S(1)}, bf16[256,2048]{1,0:T(8,128)(2,1)}, u32[]{:S(2)}) copy-start(bf16[256,2048]{1,0:T(8,128)(2,1)} %q_ref.7) | copy-start | bytes 3145732
  18.9 1.2 %copy-start.3 = (f32[7,256,256]{2,1,0:T(8,128)}, f32[7,256,256]{2,1,0:T(8,128)S(1)}, u32[]{:S(2)}) copy-start(f32[7,256,256]{2,1,0:T(8,128)S(1)} %get-tuple-element.56.bias_ref) | copy-start | bytes 5505028
  20.9 0.7 copy-start.18
  21.6 0.9 copy-start.19
  22.6 0.8 copy-start.12
  23.5 4.4 %collective-permute-start.5 = (bf16[4,256,512]{2,1,0:T(8,128)(2,1)S(1)}, bf16[4,256,512]{2,1,0:T(8,128)(2,1)S(1)}, u32[]{:S(2)}, u32[]{:S(2)}) collective-permute-start(bf16[4,256,512]{2,1,0:T(8,128)(2,1)S(1)} %shard_map.114.near_ref), channel_id=1, source_target_pairs={{0,4},{4,0},{8,12},{12,8},{16,20},{20,16},{24,28},{28,24},{1,5},{5... | collective-permute-start | bytes 3145736 | tf_op jit(solution)/shard_map/ppermute | solution.py:483
  23.5 19.3 %collective-permute-start.7 = (bf16[256,1280]{1,0:T(8,128)(2,1)}, bf16[256,1280]{1,0:T(8,128)(2,1)}, u32[]{:S(2)}, u32[]{:S(2)}) collective-permute-start(bf16[256,1280]{1,0:T(8,128)(2,1)} %copy-done.12), channel_id=1, source_target_pairs={{1,2},{2,1},{5,6},{6,5},{9,10},{10,9},{13,14},{14,13},{17,18},{18,... | collective-permute-start | bytes 1966088 | tf_op jit(solution)/shard_map/ppermute | solution.py:480
  25.7 30.2 %collective-permute-start.6 = (bf16[256,1280]{1,0:T(8,128)(2,1)}, bf16[256,1280]{1,0:T(8,128)(2,1)}, u32[]{:S(2)}, u32[]{:S(2)}) collective-permute-start(bf16[256,1280]{1,0:T(8,128)(2,1)} %collective-permute-done.4.refs_1_), channel_id=1, source_target_pairs={{1,0},{2,3},{5,4},{6,7},{9,8},{10,11},{13,12},{14,15},{17,16},{18,... | collective-permute-start | bytes 1966088 | tf_op jit(solution)/shard_map/ppermute | solution.py:480
  27.9 1.5 %copy-start.4 = (f32[7,256,256]{2,1,0:T(8,128)S(1)}, f32[7,256,256]{2,1,0:T(8,128)}, u32[]{:S(2)}) copy-start(f32[7,256,256]{2,1,0:T(8,128)} %copy-done.3) | copy-start | bytes 5505028
  29.4 15.7 %copy-start.23 = (s32[7]{0:T(128)S(1)}, s32[7]{0:T(128)}, u32[]{:S(2)}) copy-start(s32[7]{0:T(128)} %constant.98.clone) | copy-start | bytes 88
  42.8 21.7 %collective-permute-start.8 = (bf16[256,1280]{1,0:T(8,128)(2,1)}, bf16[256,1280]{1,0:T(8,128)(2,1)}, u32[]{:S(2)}, u32[]{:S(2)}) collective-permute-start(bf16[256,1280]{1,0:T(8,128)(2,1)} %collective-permute-done.7.x2_ref), channel_id=1, source_target_pairs={{1,0},{2,3},{5,4},{6,7},{9,8},{10,11},{13,12},{14,15},{17,16},{18,... | collective-permute-start | bytes 1966088 | tf_op jit(solution)/shard_map/ppermute | solution.py:480
  45.0 1.5 %copy-start.5 = (f32[7,256,256]{2,1,0:T(8,128)S(1)}, f32[7,256,256]{2,1,0:T(8,128)}, u32[]{:S(2)}) copy-start(f32[7,256,256]{2,1,0:T(8,128)} %copy-done.3) | copy-start | bytes 5505028
  46.5 9.4 %copy-start.2 = (f32[256,2048]{1,0:T(8,128)S(1)}, f32[256,2048]{1,0:T(8,128)}, u32[]{:S(2)}) copy-start(f32[256,2048]{1,0:T(8,128)} %copy-done.1) | copy-start | bytes 6291460
  46.5 9.4 %copy-start.13 = (bf16[256,1280]{1,0:T(8,128)(2,1)S(1)}, bf16[256,1280]{1,0:T(8,128)(2,1)}, u32[]{:S(2)}) copy-start(bf16[256,1280]{1,0:T(8,128)(2,1)} %copy-done.12) | copy-start | bytes 1966084
  55.9 8.6 %slice-start = ((s8[7340032]{0:T(1024)(128)(4,1)}), s8[4194304]{0:T(1024)(128)(4,1)S(1)}, s32[]{:S(2)}) async-start(s8[7340032]{0:T(1024)(128)(4,1)} %bitcast.8), calls=%async_computation | async-start | bytes 8388608
  55.9 8.6 %slice-start.1 = ((s8[7340032]{0:T(1024)(128)(4,1)}), s8[3145728]{0:T(1024)(128)(4,1)S(1)}, s32[]{:S(2)}) async-start(s8[7340032]{0:T(1024)(128)(4,1)} %bitcast.8), calls=%async_computation.1 | async-start | bytes 6291456
  55.9 8.6 %copy-start.7 = (bf16[1024,1280]{1,0:T(8,128)(2,1)S(1)}, bf16[1024,1280]{1,0:T(8,128)(2,1)}, u32[]{:S(2)}) copy-start(bf16[1024,1280]{1,0:T(8,128)(2,1)} %get-tuple-element.61.w_ref) | copy-start | bytes 7864324
  55.9 8.6 %copy-start.9 = (f32[8,256,256]{2,1,0:T(8,128)S(1)}, f32[8,256,256]{2,1,0:T(8,128)}, u32[]{:S(2)}) copy-start(f32[8,256,256]{2,1,0:T(8,128)} %get-tuple-element.62.o_ref) | copy-start | bytes 6291460
  55.9 8.6 %copy-start.14 = (bf16[1792,128]{1,0:T(8,128)(2,1)S(1)}, bf16[1792,128]{1,0:T(8,128)(2,1)}, u32[]{:S(2)}) copy-start(bf16[1792,128]{1,0:T(8,128)(2,1)} %get-tuple-element.63.k_ref) | copy-start | bytes 1376260
  55.9 8.6 %copy-start.15 = (bf16[1792,128]{1,0:T(8,128)(2,1)S(1)}, bf16[1792,128]{1,0:T(8,128)(2,1)}, u32[]{:S(2)}) copy-start(bf16[1792,128]{1,0:T(8,128)(2,1)} %get-tuple-element.64.v_ref) | copy-start | bytes 1376260
  55.9 8.6 %copy-start.21 = (f32[256]{0:T(256)S(1)}, f32[256]{0:T(256)}, u32[]{:S(2)}) copy-start(f32[256]{0:T(256)} %param.10) | copy-start | bytes 3076
  64.6 14.9 %copy-start.6 = (bf16[8,1792,256]{2,1,0:T(8,128)(2,1)S(1)}, bf16[8,1792,256]{2,1,0:T(8,128)(2,1)}, u32[]{:S(2)}) copy-start(bf16[8,1792,256]{2,1,0:T(8,128)(2,1)} %get-tuple-element.75.p_ref) | copy-start | bytes 22020100
  64.6 14.9 %copy-start.8 = (bf16[1024,1280]{1,0:T(8,128)(2,1)S(1)}, bf16[1024,1280]{1,0:T(8,128)(2,1)}, u32[]{:S(2)}) copy-start(bf16[1024,1280]{1,0:T(8,128)(2,1)} %get-tuple-element.71.w_ref) | copy-start | bytes 7864324
  64.6 14.9 %copy-start.10 = (f32[8,256,256]{2,1,0:T(8,128)S(1)}, f32[8,256,256]{2,1,0:T(8,128)}, u32[]{:S(2)}) copy-start(f32[8,256,256]{2,1,0:T(8,128)} %get-tuple-element.72.o_ref) | copy-start | bytes 6291460
  64.6 14.9 %copy-start.16 = (bf16[1792,128]{1,0:T(8,128)(2,1)S(1)}, bf16[1792,128]{1,0:T(8,128)(2,1)}, u32[]{:S(2)}) copy-start(bf16[1792,128]{1,0:T(8,128)(2,1)} %get-tuple-element.73.k_ref) | copy-start | bytes 1376260
  64.6 14.9 %copy-start.17 = (bf16[1792,128]{1,0:T(8,128)(2,1)S(1)}, bf16[1792,128]{1,0:T(8,128)(2,1)}, u32[]{:S(2)}) copy-start(bf16[1792,128]{1,0:T(8,128)(2,1)} %get-tuple-element.74.v_ref) | copy-start | bytes 1376260
  71.8 2.3 %collective-permute-start.9 = (bf16[3,2,256,128]{3,2,1,0:T(8,128)(2,1)S(1)}, bf16[3,2,256,128]{3,2,1,0:T(8,128)(2,1)S(1)}, u32[]{:S(2)}, u32[]{:S(2)}) collective-permute-start(bf16[3,2,256,128]{3,2,1,0:T(8,128)(2,1)S(1)} %get-tuple-element.67), channel_id=1, source_target_pairs={{0,4},{4,0},{8,12},{12,8},{16,20},{20,16},{24,28},{28,24},{1,5},{5... | collective-permute-start | bytes 1179656 | tf_op jit(solution)/shard_map/ppermute | solution.py:483
  74.2 12.2 %collective-permute-start.10 = (bf16[2,256,128]{2,1,0:T(8,128)(2,1)S(1)}, bf16[2,256,128]{2,1,0:T(8,128)(2,1)S(1)}, u32[]{:S(2)}, u32[]{:S(2)}) collective-permute-start(bf16[2,256,128]{2,1,0:T(8,128)(2,1)S(1)} %get-tuple-element.79), channel_id=1, source_target_pairs={{0,8},{4,12},{8,0},{12,4},{16,24},{20,28},{24,16},{28,20},{1,9},{5... | collective-permute-start | bytes 393224 | tf_op jit(solution)/shard_map/ppermute | solution.py:483
  74.2 12.1 %collective-permute-start.11 = (bf16[2,256,128]{2,1,0:T(8,128)(2,1)S(1)}, bf16[2,256,128]{2,1,0:T(8,128)(2,1)S(1)}, u32[]{:S(2)}, u32[]{:S(2)}) collective-permute-start(bf16[2,256,128]{2,1,0:T(8,128)(2,1)S(1)} %get-tuple-element.80), channel_id=1, source_target_pairs={{0,16},{4,20},{8,24},{12,28},{16,0},{20,4},{24,8},{28,12},{1,17},{... | collective-permute-start | bytes 393224 | tf_op jit(solution)/shard_map/ppermute | solution.py:483
  78.8 7.5 %collective-permute-start.12 = (bf16[2,256,128]{2,1,0:T(8,128)(2,1)S(1)}, bf16[2,256,128]{2,1,0:T(8,128)(2,1)S(1)}, u32[]{:S(2)}, u32[]{:S(2)}) collective-permute-start(bf16[2,256,128]{2,1,0:T(8,128)(2,1)S(1)} %get-tuple-element.81), channel_id=1, source_target_pairs={{0,24},{4,28},{8,16},{12,20},{16,8},{20,12},{24,0},{28,4},{1,25},{... | collective-permute-start | bytes 393224 | tf_op jit(solution)/shard_map/ppermute | solution.py:483
  86.4 2.1 %collective-permute-start.13 = (bf16[3,2,256,128]{3,2,1,0:T(8,128)(2,1)S(1)}, bf16[3,2,256,128]{3,2,1,0:T(8,128)(2,1)S(1)}, u32[]{:S(2)}, u32[]{:S(2)}) collective-permute-start(bf16[3,2,256,128]{3,2,1,0:T(8,128)(2,1)S(1)} %get-tuple-element.86), channel_id=1, source_target_pairs={{0,4},{4,0},{8,12},{12,8},{16,20},{20,16},{24,28},{28,24},{1,5},{5... | collective-permute-start | bytes 1179656 | tf_op jit(solution)/shard_map/ppermute | solution.py:483
  88.6 7.7 %collective-permute-start.14 = (bf16[2,256,128]{2,1,0:T(8,128)(2,1)S(1)}, bf16[2,256,128]{2,1,0:T(8,128)(2,1)S(1)}, u32[]{:S(2)}, u32[]{:S(2)}) collective-permute-start(bf16[2,256,128]{2,1,0:T(8,128)(2,1)S(1)} %get-tuple-element.90), channel_id=1, source_target_pairs={{0,8},{4,12},{8,0},{12,4},{16,24},{20,28},{24,16},{28,20},{1,9},{5... | collective-permute-start | bytes 393224 | tf_op jit(solution)/shard_map/ppermute | solution.py:483
  88.7 10.9 %collective-permute-start.15 = (bf16[2,256,128]{2,1,0:T(8,128)(2,1)S(1)}, bf16[2,256,128]{2,1,0:T(8,128)(2,1)S(1)}, u32[]{:S(2)}, u32[]{:S(2)}) collective-permute-start(bf16[2,256,128]{2,1,0:T(8,128)(2,1)S(1)} %get-tuple-element.91), channel_id=1, source_target_pairs={{0,16},{4,20},{8,24},{12,28},{16,0},{20,4},{24,8},{28,12},{1,17},{... | collective-permute-start | bytes 393224 | tf_op jit(solution)/shard_map/ppermute | solution.py:483
  93.8 7.7 %collective-permute-start.16 = (bf16[2,256,128]{2,1,0:T(8,128)(2,1)S(1)}, bf16[2,256,128]{2,1,0:T(8,128)(2,1)S(1)}, u32[]{:S(2)}, u32[]{:S(2)}) collective-permute-start(bf16[2,256,128]{2,1,0:T(8,128)(2,1)S(1)} %get-tuple-element.92), channel_id=1, source_target_pairs={{0,24},{4,28},{8,16},{12,20},{16,8},{20,12},{24,0},{28,4},{1,25},{... | collective-permute-start | bytes 393224 | tf_op jit(solution)/shard_map/ppermute | solution.py:483
